TPU v7x, 32 devices: a whole 2x2x4 slice. The times are simulated.
32 devices in a mesh: wide: 16 (over z, y, core), narrow: 2 (over x).
Axes of the slice: x: 2, y: 2, z: 4, core: 2. Of those that a mesh axis runs over, the one named last changes fastest.
Arguments:
- text_in: bfloat16 [32, 64, 768], P(('wide', 'narrow')), may hold values from -6 to 6
- image_in: bfloat16 [32, 144, 1024], P(('wide', 'narrow')), may hold values from -6 to 6
- text_segments: int32 [32, 64], P(('wide', 'narrow')), may hold values from 0 to 1, as said below
- text_co_in: bfloat16 [1, 768, 3072], P(None, ('wide', 'narrow')), may hold values from -0.21875 to 0.21875
- text_co_out: bfloat16 [1, 1024, 768], P(None, ('wide', 'narrow')), may hold values from -1.5 to 1.5
- image_co_in: bfloat16 [1, 1024, 3072], P(None, ('wide', 'narrow')), may hold values from -0.1875 to 0.1875
- image_co_out: bfloat16 [1, 1024, 1024], P(None, ('wide', 'narrow')), may hold values from -1 to 1
- text_self_in: bfloat16 [1, 768, 2304], P(None, ('wide', 'narrow')), may hold values from -0.21875 to 0.21875
- text_self_out: bfloat16 [1, 768, 768], P(None, ('wide', 'narrow')), may hold values from -1.25 to 1.25
- image_self_in: bfloat16 [1, 1024, 3072], P(None, ('wide', 'narrow')), may hold values from -0.1875 to 0.1875
- image_self_out: bfloat16 [1, 1024, 1024], P(None, ('wide', 'narrow')), may hold values from -1.5 to 1.5
- text_up: bfloat16 [1, 2, 768, 3072], P(None, None, ('wide', 'narrow')), may hold values from -0.21875 to 0.21875
- text_down: bfloat16 [1, 2, 3072, 768], P(None, None, ('wide', 'narrow')), may hold values from -0.109375 to 0.109375
- image_up: bfloat16 [1, 2, 1024, 1024], P(None, None, ('wide', 'narrow')), may hold values from -0.1875 to 0.1875
- image_down: bfloat16 [1, 2, 1024, 1024], P(None, None, ('wide', 'narrow')), may hold values from -0.1875 to 0.1875
- text_gains: bfloat16 [1, 4, 768], P(None, None, ('wide', 'narrow')), may hold values from 0.5 to 1.5
- text_shifts: bfloat16 [1, 4, 768], P(None, None, ('wide', 'narrow')), may hold values from -1.1953125 to 1.1953125
- image_gains: bfloat16 [1, 4, 1024], P(None, None, ('wide', 'narrow')), may hold values from 0.5 to 1.5
- image_shifts: bfloat16 [1, 4, 1024], P(None, None, ('wide', 'narrow')), may hold values from -1.1953125 to 1.1953125
- grad_text_out: bfloat16 [32, 64, 768], P(('wide', 'narrow')), may hold values from -6 to 6
- grad_image_out: bfloat16 [32, 144, 1024], P(('wide', 'narrow')), may hold values from -6 to 6
Outputs:
- text_out: bfloat16 [32, 64, 768], P(('wide', 'narrow'))
- image_out: bfloat16 [32, 144, 1024], P(('wide', 'narrow'))
- text_in_grad: float32 [32, 64, 768], P(('wide', 'narrow'))
- image_in_grad: float32 [32, 144, 1024], P(('wide', 'narrow'))
- grad_text_co_in: float32 [1, 768, 3072], P(None, ('wide', 'narrow'))
- grad_text_co_out: float32 [1, 1024, 768], P(None, ('wide', 'narrow'))
- grad_image_co_in: float32 [1, 1024, 3072], P(None, ('wide', 'narrow'))
- grad_image_co_out: float32 [1, 1024, 1024], P(None, ('wide', 'narrow'))
- grad_text_self_in: float32 [1, 768, 2304], P(None, ('wide', 'narrow'))
- grad_text_self_out: float32 [1, 768, 768], P(None, ('wide', 'narrow'))
- grad_image_self_in: float32 [1, 1024, 3072], P(None, ('wide', 'narrow'))
- grad_image_self_out: float32 [1, 1024, 1024], P(None, ('wide', 'narrow'))
- grad_text_up: float32 [1, 2, 768, 3072], P(None, None, ('wide', 'narrow'))
- grad_text_down: float32 [1, 2, 3072, 768], P(None, None, ('wide', 'narrow'))
- grad_image_up: float32 [1, 2, 1024, 1024], P(None, None, ('wide', 'narrow'))
- grad_image_down: float32 [1, 2, 1024, 1024], P(None, None, ('wide', 'narrow'))
- grad_text_gains: float32 [1, 4, 768], P(None, None, ('wide', 'narrow'))
- grad_text_shifts: float32 [1, 4, 768], P(None, None, ('wide', 'narrow'))
- grad_image_gains: float32 [1, 4, 1024], P(None, None, ('wide', 'narrow'))
- grad_image_shifts: float32 [1, 4, 1024], P(None, None, ('wide', 'narrow'))
Inputs may be any that keep to these rules, and one draw needn't show every extreme that they name: `text_segments`: in each row the text slots hold caption 0 and then caption 1, each of 8 slots or more.
All inputs are finite; a program needn't handle non-finite values.
Results may differ from a plain program's by a relative error of at most 0.024.
Values may be sent and summed in bfloat16 or wider, within the bound.
No kernel may reach another device: no remote copies, remote signals or barrier semaphores. Data moves between devices by JAX's collectives and lax.ppermute only.
A program may use at most 320 MiB of HBM per device.

v0:
```python
from functools import partial

import jax
import jax.numpy as jnp
from jax import lax
from jax.sharding import PartitionSpec as P

HT = 12
HI = 8
HC = 8
REGIONS = 36


epsilon = 1e-06


def matmul(values, weights):
    return jnp.einsum("rlk,km->rlm", values, weights, preferred_element_type=jnp.float32)


def matmul_back(upstream, weights):
    return jnp.einsum("rlm,km->rlk", upstream, weights, preferred_element_type=jnp.float32)


def weight_grad(values, upstream):
    return jnp.einsum("rlk,rlm->km", values, upstream, preferred_element_type=jnp.float32)


def keep_same(values):
    return values


def layer_norm(values, gains_row, offset):
    average = jnp.mean(values, -1, keepdims=True)
    centred = values - average
    inverse = lax.rsqrt(jnp.mean(centred * centred, -1, keepdims=True) + epsilon)
    normed = centred * inverse
    return (normed * gains_row + offset, (normed, inverse))


def norm_back(upstream, stored, gains_row):
    normed, inverse = stored
    scaled = upstream * gains_row
    values_grad = inverse * (
        scaled
        - jnp.mean(scaled, -1, keepdims=True)
        - normed * jnp.mean(scaled * normed, -1, keepdims=True)
    )
    return (values_grad, jnp.sum(upstream * normed, axis=(0, 1)), jnp.sum(upstream, axis=(0, 1)))


def split_heads(array, head_count):
    return array.reshape(array.shape[0], array.shape[1], head_count, array.shape[2] // head_count)


def attend(queries, keys_in, values_in, allowed, head_count):
    row_count, length_q, width_all = queries.shape
    factor = (width_all // head_count) ** (-0.5)
    query_heads = split_heads(queries, head_count)
    key_heads = split_heads(keys_in, head_count)
    value_heads = split_heads(values_in, head_count)
    scores = (
        jnp.einsum("rqhd,rkhd->rhqk", query_heads, key_heads, preferred_element_type=jnp.float32)
        * factor
    )
    scores = jnp.where(allowed[:, None], scores, -1e30)
    peak_score = jnp.max(scores, -1, keepdims=True)
    exponent = jnp.exp(scores - peak_score)
    denom_sum = jnp.sum(exponent, -1, keepdims=True)
    probabilities = (exponent / denom_sum).astype(jnp.bfloat16)
    context = jnp.einsum(
        "rhqk,rkhd->rqhd", probabilities, value_heads, preferred_element_type=jnp.float32
    )
    return (context.reshape(row_count, length_q, width_all), peak_score + jnp.log(denom_sum))


def attend_back(context_grad, queries, keys_in, values_in, allowed, log_total, head_count):
    row_count, length_q, width_all = queries.shape
    factor = (width_all // head_count) ** (-0.5)
    query_heads = split_heads(queries, head_count)
    key_heads = split_heads(keys_in, head_count)
    value_heads = split_heads(values_in, head_count)
    grad_heads = split_heads(context_grad, head_count)
    scores = (
        jnp.einsum("rqhd,rkhd->rhqk", query_heads, key_heads, preferred_element_type=jnp.float32)
        * factor
    )
    scores = jnp.where(allowed[:, None], scores, -1e30)
    probabilities = jnp.exp(scores - log_total)
    value_grad = jnp.einsum(
        "rhqk,rqhd->rkhd",
        probabilities.astype(jnp.bfloat16),
        grad_heads,
        preferred_element_type=jnp.float32,
    )
    prob_grad = jnp.einsum(
        "rqhd,rkhd->rhqk", grad_heads, value_heads, preferred_element_type=jnp.float32
    )
    inner = jnp.sum(prob_grad * probabilities, -1, keepdims=True)
    score_grad = (probabilities * (prob_grad - inner)).astype(jnp.bfloat16)
    query_grad = (
        jnp.einsum("rhqk,rkhd->rqhd", score_grad, key_heads, preferred_element_type=jnp.float32)
        * factor
    )
    key_grad = (
        jnp.einsum("rhqk,rqhd->rkhd", score_grad, query_heads, preferred_element_type=jnp.float32)
        * factor
    )
    return (
        query_grad.reshape(row_count, length_q, width_all),
        key_grad.reshape(row_count, keys_in.shape[1], width_all),
        value_grad.reshape(row_count, keys_in.shape[1], width_all),
    )


def project(values, w_in):
    entry_low = values.astype(jnp.bfloat16)
    mixture = matmul(entry_low, w_in).astype(jnp.bfloat16)
    return (entry_low, jnp.split(mixture, 3, axis=-1))


def project_back(entry_low, grads_three, w_in, combine):
    joined = jnp.concatenate(grads_three, axis=-1).astype(jnp.bfloat16)
    return (combine(matmul_back(joined, w_in)), weight_grad(entry_low, joined))


def attn_out(values, context, w_out, gains_row, offset, combine):
    context_low = context.astype(jnp.bfloat16)
    result, stored = layer_norm(values + combine(matmul(context_low, w_out)), gains_row, offset)
    return (result, (context_low, stored))


def attn_out_back(upstream, saved, w_out, gains_row):
    context_low, stored = saved
    summed, gain_grad, shift_grad = norm_back(upstream, stored, gains_row)
    out_grad = summed.astype(jnp.bfloat16)
    context_grad = matmul_back(out_grad, w_out).astype(jnp.bfloat16)
    return (summed, context_grad, (weight_grad(context_low, out_grad), gain_grad, shift_grad))


def mlp_forward(values, w_up, w_down, gains_row, offset, combine):
    entry_low = values.astype(jnp.bfloat16)
    before = matmul(entry_low, w_up)
    hidden = jax.nn.gelu(before, approximate=False).astype(jnp.bfloat16)
    result, stored = layer_norm(values + combine(matmul(hidden, w_down)), gains_row, offset)
    return (result, (entry_low, before, hidden, stored))


def mlp_back(upstream, saved, w_up, w_down, gains_row, combine):
    entry_low, before, hidden, stored = saved
    summed, gain_grad, shift_grad = norm_back(upstream, stored, gains_row)
    out_grad = summed.astype(jnp.bfloat16)
    hidden_grad = matmul_back(out_grad, w_down)
    down_grad = weight_grad(hidden, out_grad)
    unused, gelu_pull = jax.vjp(partial(jax.nn.gelu, approximate=False), before)
    before_grad = gelu_pull(hidden_grad)[0].astype(jnp.bfloat16)
    entry_grad = combine(matmul_back(before_grad, w_up))
    up_grad = weight_grad(entry_low, before_grad)
    return (summed + entry_grad, (up_grad, down_grad, gain_grad, shift_grad))


def stream_forward(
    values, allowed, w_in, w_out, w_up, w_down, gains_rows, offsets, head_count, combine
):
    gains_float = gains_rows.astype(jnp.float32)
    offset_float = offsets.astype(jnp.float32)
    entry_low, (queries, keys_in, values_in) = project(values, w_in)
    context, log_total = attend(queries, keys_in, values_in, allowed, head_count)
    middle, attn_saved = attn_out(values, context, w_out, gains_float[0], offset_float[0], combine)
    result, mlp_saved = mlp_forward(middle, w_up, w_down, gains_float[1], offset_float[1], combine)
    return (result, (entry_low, queries, keys_in, values_in, log_total, attn_saved, mlp_saved))


def stream_backward(
    upstream, saved, allowed, w_in, w_out, w_up, w_down, gains_rows, head_count, combine
):
    entry_low, queries, keys_in, values_in, log_total, attn_saved, mlp_saved = saved
    gains_float = gains_rows.astype(jnp.float32)
    middle_grad, mlp_grads = mlp_back(upstream, mlp_saved, w_up, w_down, gains_float[1], combine)
    residual, context_grad, attn_grads = attn_out_back(
        middle_grad, attn_saved, w_out, gains_float[0]
    )
    query_grad, key_grad, value_grad = attend_back(
        context_grad, queries, keys_in, values_in, allowed, log_total, head_count
    )
    entry_grad, in_grad = project_back(entry_low, (query_grad, key_grad, value_grad), w_in, combine)
    return (
        residual + entry_grad,
        (
            in_grad,
            attn_grads[0],
            mlp_grads[0],
            mlp_grads[1],
            jnp.stack([attn_grads[1], mlp_grads[2]]),
            jnp.stack([attn_grads[2], mlp_grads[3]]),
        ),
    )


def co_forward(text_state, image_state, weights, cross, cross_back, head_count, combine):
    (
        text_in_w,
        text_out_w,
        image_in_w,
        image_out_w,
        text_up_w,
        text_down_w,
        image_up_w,
        image_down_w,
        text_gain,
        text_offset,
        image_gain,
        image_offset,
    ) = weights
    text_gain = text_gain.astype(jnp.float32)
    text_offset = text_offset.astype(jnp.float32)
    image_gain = image_gain.astype(jnp.float32)
    image_offset = image_offset.astype(jnp.float32)
    text_low, (text_query, text_keys, text_vals) = project(text_state, text_in_w)
    image_low, (image_query, image_keys, image_vals) = project(image_state, image_in_w)
    text_ctx, text_total = attend(text_query, image_keys, image_vals, cross, head_count)
    image_ctx, image_total = attend(image_query, text_keys, text_vals, cross_back, head_count)
    text_mid, text_att = attn_out(
        text_state, text_ctx, text_out_w, text_gain[0], text_offset[0], combine
    )
    image_mid, image_att = attn_out(
        image_state, image_ctx, image_out_w, image_gain[0], image_offset[0], combine
    )
    text_top, text_ffn = mlp_forward(
        text_mid, text_up_w, text_down_w, text_gain[1], text_offset[1], combine
    )
    image_top, image_ffn = mlp_forward(
        image_mid, image_up_w, image_down_w, image_gain[1], image_offset[1], combine
    )
    stored = (
        text_low,
        text_query,
        text_keys,
        text_vals,
        text_total,
        text_att,
        text_ffn,
        image_low,
        image_query,
        image_keys,
        image_vals,
        image_total,
        image_att,
        image_ffn,
    )
    return (text_top, image_top, stored)


def co_backward(
    text_upstream, image_upstream, stored, weights, cross, cross_back, head_count, combine
):
    (
        text_in_w,
        text_out_w,
        image_in_w,
        image_out_w,
        text_up_w,
        text_down_w,
        image_up_w,
        image_down_w,
        text_gain,
        text_offset,
        image_gain,
        image_offset,
    ) = weights
    text_gain = text_gain.astype(jnp.float32)
    image_gain = image_gain.astype(jnp.float32)
    (
        text_low,
        text_query,
        text_keys,
        text_vals,
        text_total,
        text_att,
        text_ffn,
        image_low,
        image_query,
        image_keys,
        image_vals,
        image_total,
        image_att,
        image_ffn,
    ) = stored
    text_mid_grad, text_ffn_grads = mlp_back(
        text_upstream, text_ffn, text_up_w, text_down_w, text_gain[1], combine
    )
    image_mid_grad, image_ffn_grads = mlp_back(
        image_upstream, image_ffn, image_up_w, image_down_w, image_gain[1], combine
    )
    text_res, text_ctx_grad, text_att_grads = attn_out_back(
        text_mid_grad, text_att, text_out_w, text_gain[0]
    )
    image_res, image_ctx_grad, image_att_grads = attn_out_back(
        image_mid_grad, image_att, image_out_w, image_gain[0]
    )
    text_query_grad, image_keys_grad, image_vals_grad = attend_back(
        text_ctx_grad, text_query, image_keys, image_vals, cross, text_total, head_count
    )
    image_query_grad, text_keys_grad, text_vals_grad = attend_back(
        image_ctx_grad, image_query, text_keys, text_vals, cross_back, image_total, head_count
    )
    text_entry_grad, text_in_grad = project_back(
        text_low, (text_query_grad, text_keys_grad, text_vals_grad), text_in_w, combine
    )
    image_entry_grad, image_in_grad = project_back(
        image_low, (image_query_grad, image_keys_grad, image_vals_grad), image_in_w, combine
    )
    cols = (text_in_grad, image_in_grad, text_ffn_grads[0], image_ffn_grads[0])
    rows = (text_att_grads[0], image_att_grads[0], text_ffn_grads[1], image_ffn_grads[1])
    norms = (
        jnp.stack([text_att_grads[1], text_ffn_grads[2]]),
        jnp.stack([text_att_grads[2], text_ffn_grads[3]]),
        jnp.stack([image_att_grads[1], image_ffn_grads[2]]),
        jnp.stack([image_att_grads[2], image_ffn_grads[3]]),
    )
    return (text_res + text_entry_grad, image_res + image_entry_grad, (cols, rows, norms))


def full_fetch(cols, rows, norms):
    got = (
        lax.all_gather(cols[0], ("wide", "narrow"), axis=0, tiled=True),
        lax.all_gather(cols[1], ("wide", "narrow"), axis=0, tiled=True),
        lax.all_gather(cols[2], ("wide", "narrow"), axis=0, tiled=True),
        lax.all_gather(cols[3], ("wide", "narrow"), axis=0, tiled=True),
        lax.all_gather(rows[0], ("wide", "narrow"), axis=0, tiled=True),
        lax.all_gather(rows[1], ("wide", "narrow"), axis=0, tiled=True),
        lax.all_gather(rows[2], ("wide", "narrow"), axis=0, tiled=True),
        lax.all_gather(rows[3], ("wide", "narrow"), axis=0, tiled=True),
        lax.all_gather(norms[0], ("wide", "narrow"), axis=1, tiled=True),
        lax.all_gather(norms[1], ("wide", "narrow"), axis=1, tiled=True),
        lax.all_gather(norms[2], ("wide", "narrow"), axis=1, tiled=True),
        lax.all_gather(norms[3], ("wide", "narrow"), axis=1, tiled=True),
    )
    return (got[0:4], got[4:8], got[8:12])


def full_return(cols, rows, norms):
    got = (
        lax.psum_scatter(cols[0], ("wide", "narrow"), scatter_dimension=0, tiled=True),
        lax.psum_scatter(cols[1], ("wide", "narrow"), scatter_dimension=0, tiled=True),
        lax.psum_scatter(cols[2], ("wide", "narrow"), scatter_dimension=0, tiled=True),
        lax.psum_scatter(cols[3], ("wide", "narrow"), scatter_dimension=0, tiled=True),
        lax.psum_scatter(rows[0], ("wide", "narrow"), scatter_dimension=0, tiled=True),
        lax.psum_scatter(rows[1], ("wide", "narrow"), scatter_dimension=0, tiled=True),
        lax.psum_scatter(rows[2], ("wide", "narrow"), scatter_dimension=0, tiled=True),
        lax.psum_scatter(rows[3], ("wide", "narrow"), scatter_dimension=0, tiled=True),
        lax.psum_scatter(norms[0], ("wide", "narrow"), scatter_dimension=1, tiled=True),
        lax.psum_scatter(norms[1], ("wide", "narrow"), scatter_dimension=1, tiled=True),
        lax.psum_scatter(norms[2], ("wide", "narrow"), scatter_dimension=1, tiled=True),
        lax.psum_scatter(norms[3], ("wide", "narrow"), scatter_dimension=1, tiled=True),
    )
    return (got[0:4], got[4:8], got[8:12])


def shards(
    text_in,
    image_in,
    text_segments,
    text_co_in,
    text_co_out,
    image_co_in,
    image_co_out,
    text_self_in,
    text_self_out,
    image_self_in,
    image_self_out,
    text_up,
    text_down,
    image_up,
    image_down,
    text_gains,
    text_shifts,
    image_gains,
    image_shifts,
    grad_text_out,
    grad_image_out,
):
    layer_total = text_co_in.shape[0]
    fetch, give_back, combine, head_split = (full_fetch, full_return, keep_same, 1)
    image_ids = jnp.arange(image_in.shape[1], dtype=jnp.int32) // (2 * REGIONS)
    cross = text_segments[:, :, None] == image_ids[None, None, :]
    cross_back = jnp.swapaxes(cross, 1, 2)
    text_allowed = text_segments[:, :, None] == text_segments[:, None, :]
    image_allowed = (image_ids[:, None] == image_ids[None, :])[None]

    def co_order(fetched):
        cols, rows, norms = fetched
        return (
            cols[0],
            rows[0],
            cols[1],
            rows[1],
            cols[2],
            rows[2],
            cols[3],
            rows[3],
            norms[0],
            norms[1],
            norms[2],
            norms[3],
        )

    co_heads = HC // head_split
    text_heads = HT // head_split
    image_heads = HI // head_split
    text_state = text_in.astype(jnp.float32)
    image_state = image_in.astype(jnp.float32)
    layer_no = 0
    co_fetched = fetch(
        *(
            (
                text_co_in[layer_no],
                image_co_in[layer_no],
                text_up[layer_no, 0],
                image_up[layer_no, 0],
            ),
            (
                text_co_out[layer_no],
                image_co_out[layer_no],
                text_down[layer_no, 0],
                image_down[layer_no, 0],
            ),
            (
                text_gains[layer_no, 0:2],
                text_shifts[layer_no, 0:2],
                image_gains[layer_no, 0:2],
                image_shifts[layer_no, 0:2],
            ),
        )
    )
    co_inputs = [(text_state, image_state)]
    text_state, image_state, unused = co_forward(
        text_state, image_state, co_order(co_fetched), cross, cross_back, co_heads, combine
    )
    self_fetched = fetch(
        *(
            (
                text_self_in[layer_no],
                image_self_in[layer_no],
                text_up[layer_no, 1],
                image_up[layer_no, 1],
            ),
            (
                text_self_out[layer_no],
                image_self_out[layer_no],
                text_down[layer_no, 1],
                image_down[layer_no, 1],
            ),
            (
                text_gains[layer_no, 2:4],
                text_shifts[layer_no, 2:4],
                image_gains[layer_no, 2:4],
                image_shifts[layer_no, 2:4],
            ),
        )
    )
    cols, rows, norms = self_fetched
    text_state, text_saved = stream_forward(
        text_state,
        text_allowed,
        cols[0],
        rows[0],
        cols[2],
        rows[2],
        norms[0],
        norms[1],
        text_heads,
        combine,
    )
    image_state, image_saved = stream_forward(
        image_state,
        image_allowed,
        cols[1],
        rows[1],
        cols[3],
        rows[3],
        norms[2],
        norms[3],
        image_heads,
        combine,
    )
    self_stored = [(text_saved, image_saved)]
    co_kept = [co_fetched]
    self_kept = [self_fetched]
    text_final = text_state.astype(jnp.bfloat16)
    image_final = image_state.astype(jnp.bfloat16)
    text_upstream = grad_text_out.astype(jnp.float32)
    image_upstream = grad_image_out.astype(jnp.float32)
    co_shards = [None] * layer_total
    self_shards = [None] * layer_total
    for layer_no in reversed(range(layer_total)):
        self_fetched = self_kept[layer_no]
        cols, rows, norms = self_fetched
        text_saved, image_saved = self_stored[layer_no]
        text_upstream, text_grads = stream_backward(
            text_upstream,
            text_saved,
            text_allowed,
            cols[0],
            rows[0],
            cols[2],
            rows[2],
            norms[0],
            text_heads,
            combine,
        )
        image_upstream, image_grads = stream_backward(
            image_upstream,
            image_saved,
            image_allowed,
            cols[1],
            rows[1],
            cols[3],
            rows[3],
            norms[2],
            image_heads,
            combine,
        )
        self_shards[layer_no] = give_back(
            (text_grads[0], image_grads[0], text_grads[2], image_grads[2]),
            (text_grads[1], image_grads[1], text_grads[3], image_grads[3]),
            (text_grads[4], text_grads[5], image_grads[4], image_grads[5]),
        )
        co_fetched = co_kept[layer_no]
        co_weights = co_order(co_fetched)
        text_prior, image_prior = co_inputs[layer_no]
        unused_text, unused_image, co_saved = co_forward(
            text_prior, image_prior, co_weights, cross, cross_back, co_heads, combine
        )
        text_upstream, image_upstream, co_grads = co_backward(
            text_upstream,
            image_upstream,
            co_saved,
            co_weights,
            cross,
            cross_back,
            co_heads,
            combine,
        )
        co_shards[layer_no] = give_back(co_grads[0], co_grads[1], co_grads[2])

    def stacked(source, group, index):
        return jnp.stack([source[0][group][index]])

    def paired(group, index):
        return jnp.stack([jnp.stack([co_shards[0][group][index], self_shards[0][group][index]])])

    def joined_norms(index):
        return jnp.stack([jnp.concatenate([co_shards[0][2][index], self_shards[0][2][index]])])

    return (
        text_final,
        image_final,
        text_upstream,
        image_upstream,
        stacked(co_shards, 0, 0),
        stacked(co_shards, 1, 0),
        stacked(co_shards, 0, 1),
        stacked(co_shards, 1, 1),
        stacked(self_shards, 0, 0),
        stacked(self_shards, 1, 0),
        stacked(self_shards, 0, 1),
        stacked(self_shards, 1, 1),
        paired(0, 2),
        paired(1, 2),
        paired(0, 3),
        paired(1, 3),
        joined_norms(0),
        joined_norms(1),
        joined_norms(2),
        joined_norms(3),
    )


def solution(mesh):
    placed = (
        P(("wide", "narrow"), None, None),
        P(("wide", "narrow"), None, None),
        P(("wide", "narrow"), None),
        P(None, ("wide", "narrow"), None),
        P(None, ("wide", "narrow"), None),
        P(None, ("wide", "narrow"), None),
        P(None, ("wide", "narrow"), None),
        P(None, ("wide", "narrow"), None),
        P(None, ("wide", "narrow"), None),
        P(None, ("wide", "narrow"), None),
        P(None, ("wide", "narrow"), None),
        P(None, None, ("wide", "narrow"), None),
        P(None, None, ("wide", "narrow"), None),
        P(None, None, ("wide", "narrow"), None),
        P(None, None, ("wide", "narrow"), None),
        P(None, None, ("wide", "narrow")),
        P(None, None, ("wide", "narrow")),
        P(None, None, ("wide", "narrow")),
        P(None, None, ("wide", "narrow")),
        P(("wide", "narrow"), None, None),
        P(("wide", "narrow"), None, None),
    )
    return jax.shard_map(
        shards,
        mesh=mesh,
        in_specs=placed,
        out_specs=(
            P(("wide", "narrow"), None, None),
            P(("wide", "narrow"), None, None),
            P(("wide", "narrow"), None, None),
            P(("wide", "narrow"), None, None),
            P(None, ("wide", "narrow"), None),
            P(None, ("wide", "narrow"), None),
            P(None, ("wide", "narrow"), None),
            P(None, ("wide", "narrow"), None),
            P(None, ("wide", "narrow"), None),
            P(None, ("wide", "narrow"), None),
            P(None, ("wide", "narrow"), None),
            P(None, ("wide", "narrow"), None),
            P(None, None, ("wide", "narrow"), None),
            P(None, None, ("wide", "narrow"), None),
            P(None, None, ("wide", "narrow"), None),
            P(None, None, ("wide", "narrow"), None),
            P(None, None, ("wide", "narrow")),
            P(None, None, ("wide", "narrow")),
            P(None, None, ("wide", "narrow")),
            P(None, None, ("wide", "narrow")),
        ),
        check_vma=False,
    )
```

profile of v0, /device:TPU:0, one launch (start us, length us, event | category | flops | bytes accessed | tf_op | source)
XLA Modules:
  0.0 3769.9 jit_solution(874996796813467123)
XLA Ops:
  21.9 74.1 %all-gather.14 = bf16[1,2,1024]{1,0,2:T(2,128)(2,1)S(1)} all-gather(bf16[1,2,32]{1,0,2:T(2,128)(2,1)S(1)} %copy.302), channel_id=16, replica_groups=mesh['wide'=16,'narrow'=2] {'wide','narrow'}, dimensions={2}, use_global_device_ids=true | all-gather | bytes 4224 | tf_op jit(solution)/shard_map/all_gather | solution.py:336
  96.5 6.2 slice_reduce_fusion.5
  102.8 68.1 %all-gather.15 = bf16[1,2,1024]{1,0,2:T(2,128)(2,1)S(1)} all-gather(bf16[1,2,32]{1,0,2:T(2,128)(2,1)S(1)} %copy.303), channel_id=17, replica_groups=mesh['wide'=16,'narrow'=2] {'wide','narrow'}, dimensions={2}, use_global_device_ids=true | all-gather | bytes 4224 | tf_op jit(solution)/shard_map/all_gather | solution.py:337
  171.5 6.2 slice_reduce_fusion.4
  177.8 70.0 %all-gather.20 = bf16[1,2,1024]{1,0,2:T(2,128)(2,1)S(1)} all-gather(bf16[1,2,32]{1,0,2:T(2,128)(2,1)S(1)} %copy.304), channel_id=22, replica_groups=mesh['wide'=16,'narrow'=2] {'wide','narrow'}, dimensions={2}, use_global_device_ids=true | all-gather | bytes 4224 | tf_op jit(solution)/shard_map/all_gather | solution.py:336
  248.4 6.2 slice_reduce_fusion.1
  254.7 67.2 %all-gather.21 = bf16[1,2,1024]{1,0,2:T(2,128)(2,1)S(1)} all-gather(bf16[1,2,32]{1,0,2:T(2,128)(2,1)S(1)} %copy.305), channel_id=23, replica_groups=mesh['wide'=16,'narrow'=2] {'wide','narrow'}, dimensions={2}, use_global_device_ids=true | all-gather | bytes 4224 | tf_op jit(solution)/shard_map/all_gather | solution.py:337
  322.4 6.2 slice_reduce_fusion
  332.8 3.9 fusion.41
  347.9 56.4 %all-gather.65.cloned.1.call-done = bf16[1,1024,3072]{2,1,0:T(8,128)(2,1)} async-done(((bf16[1,32,3072]{2,1,0:T(8,128)(2,1)}), bf16[1,1024,3072]{2,1,0:T(8,128)(2,1)}) %all-gather.65.cloned.1.call-update) | async-done | bytes 6291472 | tf_op jit(solution)/shard_map/all_gather | solution.py:327
  404.3 4.4 fusion.38
  410.2 52.1 %all-gather.67.cloned.1.call-done = bf16[1,1024,1024]{2,1,0:T(8,128)(2,1)} async-done(((bf16[1,32,1024]{2,1,0:T(8,128)(2,1)}), bf16[1,1024,1024]{2,1,0:T(8,128)(2,1)}) %all-gather.67.cloned.1.call-update) | async-done | bytes 2097168 | tf_op jit(solution)/shard_map/all_gather | solution.py:331
  464.8 56.4 %all-gather.69.cloned.1.call-done = bf16[1,1,1024,1024]{3,2,1,0:T(8,128)(2,1)} async-done(((bf16[1,1,32,1024]{3,2,1,0:T(8,128)(2,1)}), bf16[1,1,1024,1024]{3,2,1,0:T(8,128)(2,1)}) %all-gather.69.cloned.1.call-update) | async-done | bytes 2097168 | tf_op jit(solution)/shard_map/all_gather | solution.py:329
  524.2 56.0 %all-gather.71.cloned.1.call-done = bf16[1,1,1024,1024]{3,2,1,0:T(8,128)(2,1)} async-done(((bf16[1,1,32,1024]{3,2,1,0:T(8,128)(2,1)}), bf16[1,1,1024,1024]{3,2,1,0:T(8,128)(2,1)}) %all-gather.71.cloned.1.call-update) | async-done | bytes 2097168 | tf_op jit(solution)/shard_map/all_gather | solution.py:333
  580.2 3.6 fusion.443
  608.7 5.2 fusion.305
  614.9 4.0 fusion.300
  619.7 68.9 %all-gather.3 = bf16[1,2,768]{1,0,2:T(2,128)(2,1)S(1)} all-gather(bf16[1,2,24]{1,0,2:T(2,128)(2,1)S(1)} %copy.298), channel_id=5, replica_groups=mesh['wide'=16,'narrow'=2] {'wide','narrow'}, dimensions={2}, use_global_device_ids=true | all-gather | bytes 3168 | tf_op jit(solution)/shard_map/all_gather | solution.py:334
  689.2 66.3 %all-gather.4 = bf16[1,2,768]{1,0,2:T(2,128)(2,1)S(1)} all-gather(bf16[1,2,24]{1,0,2:T(2,128)(2,1)S(1)} %copy.299), channel_id=6, replica_groups=mesh['wide'=16,'narrow'=2] {'wide','narrow'}, dimensions={2}, use_global_device_ids=true | all-gather | bytes 3168 | tf_op jit(solution)/shard_map/all_gather | solution.py:335
  756.0 68.7 %all-gather.9 = bf16[1,2,768]{1,0,2:T(2,128)(2,1)S(1)} all-gather(bf16[1,2,24]{1,0,2:T(2,128)(2,1)S(1)} %copy.300), channel_id=11, replica_groups=mesh['wide'=16,'narrow'=2] {'wide','narrow'}, dimensions={2}, use_global_device_ids=true | all-gather | bytes 3168 | tf_op jit(solution)/shard_map/all_gather | solution.py:334
  825.8 66.8 %all-gather.10 = bf16[1,2,768]{1,0,2:T(2,128)(2,1)S(1)} all-gather(bf16[1,2,24]{1,0,2:T(2,128)(2,1)} %copy.301), channel_id=12, replica_groups=mesh['wide'=16,'narrow'=2] {'wide','narrow'}, dimensions={2}, use_global_device_ids=true | all-gather | bytes 3168 | tf_op jit(solution)/shard_map/all_gather | solution.py:335
  893.0 4.6 slice_reduce_fusion.13
  897.6 5.1 slice_reduce_fusion.12
  902.7 4.6 slice_reduce_fusion.9
  907.3 5.3 slice_reduce_fusion.8
  920.8 4.2 fusion.22
  925.1 4.9 fusion.434
  936.4 21.2 all-gather.55.cloned.1.call-done
  957.5 4.2 fusion.14
  961.8 61.6 %all-gather.57.cloned.1.call-done = bf16[1,1,3072,768]{3,2,1,0:T(8,128)(2,1)} async-done(((bf16[1,1,96,768]{3,2,1,0:T(8,128)(2,1)}), bf16[1,1,3072,768]{3,2,1,0:T(8,128)(2,1)}) %all-gather.57.cloned.1.call-update) | async-done | bytes 4718608 | tf_op jit(solution)/shard_map/all_gather | solution.py:332
  1023.4 5.1 fusion.437
  1056.5 5.0 add_convert_fusion
  1065.9 5.1 convolution_bitcast_fusion.1
  1071.0 9.6 copy.278
  1081.6 7.8 fusion.387
  1090.3 7.7 fusion.381
  1099.0 5.1 fusion.407
  1105.0 5.1 fusion.402
  1114.6 6.4 convolution_bitcast_fusion
  1121.0 12.7 copy.280
  1148.3 4.0 fusion.365
  1153.0 7.6 fusion.413
  1160.9 40.1 %all-reduce.4 = (f32[2,768]{1,0:T(2,128)S(1)}, f32[2,768]{1,0:T(2,128)S(1)}, f32[2,768]{1,0:T(2,128)S(1)}, f32[2,768]{1,0:T(2,128)S(1)}) all-reduce(f32[2,768]{1,0:T(2,128)S(1)} %pad_maximum_fusion.8, f32[2,768]{1,0:T(2,128)S(1)} %pad_maximum_fusion.7, ...), channel_id=43, replica_groups=mesh['wide'=16,'narrow'=2] {'wide','narrow'}, use_global_device_ids=true, to_apply=%region_65.66.clone | all-reduce | flops 6144 | bytes 49152
  1202.5 4.6 fusion.218
  1207.1 5.8 fusion.114
  1213.7 77.0 %reduce-scatter.71.cloned.1.call-done = f32[32,2]{1,0:T(8,128)} async-done(((f32[1024,2]{1,0:T(8,128)}), f32[32,2]{1,0:T(8,128)}) %reduce-scatter.71.cloned.1.call-update) | async-done | bytes 272
  1291.5 131.4 %reduce-scatter.73.cloned.1.call-done = f32[32,2]{1,0:T(8,128)} async-done(((f32[1024,2]{1,0:T(8,128)}), f32[32,2]{1,0:T(8,128)}) %reduce-scatter.73.cloned.1.call-update) | async-done | bytes 272
  1423.6 131.4 %reduce-scatter.75.cloned.1.call-done = f32[32,2]{1,0:T(8,128)} async-done(((f32[1024,2]{1,0:T(8,128)}), f32[32,2]{1,0:T(8,128)}) %reduce-scatter.75.cloned.1.call-update) | async-done | bytes 272
  1557.0 138.1 %reduce-scatter.63.cloned.1.call-done = f32[32,1024]{1,0:T(8,128)} async-done(((f32[1024,1024]{1,0:T(8,128)}), f32[32,1024]{1,0:T(8,128)}) %reduce-scatter.63.cloned.1.call-update) | async-done | bytes 131088 | tf_op jit(solution)/shard_map/reduce_scatter | solution.py:351
  1695.1 141.7 %reduce-scatter.61.cloned.1.call-done = f32[32,1024]{1,0:T(8,128)} async-done(((f32[1024,1024]{1,0:T(8,128)}), f32[32,1024]{1,0:T(8,128)}) %reduce-scatter.61.cloned.1.call-update) | async-done | bytes 131088 | tf_op jit(solution)/shard_map/reduce_scatter | solution.py:351
  1838.5 138.9 %reduce-scatter.59.cloned.1.call-done = f32[32,1024]{1,0:T(8,128)} async-done(((f32[1024,1024]{1,0:T(8,128)}), f32[32,1024]{1,0:T(8,128)}) %reduce-scatter.59.cloned.1.call-update) | async-done | bytes 131088 | tf_op jit(solution)/shard_map/reduce_scatter | solution.py:347
  1977.4 141.3 %reduce-scatter.57.cloned.1.call-done = f32[32,1024]{1,0:T(8,128)} async-done(((f32[1024,1024]{1,0:T(8,128)}), f32[32,1024]{1,0:T(8,128)}) %reduce-scatter.57.cloned.1.call-update) | async-done | bytes 131088 | tf_op jit(solution)/shard_map/reduce_scatter | solution.py:347
  2120.4 136.4 %reduce-scatter.65.cloned.1.call-done = f32[24,3072]{1,0:T(8,128)} async-done(((f32[768,3072]{1,0:T(8,128)}), f32[24,3072]{1,0:T(8,128)}) %reduce-scatter.65.cloned.1.call-update) | async-done | bytes 294928
  2259.3 138.8 %reduce-scatter.55.cloned.1.call-done = f32[96,768]{1,0:T(8,128)} async-done(((f32[3072,768]{1,0:T(8,128)}), f32[96,768]{1,0:T(8,128)}) %reduce-scatter.55.cloned.1.call-update) | async-done | bytes 294928 | tf_op jit(solution)/shard_map/reduce_scatter | solution.py:350
  2398.2 140.2 %reduce-scatter.53.cloned.1.call-done = f32[96,768]{1,0:T(8,128)} async-done(((f32[3072,768]{1,0:T(8,128)}), f32[96,768]{1,0:T(8,128)}) %reduce-scatter.53.cloned.1.call-update) | async-done | bytes 294928 | tf_op jit(solution)/shard_map/reduce_scatter | solution.py:350
  2540.3 139.5 %reduce-scatter.51.cloned.1.call-done = f32[24,3072]{1,0:T(8,128)} async-done(((f32[768,3072]{1,0:T(8,128)}), f32[24,3072]{1,0:T(8,128)}) %reduce-scatter.51.cloned.1.call-update) | async-done | bytes 294928 | tf_op jit(solution)/shard_map/reduce_scatter | solution.py:346
  2679.9 140.6 %reduce-scatter.49.cloned.1.call-done = f32[24,3072]{1,0:T(8,128)} async-done(((f32[768,3072]{1,0:T(8,128)}), f32[24,3072]{1,0:T(8,128)}) %reduce-scatter.49.cloned.1.call-update) | async-done | bytes 294928 | tf_op jit(solution)/shard_map/reduce_scatter | solution.py:346
  2822.4 159.6 %reduce-scatter.67.cloned.1.call-done = f32[32,3072]{1,0:T(8,128)} async-done(((f32[1024,3072]{1,0:T(8,128)}), f32[32,3072]{1,0:T(8,128)}) %reduce-scatter.67.cloned.1.call-update) | async-done | bytes 393232
  2984.6 101.4 %reduce-scatter.43.cloned.1.call-done = f32[24,768]{1,0:T(8,128)} async-done(((f32[768,768]{1,0:T(8,128)}), f32[24,768]{1,0:T(8,128)}) %reduce-scatter.43.cloned.1.call-update) | async-done | bytes 73744 | tf_op jit(solution)/shard_map/reduce_scatter | solution.py:348
  3086.1 107.4 %reduce-scatter.37.cloned.1.call-done = f32[32,768]{1,0:T(8,128)} async-done(((f32[1024,768]{1,0:T(8,128)}), f32[32,768]{1,0:T(8,128)}) %reduce-scatter.37.cloned.1.call-update) | async-done | bytes 98320 | tf_op jit(solution)/shard_map/reduce_scatter | solution.py:348
  3193.4 143.8 %reduce-scatter.39.cloned.1.call-done = f32[32,1024]{1,0:T(8,128)} async-done(((f32[1024,1024]{1,0:T(8,128)}), f32[32,1024]{1,0:T(8,128)}) %reduce-scatter.39.cloned.1.call-update) | async-done | bytes 131088 | tf_op jit(solution)/shard_map/reduce_scatter | solution.py:349
  3337.2 141.7 %reduce-scatter.47.cloned.1.call-done = f32[32,1024]{1,0:T(8,128)} async-done(((f32[1024,1024]{1,0:T(8,128)}), f32[32,1024]{1,0:T(8,128)}) %reduce-scatter.47.cloned.1.call-update) | async-done | bytes 131088 | tf_op jit(solution)/shard_map/reduce_scatter | solution.py:349
  3478.9 122.9 %reduce-scatter.41.cloned.1.call-done = f32[24,2304]{1,0:T(8,128)} async-done(((f32[768,2304]{1,0:T(8,128)}), f32[24,2304]{1,0:T(8,128)}) %reduce-scatter.41.cloned.1.call-update) | async-done | bytes 221200 | tf_op jit(solution)/shard_map/reduce_scatter | solution.py:344
  3601.8 161.3 %reduce-scatter.45.cloned.1.call-done = f32[32,3072]{1,0:T(8,128)} async-done(((f32[1024,3072]{1,0:T(8,128)}), f32[32,3072]{1,0:T(8,128)}) %reduce-scatter.45.cloned.1.call-update) | async-done | bytes 393232 | tf_op jit(solution)/shard_map/reduce_scatter | solution.py:345
  (662 shorter events, 154.6 us)
Async XLA Ops:
  7.2 14.1 copy-start.149
  7.2 14.2 copy-start.162
  7.2 321.4 %all-gather.43.cloned.1.call-start = ((), (), s32[]{:S(2)}) async-start(), calls=%async_computation.35 | async-start | bytes 4866048 | tf_op jit(solution)/shard_map/all_gather | solution.py:326
  8.0 324.8 %all-gather.41.cloned.1.call-start = ((), (), s32[]{:S(2)}) async-start(), calls=%async_computation.34 | async-start | bytes 6488064 | tf_op jit(solution)/shard_map/all_gather | solution.py:327
  8.7 330.5 %all-gather.59.cloned.1.call-start = ((), (), s32[]{:S(2)}) async-start(), calls=%async_computation.43 | async-start | bytes 2162688 | tf_op jit(solution)/shard_map/all_gather | solution.py:331
  9.4 332.3 %all-gather.61.cloned.1.call-start = ((), (), s32[]{:S(2)}) async-start(), calls=%async_computation.44 | async-start | bytes 2162688 | tf_op jit(solution)/shard_map/all_gather | solution.py:329
  11.0 333.0 %all-gather.63.cloned.1.call-start = ((), (), s32[]{:S(2)}) async-start(), calls=%async_computation.45 | async-start | bytes 2162688 | tf_op jit(solution)/shard_map/all_gather | solution.py:333
  12.6 391.7 %all-gather.65.cloned.1.call-start = ((), (), s32[]{:S(2)}) async-start(), calls=%async_computation.46 | async-start | bytes 6488064 | tf_op jit(solution)/shard_map/all_gather | solution.py:327
  13.2 449.1 %all-gather.67.cloned.1.call-start = ((), (), s32[]{:S(2)}) async-start(), calls=%async_computation.47 | async-start | bytes 2162688 | tf_op jit(solution)/shard_map/all_gather | solution.py:331
  14.0 507.3 %all-gather.69.cloned.1.call-start = ((), (), s32[]{:S(2)}) async-start(), calls=%async_computation.48 | async-start | bytes 2162688 | tf_op jit(solution)/shard_map/all_gather | solution.py:329
  14.7 565.4 %all-gather.71.cloned.1.call-start = ((), (), s32[]{:S(2)}) async-start(), calls=%async_computation.49 | async-start | bytes 2162688 | tf_op jit(solution)/shard_map/all_gather | solution.py:333
  15.5 902.3 %all-gather.45.cloned.1.call-start = ((), (), s32[]{:S(2)}) async-start(), calls=%async_computation.36 | async-start | bytes 1622016 | tf_op jit(solution)/shard_map/all_gather | solution.py:330
  16.0 904.8 %all-gather.47.cloned.1.call-start = ((), (), s32[]{:S(2)}) async-start(), calls=%async_computation.37 | async-start | bytes 4866048 | tf_op jit(solution)/shard_map/all_gather | solution.py:328
  17.8 84.9 %copy-start.163 = (bf16[1,4,32]{2,1,0:T(4,128)(2,1)S(1)}, bf16[1,4,32]{2,1,0:T(4,128)(2,1)}, u32[]{:S(2)}) copy-start(bf16[1,4,32]{2,1,0:T(4,128)(2,1)} %param.39) | copy-start | bytes 772
  17.8 907.2 %all-gather.49.cloned.1.call-start = ((), (), s32[]{:S(2)}) async-start(), calls=%async_computation.38 | async-start | bytes 4866048 | tf_op jit(solution)/shard_map/all_gather | solution.py:332
  18.6 911.6 %all-gather.51.cloned.1.call-start = ((), (), s32[]{:S(2)}) async-start(), calls=%async_computation.39 | async-start | bytes 3649536 | tf_op jit(solution)/shard_map/all_gather | solution.py:326
  19.4 915.0 %all-gather.53.cloned.1.call-start = ((), (), s32[]{:S(2)}) async-start(), calls=%async_computation.40 | async-start | bytes 1216512 | tf_op jit(solution)/shard_map/all_gather | solution.py:330
  20.0 937.6 %all-gather.55.cloned.1.call-start = ((), (), s32[]{:S(2)}) async-start(), calls=%async_computation.41 | async-start | bytes 4866048 | tf_op jit(solution)/shard_map/all_gather | solution.py:328
  20.6 1002.8 %all-gather.57.cloned.1.call-start = ((), (), s32[]{:S(2)}) async-start(), calls=%async_computation.42 | async-start | bytes 4866048 | tf_op jit(solution)/shard_map/all_gather | solution.py:332
  21.1 1191.8 %reduce-scatter.69.cloned.1.call-start = ((), (), s32[]{:S(2)}) async-start(), calls=%async_computation.52 | async-start | bytes 540672
  102.7 496.9 %copy-start.93 = (f32[1024]{0:T(1024)}, f32[1024]{0:T(1024)S(1)}, u32[]{:S(2)}) copy-start(f32[1024]{0:T(1024)S(1)} %get-tuple-element.119) | copy-start | bytes 12292
  177.7 166.4 %copy-start.102 = (f32[1024]{0:T(1024)}, f32[1024]{0:T(1024)S(1)}, u32[]{:S(2)}) copy-start(f32[1024]{0:T(1024)S(1)} %get-tuple-element.121) | copy-start | bytes 12292
  177.7 284.6 %copy-start.87 = (f32[1024]{0:T(1024)}, f32[1024]{0:T(1024)S(1)}, u32[]{:S(2)}) copy-start(f32[1024]{0:T(1024)S(1)} %get-tuple-element.120) | copy-start | bytes 12292
  248.4 80.3 %copy-start.48 = (bf16[1,64,768]{2,1,0:T(8,128)(2,1)S(1)}, bf16[1,64,768]{2,1,0:T(8,128)(2,1)}, u32[]{:S(2)}) copy-start(bf16[1,64,768]{2,1,0:T(8,128)(2,1)} %param.21) | copy-start | bytes 294916
  254.5 335.1 %copy-start.97 = (f32[1024]{0:T(1024)}, f32[1024]{0:T(1024)S(1)}, u32[]{:S(2)}) copy-start(f32[1024]{0:T(1024)S(1)} %get-tuple-element.115) | copy-start | bytes 12292
  328.6 192.7 %copy-start.104 = (f32[1024]{0:T(1024)}, f32[1024]{0:T(1024)S(1)}, u32[]{:S(2)}) copy-start(f32[1024]{0:T(1024)S(1)} %get-tuple-element.117) | copy-start | bytes 12292
  347.6 249.7 %copy-start.95 = (f32[144]{0:T(256)}, f32[144]{0:T(256)S(1)}, u32[]{:S(2)}) copy-start(f32[144]{0:T(256)S(1)} %broadcast_multiply_fusion.10) | copy-start | bytes 1732
  347.9 114.4 %copy-start.99 = (f32[144]{0:T(256)}, f32[144]{0:T(256)S(1)}, u32[]{:S(2)}) copy-start(f32[144]{0:T(256)S(1)} %add_rsqrt_fusion.2) | copy-start | bytes 1732
  410.2 114.0 %copy-start.18 = (bf16[1,144,8,128]{3,2,1,0:T(8,128)(2,1)}, bf16[1,144,8,128]{3,2,1,0:T(8,128)(2,1)S(1)}, u32[]{:S(2)}) copy-start(bf16[1,144,8,128]{3,2,1,0:T(8,128)(2,1)S(1)} %copy.227) | copy-start | bytes 884740
  464.6 56.7 %copy-start.119 = (f32[144]{0:T(256)}, f32[144]{0:T(256)S(1)}, u32[]{:S(2)}) copy-start(f32[144]{0:T(256)S(1)} %broadcast_multiply_fusion.9) | copy-start | bytes 1732
  464.8 56.4 %copy-start.131 = (f32[144]{0:T(256)}, f32[144]{0:T(256)S(1)}, u32[]{:S(2)}) copy-start(f32[144]{0:T(256)S(1)} %add_rsqrt_fusion.1) | copy-start | bytes 1732
  524.2 59.9 %copy-start.84 = (bf16[1,144,1024]{2,1,0:T(8,128)(2,1)S(1)}, bf16[1,144,1024]{2,1,0:T(8,128)(2,1)}, u32[]{:S(2)}) copy-start(bf16[1,144,1024]{2,1,0:T(8,128)(2,1)} %param.41) | copy-start | bytes 884740
  603.1 687.5 %reduce-scatter.71.cloned.1.call-start = ((), (), s32[]{:S(2)}) async-start(), calls=%async_computation.53 | async-start | bytes 540672
  605.0 817.9 %reduce-scatter.73.cloned.1.call-start = ((), (), s32[]{:S(2)}) async-start(), calls=%async_computation.54 | async-start | bytes 540672
  606.8 948.2 %reduce-scatter.75.cloned.1.call-start = ((), (), s32[]{:S(2)}) async-start(), calls=%async_computation.55 | async-start | bytes 540672
  608.6 1086.5 %reduce-scatter.63.cloned.1.call-start = ((), (), s32[]{:S(2)}) async-start(), calls=%async_computation.33 | async-start | bytes 4325376 | tf_op jit(solution)/shard_map/reduce_scatter | solution.py:351
  613.9 1222.9 %reduce-scatter.61.cloned.1.call-start = ((), (), s32[]{:S(2)}) async-start(), calls=%async_computation.32 | async-start | bytes 4325376 | tf_op jit(solution)/shard_map/reduce_scatter | solution.py:351
  618.9 70.1 %copy-start.165 = (bf16[1,4,24]{2,1,0:T(4,128)(2,1)S(1)}, bf16[1,4,24]{2,1,0:T(4,128)(2,1)}, u32[]{:S(2)}) copy-start(bf16[1,4,24]{2,1,0:T(4,128)(2,1)} %param.37) | copy-start | bytes 580
  619.0 1358.5 %reduce-scatter.59.cloned.1.call-start = ((), (), s32[]{:S(2)}) async-start(), calls=%async_computation.31 | async-start | bytes 4325376 | tf_op jit(solution)/shard_map/reduce_scatter | solution.py:347
  825.8 86.8 %copy-start.150 = (s32[1,64]{1,0:T(1,128)S(1)}, s32[1,64]{1,0:T(1,128)}, u32[]{:S(2)}) copy-start(s32[1,64]{1,0:T(1,128)} %param.23) | copy-start | bytes 772
  825.8 87.5 %copy-start.143 = (s32[144]{0:T(256)S(1)}, s32[144]{0:T(256)}, u32[]{:S(2)}) copy-start(s32[144]{0:T(256)} %copy-done.142) | copy-start | bytes 1732
  892.6 20.7 copy-start.72
  892.6 20.8 copy-start.38
  893.0 20.5 copy-start.37
  917.7 1201.0 %reduce-scatter.57.cloned.1.call-start = ((), (), s32[]{:S(2)}) async-start(), calls=%async_computation.30 | async-start | bytes 4325376 | tf_op jit(solution)/shard_map/reduce_scatter | solution.py:347
  934.0 23.6 copy-start.91
  934.3 27.4 copy-start.62
  936.4 101.1 %copy-start.146 = (f32[64]{0:T(128)}, f32[64]{0:T(128)S(1)}, u32[]{:S(2)}) copy-start(f32[64]{0:T(128)S(1)} %add_rsqrt_fusion.5) | copy-start | bytes 772
  961.8 66.9 %copy-start.73 = (bf16[1,64,768]{2,1,0:T(8,128)(2,1)S(1)}, bf16[1,64,768]{2,1,0:T(8,128)(2,1)}, u32[]{:S(2)}) copy-start(bf16[1,64,768]{2,1,0:T(8,128)(2,1)} %param.40) | copy-start | bytes 294916
  961.8 66.9 %copy-start.106 = (f32[768]{0:T(1024)S(1)}, f32[768]{0:T(1024)}, u32[]{:S(2)}) copy-start(f32[768]{0:T(1024)} %get-tuple-element.128) | copy-start | bytes 9220
  961.8 66.9 %copy-start.136 = (f32[768]{0:T(1024)S(1)}, f32[768]{0:T(1024)}, u32[]{:S(2)}) copy-start(f32[768]{0:T(1024)} %get-tuple-element.130) | copy-start | bytes 9220
  1037.4 1219.3 %reduce-scatter.65.cloned.1.call-start = ((), (), s32[]{:S(2)}) async-start(), calls=%async_computation.50 | async-start | bytes 9732096
  1080.6 1317.6 %reduce-scatter.55.cloned.1.call-start = ((), (), s32[]{:S(2)}) async-start(), calls=%async_computation.29 | async-start | bytes 9732096 | tf_op jit(solution)/shard_map/reduce_scatter | solution.py:350
  1089.4 1449.1 %reduce-scatter.53.cloned.1.call-start = ((), (), s32[]{:S(2)}) async-start(), calls=%async_computation.28 | async-start | bytes 9732096 | tf_op jit(solution)/shard_map/reduce_scatter | solution.py:350
  1098.0 1581.8 %reduce-scatter.51.cloned.1.call-start = ((), (), s32[]{:S(2)}) async-start(), calls=%async_computation.27 | async-start | bytes 9732096 | tf_op jit(solution)/shard_map/reduce_scatter | solution.py:346
  1104.1 1716.4 %reduce-scatter.49.cloned.1.call-start = ((), (), s32[]{:S(2)}) async-start(), calls=%async_computation.26 | async-start | bytes 9732096 | tf_op jit(solution)/shard_map/reduce_scatter | solution.py:346
  1110.2 1871.8 %reduce-scatter.67.cloned.1.call-start = ((), (), s32[]{:S(2)}) async-start(), calls=%async_computation.51 | async-start | bytes 12976128
  1133.7 1952.3 %reduce-scatter.43.cloned.1.call-start = ((), (), s32[]{:S(2)}) async-start(), calls=%async_computation.23 | async-start | bytes 2433024 | tf_op jit(solution)/shard_map/reduce_scatter | solution.py:348
  1137.4 2056.1 %reduce-scatter.37.cloned.1.call-start = ((), (), s32[]{:S(2)}) async-start(), calls=%async_computation.20 | async-start | bytes 3244032 | tf_op jit(solution)/shard_map/reduce_scatter | solution.py:348
  1139.9 2197.4 %reduce-scatter.39.cloned.1.call-start = ((), (), s32[]{:S(2)}) async-start(), calls=%async_computation.21 | async-start | bytes 4325376 | tf_op jit(solution)/shard_map/reduce_scatter | solution.py:349
  1143.6 2335.4 %reduce-scatter.47.cloned.1.call-start = ((), (), s32[]{:S(2)}) async-start(), calls=%async_computation.25 | async-start | bytes 4325376 | tf_op jit(solution)/shard_map/reduce_scatter | solution.py:349
  1147.3 2454.5 %reduce-scatter.41.cloned.1.call-start = ((), (), s32[]{:S(2)}) async-start(), calls=%async_computation.22 | async-start | bytes 7299072 | tf_op jit(solution)/shard_map/reduce_scatter | solution.py:344
  1152.4 2610.8 %reduce-scatter.45.cloned.1.call-start = ((), (), s32[]{:S(2)}) async-start(), calls=%async_computation.24 | async-start | bytes 12976128 | tf_op jit(solution)/shard_map/reduce_scatter | solution.py:345
  1160.7 41.8 %copy-start.12 = (bf16[64,3072]{1,0:T(8,128)(2,1)S(1)}, bf16[64,3072]{1,0:T(8,128)(2,1)}, u32[]{:S(2)}) copy-start(bf16[64,3072]{1,0:T(8,128)(2,1)} %copy-done.11) | copy-start | bytes 1179652
  (149 other events, 393.3 us)
Sparse Core Ops, SparseCore 0:
  11.0 70.2 all-gather.42
  84.2 70.3 all-gather.40
  157.6 56.5 all-gather.58
  217.6 56.5 all-gather.60
  277.6 55.5 all-gather.62
  335.9 68.3 all-gather.64
  407.3 54.9 all-gather.66
  465.9 55.3 all-gather.68
  524.8 55.3 all-gather.70
  582.9 54.4 all-gather.44
  640.9 64.1 all-gather.46
  708.5 64.2 all-gather.48
  775.7 60.2 all-gather.50
  838.8 53.3 all-gather.52
  894.9 62.5 all-gather.54
  960.9 62.4 all-gather.56
  1025.4 132.9 reduce-scatter.68
  1160.6 130.0 reduce-scatter.70
  1292.9 129.8 reduce-scatter.72
  1425.0 129.9 reduce-scatter.74
  1557.3 137.7 reduce-scatter.62
  1697.4 139.3 reduce-scatter.60
  1839.1 138.3 reduce-scatter.58
  1979.6 139.0 reduce-scatter.56
  2124.6 132.1 reduce-scatter.64
  2263.5 134.6 reduce-scatter.54
  2403.9 134.4 reduce-scatter.52
  2545.3 134.4 reduce-scatter.50
  2685.8 134.6 reduce-scatter.48
  2827.4 154.5 reduce-scatter.66
  2987.8 98.1 reduce-scatter.42
  3092.9 100.4 reduce-scatter.36
  3196.2 140.9 reduce-scatter.38
  3340.2 138.6 reduce-scatter.46
  3486.1 115.6 reduce-scatter.40
  3608.3 154.8 reduce-scatter.44
where the time goes:
time: 3780 us; the launch traced here: 3770 us
  waiting for transfers between devices  2850 us (75%)
  blocking collectives  590 us (16%)
  matrix products  180 us (5%)
  local copies, waits for them, and re-layouts  111 us (3%)
    unnamed x42, waiting for transfers between devices  644 us
    reduce_scatter x2, waiting for transfers between devices, full_return(): lax.psum_scatter(rows[1], ('wide', 'narrow'), scatter_dimension=0, tiled=...  286 us
    reduce_scatter x2, waiting for transfers between devices, full_return(): lax.psum_scatter(cols[3], ('wide', 'narrow'), scatter_dimension=0, tiled=...  280 us
    reduce_scatter x2, waiting for transfers between devices, full_return(): lax.psum_scatter(cols[2], ('wide', 'narrow'), scatter_dimension=0, tiled=...  280 us
    reduce_scatter x2, waiting for transfers between devices, full_return(): lax.psum_scatter(rows[3], ('wide', 'narrow'), scatter_dimension=0, tiled=...  280 us
    reduce_scatter x2, waiting for transfers between devices, full_return(): lax.psum_scatter(rows[2], ('wide', 'narrow'), scatter_dimension=0, tiled=...  279 us
    reduce_scatter x2, waiting for transfers between devices, full_return(): lax.psum_scatter(rows[0], ('wide', 'narrow'), scatter_dimension=0, tiled=...  209 us
    reduce_scatter x1, waiting for transfers between devices, full_return(): lax.psum_scatter(cols[1], ('wide', 'narrow'), scatter_dimension=0, tiled=...  161 us
  transfers between devices with their start and end apart: 36, of which 25 were waited for; matrix products, arithmetic and copies ran while one was open for 8% of the time, Pallas kernels for 0%

commit v1 on v0

v1 whole, which is shorter than its diff:
```python
from functools import partial

import jax
import jax.numpy as jnp
from jax import lax
from jax.sharding import PartitionSpec as P

HT = 12
HI = 8
HC = 8
REGIONS = 36
AXES = ("wide", "narrow")
EPS = 1e-06
F32 = jnp.float32
BF16 = jnp.bfloat16


class Grid:
    def __init__(self, wide, narrow):
        self.depth = wide // 4
        self.narrow = narrow
        self.count = wide * narrow
        w = lax.axis_index("wide")
        self.x = lax.axis_index("narrow")
        self.core = w % 2
        self.y = (w // 2) % 2
        self.z = w // 4

    def split(self, i):
        x = i % self.narrow
        i = i // self.narrow
        return i // 4, (i // 2) % 2, i % 2, x

    def join(self, z, y, c, x):
        return ((z * 2 + y) * 2 + c) * self.narrow + x

    def move(self, value, to):
        pairs = [(i, self.join(*to(*self.split(i)))) for i in range(self.count)]
        return lax.ppermute(value, AXES, pairs)

    def to_core(self, value):
        return self.move(value, lambda z, y, c, x: (z, y, 1 - c, x))

    def to_x(self, value):
        return self.move(value, lambda z, y, c, x: (z, y, c, 1 - x))

    def to_y(self, value):
        return self.move(value, lambda z, y, c, x: (z, 1 - y, c, x))

    def to_z(self, value, step):
        return self.move(value, lambda z, y, c, x: ((z + step) % self.depth, y, c, x))

    def swap_half(self, value):
        half = self.depth // 2
        return self.move(value, lambda z, y, c, x: (c * half + z % half, y, z // half, x))


def pick(value, index, axis):
    return lax.dynamic_index_in_dim(value, index, axis, keepdims=False)


def paired(own, other, index, axis):
    low = jnp.expand_dims(jnp.where(index == 0, own, other), axis)
    high = jnp.expand_dims(jnp.where(index == 0, other, own), axis)
    return jnp.concatenate([low, high], axis)


def halves(width, groups):
    return groups, 2, width // groups // 2


def chunk_in(grid, w, groups):
    r, n = w.shape
    parts = w.reshape((r,) + halves(n, groups))
    keep = pick(parts, grid.core, 2).reshape(r, n // 2)
    give = pick(parts, 1 - grid.core, 2).reshape(r, n // 2)
    return paired(keep, grid.to_core(give), grid.core, 0)


def chunk_out(grid, mats):
    joined = jnp.concatenate(mats, 0) if len(mats) > 1 else mats[0]
    return grid.swap_half(joined)[None]


def gather_z(grid, chunk):
    got = [chunk] + [grid.to_z(chunk, k) for k in range(1, grid.depth)]
    places = []
    for place in range(grid.depth):
        value = got[0]
        for k in range(1, grid.depth):
            value = jnp.where((grid.z - place) % grid.depth == k, got[k], value)
        places.append(value)
    return jnp.stack(places)


def gather_plane(grid, block, order):
    if order == "xy":
        both = paired(block, grid.to_x(block), grid.x, 2)
        return paired(both, grid.to_y(both), grid.y, 1)
    both = paired(block, grid.to_y(block), grid.y, 1)
    return paired(both, grid.to_x(both), grid.x, 3)


def finish_in(full):
    return full.reshape(-1, full.shape[-1])


def finish_out(grid, full, rows):
    z, _, p, _, r, c = full.shape
    full = full.reshape(2, z // 2, 2, 2, r, c).transpose(1, 2, 0, 3, 4, 5)
    out, at = [], 0
    for count in rows:
        out.append(full[..., at : at + count, :].reshape(-1, c))
        at += count
    return out


def add_low(a, b):
    return (a.astype(F32) + b.astype(F32)).astype(BF16)


def reduce_plane(grid, view, order):
    if order == "xy":
        got = grid.to_y(pick(view, 1 - grid.y, 1))
        both = add_low(pick(view, grid.y, 1), got)
        got = grid.to_x(pick(both, 1 - grid.x, 2))
        return add_low(pick(both, grid.x, 2), got)
    got = grid.to_x(pick(view, 1 - grid.x, 3))
    both = add_low(pick(view, grid.x, 3), got)
    got = grid.to_y(pick(both, 1 - grid.y, 1))
    return add_low(pick(both, grid.y, 1), got)


def reduce_z(grid, block):
    total = pick(block, grid.z, 0).astype(F32)
    for k in range(1, grid.depth):
        give = pick(block, (grid.z + k) % grid.depth, 0)
        total = total + grid.to_z(give, k).astype(F32)
    return total


def return_in(grid, grad, groups, order):
    k, c = grad.shape
    view = grad.reshape(grid.depth, 2, 2, 2, k // grid.count, c)
    total = reduce_z(grid, reduce_plane(grid, view, order))
    keep = pick(total, grid.core, 0)
    got = grid.to_core(pick(total, 1 - grid.core, 0).astype(BF16)).astype(F32)
    r = keep.shape[0]
    shape = (r, groups, c // groups)
    return paired(keep.reshape(shape), got.reshape(shape), grid.core, 2).reshape(r, 2 * c)


def return_out(grid, grads, order):
    half = grid.depth // 2
    views = []
    for grad in grads:
        k, c = grad.shape
        view = grad.reshape(half, 2, 2, 2, 2 * k // grid.count, c).transpose(2, 0, 1, 3, 4, 5)
        views.append(view.reshape(grid.depth, 2, 1, 2, 2 * k // grid.count, c))
    view = jnp.concatenate(views, 4) if len(views) > 1 else views[0]
    total = reduce_z(grid, reduce_plane(grid, view, order))[0]
    total = grid.swap_half(total.astype(BF16)).astype(F32)
    out, at = [], 0
    for view in views:
        out.append(total[at : at + view.shape[4]])
        at += view.shape[4]
    return out


def gather_norms(grid, packed):
    both = paired(packed[None], grid.to_core(packed[None]), grid.core, 0)
    full = gather_plane(grid, gather_z(grid, both), "xy")
    return full.reshape(grid.count, packed.shape[0])


def reduce_norms(grid, packed):
    view = packed.reshape(grid.depth, 2, 2, 2, 1, packed.shape[1])
    view = pick(view, grid.core, 2) + grid.to_core(pick(view, 1 - grid.core, 2))
    view = pick(view, grid.y, 1) + grid.to_y(pick(view, 1 - grid.y, 1))
    view = pick(view, grid.x, 1) + grid.to_x(pick(view, 1 - grid.x, 1))
    return reduce_z(grid, view)[0]


def dot(a, b):
    return jnp.einsum("rlk,km->rlm", a, b, preferred_element_type=F32)


def dot_back(a, b):
    return jnp.einsum("rlm,km->rlk", a, b, preferred_element_type=F32)


def dot_weight(a, b):
    return jnp.einsum("rlk,rlm->km", a, b, preferred_element_type=F32).astype(BF16)


def layer_norm(values, gain, shift):
    average = jnp.mean(values, -1, keepdims=True)
    centred = values - average
    inverse = lax.rsqrt(jnp.mean(centred * centred, -1, keepdims=True) + EPS)
    normed = centred * inverse
    return normed * gain + shift, (normed, inverse)


def norm_back(upstream, stored, gain):
    normed, inverse = stored
    scaled = upstream * gain
    grad = inverse * (
        scaled
        - jnp.mean(scaled, -1, keepdims=True)
        - normed * jnp.mean(scaled * normed, -1, keepdims=True)
    )
    return grad, jnp.sum(upstream * normed, axis=0), jnp.sum(upstream, axis=0)


def heads_of(array, count):
    return array.reshape(array.shape[0], array.shape[1], count, array.shape[2] // count)


def attend(q, k, v, allowed, count):
    rows, length, width = q.shape
    factor = (width // count) ** (-0.5)
    qh, kh, vh = heads_of(q, count), heads_of(k, count), heads_of(v, count)
    scores = jnp.einsum("rqhd,rkhd->rhqk", qh, kh, preferred_element_type=F32) * factor
    scores = jnp.where(allowed[:, None], scores, -1e30)
    exponent = jnp.exp(scores - jnp.max(scores, -1, keepdims=True))
    probs = exponent / jnp.sum(exponent, -1, keepdims=True)
    context = jnp.einsum("rhqk,rkhd->rqhd", probs.astype(BF16), vh, preferred_element_type=F32)
    return context.reshape(rows, length, width).astype(BF16), probs


def attend_back(grad, q, k, v, probs, count):
    rows, length, width = q.shape
    factor = (width // count) ** (-0.5)
    qh, kh, vh, gh = (heads_of(a, count) for a in (q, k, v, grad))
    dv = jnp.einsum("rhqk,rqhd->rkhd", probs.astype(BF16), gh, preferred_element_type=F32)
    dp = jnp.einsum("rqhd,rkhd->rhqk", gh, vh, preferred_element_type=F32)
    ds = (probs * (dp - jnp.sum(dp * probs, -1, keepdims=True))).astype(BF16)
    dq = jnp.einsum("rhqk,rkhd->rqhd", ds, kh, preferred_element_type=F32) * factor
    dk = jnp.einsum("rhqk,rqhd->rkhd", ds, qh, preferred_element_type=F32) * factor
    flat = lambda a: a.reshape(a.shape[0], a.shape[1], width).astype(BF16)
    return flat(dq), flat(dk), flat(dv)


def share(grid, own):
    return jnp.stack([own, grid.to_core(own)])


def settle(grid, partial_sums):
    return partial_sums[0] + grid.to_core(partial_sums[1])


def project(low, w):
    return jnp.split(dot(low, w).astype(BF16), 3, axis=-1)


def attn_out(grid, values, context, w, gain, shift):
    result, stored = layer_norm(values + settle(grid, dot(context, w)), gain, shift)
    return result, stored


def feed_forward(grid, values, up, down, gain, shift):
    low = share(grid, values.astype(BF16))
    before = dot(low, up)
    hidden = jax.nn.gelu(before, approximate=False).astype(BF16)
    result, stored = layer_norm(values + settle(grid, dot(hidden, down)), gain, shift)
    return result, (low, before, hidden, stored)


def feed_back(grid, upstream, saved, up, down, gain):
    low, before, hidden, stored = saved
    summed, dgain, dshift = norm_back(upstream, stored, gain)
    out = share(grid, summed.astype(BF16))
    hidden_grad = dot_back(out, down)
    _, pull = jax.vjp(partial(jax.nn.gelu, approximate=False), before)
    before_grad = pull(hidden_grad)[0].astype(BF16)
    entry = settle(grid, dot_back(before_grad, up))
    ddown = dot_weight(hidden, out)
    dup = dot_weight(low, before_grad)
    return summed + entry, dup, ddown, dgain, dshift


def attn_out_back(grid, upstream, context, stored, w, gain):
    summed, dgain, dshift = norm_back(upstream, stored, gain)
    out = share(grid, summed.astype(BF16))
    context_grad = dot_back(out, w).astype(BF16)
    return summed, context_grad, dot_weight(context, out), dgain, dshift


def project_back(grid, low, grads, w):
    joined = jnp.concatenate(grads, axis=-1)
    return settle(grid, dot_back(joined, w)), dot_weight(low, joined)


def pack_norms(text_gains, text_shifts, image_gains, image_shifts):
    return jnp.concatenate([a.reshape(-1) for a in (text_gains, text_shifts, image_gains, image_shifts)])


def unpack_norms(full, tw, iw):
    out, at = [], 0
    for width in (tw, tw, iw, iw):
        part = full[:, at : at + 4 * width].reshape(-1, 4, width)
        out.append(part.transpose(1, 0, 2).reshape(4, -1).astype(F32))
        at += 4 * width
    return out


def shards(
    wide,
    narrow,
    text_in,
    image_in,
    text_segments,
    text_co_in,
    text_co_out,
    image_co_in,
    image_co_out,
    text_self_in,
    text_self_out,
    image_self_in,
    image_self_out,
    text_up,
    text_down,
    image_up,
    image_down,
    text_gains,
    text_shifts,
    image_gains,
    image_shifts,
    grad_text_out,
    grad_image_out,
):
    grid = Grid(wide, narrow)
    tw, iw = text_gains.shape[2], image_gains.shape[2]

    norms = gather_norms(
        grid, pack_norms(text_gains[0], text_shifts[0], image_gains[0], image_shifts[0])
    )
    gain_t, shift_t, gain_i, shift_i = unpack_norms(norms, tw, iw)

    specs = [
        ("tci", "in", [text_co_in[0]], 3, "xy"),
        ("ici", "in", [image_co_in[0]], 3, "yx"),
        ("to0", "out", [text_co_out[0], text_down[0, 0]], 1, "xy"),
        ("tu0", "in", [text_up[0, 0]], 1, "yx"),
        ("io0", "out", [image_co_out[0], image_down[0, 0]], 1, "xy"),
        ("iu0", "in", [image_up[0, 0]], 1, "yx"),
        ("tsi", "in", [text_self_in[0]], 3, "yx"),
        ("isi", "in", [image_self_in[0]], 3, "xy"),
        ("to1", "out", [text_self_out[0], text_down[0, 1]], 1, "yx"),
        ("tu1", "in", [text_up[0, 1]], 1, "xy"),
        ("io1", "out", [image_self_out[0], image_down[0, 1]], 1, "yx"),
        ("iu1", "in", [image_up[0, 1]], 1, "xy"),
    ]
    full = {}
    order_of = {}
    blocks = []
    for name, kind, mats, groups, order in specs:
        chunk = chunk_in(grid, mats[0], groups) if kind == "in" else chunk_out(grid, mats)
        if len(blocks) >= 2:
            chunk, _ = lax.optimization_barrier((chunk, blocks[-2]))
        block = gather_z(grid, chunk)
        blocks.append(block)
        whole = gather_plane(grid, block, order)
        order_of[name] = order
        if kind == "in":
            full[name] = finish_in(whole)
        else:
            full[name] = finish_out(grid, whole, [m.shape[0] for m in mats])
    tco, td0 = full["to0"]
    ico, id0 = full["io0"]
    tso, td1 = full["to1"]
    iso, id1 = full["io1"]

    segments = share(grid, text_segments[0].astype(F32))
    image_ids = (jnp.arange(image_in.shape[1], dtype=jnp.int32) // (2 * REGIONS)).astype(F32)
    cross = segments[:, :, None] == image_ids[None, None, :]
    cross_back = jnp.swapaxes(cross, 1, 2)
    text_allowed = segments[:, :, None] == segments[:, None, :]
    image_allowed = (image_ids[:, None] == image_ids[None, :])[None]

    hc, ht, hi = HC // 2, HT // 2, HI // 2
    xt, xi = text_in[0].astype(F32), image_in[0].astype(F32)
    low_t, low_i = share(grid, text_in[0]), share(grid, image_in[0])
    qt, kt, vt = project(low_t, full["tci"])
    qi, ki, vi = project(low_i, full["ici"])
    ct, pt = attend(qt, ki, vi, cross, hc)
    ci, pi = attend(qi, kt, vt, cross_back, hc)
    yt, yt_saved = attn_out(grid, xt, ct, tco, gain_t[0], shift_t[0])
    yi, yi_saved = attn_out(grid, xi, ci, ico, gain_i[0], shift_i[0])
    zt, zt_saved = feed_forward(grid, yt, full["tu0"], td0, gain_t[1], shift_t[1])
    zi, zi_saved = feed_forward(grid, yi, full["iu0"], id0, gain_i[1], shift_i[1])

    def self_forward(values, w_in, w_out, up, down, allowed, count, gain, shift):
        low = share(grid, values.astype(BF16))
        q, k, v = project(low, w_in)
        context, probs = attend(q, k, v, allowed, count)
        middle, mid_saved = attn_out(grid, values, context, w_out, gain[2], shift[2])
        top, top_saved = feed_forward(grid, middle, up, down, gain[3], shift[3])
        return top, (low, q, k, v, context, probs, mid_saved, top_saved)

    ot, ot_saved = self_forward(
        zt, full["tsi"], tso, full["tu1"], td1, text_allowed, ht, gain_t, shift_t
    )
    oi, oi_saved = self_forward(
        zi, full["isi"], iso, full["iu1"], id1, image_allowed, hi, gain_i, shift_i
    )

    grads = {}

    def self_backward(upstream, saved, w_in, w_out, up, down, count, gain):
        low, q, k, v, context, probs, mid_saved, top_saved = saved
        middle, dup, ddown, dg3, db3 = feed_back(grid, upstream, top_saved, up, down, gain[3])
        residual, context_grad, dout, dg2, db2 = attn_out_back(
            grid, middle, context, mid_saved, w_out, gain[2]
        )
        joined = attend_back(context_grad, q, k, v, probs, count)
        entry, din = project_back(grid, low, joined, w_in)
        return residual + entry, din, dout, dup, ddown, (dg2, dg3), (db2, db3)

    gt, d_tsi, d_tso, d_tu1, d_td1, dgt_top, dbt_top = self_backward(
        grad_text_out[0].astype(F32), ot_saved, full["tsi"], tso, full["tu1"], td1, ht, gain_t
    )
    gi, d_isi, d_iso, d_iu1, d_id1, dgi_top, dbi_top = self_backward(
        grad_image_out[0].astype(F32), oi_saved, full["isi"], iso, full["iu1"], id1, hi, gain_i
    )

    gt, d_tu0, d_td0, dgt1, dbt1 = feed_back(grid, gt, zt_saved, full["tu0"], td0, gain_t[1])
    gi, d_iu0, d_id0, dgi1, dbi1 = feed_back(grid, gi, zi_saved, full["iu0"], id0, gain_i[1])
    rt, ct_grad, d_tco, dgt0, dbt0 = attn_out_back(grid, gt, ct, yt_saved, tco, gain_t[0])
    ri, ci_grad, d_ico, dgi0, dbi0 = attn_out_back(grid, gi, ci, yi_saved, ico, gain_i[0])
    dqt, dki, dvi = attend_back(ct_grad, qt, ki, vi, pt, hc)
    dqi, dkt, dvt = attend_back(ci_grad, qi, kt, vt, pi, hc)
    et, d_tci = project_back(grid, low_t, (dqt, dkt, dvt), full["tci"])
    ei, d_ici = project_back(grid, low_i, (dqi, dki, dvi), full["ici"])

    groups_of = {name: groups for name, _, _, groups, _ in specs}

    def give_in(name, grad):
        return return_in(grid, grad, groups_of[name], order_of[name])

    g_tu1 = give_in("tu1", d_tu1)
    g_iu1 = give_in("iu1", d_iu1)
    g_tso, g_td1 = return_out(grid, [d_tso, d_td1], order_of["to1"])
    g_iso, g_id1 = return_out(grid, [d_iso, d_id1], order_of["io1"])
    g_tsi = give_in("tsi", d_tsi)
    g_isi = give_in("isi", d_isi)
    g_tu0 = give_in("tu0", d_tu0)
    g_iu0 = give_in("iu0", d_iu0)
    g_tco, g_td0 = return_out(grid, [d_tco, d_td0], order_of["to0"])
    g_ico, g_id0 = return_out(grid, [d_ico, d_id0], order_of["io0"])
    g_tci = give_in("tci", d_tci)
    g_ici = give_in("ici", d_ici)

    def by_device(rows, width):
        return jnp.stack(rows).reshape(4, grid.count, width).transpose(1, 0, 2).reshape(grid.count, 4 * width)

    sums = jnp.concatenate(
        [
            by_device([dgt0, dgt1, *dgt_top], tw),
            by_device([dbt0, dbt1, *dbt_top], tw),
            by_device([dgi0, dgi1, *dgi_top], iw),
            by_device([dbi0, dbi1, *dbi_top], iw),
        ],
        1,
    )
    own = reduce_norms(grid, sums)
    norm_grads, at = [], 0
    for width in (tw, tw, iw, iw):
        norm_grads.append(own[at : at + 4 * width].reshape(1, 4, width))
        at += 4 * width

    return (
        ot.astype(BF16)[None],
        oi.astype(BF16)[None],
        (rt + et)[None],
        (ri + ei)[None],
        g_tci[None],
        g_tco[None],
        g_ici[None],
        g_ico[None],
        g_tsi[None],
        g_tso[None],
        g_isi[None],
        g_iso[None],
        jnp.stack([g_tu0, g_tu1])[None],
        jnp.stack([g_td0, g_td1])[None],
        jnp.stack([g_iu0, g_iu1])[None],
        jnp.stack([g_id0, g_id1])[None],
        *norm_grads,
    )


def solution(mesh):
    rows = P(AXES, None, None)
    weight = P(None, AXES, None)
    pair = P(None, None, AXES, None)
    norm = P(None, None, AXES)
    return jax.shard_map(
        partial(shards, mesh.shape["wide"], mesh.shape["narrow"]),
        mesh=mesh,
        in_specs=(rows, rows, P(AXES, None), *[weight] * 8, *[pair] * 4, *[norm] * 4, rows, rows),
        out_specs=(rows, rows, rows, rows, *[weight] * 8, *[pair] * 4, *[norm] * 4),
        check_vma=False,
    )
```

time: 3780 us -> 1010 us (0.27)
  waiting for transfers between devices: 2850 us -> 413 us
  blocking collectives: 590 us -> 0 us
  starting transfers between devices: 1.84 us -> 244 us
  matrix products: 180 us -> 77.4 us
  other arithmetic: 24.2 us -> 121 us
    reduce_scatter x14 -> x0, waiting for transfers between devices: 1900 us -> none  [the longest x2 286 us: full_return(): lax.psum_scatter(rows[1], ('wide', 'narrow'), scatter_dimension=0, tiled=...]
    unnamed x42 -> x0, waiting for transfers between devices: 644 us -> none
    all_gather x8 -> x0, blocking collectives: 550 us -> none  [the longest x2 144 us: full_fetch(): lax.all_gather(norms[2], ('wide', 'narrow'), axis=1, tiled=True)]
    ppermute x0 -> x189, waiting for transfers between devices: none -> 413 us  [move(): return lax.ppermute(value, AXES, pairs)]
    all_gather x16 -> x0, waiting for transfers between devices: 304 us -> none  [the longest x2 61.6 us: full_fetch(): lax.all_gather(rows[2], ('wide', 'narrow'), axis=0, tiled=True)]
    ppermute x0 -> x189, starting transfers between devices: none -> 244 us  [move(): return lax.ppermute(value, AXES, pairs)]
    dot_general x72 -> x69, matrix products: 180 us -> 73.4 us  [the longest x16 23.4 us: dot_weight(): jnp.einsum('rlk,rlm->km', a, b, preferred_element_type=F32).astype(BF16)]
    convert_element_type x12 -> x58, other arithmetic: 4.46 us -> 53.9 us  [the longest x24 27.5 us: add_low(): return (a.astype(F32) + b.astype(F32)).astype(BF16)]
  transfers between devices with their start and end apart: 36 -> 189, of which waited for: 25 -> 76; matrix products, arithmetic and copies ran while one was open for 8% -> 31% of each run, Pallas kernels for 0% -> 0%
where the time goes in v1:
time: 1010 us; the launch traced here: 1000 us
  waiting for transfers between devices  413 us (41%)
  starting transfers between devices  244 us (24%)
  local copies, waits for them, and re-layouts  138 us (14%)
  other arithmetic  121 us (12%)
  matrix products  77.4 us (8%)
    ppermute x189, waiting for transfers between devices, move(): return lax.ppermute(value, AXES, pairs)  413 us
    ppermute x189, starting transfers between devices, move(): return lax.ppermute(value, AXES, pairs)  244 us
    convert_element_type x24, other arithmetic, add_low(): return (a.astype(F32) + b.astype(F32)).astype(BF16)  27.5 us
    dot_general x16, matrix products, dot_weight(): jnp.einsum('rlk,rlm->km', a, b, preferred_element_type=F32).astype(BF16)  23.4 us
    unnamed x553, local copies, waits for them, and re-layouts  23.4 us
    dot_general x16, matrix products, dot_back(): return jnp.einsum('rlm,km->rlk', a, b, preferred_element_type=F32)  22.8 us
    dynamic_slice x26, local copies, waits for them, and re-layouts, pick(): return lax.dynamic_index_in_dim(value, index, axis, keepdims=False)  22.1 us
  transfers between devices with their start and end apart: 189, of which 76 were waited for; matrix products, arithmetic and copies ran while one was open for 31% of the time, Pallas kernels for 0%

profile of v1, /device:TPU:0, one launch (start us, length us, event | category | flops | bytes accessed | tf_op | source)
XLA Modules:
  0.0 999.7 jit_solution(16042352617068190129)
XLA Ops:
  13.3 4.9 collective-permute-start.23
  19.5 3.2 collective-permute-done.24
  41.0 5.7 collective-permute-start.42
  50.3 8.7 collective-permute-start.8
  59.0 4.8 collective-permute-done.43
  64.7 3.2 collective-permute-done.10
  67.9 8.2 collective-permute-start.39
  80.6 11.1 %collective-permute-start.2 = (bf16[2,32,1536]{2,1,0:T(8,128)(2,1)S(1)}, bf16[2,32,1536]{2,1,0:T(8,128)(2,1)S(1)}, u32[]{:S(2)}, u32[]{:S(2)}) collective-permute-start(bf16[2,32,1536]{2,1,0:T(8,128)(2,1)S(1)} %pad_maximum_fusion.68), channel_id=1, source_target_pairs={{0,24},{1,25},{2,26},{3,27},{4,28},{5,29},{6,30},{7,31},{8,0},{9,1... | collective-permute-start | bytes 589832 | tf_op jit(solution)/shard_map/ppermute | solution.py:39
  91.7 3.8 collective-permute-done.40
  95.5 3.1 collective-permute-done.81
  98.7 8.0 collective-permute-start.3
  106.7 9.7 collective-permute-done.82
  118.1 3.9 collective-permute-start.48
  126.1 3.4 collective-permute-start.16
  129.5 9.5 collective-permute-done.49
  143.1 12.5 %collective-permute-done.17 = bf16[1,128,768]{2,1,0:T(8,128)(2,1)S(1)} collective-permute-done((bf16[1,128,768]{2,1,0:T(8,128)(2,1)S(1)}, bf16[1,128,768]{2,1,0:T(8,128)(2,1)S(1)}, u32[]{:S(2)}, u32[]{:S(2)}) %collective-permute-start.17) | collective-permute-done | bytes 196640 | tf_op jit(solution)/shard_map/ppermute | solution.py:39
  157.4 9.2 collective-permute-done.31
  172.7 3.1 collective-permute-done.59
  179.9 3.0 collective-permute-done.61
  184.4 10.8 %collective-permute-done.62 = bf16[2,32,1536]{2,1,0:T(8,128)(2,1)S(1)} collective-permute-done((bf16[2,32,1536]{2,1,0:T(8,128)(2,1)S(1)}, bf16[2,32,1536]{2,1,0:T(8,128)(2,1)S(1)}, u32[]{:S(2)}, u32[]{:S(2)}) %collective-permute-start.62) | collective-permute-done | bytes 196640 | tf_op jit(solution)/shard_map/ppermute | solution.py:39
  197.4 16.5 %collective-permute-done.74 = bf16[4,2,32,512]{3,2,1,0:T(8,128)(2,1)S(1)} collective-permute-done((bf16[4,2,32,512]{3,2,1,0:T(8,128)(2,1)S(1)}, bf16[4,2,32,512]{3,2,1,0:T(8,128)(2,1)S(1)}, u32[]{:S(2)}, u32[]{:S(2)}) %collective-permute-start.74) | collective-permute-done | bytes 262176 | tf_op jit(solution)/shard_map/ppermute | solution.py:39
  217.4 4.0 collective-permute-done.64
  221.4 5.3 collective-permute-done.65
  231.7 4.2 collective-permute-done.90
  239.8 16.6 %collective-permute-done.5 = bf16[4,2,32,1536]{3,2,1,0:T(8,128)(2,1)S(1)} collective-permute-done((bf16[4,2,32,1536]{3,2,1,0:T(8,128)(2,1)S(1)}, bf16[4,2,32,1536]{3,2,1,0:T(8,128)(2,1)S(1)}, u32[]{:S(2)}, u32[]{:S(2)}) %collective-permute-start.5) | collective-permute-done | bytes 786464 | tf_op jit(solution)/shard_map/ppermute | solution.py:39
  258.2 10.2 %collective-permute-done.51 = bf16[4,1,120,768]{3,2,0,1:T(8,128)(2,1)S(1)} collective-permute-done((bf16[4,1,120,768]{3,2,0,1:T(8,128)(2,1)S(1)}, bf16[4,1,120,768]{3,2,0,1:T(8,128)(2,1)S(1)}, u32[]{:S(2)}, u32[]{:S(2)}) %collective-permute-start.51) | collective-permute-done | bytes 737312 | tf_op jit(solution)/shard_map/ppermute | solution.py:39
  270.3 11.6 %collective-permute-done.92 = bf16[4,2,32,512]{3,2,1,0:T(8,128)(2,1)S(1)} collective-permute-done((bf16[4,2,32,512]{3,2,1,0:T(8,128)(2,1)S(1)}, bf16[4,2,32,512]{3,2,1,0:T(8,128)(2,1)S(1)}, u32[]{:S(2)}, u32[]{:S(2)}) %collective-permute-start.92) | collective-permute-done | bytes 262176 | tf_op jit(solution)/shard_map/ppermute | solution.py:39
  285.8 10.9 %collective-permute-done.75 = bf16[4,2,2,32,512]{4,3,2,0,1:T(8,128)(2,1)S(1)} collective-permute-done((bf16[4,2,2,32,512]{4,3,2,0,1:T(8,128)(2,1)S(1)}, bf16[4,2,2,32,512]{4,3,2,0,1:T(8,128)(2,1)S(1)}, u32[]{:S(2)}, u32[]{:S(2)}) %collective-permute-start.75) | collective-permute-done | bytes 524320 | tf_op jit(solution)/shard_map/ppermute | solution.py:39
  299.5 9.8 collective-permute-done.67
  311.1 12.3 %collective-permute-done.78 = bf16[4,2,32,1536]{3,2,1,0:T(8,128)(2,1)S(1)} collective-permute-done((bf16[4,2,32,1536]{3,2,1,0:T(8,128)(2,1)S(1)}, bf16[4,2,32,1536]{3,2,1,0:T(8,128)(2,1)S(1)}, u32[]{:S(2)}, u32[]{:S(2)}) %collective-permute-start.78) | collective-permute-done | bytes 786464 | tf_op jit(solution)/shard_map/ppermute | solution.py:39
  328.8 10.0 %collective-permute-done.93 = bf16[4,2,2,32,512]{4,3,1,0,2:T(8,128)(2,1)S(1)} collective-permute-done((bf16[4,2,2,32,512]{4,3,1,0,2:T(8,128)(2,1)S(1)}, bf16[4,2,2,32,512]{4,3,1,0,2:T(8,128)(2,1)S(1)}, u32[]{:S(2)}, u32[]{:S(2)}) %collective-permute-start.93) | collective-permute-done | bytes 524320 | tf_op jit(solution)/shard_map/ppermute | solution.py:39
  342.5 7.0 collective-permute-done.85
  354.4 7.4 collective-permute-done.14
  367.9 6.9 collective-permute-done.34
  378.3 56.1 %collective-permute-done.52 = bf16[4,2,1,120,768]{4,3,0,2,1:T(8,128)(2,1)S(1)} collective-permute-done((bf16[4,2,1,120,768]{4,3,0,2,1:T(8,128)(2,1)S(1)}, bf16[4,2,1,120,768]{4,3,0,2,1:T(8,128)(2,1)S(1)}, u32[]{:S(2)}, u32[]{:S(2)}) %collective-permute-start.52) | collective-permute-done | bytes 1474592 | tf_op jit(solution)/shard_map/ppermute | solution.py:39
  452.6 9.0 copy_bitcast_fusion
  608.4 4.3 collective-permute-done.136
  612.9 5.1 collective-permute-start.138
  626.5 10.7 %collective-permute-done.166 = bf16[4,2,24,1536]{3,2,1,0:T(8,128)(2,1)} collective-permute-done((bf16[4,2,24,1536]{3,2,1,0:T(8,128)(2,1)}, bf16[4,2,24,1536]{3,2,1,0:T(8,128)(2,1)}, u32[]{:S(2)}, u32[]{:S(2)}) %collective-permute-start.166) | collective-permute-done | bytes 589856 | tf_op jit(solution)/shard_map/ppermute | solution.py:39
  639.4 3.8 collective-permute-start.167
  646.4 3.2 collective-permute-start.168
  679.5 7.3 collective-permute-done.160
  697.8 3.1 collective-permute-done.162
  704.1 3.4 collective-permute-start.143
  716.0 5.2 collective-permute-done.144
  772.1 3.0 collective-permute-done.119
  775.0 7.2 collective-permute-done.120
  790.2 4.7 collective-permute-start.106
  808.4 6.2 collective-permute-done.171
  818.6 12.1 %collective-permute-done.184 = f32[4,2,1,448]{3,1,0,2:T(2,128)S(1)} collective-permute-done((f32[4,2,1,448]{3,1,0,2:T(2,128)S(1)}, f32[4,2,1,448]{3,1,0,2:T(2,128)S(1)}, u32[]{:S(2)}, u32[]{:S(2)}) %collective-permute-start.184) | collective-permute-done | bytes 14368 | tf_op jit(solution)/shard_map/ppermute | solution.py:39
  834.5 8.6 collective-permute-start.186
  852.6 3.2 collective-permute-start.156
  862.0 4.0 collective-permute-done.156
  866.0 3.1 collective-permute-start.175
  905.5 3.0 collective-permute-start.151
  910.5 3.7 collective-permute-done.149
  915.2 6.5 collective-permute-done.150
  928.2 12.3 %collective-permute-done.111 = bf16[4,2,2,24,1536]{4,3,1,0,2:T(8,128)(2,1)} collective-permute-done((bf16[4,2,2,24,1536]{4,3,1,0,2:T(8,128)(2,1)}, bf16[4,2,2,24,1536]{4,3,1,0,2:T(8,128)(2,1)}, u32[]{:S(2)}, u32[]{:S(2)}) %collective-permute-start.111) | collective-permute-done | bytes 1179680 | tf_op jit(solution)/shard_map/ppermute | solution.py:39
  951.7 3.8 collective-permute-done.132
  963.5 3.8 collective-permute-done.113
  967.3 6.0 collective-permute-done.114
  976.9 3.8 collective-permute-start.125
  984.5 3.6 collective-permute-done.125
  988.1 8.1 collective-permute-done.126
  (1429 shorter events, 512.6 us)
Async XLA Ops:
  2.5 36.8 %collective-permute-start.37 = (bf16[24,1152]{1,0:T(8,128)(2,1)S(1)}, bf16[24,1152]{1,0:T(8,128)(2,1)S(1)}, u32[]{:S(2)}, u32[]{:S(2)}) collective-permute-start(bf16[24,1152]{1,0:T(8,128)(2,1)S(1)} %bitcast.1557), channel_id=1, source_target_pairs={{0,2},{1,3},{2,0},{3,1},{4,6},{5,7},{6,4},{7,5},{8,10},{9,11},{10,... | collective-permute-start | bytes 165896 | tf_op jit(solution)/shard_map/ppermute | solution.py:39
  5.0 34.5 %collective-permute-start.9 = (bf16[24,1536]{1,0:T(8,128)(2,1)S(1)}, bf16[24,1536]{1,0:T(8,128)(2,1)S(1)}, u32[]{:S(2)}, u32[]{:S(2)}) collective-permute-start(bf16[24,1536]{1,0:T(8,128)(2,1)S(1)} %bitcast.1554), channel_id=1, source_target_pairs={{0,2},{1,3},{2,0},{3,1},{4,6},{5,7},{6,4},{7,5},{8,10},{9,11},{10,... | collective-permute-start | bytes 221192 | tf_op jit(solution)/shard_map/ppermute | solution.py:39
  19.5 27.3 %collective-permute-start.1 = (bf16[32,1536]{1,0:T(8,128)(2,1)S(1)}, bf16[32,1536]{1,0:T(8,128)(2,1)S(1)}, u32[]{:S(2)}, u32[]{:S(2)}) collective-permute-start(bf16[32,1536]{1,0:T(8,128)(2,1)S(1)} %bitcast.1550), channel_id=1, source_target_pairs={{0,2},{1,3},{2,0},{3,1},{4,6},{5,7},{6,4},{7,5},{8,10},{9,11},{10,... | collective-permute-start | bytes 294920 | tf_op jit(solution)/shard_map/ppermute | solution.py:39
  22.7 17.6 %collective-permute-start.29 = (bf16[24,1536]{1,0:T(8,128)(2,1)S(1)}, bf16[24,1536]{1,0:T(8,128)(2,1)S(1)}, u32[]{:S(2)}, u32[]{:S(2)}) collective-permute-start(bf16[24,1536]{1,0:T(8,128)(2,1)S(1)} %bitcast.1552), channel_id=1, source_target_pairs={{0,2},{1,3},{2,0},{3,1},{4,6},{5,7},{6,4},{7,5},{8,10},{9,11},{10,... | collective-permute-start | bytes 221192 | tf_op jit(solution)/shard_map/ppermute | solution.py:39
  41.0 18.0 %collective-permute-start.42 = (bf16[2,24,1152]{2,1,0:T(8,128)(2,1)S(1)}, bf16[2,24,1152]{2,1,0:T(8,128)(2,1)S(1)}, u32[]{:S(2)}, u32[]{:S(2)}) collective-permute-start(bf16[2,24,1152]{2,1,0:T(8,128)(2,1)S(1)} %pad_maximum_fusion.104), channel_id=1, source_target_pairs={{0,24},{1,25},{2,26},{3,27},{4,28},{5,29},{6,30},{7,31},{8,0},{9,1... | collective-permute-start | bytes 331784 | tf_op jit(solution)/shard_map/ppermute | solution.py:39
  50.3 314.8 %collective-permute-start.8 = (bf16[64,768]{1,0:T(8,128)(2,1)S(1)}, bf16[64,768]{1,0:T(8,128)(2,1)S(1)}, u32[]{:S(2)}, u32[]{:S(2)}) collective-permute-start(bf16[64,768]{1,0:T(8,128)(2,1)S(1)} %bitcast.1498), channel_id=1, source_target_pairs={{0,2},{1,3},{2,0},{3,1},{4,6},{5,7},{6,4},{7,5},{8,10},{9,11},{10,... | collective-permute-start | bytes 294920 | tf_op jit(solution)/shard_map/ppermute | solution.py:39
  67.9 23.7 %collective-permute-start.39 = (bf16[1,64,1024]{2,1,0:T(8,128)(2,1)S(1)}, bf16[1,64,1024]{2,1,0:T(8,128)(2,1)S(1)}, u32[]{:S(2)}, u32[]{:S(2)}) collective-permute-start(bf16[1,64,1024]{2,1,0:T(8,128)(2,1)S(1)} %bitcast.1538), channel_id=1, source_target_pairs={{0,24},{1,25},{2,26},{3,27},{4,28},{5,29},{6,30},{7,31},{8,0},{9,1... | collective-permute-start | bytes 393224 | tf_op jit(solution)/shard_map/ppermute | solution.py:39
  77.0 18.5 %collective-permute-start.40 = (bf16[1,64,1024]{2,1,0:T(8,128)(2,1)S(1)}, bf16[1,64,1024]{2,1,0:T(8,128)(2,1)S(1)}, u32[]{:S(2)}, u32[]{:S(2)}) collective-permute-start(bf16[1,64,1024]{2,1,0:T(8,128)(2,1)S(1)} %bitcast.1539), channel_id=1, source_target_pairs={{0,16},{1,17},{2,18},{3,19},{4,20},{5,21},{6,22},{7,23},{8,24},{9,... | collective-permute-start | bytes 393224 | tf_op jit(solution)/shard_map/ppermute | solution.py:39
  78.2 17.2 %collective-permute-start.41 = (bf16[1,64,1024]{2,1,0:T(8,128)(2,1)S(1)}, bf16[1,64,1024]{2,1,0:T(8,128)(2,1)S(1)}, u32[]{:S(2)}, u32[]{:S(2)}) collective-permute-start(bf16[1,64,1024]{2,1,0:T(8,128)(2,1)S(1)} %bitcast.1540), channel_id=1, source_target_pairs={{0,8},{1,9},{2,10},{3,11},{4,12},{5,13},{6,14},{7,15},{8,16},{9,17... | collective-permute-start | bytes 393224 | tf_op jit(solution)/shard_map/ppermute | solution.py:39
  80.6 37.5 %collective-permute-start.2 = (bf16[2,32,1536]{2,1,0:T(8,128)(2,1)S(1)}, bf16[2,32,1536]{2,1,0:T(8,128)(2,1)S(1)}, u32[]{:S(2)}, u32[]{:S(2)}) collective-permute-start(bf16[2,32,1536]{2,1,0:T(8,128)(2,1)S(1)} %pad_maximum_fusion.68), channel_id=1, source_target_pairs={{0,24},{1,25},{2,26},{3,27},{4,28},{5,29},{6,30},{7,31},{8,0},{9,1... | collective-permute-start | bytes 589832 | tf_op jit(solution)/shard_map/ppermute | solution.py:39
  95.4 20.9 %collective-permute-start.82 = (bf16[1,64,1024]{2,1,0:T(8,128)(2,1)S(1)}, bf16[1,64,1024]{2,1,0:T(8,128)(2,1)S(1)}, u32[]{:S(2)}, u32[]{:S(2)}) collective-permute-start(bf16[1,64,1024]{2,1,0:T(8,128)(2,1)S(1)} %bitcast.1535), channel_id=1, source_target_pairs={{0,16},{1,17},{2,18},{3,19},{4,20},{5,21},{6,22},{7,23},{8,24},{9,... | collective-permute-start | bytes 393224 | tf_op jit(solution)/shard_map/ppermute | solution.py:39
  95.4 20.9 %collective-permute-start.83 = (bf16[1,64,1024]{2,1,0:T(8,128)(2,1)S(1)}, bf16[1,64,1024]{2,1,0:T(8,128)(2,1)S(1)}, u32[]{:S(2)}, u32[]{:S(2)}) collective-permute-start(bf16[1,64,1024]{2,1,0:T(8,128)(2,1)S(1)} %bitcast.1536), channel_id=1, source_target_pairs={{0,8},{1,9},{2,10},{3,11},{4,12},{5,13},{6,14},{7,15},{8,16},{9,17... | collective-permute-start | bytes 393224 | tf_op jit(solution)/shard_map/ppermute | solution.py:39
  98.7 23.3 %collective-permute-start.3 = (bf16[2,32,1536]{2,1,0:T(8,128)(2,1)S(1)}, bf16[2,32,1536]{2,1,0:T(8,128)(2,1)S(1)}, u32[]{:S(2)}, u32[]{:S(2)}) collective-permute-start(bf16[2,32,1536]{2,1,0:T(8,128)(2,1)S(1)} %pad_maximum_fusion.68), channel_id=1, source_target_pairs={{0,16},{1,17},{2,18},{3,19},{4,20},{5,21},{6,22},{7,23},{8,24},{9,... | collective-permute-start | bytes 589832 | tf_op jit(solution)/shard_map/ppermute | solution.py:39
  116.4 61.4 %collective-permute-start.45 = (bf16[4,2,24,1152]{3,2,1,0:T(8,128)(2,1)S(1)}, bf16[4,2,24,1152]{3,2,1,0:T(8,128)(2,1)S(1)}, u32[]{:S(2)}, u32[]{:S(2)}) collective-permute-start(bf16[4,2,24,1152]{3,2,1,0:T(8,128)(2,1)S(1)} %pad_maximum_fusion.43), channel_id=1, source_target_pairs={{0,4},{1,5},{2,6},{3,7},{4,0},{5,1},{6,2},{7,3},{8,12},{9,13},{10,... | collective-permute-start | bytes 1327112 | tf_op jit(solution)/shard_map/ppermute | solution.py:39
  171.2 44.1 %collective-permute-start.13 = (bf16[4,2,24,1536]{3,2,1,0:T(8,128)(2,1)S(1)}, bf16[4,2,24,1536]{3,2,1,0:T(8,128)(2,1)S(1)}, u32[]{:S(2)}, u32[]{:S(2)}) collective-permute-start(bf16[4,2,24,1536]{3,2,1,0:T(8,128)(2,1)S(1)} %pad_maximum_fusion.26), channel_id=1, source_target_pairs={{0,1},{1,0},{2,3},{3,2},{4,5},{5,4},{6,7},{7,6},{8,9},{9,8},{10,11... | collective-permute-start | bytes 1769480 | tf_op jit(solution)/shard_map/ppermute | solution.py:39
  177.4 17.7 %collective-permute-start.62 = (bf16[2,32,1536]{2,1,0:T(8,128)(2,1)S(1)}, bf16[2,32,1536]{2,1,0:T(8,128)(2,1)S(1)}, u32[]{:S(2)}, u32[]{:S(2)}) collective-permute-start(bf16[2,32,1536]{2,1,0:T(8,128)(2,1)S(1)} %pad_maximum_fusion.73), channel_id=1, source_target_pairs={{0,16},{1,17},{2,18},{3,19},{4,20},{5,21},{6,22},{7,23},{8,24},{9,... | collective-permute-start | bytes 589832 | tf_op jit(solution)/shard_map/ppermute | solution.py:39
  177.7 18.0 %collective-permute-start.63 = (bf16[2,32,1536]{2,1,0:T(8,128)(2,1)S(1)}, bf16[2,32,1536]{2,1,0:T(8,128)(2,1)S(1)}, u32[]{:S(2)}, u32[]{:S(2)}) collective-permute-start(bf16[2,32,1536]{2,1,0:T(8,128)(2,1)S(1)} %pad_maximum_fusion.73), channel_id=1, source_target_pairs={{0,8},{1,9},{2,10},{3,11},{4,12},{5,13},{6,14},{7,15},{8,16},{9,17... | collective-permute-start | bytes 589832 | tf_op jit(solution)/shard_map/ppermute | solution.py:39
  182.9 31.6 %collective-permute-start.70 = (bf16[4,1,64,1024]{3,2,0,1:T(8,128)(2,1)S(1)}, bf16[4,1,64,1024]{3,2,0,1:T(8,128)(2,1)S(1)}, u32[]{:S(2)}, u32[]{:S(2)}) collective-permute-start(bf16[4,1,64,1024]{3,2,0,1:T(8,128)(2,1)S(1)} %fusion.413), channel_id=1, source_target_pairs={{0,1},{1,0},{2,3},{3,2},{4,5},{5,4},{6,7},{7,6},{8,9},{9,8},{10,11... | collective-permute-start | bytes 1572872 | tf_op jit(solution)/shard_map/ppermute | solution.py:39
  195.2 19.7 %collective-permute-start.84 = (bf16[4,1,64,1024]{3,2,0,1:T(8,128)(2,1)S(1)}, bf16[4,1,64,1024]{3,2,0,1:T(8,128)(2,1)S(1)}, u32[]{:S(2)}, u32[]{:S(2)}) collective-permute-start(bf16[4,1,64,1024]{3,2,0,1:T(8,128)(2,1)S(1)} %fusion.299), channel_id=1, source_target_pairs={{0,4},{1,5},{2,6},{3,7},{4,0},{5,1},{6,2},{7,3},{8,12},{9,13},{10,... | collective-permute-start | bytes 1572872 | tf_op jit(solution)/shard_map/ppermute | solution.py:39
  195.7 18.2 %collective-permute-start.74 = (bf16[4,2,32,512]{3,2,1,0:T(8,128)(2,1)S(1)}, bf16[4,2,32,512]{3,2,1,0:T(8,128)(2,1)S(1)}, u32[]{:S(2)}, u32[]{:S(2)}) collective-permute-start(bf16[4,2,32,512]{3,2,1,0:T(8,128)(2,1)S(1)} %pad_maximum_fusion.65), channel_id=1, source_target_pairs={{0,4},{1,5},{2,6},{3,7},{4,0},{5,1},{6,2},{7,3},{8,12},{9,13},{10,... | collective-permute-start | bytes 786440 | tf_op jit(solution)/shard_map/ppermute | solution.py:39
  213.9 24.2 %collective-permute-start.33 = (bf16[4,2,24,1536]{3,2,1,0:T(8,128)(2,1)S(1)}, bf16[4,2,24,1536]{3,2,1,0:T(8,128)(2,1)S(1)}, u32[]{:S(2)}, u32[]{:S(2)}) collective-permute-start(bf16[4,2,24,1536]{3,2,1,0:T(8,128)(2,1)S(1)} %pad_maximum_fusion.28), channel_id=1, source_target_pairs={{0,4},{1,5},{2,6},{3,7},{4,0},{5,1},{6,2},{7,3},{8,12},{9,13},{10,... | collective-permute-start | bytes 1769480 | tf_op jit(solution)/shard_map/ppermute | solution.py:39
  231.6 209.1 %collective-permute-start = (bf16[144,1024]{1,0:T(8,128)(2,1)S(1)}, bf16[144,1024]{1,0:T(8,128)(2,1)S(1)}, u32[]{:S(2)}, u32[]{:S(2)}) collective-permute-start(bf16[144,1024]{1,0:T(8,128)(2,1)S(1)} %bitcast.1514), channel_id=1, source_target_pairs={{0,2},{1,3},{2,0},{3,1},{4,6},{5,7},{6,4},{7,5},{8,10},{9,11},{10,... | collective-permute-start | bytes 884744 | tf_op jit(solution)/shard_map/ppermute | solution.py:39
  235.9 20.5 %collective-permute-start.5 = (bf16[4,2,32,1536]{3,2,1,0:T(8,128)(2,1)S(1)}, bf16[4,2,32,1536]{3,2,1,0:T(8,128)(2,1)S(1)}, u32[]{:S(2)}, u32[]{:S(2)}) collective-permute-start(bf16[4,2,32,1536]{3,2,1,0:T(8,128)(2,1)S(1)} %pad_maximum_fusion.22), channel_id=1, source_target_pairs={{0,4},{1,5},{2,6},{3,7},{4,0},{5,1},{6,2},{7,3},{8,12},{9,13},{10,... | collective-permute-start | bytes 2359304 | tf_op jit(solution)/shard_map/ppermute | solution.py:39
  237.4 31.0 %collective-permute-start.51 = (bf16[4,1,120,768]{3,2,0,1:T(8,128)(2,1)S(1)}, bf16[4,1,120,768]{3,2,0,1:T(8,128)(2,1)S(1)}, u32[]{:S(2)}, u32[]{:S(2)}) collective-permute-start(bf16[4,1,120,768]{3,2,0,1:T(8,128)(2,1)S(1)} %fusion.414), channel_id=1, source_target_pairs={{0,4},{1,5},{2,6},{3,7},{4,0},{5,1},{6,2},{7,3},{8,12},{9,13},{10,... | collective-permute-start | bytes 2211848 | tf_op jit(solution)/shard_map/ppermute | solution.py:39
  238.0 45.4 %collective-permute-start.19 = (bf16[4,1,128,768]{3,2,0,1:T(8,128)(2,1)S(1)}, bf16[4,1,128,768]{3,2,0,1:T(8,128)(2,1)S(1)}, u32[]{:S(2)}, u32[]{:S(2)}) collective-permute-start(bf16[4,1,128,768]{3,2,0,1:T(8,128)(2,1)S(1)} %fusion.415), channel_id=1, source_target_pairs={{0,1},{1,0},{2,3},{3,2},{4,5},{5,4},{6,7},{7,6},{8,9},{9,8},{10,11... | collective-permute-start | bytes 2359304 | tf_op jit(solution)/shard_map/ppermute | solution.py:39
  256.4 70.3 %collective-permute-start.46 = (bf16[4,2,2,24,1152]{4,3,2,0,1:T(8,128)(2,1)S(1)}, bf16[4,2,2,24,1152]{4,3,2,0,1:T(8,128)(2,1)S(1)}, u32[]{:S(2)}, u32[]{:S(2)}) collective-permute-start(bf16[4,2,2,24,1152]{4,3,2,0,1:T(8,128)(2,1)S(1)} %pad_maximum_fusion.21), channel_id=1, source_target_pairs={{0,1},{1,0},{2,3},{3,2},{4,5},{5,4},{6,7},{7,6},{8,9},{9,8},{10,11... | collective-permute-start | bytes 2654216 | tf_op jit(solution)/shard_map/ppermute | solution.py:39
  283.5 25.9 %collective-permute-start.67 = (bf16[4,2,24,1536]{3,2,1,0:T(8,128)(2,1)S(1)}, bf16[4,2,24,1536]{3,2,1,0:T(8,128)(2,1)S(1)}, u32[]{:S(2)}, u32[]{:S(2)}) collective-permute-start(bf16[4,2,24,1536]{3,2,1,0:T(8,128)(2,1)S(1)} %pad_maximum_fusion.29), channel_id=1, source_target_pairs={{0,1},{1,0},{2,3},{3,2},{4,5},{5,4},{6,7},{7,6},{8,9},{9,8},{10,11... | collective-permute-start | bytes 1769480 | tf_op jit(solution)/shard_map/ppermute | solution.py:39
  296.7 26.7 %collective-permute-start.78 = (bf16[4,2,32,1536]{3,2,1,0:T(8,128)(2,1)S(1)}, bf16[4,2,32,1536]{3,2,1,0:T(8,128)(2,1)S(1)}, u32[]{:S(2)}, u32[]{:S(2)}) collective-permute-start(bf16[4,2,32,1536]{3,2,1,0:T(8,128)(2,1)S(1)} %pad_maximum_fusion.24), channel_id=1, source_target_pairs={{0,1},{1,0},{2,3},{3,2},{4,5},{5,4},{6,7},{7,6},{8,9},{9,8},{10,11... | collective-permute-start | bytes 2359304 | tf_op jit(solution)/shard_map/ppermute | solution.py:39
  309.3 32.7 %collective-permute-start.71 = (bf16[4,1,2,64,1024]{4,3,0,2,1:T(8,128)(2,1)S(1)}, bf16[4,1,2,64,1024]{4,3,0,2,1:T(8,128)(2,1)S(1)}, u32[]{:S(2)}, u32[]{:S(2)}) collective-permute-start(bf16[4,1,2,64,1024]{4,3,0,2,1:T(8,128)(2,1)S(1)} %pad_maximum_fusion.17), channel_id=1, source_target_pairs={{0,4},{1,5},{2,6},{3,7},{4,0},{5,1},{6,2},{7,3},{8,12},{9,13},{10,... | collective-permute-start | bytes 3145736 | tf_op jit(solution)/shard_map/ppermute | solution.py:39
  323.4 26.1 %collective-permute-start.85 = (bf16[4,2,1,64,1024]{4,3,0,2,1:T(8,128)(2,1)S(1)}, bf16[4,2,1,64,1024]{4,3,0,2,1:T(8,128)(2,1)S(1)}, u32[]{:S(2)}, u32[]{:S(2)}) collective-permute-start(bf16[4,2,1,64,1024]{4,3,0,2,1:T(8,128)(2,1)S(1)} %pad_maximum_fusion.19), channel_id=1, source_target_pairs={{0,1},{1,0},{2,3},{3,2},{4,5},{5,4},{6,7},{7,6},{8,9},{9,8},{10,11... | collective-permute-start | bytes 3145736 | tf_op jit(solution)/shard_map/ppermute | solution.py:39
  338.8 23.0 %collective-permute-start.14 = (bf16[4,2,2,24,1536]{4,3,1,0,2:T(8,128)(2,1)S(1)}, bf16[4,2,2,24,1536]{4,3,1,0,2:T(8,128)(2,1)S(1)}, u32[]{:S(2)}, u32[]{:S(2)}) collective-permute-start(bf16[4,2,2,24,1536]{4,3,1,0,2:T(8,128)(2,1)S(1)} %pad_maximum_fusion.14), channel_id=1, source_target_pairs={{0,4},{1,5},{2,6},{3,7},{4,0},{5,1},{6,2},{7,3},{8,12},{9,13},{10,... | collective-permute-start | bytes 3538952 | tf_op jit(solution)/shard_map/ppermute | solution.py:39
  342.1 32.7 %collective-permute-start.34 = (bf16[4,2,2,24,1536]{4,3,2,0,1:T(8,128)(2,1)S(1)}, bf16[4,2,2,24,1536]{4,3,2,0,1:T(8,128)(2,1)S(1)}, u32[]{:S(2)}, u32[]{:S(2)}) collective-permute-start(bf16[4,2,2,24,1536]{4,3,2,0,1:T(8,128)(2,1)S(1)} %pad_maximum_fusion.15), channel_id=1, source_target_pairs={{0,1},{1,0},{2,3},{3,2},{4,5},{5,4},{6,7},{7,6},{8,9},{9,8},{10,11... | collective-permute-start | bytes 3538952 | tf_op jit(solution)/shard_map/ppermute | solution.py:39
  349.5 90.3 %collective-permute-start.6 = (bf16[4,2,2,32,1536]{4,3,2,0,1:T(8,128)(2,1)S(1)}, bf16[4,2,2,32,1536]{4,3,2,0,1:T(8,128)(2,1)S(1)}, u32[]{:S(2)}, u32[]{:S(2)}) collective-permute-start(bf16[4,2,2,32,1536]{4,3,2,0,1:T(8,128)(2,1)S(1)} %pad_maximum_fusion.10), channel_id=1, source_target_pairs={{0,1},{1,0},{2,3},{3,2},{4,5},{5,4},{6,7},{7,6},{8,9},{9,8},{10,11... | collective-permute-start | bytes 4718600 | tf_op jit(solution)/shard_map/ppermute | solution.py:39
  361.8 72.6 %collective-permute-start.52 = (bf16[4,2,1,120,768]{4,3,0,2,1:T(8,128)(2,1)S(1)}, bf16[4,2,1,120,768]{4,3,0,2,1:T(8,128)(2,1)S(1)}, u32[]{:S(2)}, u32[]{:S(2)}) collective-permute-start(bf16[4,2,1,120,768]{4,3,0,2,1:T(8,128)(2,1)S(1)} %pad_maximum_fusion.13), channel_id=1, source_target_pairs={{0,1},{1,0},{2,3},{3,2},{4,5},{5,4},{6,7},{7,6},{8,9},{9,8},{10,11... | collective-permute-start | bytes 4423688 | tf_op jit(solution)/shard_map/ppermute | solution.py:39
  365.2 85.1 %collective-permute-start.20 = (bf16[4,1,2,128,768]{4,3,0,2,1:T(8,128)(2,1)}, bf16[4,1,2,128,768]{4,3,0,2,1:T(8,128)(2,1)}, u32[]{:S(2)}, u32[]{:S(2)}) collective-permute-start(bf16[4,1,2,128,768]{4,3,0,2,1:T(8,128)(2,1)} %pad_maximum_fusion.11), channel_id=1, source_target_pairs={{0,4},{1,5},{2,6},{3,7},{4,0},{5,1},{6,2},{7,3},{8,12},{9,13},{10,... | collective-permute-start | bytes 4718600 | tf_op jit(solution)/shard_map/ppermute | solution.py:39
  374.8 63.0 %collective-permute-start.68 = (bf16[4,2,2,24,1536]{4,3,1,0,2:T(8,128)(2,1)S(1)}, bf16[4,2,2,24,1536]{4,3,1,0,2:T(8,128)(2,1)S(1)}, u32[]{:S(2)}, u32[]{:S(2)}) collective-permute-start(bf16[4,2,2,24,1536]{4,3,1,0,2:T(8,128)(2,1)S(1)} %pad_maximum_fusion.16), channel_id=1, source_target_pairs={{0,4},{1,5},{2,6},{3,7},{4,0},{5,1},{6,2},{7,3},{8,12},{9,13},{10,... | collective-permute-start | bytes 3538952 | tf_op jit(solution)/shard_map/ppermute | solution.py:39
  434.4 31.0 %collective-permute-start.79 = (bf16[4,2,2,32,1536]{4,3,1,0,2:T(8,128)(2,1)}, bf16[4,2,2,32,1536]{4,3,1,0,2:T(8,128)(2,1)}, u32[]{:S(2)}, u32[]{:S(2)}) collective-permute-start(bf16[4,2,2,32,1536]{4,3,1,0,2:T(8,128)(2,1)} %pad_maximum_fusion.12), channel_id=1, source_target_pairs={{0,4},{1,5},{2,6},{3,7},{4,0},{5,1},{6,2},{7,3},{8,12},{9,13},{10,... | collective-permute-start | bytes 4718600 | tf_op jit(solution)/shard_map/ppermute | solution.py:39
  509.5 92.8 %collective-permute-start.165 = (bf16[4,2,2,24,1536]{4,3,1,0,2:T(8,128)(2,1)}, bf16[4,2,2,24,1536]{4,3,1,0,2:T(8,128)(2,1)}, u32[]{:S(2)}, u32[]{:S(2)}) collective-permute-start(bf16[4,2,2,24,1536]{4,3,1,0,2:T(8,128)(2,1)} %bitcast.1411), channel_id=1, source_target_pairs={{0,4},{1,5},{2,6},{3,7},{4,0},{5,1},{6,2},{7,3},{8,12},{9,13},{10,... | collective-permute-start | bytes 3538952 | tf_op jit(solution)/shard_map/ppermute | solution.py:39
  516.4 33.1 %collective-permute-start.77 = (bf16[144,1024]{1,0:T(8,128)(2,1)}, bf16[144,1024]{1,0:T(8,128)(2,1)}, u32[]{:S(2)}, u32[]{:S(2)}) collective-permute-start(bf16[144,1024]{1,0:T(8,128)(2,1)} %fusion.138), channel_id=1, source_target_pairs={{0,2},{1,3},{2,0},{3,1},{4,6},{5,7},{6,4},{7,5},{8,10},{9,11},{10,... | collective-permute-start | bytes 884744 | tf_op jit(solution)/shard_map/ppermute | solution.py:39
  545.3 100.8 %collective-permute-start.141 = (bf16[4,2,1,120,768]{4,3,0,2,1:T(8,128)(2,1)}, bf16[4,2,1,120,768]{4,3,0,2,1:T(8,128)(2,1)}, u32[]{:S(2)}, u32[]{:S(2)}) collective-permute-start(bf16[4,2,1,120,768]{4,3,0,2,1:T(8,128)(2,1)} %fusion.24), channel_id=1, source_target_pairs={{0,1},{1,0},{2,3},{3,2},{4,5},{5,4},{6,7},{7,6},{8,9},{9,8},{10,11... | collective-permute-start | bytes 4423688 | tf_op jit(solution)/shard_map/ppermute | solution.py:39
  549.0 50.7 %collective-permute-start.135 = (bf16[4,2,2,24,1152]{4,3,2,0,1:T(8,128)(2,1)}, bf16[4,2,2,24,1152]{4,3,2,0,1:T(8,128)(2,1)}, u32[]{:S(2)}, u32[]{:S(2)}) collective-permute-start(bf16[4,2,2,24,1152]{4,3,2,0,1:T(8,128)(2,1)} %bitcast.1414), channel_id=1, source_target_pairs={{0,1},{1,0},{2,3},{3,2},{4,5},{5,4},{6,7},{7,6},{8,9},{9,8},{10,11... | collective-permute-start | bytes 2654216 | tf_op jit(solution)/shard_map/ppermute | solution.py:39
  559.4 36.6 %collective-permute-start.86 = (f32[144,1024]{1,0:T(8,128)}, f32[144,1024]{1,0:T(8,128)}, u32[]{:S(2)}, u32[]{:S(2)}) collective-permute-start(f32[144,1024]{1,0:T(8,128)} %slice_bitcast_fusion.10), channel_id=1, source_target_pairs={{0,2},{1,3},{2,0},{3,1},{4,6},{5,7},{6,4},{7,5},{8,10},{9,11},{10,... | collective-permute-start | bytes 1769480 | tf_op jit(solution)/shard_map/ppermute | solution.py:39
  585.6 53.8 %collective-permute-start.159 = (bf16[4,2,2,24,1536]{4,3,2,0,1:T(8,128)(2,1)}, bf16[4,2,2,24,1536]{4,3,2,0,1:T(8,128)(2,1)}, u32[]{:S(2)}, u32[]{:S(2)}) collective-permute-start(bf16[4,2,2,24,1536]{4,3,2,0,1:T(8,128)(2,1)} %bitcast.1491), channel_id=1, source_target_pairs={{0,1},{1,0},{2,3},{3,2},{4,5},{5,4},{6,7},{7,6},{8,9},{9,8},{10,11... | collective-permute-start | bytes 3538952 | tf_op jit(solution)/shard_map/ppermute | solution.py:39
  621.8 67.5 %collective-permute-start.117 = (bf16[4,1,2,128,768]{4,3,0,2,1:T(8,128)(2,1)}, bf16[4,1,2,128,768]{4,3,0,2,1:T(8,128)(2,1)}, u32[]{:S(2)}, u32[]{:S(2)}) collective-permute-start(bf16[4,1,2,128,768]{4,3,0,2,1:T(8,128)(2,1)} %fusion.16), channel_id=1, source_target_pairs={{0,4},{1,5},{2,6},{3,7},{4,0},{5,1},{6,2},{7,3},{8,12},{9,13},{10,... | collective-permute-start | bytes 4718600 | tf_op jit(solution)/shard_map/ppermute | solution.py:39
  625.6 36.8 %collective-permute-start.94 = (f32[144,1024]{1,0:T(8,128)}, f32[144,1024]{1,0:T(8,128)}, u32[]{:S(2)}, u32[]{:S(2)}) collective-permute-start(f32[144,1024]{1,0:T(8,128)} %slice_bitcast_fusion.8), channel_id=1, source_target_pairs={{0,2},{1,3},{2,0},{3,1},{4,6},{5,7},{6,4},{7,5},{8,10},{9,11},{10,... | collective-permute-start | bytes 1769480 | tf_op jit(solution)/shard_map/ppermute | solution.py:39
  655.8 45.3 %collective-permute-start.142 = (bf16[4,1,120,768]{3,2,1,0:T(8,128)(2,1)}, bf16[4,1,120,768]{3,2,1,0:T(8,128)(2,1)}, u32[]{:S(2)}, u32[]{:S(2)}) collective-permute-start(bf16[4,1,120,768]{3,2,1,0:T(8,128)(2,1)} %dynamic-slice_bitcast_fusion.3), channel_id=1, source_target_pairs={{0,4},{1,5},{2,6},{3,7},{4,0},{5,1},{6,2},{7,3},{8,12},{9,13},{10,... | collective-permute-start | bytes 2211848 | tf_op jit(solution)/shard_map/ppermute | solution.py:39
  657.7 29.1 %collective-permute-start.160 = (bf16[4,2,24,1536]{3,2,1,0:T(8,128)(2,1)}, bf16[4,2,24,1536]{3,2,1,0:T(8,128)(2,1)}, u32[]{:S(2)}, u32[]{:S(2)}) collective-permute-start(bf16[4,2,24,1536]{3,2,1,0:T(8,128)(2,1)} %dynamic-slice_bitcast_fusion.5), channel_id=1, source_target_pairs={{0,4},{1,5},{2,6},{3,7},{4,0},{5,1},{6,2},{7,3},{8,12},{9,13},{10,... | collective-permute-start | bytes 1769480 | tf_op jit(solution)/shard_map/ppermute | solution.py:39
  674.1 54.9 %collective-permute-start.103 = (f32[144,1024]{1,0:T(8,128)}, f32[144,1024]{1,0:T(8,128)}, u32[]{:S(2)}, u32[]{:S(2)}) collective-permute-start(f32[144,1024]{1,0:T(8,128)} %slice_bitcast_fusion.6), channel_id=1, source_target_pairs={{0,2},{1,3},{2,0},{3,1},{4,6},{5,7},{6,4},{7,5},{8,10},{9,11},{10,... | collective-permute-start | bytes 1769480 | tf_op jit(solution)/shard_map/ppermute | solution.py:39
  696.7 29.4 %collective-permute-start.177 = (bf16[4,2,2,32,512]{4,3,1,0,2:T(8,128)(2,1)}, bf16[4,2,2,32,512]{4,3,1,0,2:T(8,128)(2,1)}, u32[]{:S(2)}, u32[]{:S(2)}) collective-permute-start(bf16[4,2,2,32,512]{4,3,1,0,2:T(8,128)(2,1)} %bitcast.1415), channel_id=1, source_target_pairs={{0,4},{1,5},{2,6},{3,7},{4,0},{5,1},{6,2},{7,3},{8,12},{9,13},{10,... | collective-permute-start | bytes 1572872 | tf_op jit(solution)/shard_map/ppermute | solution.py:39
  714.8 48.8 %collective-permute-start.118 = (bf16[4,1,128,768]{3,2,1,0:T(8,128)(2,1)}, bf16[4,1,128,768]{3,2,1,0:T(8,128)(2,1)}, u32[]{:S(2)}, u32[]{:S(2)}) collective-permute-start(bf16[4,1,128,768]{3,2,1,0:T(8,128)(2,1)} %dynamic-slice_bitcast_fusion.2), channel_id=1, source_target_pairs={{0,1},{1,0},{2,3},{3,2},{4,5},{5,4},{6,7},{7,6},{8,9},{9,8},{10,11... | collective-permute-start | bytes 2359304 | tf_op jit(solution)/shard_map/ppermute | solution.py:39
  732.6 17.6 %collective-permute-start.104 = (bf16[144,1024]{1,0:T(8,128)(2,1)}, bf16[144,1024]{1,0:T(8,128)(2,1)}, u32[]{:S(2)}, u32[]{:S(2)}) collective-permute-start(bf16[144,1024]{1,0:T(8,128)(2,1)} %get-tuple-element.112), channel_id=1, source_target_pairs={{0,2},{1,3},{2,0},{3,1},{4,6},{5,7},{6,4},{7,5},{8,10},{9,11},{10,... | collective-permute-start | bytes 884744 | tf_op jit(solution)/shard_map/ppermute | solution.py:39
  758.0 29.5 %collective-permute-start.105 = (f32[144,1024]{1,0:T(8,128)}, f32[144,1024]{1,0:T(8,128)}, u32[]{:S(2)}, u32[]{:S(2)}) collective-permute-start(f32[144,1024]{1,0:T(8,128)} %slice_bitcast_fusion.4), channel_id=1, source_target_pairs={{0,2},{1,3},{2,0},{3,1},{4,6},{5,7},{6,4},{7,5},{8,10},{9,11},{10,... | collective-permute-start | bytes 1769480 | tf_op jit(solution)/shard_map/ppermute | solution.py:39
  761.7 42.3 %collective-permute-start.153 = (bf16[4,2,1,64,1024]{4,3,0,2,1:T(8,128)(2,1)}, bf16[4,2,1,64,1024]{4,3,0,2,1:T(8,128)(2,1)}, u32[]{:S(2)}, u32[]{:S(2)}) collective-permute-start(bf16[4,2,1,64,1024]{4,3,0,2,1:T(8,128)(2,1)} %fusion.69), channel_id=1, source_target_pairs={{0,1},{1,0},{2,3},{3,2},{4,5},{5,4},{6,7},{7,6},{8,9},{9,8},{10,11... | collective-permute-start | bytes 3145736 | tf_op jit(solution)/shard_map/ppermute | solution.py:39
  785.8 70.1 %collective-permute-start.147 = (bf16[4,2,2,32,1536]{4,3,1,0,2:T(8,128)(2,1)}, bf16[4,2,2,32,1536]{4,3,1,0,2:T(8,128)(2,1)}, u32[]{:S(2)}, u32[]{:S(2)}) collective-permute-start(bf16[4,2,2,32,1536]{4,3,1,0,2:T(8,128)(2,1)} %bitcast.1409), channel_id=1, source_target_pairs={{0,4},{1,5},{2,6},{3,7},{4,0},{5,1},{6,2},{7,3},{8,12},{9,13},{10,... | collective-permute-start | bytes 4718600 | tf_op jit(solution)/shard_map/ppermute | solution.py:39
  807.5 43.6 %collective-permute-start.154 = (bf16[4,1,64,1024]{3,2,1,0:T(8,128)(2,1)}, bf16[4,1,64,1024]{3,2,1,0:T(8,128)(2,1)}, u32[]{:S(2)}, u32[]{:S(2)}) collective-permute-start(bf16[4,1,64,1024]{3,2,1,0:T(8,128)(2,1)} %dynamic-slice_bitcast_fusion.7), channel_id=1, source_target_pairs={{0,4},{1,5},{2,6},{3,7},{4,0},{5,1},{6,2},{7,3},{8,12},{9,13},{10,... | collective-permute-start | bytes 1572872 | tf_op jit(solution)/shard_map/ppermute | solution.py:39
  848.3 27.5 %collective-permute-start.108 = (bf16[144,1024]{1,0:T(8,128)(2,1)}, bf16[144,1024]{1,0:T(8,128)(2,1)}, u32[]{:S(2)}, u32[]{:S(2)}) collective-permute-start(bf16[144,1024]{1,0:T(8,128)(2,1)} %get-tuple-element.106), channel_id=1, source_target_pairs={{0,2},{1,3},{2,0},{3,1},{4,6},{5,7},{6,4},{7,5},{8,10},{9,11},{10,... | collective-permute-start | bytes 884744 | tf_op jit(solution)/shard_map/ppermute | solution.py:39
  859.8 44.4 %collective-permute-start.148 = (bf16[4,2,32,1536]{3,2,1,0:T(8,128)(2,1)}, bf16[4,2,32,1536]{3,2,1,0:T(8,128)(2,1)S(1)}, u32[]{:S(2)}, u32[]{:S(2)}) collective-permute-start(bf16[4,2,32,1536]{3,2,1,0:T(8,128)(2,1)} %dynamic-slice_bitcast_fusion), channel_id=1, source_target_pairs={{0,1},{1,0},{2,3},{3,2},{4,5},{5,4},{6,7},{7,6},{8,9},{9,8},{10,11... | collective-permute-start | bytes 2359304 | tf_op jit(solution)/shard_map/ppermute | solution.py:39
  869.9 31.4 %collective-permute-start.158 = (bf16[64,1024]{1,0:T(8,128)(2,1)}, bf16[64,1024]{1,0:T(8,128)(2,1)}, u32[]{:S(2)}, u32[]{:S(2)}) collective-permute-start(bf16[64,1024]{1,0:T(8,128)(2,1)} %fusion.261), channel_id=1, source_target_pairs={{0,0},{1,1},{2,16},{3,17},{4,4},{5,5},{6,20},{7,21},{8,8},{9,9},{1... | collective-permute-start | bytes 393224 | tf_op jit(solution)/shard_map/ppermute | solution.py:39
  873.7 23.3 %collective-permute-start.176 = (bf16[32,512]{1,0:T(8,128)(2,1)S(1)}, bf16[32,512]{1,0:T(8,128)(2,1)S(1)}, u32[]{:S(2)}, u32[]{:S(2)}) collective-permute-start(bf16[32,512]{1,0:T(8,128)(2,1)S(1)} %fusion.319), channel_id=1, source_target_pairs={{0,2},{1,3},{2,0},{3,1},{4,6},{5,7},{6,4},{7,5},{8,10},{9,11},{10,... | collective-permute-start | bytes 98312 | tf_op jit(solution)/shard_map/ppermute | solution.py:39
  888.9 36.1 %collective-permute-start.129 = (bf16[4,1,2,64,1024]{4,3,0,2,1:T(8,128)(2,1)}, bf16[4,1,2,64,1024]{4,3,0,2,1:T(8,128)(2,1)}, u32[]{:S(2)}, u32[]{:S(2)}) collective-permute-start(bf16[4,1,2,64,1024]{4,3,0,2,1:T(8,128)(2,1)} %fusion.73), channel_id=1, source_target_pairs={{0,4},{1,5},{2,6},{3,7},{4,0},{5,1},{6,2},{7,3},{8,12},{9,13},{10,... | collective-permute-start | bytes 3145736 | tf_op jit(solution)/shard_map/ppermute | solution.py:39
  892.4 55.8 %collective-permute-start.123 = (bf16[4,2,2,32,1536]{4,3,2,0,1:T(8,128)(2,1)}, bf16[4,2,2,32,1536]{4,3,2,0,1:T(8,128)(2,1)}, u32[]{:S(2)}, u32[]{:S(2)}) collective-permute-start(bf16[4,2,2,32,1536]{4,3,2,0,1:T(8,128)(2,1)} %bitcast.1410), channel_id=1, source_target_pairs={{0,1},{1,0},{2,3},{3,2},{4,5},{5,4},{6,7},{7,6},{8,9},{9,8},{10,11... | collective-permute-start | bytes 4718600 | tf_op jit(solution)/shard_map/ppermute | solution.py:39
  904.6 17.1 %collective-permute-start.150 = (bf16[2,32,1536]{2,1,0:T(8,128)(2,1)S(1)}, bf16[2,32,1536]{2,1,0:T(8,128)(2,1)S(1)}, u32[]{:S(2)}, u32[]{:S(2)}) collective-permute-start(bf16[2,32,1536]{2,1,0:T(8,128)(2,1)S(1)} %get-tuple-element.212), channel_id=1, source_target_pairs={{0,16},{1,17},{2,18},{3,19},{4,20},{5,21},{6,22},{7,23},{8,24},{9,... | collective-permute-start | bytes 589832 | tf_op jit(solution)/shard_map/ppermute | solution.py:39
  914.2 26.4 %collective-permute-start.111 = (bf16[4,2,2,24,1536]{4,3,1,0,2:T(8,128)(2,1)}, bf16[4,2,2,24,1536]{4,3,1,0,2:T(8,128)(2,1)}, u32[]{:S(2)}, u32[]{:S(2)}) collective-permute-start(bf16[4,2,2,24,1536]{4,3,1,0,2:T(8,128)(2,1)} %bitcast.1413), channel_id=1, source_target_pairs={{0,4},{1,5},{2,6},{3,7},{4,0},{5,1},{6,2},{7,3},{8,12},{9,13},{10,... | collective-permute-start | bytes 3538952 | tf_op jit(solution)/shard_map/ppermute | solution.py:39
  950.1 26.5 %collective-permute-start.124 = (bf16[4,2,32,1536]{3,2,1,0:T(8,128)(2,1)S(1)}, bf16[4,2,32,1536]{3,2,1,0:T(8,128)(2,1)S(1)}, u32[]{:S(2)}, u32[]{:S(2)}) collective-permute-start(bf16[4,2,32,1536]{3,2,1,0:T(8,128)(2,1)S(1)} %dynamic-slice_bitcast_fusion.1), channel_id=1, source_target_pairs={{0,4},{1,5},{2,6},{3,7},{4,0},{5,1},{6,2},{7,3},{8,12},{9,13},{10,... | collective-permute-start | bytes 2359304 | tf_op jit(solution)/shard_map/ppermute | solution.py:39
  (391 other events, 3861.2 us)

commit v2 on v1

v2 whole, which is shorter than its diff:
```python
from functools import partial

import jax
import jax.numpy as jnp
from jax import lax
from jax.sharding import Mesh, PartitionSpec as P

HT = 12
HI = 8
HC = 8
REGIONS = 36
EPS = 1e-06
F32 = jnp.float32
BF16 = jnp.bfloat16
ALL = ("z", "y", "core", "x")
TEAM = 4
FLIP = ((0, 1), (1, 0))


class Grid:
    def __init__(self, depth):
        self.depth = depth
        self.low = depth // TEAM
        self.z, self.y, self.core, self.x = (lax.axis_index(name) for name in ALL)

    def to_core(self, value):
        return lax.ppermute(value, "core", FLIP)

    def to_x(self, value):
        return lax.ppermute(value, "x", FLIP)

    def to_y(self, value):
        return lax.ppermute(value, "y", FLIP)

    def to_z(self, value, step):
        return lax.ppermute(value, "z", [(z, (z + step) % self.depth) for z in range(self.depth)])

    def swap_team(self, value):
        pairs = []
        for high in range(TEAM):
            for low in range(self.low):
                for y in range(2):
                    for place in range(TEAM):
                        here = ((high * self.low + low) * 2 + y) * TEAM + place
                        there = ((place * self.low + low) * 2 + y) * TEAM + high
                        pairs.append((here, there))
        return lax.ppermute(value, ALL, pairs)


def pick(value, index, axis):
    return lax.dynamic_index_in_dim(value, index, axis, keepdims=False)


def paired(own, other, index, axis):
    own, other = jnp.expand_dims(own, axis), jnp.expand_dims(other, axis)
    shape = list(own.shape)
    shape[axis] = 2
    place = lax.broadcasted_iota(jnp.int32, shape, axis)
    return jnp.where(place == index, own, other)


def quarter(w, groups):
    r, n = w.shape
    parts = w.reshape(r, groups, TEAM, n // groups // TEAM)
    return parts.transpose(2, 0, 1, 3).reshape(2, 2, r, n // TEAM)


def unquarter(parts, groups):
    _, _, r, c = parts.shape
    parts = parts.reshape(TEAM, r, groups, c // groups)
    return parts.transpose(1, 2, 0, 3).reshape(r, TEAM * c)


def team_trade(grid, parts):
    got = grid.to_x(pick(parts, 1 - grid.x, 1))
    parts = paired(pick(parts, grid.x, 1), got, grid.x, 1)
    got = grid.to_core(pick(parts, 1 - grid.core, 0))
    return paired(pick(parts, grid.core, 0), got, grid.core, 0)


def widen(value, width):
    lack = width - value.shape[-1]
    if lack == 0:
        return value
    return jnp.pad(value, [(0, 0)] * (value.ndim - 1) + [(0, lack)])


class Bundle:
    def __init__(self, width, ins, outs, z_by, extra=0):
        self.width, self.ins, self.outs, self.z_by, self.extra = width, ins, outs, z_by, extra

    def flat(self, parts):
        c = parts.shape[-1]
        if c * TEAM == self.width:
            return jnp.concatenate([parts[..., k, :, :] for k in range(TEAM)], -1)
        parts = widen(parts, self.width)
        return parts.reshape(parts.shape[:-3] + (TEAM * parts.shape[-2], self.width))

    def unflat(self, rows, c):
        if c * TEAM == self.width:
            return jnp.stack([rows[..., k * c : (k + 1) * c] for k in range(TEAM)], -3)
        rows = rows.reshape(rows.shape[:-2] + (TEAM, rows.shape[-2] // TEAM, self.width))
        return rows[..., :c]


def gather(grid, bundle, weights, extra=None, after=None):
    pieces = []
    if bundle.ins:
        parts = [quarter(weights[name], groups) for name, groups in bundle.ins]
        kinds = {}
        for i, part in enumerate(parts):
            kinds.setdefault(part.shape[-1], []).append(i)
        traded = [None] * len(parts)
        for members in kinds.values():
            joined = jnp.concatenate([parts[i] for i in members], 2) if len(members) > 1 else parts[members[0]]
            joined = team_trade(grid, joined)
            at = 0
            for i in members:
                r = parts[i].shape[2]
                traded[i] = joined[:, :, at : at + r].reshape(TEAM, r, parts[i].shape[3])
                at += r
        pieces += [bundle.flat(t) for t in traded]
    if bundle.outs:
        outs = [weights[name] for name in bundle.outs]
        pieces.append(grid.swap_team(jnp.concatenate(outs, 0) if len(outs) > 1 else outs[0]))
    if extra is not None:
        lines = team_trade(grid, jnp.broadcast_to(extra, (2, 2) + extra.shape)).reshape(TEAM, -1)
        lines = jnp.pad(lines, ((0, bundle.extra - TEAM), (0, bundle.width - lines.shape[1])))
        pieces.append(lines)
    chunk = jnp.concatenate(pieces, 0) if len(pieces) > 1 else pieces[0]
    if after is not None:
        chunk, _ = lax.optimization_barrier((chunk, after))

    if bundle.z_by == "gather":
        block = lax.all_gather(chunk, "z", axis=0, tiled=False)
    else:
        got = [chunk] + [grid.to_z(chunk, k) for k in range(1, grid.depth)]
        places = []
        for place in range(grid.depth):
            value = got[0]
            for k in range(1, grid.depth):
                value = jnp.where((grid.z - place) % grid.depth == k, got[k], value)
            places.append(value)
        block = jnp.stack(places)
    other = grid.to_y(block)

    full, at = {}, 0
    for name, groups in bundle.ins:
        r, n = weights[name].shape
        c = n // TEAM
        rows = r if c * TEAM == bundle.width else r * TEAM
        own, got = block[:, at : at + rows], other[:, at : at + rows]
        own, got = bundle.unflat(own, c), bundle.unflat(got, c)
        full[name] = paired(own, got, grid.y, 1).reshape(-1, c)
        at += rows
    for name in bundle.outs:
        r, n = weights[name].shape

        def ordered(part):
            part = part[:, at : at + r].reshape(TEAM, grid.low, r, n)
            return part.transpose(1, 0, 2, 3)

        full[name] = paired(ordered(block), ordered(other), grid.y, 1).reshape(-1, n)
        at += r
    if extra is not None:
        own, got = block[:, at : at + TEAM], other[:, at : at + TEAM]
        full["extra"] = paired(own, got, grid.y, 1).reshape(-1, bundle.width)[:, : extra.shape[0]]
    return full, block


def give(grid, bundle, grads, extra=None):
    views, spans = [], []
    for name, groups in bundle.ins:
        k, c = grads[name].shape
        r = k // (grid.depth * 2 * TEAM)
        views.append(bundle.flat(grads[name].reshape(grid.depth, 2, TEAM, r, c)))
    for name in bundle.outs:
        k, n = grads[name].shape
        r = k // (grid.low * 2 * TEAM)
        view = grads[name].reshape(grid.low, 2, TEAM, r, n).transpose(2, 0, 1, 3, 4)
        views.append(view.reshape(grid.depth, 2, r, n))
    if extra is not None:
        view = extra.astype(BF16).reshape(grid.depth, 2, TEAM, -1)
        lack = (bundle.extra - TEAM, bundle.width - view.shape[-1])
        views.append(jnp.pad(view, ((0, 0), (0, 0), (0, lack[0]), (0, lack[1]))))

    away = [pick(v, 1 - grid.y, 1) for v in views]
    home = [pick(v, grid.y, 1) for v in views]
    away = jnp.concatenate(away, 1) if len(away) > 1 else away[0]
    home = jnp.concatenate(home, 1) if len(home) > 1 else home[0]
    block = (home.astype(F32) + grid.to_y(away).astype(F32)).astype(BF16)
    if bundle.z_by == "gather":
        total = lax.psum_scatter(block, "z", scatter_dimension=0, tiled=False).astype(F32)
    else:
        total = pick(block, grid.z, 0).astype(F32)
        for k in range(1, grid.depth):
            total = total + grid.to_z(pick(block, (grid.z + k) % grid.depth, 0), k).astype(F32)
    total = total.astype(BF16)

    done, at = {}, 0
    kinds, parts = {}, {}
    for (name, groups), view in zip(bundle.ins, views):
        rows, c = view.shape[2], grads[name].shape[1]
        parts[name] = bundle.unflat(total[at : at + rows], c)
        kinds.setdefault(c, []).append((name, groups))
        at += rows
    for members in kinds.values():
        joined = jnp.concatenate([parts[name] for name, _ in members], 1) if len(members) > 1 else parts[members[0][0]]
        joined = team_trade(grid, joined.reshape((2, 2) + joined.shape[1:]))
        start = 0
        for name, groups in members:
            r = parts[name].shape[1]
            done[name] = unquarter(joined[:, :, start : start + r], groups).astype(F32)
            start += r
    if bundle.outs:
        rows = sum(v.shape[2] for v in views[len(bundle.ins) : len(bundle.ins) + len(bundle.outs)])
        mine = grid.swap_team(total[at : at + rows]).astype(F32)
        start = 0
        for name, view in zip(bundle.outs, views[len(bundle.ins) :]):
            r = view.shape[2]
            done[name] = mine[start : start + r]
            start += r
        at += rows
    if extra is not None:
        lines = total[at : at + TEAM].reshape(2, 2, -1)
        lines = pick(lines, grid.x, 1).astype(F32) + grid.to_x(pick(lines, 1 - grid.x, 1)).astype(F32)
        lines = pick(lines, grid.core, 0) + grid.to_core(pick(lines, 1 - grid.core, 0))
        done["extra"] = lines[: extra.shape[1]]
    return done


def dot(a, b):
    return jnp.einsum("rlk,km->rlm", a, b, preferred_element_type=F32)


def dot_back(a, b):
    return jnp.einsum("rlm,km->rlk", a, b, preferred_element_type=F32)


def dot_weight(a, b):
    return jnp.einsum("rlk,rlm->km", a, b, preferred_element_type=F32).astype(BF16)


def layer_norm(values, gain, shift):
    average = jnp.mean(values, -1, keepdims=True)
    centred = values - average
    inverse = lax.rsqrt(jnp.mean(centred * centred, -1, keepdims=True) + EPS)
    normed = centred * inverse
    return normed * gain + shift, (normed, inverse)


def norm_back(upstream, stored, gain):
    normed, inverse = stored
    scaled = upstream * gain
    grad = inverse * (
        scaled
        - jnp.mean(scaled, -1, keepdims=True)
        - normed * jnp.mean(scaled * normed, -1, keepdims=True)
    )
    return grad, jnp.sum(upstream * normed, axis=0), jnp.sum(upstream, axis=0)


def heads_of(array, count):
    return array.reshape(array.shape[0], array.shape[1], count, array.shape[2] // count)


def attend(q, k, v, allowed, count):
    rows, length, width = q.shape
    factor = (width // count) ** (-0.5)
    qh, kh, vh = heads_of(q, count), heads_of(k, count), heads_of(v, count)
    scores = jnp.einsum("rqhd,rkhd->rhqk", qh, kh, preferred_element_type=F32) * factor
    scores = jnp.where(allowed[:, None], scores, -1e30)
    exponent = jnp.exp(scores - jnp.max(scores, -1, keepdims=True))
    probs = exponent / jnp.sum(exponent, -1, keepdims=True)
    context = jnp.einsum("rhqk,rkhd->rqhd", probs.astype(BF16), vh, preferred_element_type=F32)
    return context.reshape(rows, length, width).astype(BF16), probs


def attend_back(grad, q, k, v, probs, count):
    rows, length, width = q.shape
    factor = (width // count) ** (-0.5)
    qh, kh, vh, gh = (heads_of(a, count) for a in (q, k, v, grad))
    dv = jnp.einsum("rhqk,rqhd->rkhd", probs.astype(BF16), gh, preferred_element_type=F32)
    dp = jnp.einsum("rqhd,rkhd->rhqk", gh, vh, preferred_element_type=F32)
    ds = (probs * (dp - jnp.sum(dp * probs, -1, keepdims=True))).astype(BF16)
    dq = jnp.einsum("rhqk,rkhd->rqhd", ds, kh, preferred_element_type=F32) * factor
    dk = jnp.einsum("rhqk,rqhd->rkhd", ds, qh, preferred_element_type=F32) * factor
    flat = lambda a: a.reshape(a.shape[0], a.shape[1], width).astype(BF16)
    return flat(dq), flat(dk), flat(dv)


def share(grid, own):
    both = jnp.stack([own, grid.to_x(own)])
    return jnp.concatenate([both, grid.to_core(both)])


def settle(grid, sums):
    both = sums[:2] + grid.to_core(sums[2:].astype(BF16)).astype(F32)
    return both[0] + grid.to_x(both[1].astype(BF16)).astype(F32)


def project(low, w):
    return jnp.split(dot(low, w).astype(BF16), 3, axis=-1)


def attn_out(grid, values, context, w, gain, shift):
    return layer_norm(values + settle(grid, dot(context, w)), gain, shift)


def feed_forward(grid, values, up, down, gain, shift):
    low = share(grid, values.astype(BF16))
    before = dot(low, up)
    hidden = jax.nn.gelu(before, approximate=False).astype(BF16)
    result, stored = layer_norm(values + settle(grid, dot(hidden, down)), gain, shift)
    return result, (low, before, hidden, stored)


def feed_back(grid, upstream, saved, up, down, gain):
    low, before, hidden, stored = saved
    summed, dgain, dshift = norm_back(upstream, stored, gain)
    out = share(grid, summed.astype(BF16))
    hidden_grad = dot_back(out, down)
    _, pull = jax.vjp(partial(jax.nn.gelu, approximate=False), before)
    before_grad = pull(hidden_grad)[0].astype(BF16)
    entry = settle(grid, dot_back(before_grad, up))
    ddown = dot_weight(hidden, out)
    dup = dot_weight(low, before_grad)
    return summed + entry, dup, ddown, dgain, dshift


def attn_out_back(grid, upstream, context, stored, w, gain):
    summed, dgain, dshift = norm_back(upstream, stored, gain)
    out = share(grid, summed.astype(BF16))
    context_grad = dot_back(out, w).astype(BF16)
    return summed, context_grad, dot_weight(context, out), dgain, dshift


def project_back(grid, low, grads, w):
    joined = jnp.concatenate(grads, axis=-1)
    return settle(grid, dot_back(joined, w)), dot_weight(low, joined)


def unpack_norms(full, tw, iw):
    out, at = [], 0
    for width in (tw, tw, iw, iw):
        part = full[:, at : at + 4 * width].reshape(-1, 4, width)
        out.append(part.transpose(1, 0, 2).reshape(4, -1).astype(F32))
        at += 4 * width
    return out


FETCH = (
    Bundle(768, [("tci", 3), ("ici", 3)], [], "permute", extra=16),
    Bundle(768, [("tu0", 1)], ["tco", "td0"], "gather"),
    Bundle(1024, [("iu0", 1)], ["ico", "id0"], "permute"),
    Bundle(768, [("tsi", 3), ("isi", 3)], [], "gather"),
    Bundle(768, [("tu1", 1)], ["tso", "td1"], "gather"),
    Bundle(1024, [("iu1", 1)], ["iso", "id1"], "permute"),
)
RETURN = (
    Bundle(768, [("tu1", 1)], ["td1"], "gather"),
    Bundle(1024, [("iu1", 1)], ["id1"], "permute"),
    Bundle(768, [("tsi", 3), ("isi", 3)], ["tso"], "gather"),
    Bundle(768, [("tu0", 1)], ["td0"], "gather"),
    Bundle(1024, [("iu0", 1)], ["iso", "id0", "ico"], "permute"),
    Bundle(768, [("tci", 3), ("ici", 3)], ["tco"], "permute", extra=16),
)


def shards(
    text_in,
    image_in,
    text_segments,
    text_co_in,
    text_co_out,
    image_co_in,
    image_co_out,
    text_self_in,
    text_self_out,
    image_self_in,
    image_self_out,
    text_up,
    text_down,
    image_up,
    image_down,
    text_gains,
    text_shifts,
    image_gains,
    image_shifts,
    grad_text_out,
    grad_image_out,
    depth,
):
    grid = Grid(depth)
    tw, iw = text_gains.shape[2], image_gains.shape[2]
    weights = {
        "tci": text_co_in[0],
        "tco": text_co_out[0],
        "ici": image_co_in[0],
        "ico": image_co_out[0],
        "tsi": text_self_in[0],
        "tso": text_self_out[0],
        "isi": image_self_in[0],
        "iso": image_self_out[0],
        "tu0": text_up[0, 0],
        "tu1": text_up[0, 1],
        "td0": text_down[0, 0],
        "td1": text_down[0, 1],
        "iu0": image_up[0, 0],
        "iu1": image_up[0, 1],
        "id0": image_down[0, 0],
        "id1": image_down[0, 1],
    }

    norms = jnp.concatenate(
        [a[0].reshape(-1) for a in (text_gains, text_shifts, image_gains, image_shifts)]
    )
    full, blocks = {}, []
    for bundle in FETCH:
        after = blocks[-2] if len(blocks) >= 2 and bundle.z_by == "permute" else None
        got, block = gather(grid, bundle, weights, norms if bundle.extra else None, after)
        full.update(got)
        blocks.append(block)
    gain_t, shift_t, gain_i, shift_i = unpack_norms(full["extra"], tw, iw)

    segments = share(grid, text_segments[0].astype(F32))
    image_ids = (jnp.arange(image_in.shape[1], dtype=jnp.int32) // (2 * REGIONS)).astype(F32)
    cross = segments[:, :, None] == image_ids[None, None, :]
    cross_back = jnp.swapaxes(cross, 1, 2)
    text_allowed = segments[:, :, None] == segments[:, None, :]
    image_allowed = (image_ids[:, None] == image_ids[None, :])[None]

    hc, ht, hi = HC // TEAM, HT // TEAM, HI // TEAM
    xt, xi = text_in[0].astype(F32), image_in[0].astype(F32)
    low_t, low_i = share(grid, text_in[0]), share(grid, image_in[0])
    qt, kt, vt = project(low_t, full["tci"])
    qi, ki, vi = project(low_i, full["ici"])
    ct, pt = attend(qt, ki, vi, cross, hc)
    ci, pi = attend(qi, kt, vt, cross_back, hc)
    yt, yt_saved = attn_out(grid, xt, ct, full["tco"], gain_t[0], shift_t[0])
    yi, yi_saved = attn_out(grid, xi, ci, full["ico"], gain_i[0], shift_i[0])
    zt, zt_saved = feed_forward(grid, yt, full["tu0"], full["td0"], gain_t[1], shift_t[1])
    zi, zi_saved = feed_forward(grid, yi, full["iu0"], full["id0"], gain_i[1], shift_i[1])

    def self_forward(values, w_in, w_out, up, down, allowed, count, gain, shift):
        low = share(grid, values.astype(BF16))
        q, k, v = project(low, w_in)
        context, probs = attend(q, k, v, allowed, count)
        middle, mid_saved = attn_out(grid, values, context, w_out, gain[2], shift[2])
        top, top_saved = feed_forward(grid, middle, up, down, gain[3], shift[3])
        return top, (low, q, k, v, context, probs, mid_saved, top_saved)

    ot, ot_saved = self_forward(
        zt, full["tsi"], full["tso"], full["tu1"], full["td1"], text_allowed, ht, gain_t, shift_t
    )
    oi, oi_saved = self_forward(
        zi, full["isi"], full["iso"], full["iu1"], full["id1"], image_allowed, hi, gain_i, shift_i
    )

    def self_backward(upstream, saved, w_in, w_out, up, down, count, gain):
        low, q, k, v, context, probs, mid_saved, top_saved = saved
        middle, dup, ddown, dg3, db3 = feed_back(grid, upstream, top_saved, up, down, gain[3])
        residual, context_grad, dout, dg2, db2 = attn_out_back(
            grid, middle, context, mid_saved, w_out, gain[2]
        )
        joined = attend_back(context_grad, q, k, v, probs, count)
        entry, din = project_back(grid, low, joined, w_in)
        return residual + entry, din, dout, dup, ddown, (dg2, dg3), (db2, db3)

    grads = {}
    gt, grads["tsi"], grads["tso"], grads["tu1"], grads["td1"], dgt_top, dbt_top = self_backward(
        grad_text_out[0].astype(F32),
        ot_saved,
        full["tsi"],
        full["tso"],
        full["tu1"],
        full["td1"],
        ht,
        gain_t,
    )
    gi, grads["isi"], grads["iso"], grads["iu1"], grads["id1"], dgi_top, dbi_top = self_backward(
        grad_image_out[0].astype(F32),
        oi_saved,
        full["isi"],
        full["iso"],
        full["iu1"],
        full["id1"],
        hi,
        gain_i,
    )

    gt, grads["tu0"], grads["td0"], dgt1, dbt1 = feed_back(
        grid, gt, zt_saved, full["tu0"], full["td0"], gain_t[1]
    )
    gi, grads["iu0"], grads["id0"], dgi1, dbi1 = feed_back(
        grid, gi, zi_saved, full["iu0"], full["id0"], gain_i[1]
    )
    rt, ct_grad, grads["tco"], dgt0, dbt0 = attn_out_back(
        grid, gt, ct, yt_saved, full["tco"], gain_t[0]
    )
    ri, ci_grad, grads["ico"], dgi0, dbi0 = attn_out_back(
        grid, gi, ci, yi_saved, full["ico"], gain_i[0]
    )
    dqt, dki, dvi = attend_back(ct_grad, qt, ki, vi, pt, hc)
    dqi, dkt, dvt = attend_back(ci_grad, qi, kt, vt, pi, hc)
    et, grads["tci"] = project_back(grid, low_t, (dqt, dkt, dvt), full["tci"])
    ei, grads["ici"] = project_back(grid, low_i, (dqi, dki, dvi), full["ici"])

    count = depth * 2 * TEAM

    def by_device(rows, width):
        lines = jnp.stack(rows).reshape(4, count, width)
        return lines.transpose(1, 0, 2).reshape(count, 4 * width)

    sums = jnp.concatenate(
        [
            by_device([dgt0, dgt1, *dgt_top], tw),
            by_device([dbt0, dbt1, *dbt_top], tw),
            by_device([dgi0, dgi1, *dgi_top], iw),
            by_device([dbi0, dbi1, *dbi_top], iw),
        ],
        1,
    )
    done = {}
    for bundle in RETURN:
        done.update(give(grid, bundle, grads, sums if bundle.extra else None))
    norm_grads, at = [], 0
    for width in (tw, tw, iw, iw):
        norm_grads.append(done["extra"][at : at + 4 * width].reshape(1, 4, width))
        at += 4 * width

    def both(first, second):
        return jnp.stack([done[first], done[second]])[None]

    return (
        ot.astype(BF16)[None],
        oi.astype(BF16)[None],
        (rt + et)[None],
        (ri + ei)[None],
        *(done[n][None] for n in ("tci", "tco", "ici", "ico", "tsi", "tso", "isi", "iso")),
        both("tu0", "tu1"),
        both("td0", "td1"),
        both("iu0", "iu1"),
        both("id0", "id1"),
        *norm_grads,
    )


def solution(mesh):
    depth = mesh.shape["wide"] // 4
    fine = Mesh(mesh.devices.reshape(depth, 2, 2, mesh.shape["narrow"]), ALL)
    rows = P(ALL, None, None)
    weight = P(None, ALL, None)
    pair = P(None, None, ALL, None)
    norm = P(None, None, ALL)
    return jax.shard_map(
        partial(shards, depth=depth),
        mesh=fine,
        in_specs=(rows, rows, P(ALL, None), *[weight] * 8, *[pair] * 4, *[norm] * 4, rows, rows),
        out_specs=(rows, rows, rows, rows, *[weight] * 8, *[pair] * 4, *[norm] * 4),
        check_vma=False,
    )
```

time: 1010 us -> 884 us (0.88)
  starting transfers between devices: 244 us -> 157 us
  waiting for transfers between devices: 413 us -> 364 us
  other arithmetic: 121 us -> 107 us
  between operations: 6.53 us -> 20.1 us
    ppermute x189 -> x138, starting transfers between devices: 244 us -> 157 us  [the longest x49 65.3 us: to_x(): return lax.ppermute(value, 'x', FLIP)]
    ppermute x189 -> x138, waiting for transfers between devices: 413 us -> 356 us  [the longest x18 134 us: to_z(): lax.ppermute(value, 'z', [(z, (z + step) % self.depth) for z in range(sel...]
    slice x9 -> x61, local copies, waits for them, and re-layouts: 5.92 us -> 34.7 us  [the longest x12 12.8 us: ordered(): part = part[:, at:at + r].reshape(TEAM, grid.low, r, n)]
    dynamic_slice x26 -> x11, local copies, waits for them, and re-layouts: 22.1 us -> 1.08 us  [pick(): return lax.dynamic_index_in_dim(value, index, axis, keepdims=False)]
    convert_element_type x32 -> x16, other arithmetic: 32.3 us -> 19.3 us  [the longest x6 13.1 us: give(): block = (home.astype(F32) + grid.to_y(away).astype(F32)).astype(BF16)]
    select_n x8 -> x30, other arithmetic: 2.4 us -> 15.1 us  [paired(): return jnp.where(place == index, own, other)]
    concatenate x17 -> x1, local copies, waits for them, and re-layouts: 12.1 us -> 0.02 us  [gather(): jnp.concatenate([parts[i] for i in members], 2)]
    dot_general x16, matrix products: 11.9 us -> 23.5 us  [dot(): return jnp.einsum('rlk,km->rlm', a, b, preferred_element_type=F32)]
  transfers between devices with their start and end apart: 189 -> 144, of which waited for: 76 -> 59; matrix products, arithmetic and copies ran while one was open for 31% -> 32% of each run, Pallas kernels for 0% -> 0%
where the time goes in v2:
time: 884 us; the launch traced here: 873 us
  waiting for transfers between devices  364 us (41%)
  starting transfers between devices  157 us (18%)
  local copies, waits for them, and re-layouts  140 us (16%)
  other arithmetic  107 us (12%)
  matrix products  85.3 us (10%)
  between operations  20.1 us (2%)
    ppermute x18, waiting for transfers between devices, to_z(): lax.ppermute(value, 'z', [(z, (z + step) % self.depth) for z in range(sel...  134 us
    ppermute x12, waiting for transfers between devices, to_y(): return lax.ppermute(value, 'y', FLIP)  118 us
    ppermute x49, waiting for transfers between devices, to_x(): return lax.ppermute(value, 'x', FLIP)  99 us
    ppermute x49, starting transfers between devices, to_x(): return lax.ppermute(value, 'x', FLIP)  65.3 us
    ppermute x18, starting transfers between devices, to_z(): lax.ppermute(value, 'z', [(z, (z + step) % self.depth) for z in range(sel...  49.2 us
    unnamed x663, local copies, waits for them, and re-layouts  30.1 us
    dot_general x16, matrix products, dot(): return jnp.einsum('rlk,km->rlm', a, b, preferred_element_type=F32)  23.5 us
    dot_general x16, matrix products, dot_weight(): jnp.einsum('rlk,rlm->km', a, b, preferred_element_type=F32).astype(BF16)  23.2 us
  transfers between devices with their start and end apart: 144, of which 59 were waited for; matrix products, arithmetic and copies ran while one was open for 32% of the time, Pallas kernels for 0%

profile of v2, /device:TPU:0, one launch (start us, length us, event | category | flops | bytes accessed | tf_op | source)
XLA Modules:
  0.0 873.5 jit_solution(11105750777745607439)
XLA Ops:
  7.9 2.9 collective-permute-start.10
  35.7 2.5 collective-permute-start.26
  40.3 4.7 collective-permute-start.28
  53.5 2.9 collective-permute-start.8
  60.7 18.5 %collective-permute-done.8 = bf16[240,768]{1,0:T(8,128)(2,1)S(1)} collective-permute-done((bf16[240,768]{1,0:T(8,128)(2,1)S(1)}, bf16[240,768]{1,0:T(8,128)(2,1)S(1)}, u32[]{:S(2)}, u32[]{:S(2)}) %collective-permute-start.8) | collective-permute-done | bytes 368672 | tf_op jit(solution)/shard_map/ppermute | solution.py:36
  80.7 22.0 %collective-permute-done.7 = bf16[240,768]{1,0:T(8,128)(2,1)S(1)} collective-permute-done((bf16[240,768]{1,0:T(8,128)(2,1)S(1)}, bf16[240,768]{1,0:T(8,128)(2,1)S(1)}, u32[]{:S(2)}, u32[]{:S(2)}) %collective-permute-start.7) | collective-permute-done | bytes 368672 | tf_op jit(solution)/shard_map/ppermute | solution.py:36
  103.5 11.0 %collective-permute-start.46 = (bf16[96,1024]{1,0:T(8,128)(2,1)S(1)}, bf16[96,1024]{1,0:T(8,128)(2,1)S(1)}, u32[]{:S(2)}, u32[]{:S(2)}) collective-permute-start(bf16[96,1024]{1,0:T(8,128)(2,1)S(1)} %pad_maximum_fusion.64), channel_id=1, source_target_pairs={{0,8},{8,16},{16,24},{24,0},{1,9},{9,17},{17,25},{25,1},{2,10},{10... | collective-permute-start | bytes 589832 | tf_op jit(solution)/shard_map/ppermute | solution.py:36
  114.6 2.4 collective-permute-start.44
  119.3 4.7 collective-permute-done.46
  124.0 20.6 %collective-permute-done.45 = bf16[96,1024]{1,0:T(8,128)(2,1)S(1)} collective-permute-done((bf16[96,1024]{1,0:T(8,128)(2,1)S(1)}, bf16[96,1024]{1,0:T(8,128)(2,1)S(1)}, u32[]{:S(2)}, u32[]{:S(2)}) %collective-permute-start.45) | collective-permute-done | bytes 196640 | tf_op jit(solution)/shard_map/ppermute | solution.py:36
  151.2 14.2 %collective-permute-done.47 = bf16[4,96,1024]{2,1,0:T(8,128)(2,1)} collective-permute-done((bf16[4,96,1024]{2,1,0:T(8,128)(2,1)S(1)}, bf16[4,96,1024]{2,1,0:T(8,128)(2,1)}, u32[]{:S(2)}, u32[]{:S(2)}) %collective-permute-start.47) | collective-permute-done | bytes 786464 | tf_op jit(solution)/shard_map/ppermute | solution.py:33
  169.9 2.4 fusion.437
  172.3 17.5 %collective-permute-done.9 = bf16[4,240,768]{2,1,0:T(8,128)(2,1)} collective-permute-done((bf16[4,240,768]{2,1,0:T(8,128)(2,1)S(1)}, bf16[4,240,768]{2,1,0:T(8,128)(2,1)}, u32[]{:S(2)}, u32[]{:S(2)}) %collective-permute-start.9) | collective-permute-done | bytes 1474592 | tf_op jit(solution)/shard_map/ppermute | solution.py:33
  192.0 14.6 %collective-permute-start.61 = (bf16[96,1024]{1,0:T(8,128)(2,1)S(1)}, bf16[96,1024]{1,0:T(8,128)(2,1)S(1)}, u32[]{:S(2)}, u32[]{:S(2)}) collective-permute-start(bf16[96,1024]{1,0:T(8,128)(2,1)S(1)} %pad_maximum_fusion.65), channel_id=1, source_target_pairs={{0,8},{8,16},{16,24},{24,0},{1,9},{9,17},{17,25},{25,1},{2,10},{10... | collective-permute-start | bytes 589832 | tf_op jit(solution)/shard_map/ppermute | solution.py:36
  213.2 7.8 collective-permute-done.60
  233.9 27.4 %collective-permute-done.62 = bf16[4,96,1024]{2,1,0:T(8,128)(2,1)} collective-permute-done((bf16[4,96,1024]{2,1,0:T(8,128)(2,1)S(1)}, bf16[4,96,1024]{2,1,0:T(8,128)(2,1)}, u32[]{:S(2)}, u32[]{:S(2)}) %collective-permute-start.62) | collective-permute-done | bytes 786464 | tf_op jit(solution)/shard_map/ppermute | solution.py:33
  272.6 18.2 %collective-permute-done.17 = bf16[4,224,768]{2,1,0:T(8,128)(2,1)S(1)} collective-permute-done((bf16[4,224,768]{2,1,0:T(8,128)(2,1)}, bf16[4,224,768]{2,1,0:T(8,128)(2,1)S(1)}, u32[]{:S(2)}, u32[]{:S(2)}) %collective-permute-start.17) | collective-permute-done | bytes 1376288 | tf_op jit(solution)/shard_map/ppermute | solution.py:33
  291.6 28.4 %collective-permute-done.30 = bf16[4,224,768]{2,1,0:T(8,128)(2,1)S(1)} collective-permute-done((bf16[4,224,768]{2,1,0:T(8,128)(2,1)S(1)}, bf16[4,224,768]{2,1,0:T(8,128)(2,1)S(1)}, u32[]{:S(2)}, u32[]{:S(2)}) %collective-permute-start.30) | collective-permute-done | bytes 1376288 | tf_op jit(solution)/shard_map/ppermute | solution.py:33
  340.5 3.9 collective-permute-done.20
  346.6 2.6 multiply_convert_fusion.2
  352.5 7.7 collective-permute-done.49
  363.1 3.9 collective-permute-done.24
  381.8 3.1 collective-permute-done.37
  385.1 10.5 %fusion.282 = (u8[144,256]{1,0:T(8,128)(4,1)S(1)}, u8[144,256]{1,0:T(8,128)(4,1)S(1)}, f32[4,144,256]{2,1,0:T(8,128)S(1)}) fusion(bf16[1024,256]{1,0:T(8,128)(2,1)S(1)} %copy-done.37, bf16[2,144,1024]{2,1,0:T(8,128)(2,1)S(1)} %collective-permute-done.51, bf16[1,144,1024]{2,1,0:T(8,128)(2,1)} %bitcast.142, bf16[1,144,1024]{2,1,0:T(8,128)(2,1)S(1)} %fusion.512), kind=kOutput, calls=%fused_computation.694 | convolution fusion | flops 305012736 | bytes 2367488 | tf_op jit(solution)/shard_map/rlk,km->rlm/dot_general | solution.py:233
  396.5 2.6 multiply_convert_fusion.1
  404.9 2.5 collective-permute-done.40
  433.1 2.6 collective-permute-done.72
  440.2 3.2 collective-permute-done.73
  472.8 3.9 collective-permute-done.76
  480.4 2.5 collective-permute-done.77
  502.3 2.7 fusion.460
  510.4 2.6 add_convert_fusion.2
  521.4 6.3 collective-permute-done.64
  532.1 4.1 collective-permute-done.65
  555.6 2.6 add_convert_fusion.3
  558.3 4.0 collective-permute-done.68
  567.4 5.3 collective-permute-done.83
  577.3 2.8 collective-permute-start.126
  580.8 7.9 reduce-scatter.6.cloned.1.call-done
  591.2 3.0 collective-permute-start.125
  602.5 3.6 collective-permute-start.86
  607.7 5.9 collective-permute-done.86
  620.8 4.4 collective-permute-done.87
  642.7 3.8 collective-permute-start.132
  647.4 3.5 collective-permute-done.130
  650.9 3.2 collective-permute-done.132
  658.3 2.6 bitcast_convert_fusion
  660.9 2.6 collective-permute-done.90
  680.3 5.5 collective-permute-start.93
  689.7 11.4 %collective-permute-done.113 = bf16[4,248,768]{2,1,0:T(8,128)(2,1)} collective-permute-done((bf16[4,248,768]{2,1,0:T(8,128)(2,1)}, bf16[4,248,768]{2,1,0:T(8,128)(2,1)}, u32[]{:S(2)}, u32[]{:S(2)}) %collective-permute-start.113) | collective-permute-done | bytes 1523744 | tf_op jit(solution)/shard_map/ppermute | solution.py:33
  701.1 3.1 add_convert_fusion.1
  708.0 7.2 collective-permute-done.94
  718.5 4.3 collective-permute-done.95
  738.8 2.5 bitcast_convert_fusion.1
  750.3 4.4 collective-permute-done.100
  758.5 4.8 collective-permute-start.114
  776.1 2.5 collective-permute-done.109
  778.6 5.7 collective-permute-done.111
  784.3 9.1 %collective-permute-done.110 = bf16[128,1024]{1,0:T(8,128)(2,1)} collective-permute-done((bf16[128,1024]{1,0:T(8,128)(2,1)}, bf16[128,1024]{1,0:T(8,128)(2,1)}, u32[]{:S(2)}, u32[]{:S(2)}) %collective-permute-start.110) | collective-permute-done | bytes 262176 | tf_op jit(solution)/shard_map/ppermute | solution.py:36
  803.0 3.0 collective-permute-start.112
  811.0 2.5 collective-permute-start.104
  816.2 8.0 collective-permute-done.102
  824.2 9.4 %collective-permute-done.104 = bf16[272,768]{1,0:T(8,128)(2,1)} collective-permute-done((bf16[272,768]{1,0:T(8,128)(2,1)S(1)}, bf16[272,768]{1,0:T(8,128)(2,1)}, u32[]{:S(2)}, u32[]{:S(2)}) %collective-permute-start.104) | collective-permute-done | bytes 417824 | tf_op jit(solution)/shard_map/ppermute | solution.py:36
  833.6 15.8 %collective-permute-done.103 = bf16[272,768]{1,0:T(8,128)(2,1)} collective-permute-done((bf16[272,768]{1,0:T(8,128)(2,1)S(1)}, bf16[272,768]{1,0:T(8,128)(2,1)}, u32[]{:S(2)}, u32[]{:S(2)}) %collective-permute-start.103) | collective-permute-done | bytes 417824 | tf_op jit(solution)/shard_map/ppermute | solution.py:36
  (1493 shorter events, 411.4 us)
Async XLA Ops:
  7.2 161.7 %all-gather.11.cloned.1.call-start = ((), (), s32[]{:S(2)}) async-start(), calls=%async_computation.8 | async-start | bytes 1658880 | tf_op jit(solution)/shard_map/all_gather | solution.py:135
  7.9 16.9 %collective-permute-start.10 = (f32[64]{0:T(128)S(1)}, f32[64]{0:T(128)S(1)}, u32[]{:S(2)}, u32[]{:S(2)}) collective-permute-start(f32[64]{0:T(128)S(1)} %get-tuple-element.358), channel_id=1, source_target_pairs={{0,1},{1,0},{2,3},{3,2},{4,5},{5,4},{6,7},{7,6},{8,9},{9,8},{10,11... | collective-permute-start | bytes 776 | tf_op jit(solution)/shard_map/ppermute | solution.py:30
  14.0 15.4 %collective-permute-start.4 = (bf16[2,448]{1,0:T(2,128)(2,1)S(1)}, bf16[2,448]{1,0:T(2,128)(2,1)S(1)}, u32[]{:S(2)}, u32[]{:S(2)}) collective-permute-start(bf16[2,448]{1,0:T(2,128)(2,1)S(1)} %squeeze.436), channel_id=1, source_target_pairs={{0,1},{1,0},{2,3},{3,2},{4,5},{5,4},{6,7},{7,6},{8,9},{9,8},{10,11... | collective-permute-start | bytes 5384 | tf_op jit(solution)/shard_map/ppermute | solution.py:30
  15.1 30.0 %collective-permute-start.41 = (bf16[2,32,256]{2,1,0:T(8,128)(2,1)S(1)}, bf16[2,32,256]{2,1,0:T(8,128)(2,1)S(1)}, u32[]{:S(2)}, u32[]{:S(2)}) collective-permute-start(bf16[2,32,256]{2,1,0:T(8,128)(2,1)S(1)} %get-tuple-element.309), channel_id=1, source_target_pairs={{0,1},{1,0},{2,3},{3,2},{4,5},{5,4},{6,7},{7,6},{8,9},{9,8},{10,11... | collective-permute-start | bytes 98312 | tf_op jit(solution)/shard_map/ppermute | solution.py:30
  17.2 27.8 %collective-permute-start.56 = (bf16[2,32,256]{2,1,0:T(8,128)(2,1)S(1)}, bf16[2,32,256]{2,1,0:T(8,128)(2,1)S(1)}, u32[]{:S(2)}, u32[]{:S(2)}) collective-permute-start(bf16[2,32,256]{2,1,0:T(8,128)(2,1)S(1)} %get-tuple-element.317), channel_id=1, source_target_pairs={{0,1},{1,0},{2,3},{3,2},{4,5},{5,4},{6,7},{7,6},{8,9},{9,8},{10,11... | collective-permute-start | bytes 98312 | tf_op jit(solution)/shard_map/ppermute | solution.py:30
  17.5 12.7 %collective-permute-start.14 = (bf16[2,24,768]{2,1,0:T(8,128)(2,1)S(1)}, bf16[2,24,768]{2,1,0:T(8,128)(2,1)S(1)}, u32[]{:S(2)}, u32[]{:S(2)}) collective-permute-start(bf16[2,24,768]{2,1,0:T(8,128)(2,1)S(1)} %get-tuple-element.273), channel_id=1, source_target_pairs={{0,1},{1,0},{2,3},{3,2},{4,5},{5,4},{6,7},{7,6},{8,9},{9,8},{10,11... | collective-permute-start | bytes 221192 | tf_op jit(solution)/shard_map/ppermute | solution.py:30
  39.5 152.5 %all-gather.9.cloned.1.call-start = ((), (), s32[]{:S(2)}) async-start(), calls=%async_computation.7 | async-start | bytes 1720320 | tf_op jit(solution)/shard_map/all_gather | solution.py:135
  49.5 65.1 %collective-permute-start.12 = (bf16[64,768]{1,0:T(8,128)(2,1)S(1)}, bf16[64,768]{1,0:T(8,128)(2,1)S(1)}, u32[]{:S(2)}, u32[]{:S(2)}) collective-permute-start(bf16[64,768]{1,0:T(8,128)(2,1)S(1)} %bitcast.1340), channel_id=1, source_target_pairs={{0,1},{1,0},{2,3},{3,2},{4,5},{5,4},{6,7},{7,6},{8,9},{9,8},{10,11... | collective-permute-start | bytes 294920 | tf_op jit(solution)/shard_map/ppermute | solution.py:30
  53.2 176.0 %all-gather.7.cloned.1.call-start = ((), (), s32[]{:S(2)}) async-start(), calls=%async_computation.6 | async-start | bytes 1720320 | tf_op jit(solution)/shard_map/all_gather | solution.py:135
  53.5 25.7 %collective-permute-start.8 = (bf16[240,768]{1,0:T(8,128)(2,1)S(1)}, bf16[240,768]{1,0:T(8,128)(2,1)S(1)}, u32[]{:S(2)}, u32[]{:S(2)}) collective-permute-start(bf16[240,768]{1,0:T(8,128)(2,1)S(1)} %fusion.169), channel_id=1, source_target_pairs={{0,8},{8,16},{16,24},{24,0},{1,9},{9,17},{17,25},{25,1},{2,10},{10... | collective-permute-start | bytes 1105928 | tf_op jit(solution)/shard_map/ppermute | solution.py:36
  56.3 46.4 %collective-permute-start.7 = (bf16[240,768]{1,0:T(8,128)(2,1)S(1)}, bf16[240,768]{1,0:T(8,128)(2,1)S(1)}, u32[]{:S(2)}, u32[]{:S(2)}) collective-permute-start(bf16[240,768]{1,0:T(8,128)(2,1)S(1)} %fusion.169), channel_id=1, source_target_pairs={{0,16},{8,24},{16,0},{24,8},{1,17},{9,25},{17,1},{25,9},{2,18},{10... | collective-permute-start | bytes 1105928 | tf_op jit(solution)/shard_map/ppermute | solution.py:36
  58.2 44.5 %collective-permute-start.6 = (bf16[240,768]{1,0:T(8,128)(2,1)S(1)}, bf16[240,768]{1,0:T(8,128)(2,1)S(1)}, u32[]{:S(2)}, u32[]{:S(2)}) collective-permute-start(bf16[240,768]{1,0:T(8,128)(2,1)S(1)} %fusion.169), channel_id=1, source_target_pairs={{0,24},{8,0},{16,8},{24,16},{1,25},{9,1},{17,9},{25,17},{2,26},{10... | collective-permute-start | bytes 1105928 | tf_op jit(solution)/shard_map/ppermute | solution.py:36
  60.0 57.6 %collective-permute-start.58 = (bf16[64,1024]{1,0:T(8,128)(2,1)S(1)}, bf16[64,1024]{1,0:T(8,128)(2,1)S(1)}, u32[]{:S(2)}, u32[]{:S(2)}) collective-permute-start(bf16[64,1024]{1,0:T(8,128)(2,1)S(1)} %pad_maximum_fusion.88), channel_id=1, source_target_pairs={{0,0},{1,8},{2,16},{3,24},{4,4},{5,12},{6,20},{7,28},{8,1},{9,9},{... | collective-permute-start | bytes 393224 | tf_op jit(solution)/shard_map/ppermute | solution.py:47
  79.2 67.3 %collective-permute-start.16 = (bf16[128,768]{1,0:T(8,128)(2,1)}, bf16[128,768]{1,0:T(8,128)(2,1)S(1)}, u32[]{:S(2)}, u32[]{:S(2)}) collective-permute-start(bf16[128,768]{1,0:T(8,128)(2,1)} %pad_maximum_fusion.60), channel_id=1, source_target_pairs={{0,0},{1,8},{2,16},{3,24},{4,4},{5,12},{6,20},{7,28},{8,1},{9,9},{... | collective-permute-start | bytes 589832 | tf_op jit(solution)/shard_map/ppermute | solution.py:47
  103.5 20.5 %collective-permute-start.46 = (bf16[96,1024]{1,0:T(8,128)(2,1)S(1)}, bf16[96,1024]{1,0:T(8,128)(2,1)S(1)}, u32[]{:S(2)}, u32[]{:S(2)}) collective-permute-start(bf16[96,1024]{1,0:T(8,128)(2,1)S(1)} %pad_maximum_fusion.64), channel_id=1, source_target_pairs={{0,8},{8,16},{16,24},{24,0},{1,9},{9,17},{17,25},{25,1},{2,10},{10... | collective-permute-start | bytes 589832 | tf_op jit(solution)/shard_map/ppermute | solution.py:36
  114.5 30.1 %collective-permute-start.45 = (bf16[96,1024]{1,0:T(8,128)(2,1)S(1)}, bf16[96,1024]{1,0:T(8,128)(2,1)S(1)}, u32[]{:S(2)}, u32[]{:S(2)}) collective-permute-start(bf16[96,1024]{1,0:T(8,128)(2,1)S(1)} %pad_maximum_fusion.64), channel_id=1, source_target_pairs={{0,16},{8,24},{16,0},{24,8},{1,17},{9,25},{17,1},{25,9},{2,18},{10... | collective-permute-start | bytes 589832 | tf_op jit(solution)/shard_map/ppermute | solution.py:36
  114.6 30.0 %collective-permute-start.44 = (bf16[96,1024]{1,0:T(8,128)(2,1)S(1)}, bf16[96,1024]{1,0:T(8,128)(2,1)S(1)}, u32[]{:S(2)}, u32[]{:S(2)}) collective-permute-start(bf16[96,1024]{1,0:T(8,128)(2,1)S(1)} %pad_maximum_fusion.64), channel_id=1, source_target_pairs={{0,24},{8,0},{16,8},{24,16},{1,25},{9,1},{17,9},{25,17},{2,26},{10... | collective-permute-start | bytes 589832 | tf_op jit(solution)/shard_map/ppermute | solution.py:36
  117.6 30.2 %collective-permute-start = (bf16[144,1024]{1,0:T(8,128)(2,1)S(1)}, bf16[144,1024]{1,0:T(8,128)(2,1)S(1)}, u32[]{:S(2)}, u32[]{:S(2)}) collective-permute-start(bf16[144,1024]{1,0:T(8,128)(2,1)S(1)} %bitcast.1295), channel_id=1, source_target_pairs={{0,1},{1,0},{2,3},{3,2},{4,5},{5,4},{6,7},{7,6},{8,9},{9,8},{10,11... | collective-permute-start | bytes 884744 | tf_op jit(solution)/shard_map/ppermute | solution.py:30
  124.0 200.4 %collective-permute-start.13 = (bf16[2,64,768]{2,1,0:T(8,128)(2,1)}, bf16[2,64,768]{2,1,0:T(8,128)(2,1)}, u32[]{:S(2)}, u32[]{:S(2)}) collective-permute-start(bf16[2,64,768]{2,1,0:T(8,128)(2,1)} %pad_maximum_fusion.59), channel_id=1, source_target_pairs={{0,2},{2,0},{1,3},{3,1},{4,6},{6,4},{5,7},{7,5},{8,10},{10,8},{9,1... | collective-permute-start | bytes 589832 | tf_op jit(solution)/shard_map/ppermute | solution.py:27
  144.8 20.6 %collective-permute-start.47 = (bf16[4,96,1024]{2,1,0:T(8,128)(2,1)S(1)}, bf16[4,96,1024]{2,1,0:T(8,128)(2,1)}, u32[]{:S(2)}, u32[]{:S(2)}) collective-permute-start(bf16[4,96,1024]{2,1,0:T(8,128)(2,1)S(1)} %pad_maximum_fusion.14), channel_id=1, source_target_pairs={{0,4},{4,0},{1,5},{5,1},{2,6},{6,2},{3,7},{7,3},{8,12},{12,8},{9,1... | collective-permute-start | bytes 2359304 | tf_op jit(solution)/shard_map/ppermute | solution.py:33
  147.2 426.5 %reduce-scatter.8.cloned.1.call-start = ((), (), s32[]{:S(2)}) async-start(), calls=%async_computation.5 | async-start | bytes 1474560 | tf_op jit(solution)/shard_map/reduce_scatter | solution.py:193
  147.2 42.5 %collective-permute-start.9 = (bf16[4,240,768]{2,1,0:T(8,128)(2,1)S(1)}, bf16[4,240,768]{2,1,0:T(8,128)(2,1)}, u32[]{:S(2)}, u32[]{:S(2)}) collective-permute-start(bf16[4,240,768]{2,1,0:T(8,128)(2,1)S(1)} %pad_maximum_fusion.2), channel_id=1, source_target_pairs={{0,4},{4,0},{1,5},{5,1},{2,6},{6,2},{3,7},{7,3},{8,12},{12,8},{9,1... | collective-permute-start | bytes 4423688 | tf_op jit(solution)/shard_map/ppermute | solution.py:33
  148.7 177.5 %collective-permute-start.1 = (bf16[2,144,1024]{2,1,0:T(8,128)(2,1)}, bf16[2,144,1024]{2,1,0:T(8,128)(2,1)}, u32[]{:S(2)}, u32[]{:S(2)}) collective-permute-start(bf16[2,144,1024]{2,1,0:T(8,128)(2,1)} %pad_maximum_fusion.16), channel_id=1, source_target_pairs={{0,2},{2,0},{1,3},{3,1},{4,6},{6,4},{5,7},{7,5},{8,10},{10,8},{9,1... | collective-permute-start | bytes 1769480 | tf_op jit(solution)/shard_map/ppermute | solution.py:27
  192.0 20.1 %collective-permute-start.61 = (bf16[96,1024]{1,0:T(8,128)(2,1)S(1)}, bf16[96,1024]{1,0:T(8,128)(2,1)S(1)}, u32[]{:S(2)}, u32[]{:S(2)}) collective-permute-start(bf16[96,1024]{1,0:T(8,128)(2,1)S(1)} %pad_maximum_fusion.65), channel_id=1, source_target_pairs={{0,8},{8,16},{16,24},{24,0},{1,9},{9,17},{17,25},{25,1},{2,10},{10... | collective-permute-start | bytes 589832 | tf_op jit(solution)/shard_map/ppermute | solution.py:36
  206.6 14.4 %collective-permute-start.60 = (bf16[96,1024]{1,0:T(8,128)(2,1)S(1)}, bf16[96,1024]{1,0:T(8,128)(2,1)S(1)}, u32[]{:S(2)}, u32[]{:S(2)}) collective-permute-start(bf16[96,1024]{1,0:T(8,128)(2,1)S(1)} %pad_maximum_fusion.65), channel_id=1, source_target_pairs={{0,16},{8,24},{16,0},{24,8},{1,17},{9,25},{17,1},{25,9},{2,18},{10... | collective-permute-start | bytes 589832 | tf_op jit(solution)/shard_map/ppermute | solution.py:36
  207.3 13.7 %collective-permute-start.59 = (bf16[96,1024]{1,0:T(8,128)(2,1)S(1)}, bf16[96,1024]{1,0:T(8,128)(2,1)S(1)}, u32[]{:S(2)}, u32[]{:S(2)}) collective-permute-start(bf16[96,1024]{1,0:T(8,128)(2,1)S(1)} %pad_maximum_fusion.65), channel_id=1, source_target_pairs={{0,24},{8,0},{16,8},{24,16},{1,25},{9,1},{17,9},{25,17},{2,26},{10... | collective-permute-start | bytes 589832 | tf_op jit(solution)/shard_map/ppermute | solution.py:36
  212.2 56.5 %collective-permute-start.34 = (bf16[4,216,768]{2,1,0:T(8,128)(2,1)}, bf16[4,216,768]{2,1,0:T(8,128)(2,1)}, u32[]{:S(2)}, u32[]{:S(2)}) collective-permute-start(bf16[4,216,768]{2,1,0:T(8,128)(2,1)} %bitcast.1288), channel_id=1, source_target_pairs={{0,4},{4,0},{1,5},{5,1},{2,6},{6,2},{3,7},{7,3},{8,12},{12,8},{9,1... | collective-permute-start | bytes 3981320 | tf_op jit(solution)/shard_map/ppermute | solution.py:33
  221.3 40.1 %collective-permute-start.62 = (bf16[4,96,1024]{2,1,0:T(8,128)(2,1)S(1)}, bf16[4,96,1024]{2,1,0:T(8,128)(2,1)}, u32[]{:S(2)}, u32[]{:S(2)}) collective-permute-start(bf16[4,96,1024]{2,1,0:T(8,128)(2,1)S(1)} %pad_maximum_fusion.15), channel_id=1, source_target_pairs={{0,4},{4,0},{1,5},{5,1},{2,6},{6,2},{3,7},{7,3},{8,12},{12,8},{9,1... | collective-permute-start | bytes 2359304 | tf_op jit(solution)/shard_map/ppermute | solution.py:33
  230.2 60.5 %collective-permute-start.17 = (bf16[4,224,768]{2,1,0:T(8,128)(2,1)}, bf16[4,224,768]{2,1,0:T(8,128)(2,1)S(1)}, u32[]{:S(2)}, u32[]{:S(2)}) collective-permute-start(bf16[4,224,768]{2,1,0:T(8,128)(2,1)} %bitcast.1284), channel_id=1, source_target_pairs={{0,4},{4,0},{1,5},{5,1},{2,6},{6,2},{3,7},{7,3},{8,12},{12,8},{9,1... | collective-permute-start | bytes 4128776 | tf_op jit(solution)/shard_map/ppermute | solution.py:33
  261.3 58.7 %collective-permute-start.30 = (bf16[4,224,768]{2,1,0:T(8,128)(2,1)S(1)}, bf16[4,224,768]{2,1,0:T(8,128)(2,1)S(1)}, u32[]{:S(2)}, u32[]{:S(2)}) collective-permute-start(bf16[4,224,768]{2,1,0:T(8,128)(2,1)S(1)} %bitcast.1282), channel_id=1, source_target_pairs={{0,4},{4,0},{1,5},{5,1},{2,6},{6,2},{3,7},{7,3},{8,12},{12,8},{9,1... | collective-permute-start | bytes 4128776 | tf_op jit(solution)/shard_map/ppermute | solution.py:33
  404.8 15.7 %collective-permute-start.52 = (bf16[2,144,1024]{2,1,0:T(8,128)(2,1)S(1)}, bf16[2,144,1024]{2,1,0:T(8,128)(2,1)}, u32[]{:S(2)}, u32[]{:S(2)}) collective-permute-start(bf16[2,144,1024]{2,1,0:T(8,128)(2,1)S(1)} %slice.1309), channel_id=1, source_target_pairs={{0,2},{2,0},{1,3},{3,1},{4,6},{6,4},{5,7},{7,5},{8,10},{10,8},{9,1... | collective-permute-start | bytes 1769480 | tf_op jit(solution)/shard_map/ppermute | solution.py:27
  408.7 11.7 %collective-permute-start.69 = (bf16[64,768]{1,0:T(8,128)(2,1)S(1)}, bf16[64,768]{1,0:T(8,128)(2,1)S(1)}, u32[]{:S(2)}, u32[]{:S(2)}) collective-permute-start(bf16[64,768]{1,0:T(8,128)(2,1)S(1)} %fusion.401), channel_id=1, source_target_pairs={{0,1},{1,0},{2,3},{3,2},{4,5},{5,4},{6,7},{7,6},{8,9},{9,8},{10,11... | collective-permute-start | bytes 294920 | tf_op jit(solution)/shard_map/ppermute | solution.py:30
  429.4 81.0 %collective-permute-start.122 = (bf16[4,192,768]{2,1,0:T(8,128)(2,1)}, bf16[4,192,768]{2,1,0:T(8,128)(2,1)}, u32[]{:S(2)}, u32[]{:S(2)}) collective-permute-start(bf16[4,192,768]{2,1,0:T(8,128)(2,1)} %pad_maximum_fusion.12), channel_id=1, source_target_pairs={{0,4},{4,0},{1,5},{5,1},{2,6},{6,2},{3,7},{7,3},{8,12},{12,8},{9,1... | collective-permute-start | bytes 3538952 | tf_op jit(solution)/shard_map/ppermute | solution.py:33
  444.4 24.1 %collective-permute-start.54 = (bf16[144,1024]{1,0:T(8,128)(2,1)}, bf16[144,1024]{1,0:T(8,128)(2,1)}, u32[]{:S(2)}, u32[]{:S(2)}) collective-permute-start(bf16[144,1024]{1,0:T(8,128)(2,1)} %fusion.158), channel_id=1, source_target_pairs={{0,1},{1,0},{2,3},{3,2},{4,5},{5,4},{6,7},{7,6},{8,9},{9,8},{10,11... | collective-permute-start | bytes 884744 | tf_op jit(solution)/shard_map/ppermute | solution.py:30
  470.5 28.4 %collective-permute-start.55 = (bf16[2,144,1024]{2,1,0:T(8,128)(2,1)}, bf16[2,144,1024]{2,1,0:T(8,128)(2,1)}, u32[]{:S(2)}, u32[]{:S(2)}) collective-permute-start(bf16[2,144,1024]{2,1,0:T(8,128)(2,1)} %pad_maximum_fusion.18), channel_id=1, source_target_pairs={{0,2},{2,0},{1,3},{3,1},{4,6},{6,4},{5,7},{7,5},{8,10},{10,8},{9,1... | collective-permute-start | bytes 1769480 | tf_op jit(solution)/shard_map/ppermute | solution.py:27
  492.7 15.8 %collective-permute-start.79 = (bf16[2,64,768]{2,1,0:T(8,128)(2,1)}, bf16[2,64,768]{2,1,0:T(8,128)(2,1)}, u32[]{:S(2)}, u32[]{:S(2)}) collective-permute-start(bf16[2,64,768]{2,1,0:T(8,128)(2,1)} %slice.1312), channel_id=1, source_target_pairs={{0,2},{2,0},{1,3},{3,1},{4,6},{6,4},{5,7},{7,5},{8,10},{10,8},{9,1... | collective-permute-start | bytes 589832 | tf_op jit(solution)/shard_map/ppermute | solution.py:27
  498.3 57.3 %collective-permute-start.119 = (bf16[4,192,768]{2,1,0:T(8,128)(2,1)}, bf16[4,192,768]{2,1,0:T(8,128)(2,1)}, u32[]{:S(2)}, u32[]{:S(2)}) collective-permute-start(bf16[4,192,768]{2,1,0:T(8,128)(2,1)} %pad_maximum_fusion.11), channel_id=1, source_target_pairs={{0,4},{4,0},{1,5},{5,1},{2,6},{6,2},{3,7},{7,3},{8,12},{12,8},{9,1... | collective-permute-start | bytes 3538952 | tf_op jit(solution)/shard_map/ppermute | solution.py:33
  513.0 75.7 %reduce-scatter.6.cloned.1.call-start = ((), (), s32[]{:S(2)}) async-start(), calls=%async_computation.4 | async-start | bytes 1474560 | tf_op jit(solution)/shard_map/reduce_scatter | solution.py:193
  558.3 197.4 %reduce-scatter.4.cloned.1.call-start = ((), (), s32[]{:S(2)}) async-start(), calls=%async_computation.3 | async-start | bytes 1904640 | tf_op jit(solution)/shard_map/reduce_scatter | solution.py:193
  573.7 20.5 %collective-permute-start.84 = (bf16[2,144,1024]{2,1,0:T(8,128)(2,1)}, bf16[2,144,1024]{2,1,0:T(8,128)(2,1)}, u32[]{:S(2)}, u32[]{:S(2)}) collective-permute-start(bf16[2,144,1024]{2,1,0:T(8,128)(2,1)} %pad_maximum_fusion.20), channel_id=1, source_target_pairs={{0,2},{2,0},{1,3},{3,1},{4,6},{6,4},{5,7},{7,5},{8,10},{10,8},{9,1... | collective-permute-start | bytes 1769480 | tf_op jit(solution)/shard_map/ppermute | solution.py:27
  576.0 40.7 %collective-permute-start.123 = (bf16[2,24,768]{2,1,0:T(8,128)(2,1)}, bf16[2,24,768]{2,1,0:T(8,128)(2,1)}, u32[]{:S(2)}, u32[]{:S(2)}) collective-permute-start(bf16[2,24,768]{2,1,0:T(8,128)(2,1)} %get-tuple-element.269), channel_id=1, source_target_pairs={{0,1},{1,0},{2,3},{3,2},{4,5},{5,4},{6,7},{7,6},{8,9},{9,8},{10,11... | collective-permute-start | bytes 221192 | tf_op jit(solution)/shard_map/ppermute | solution.py:30
  577.3 48.8 %collective-permute-start.126 = (bf16[96,768]{1,0:T(8,128)(2,1)}, bf16[96,768]{1,0:T(8,128)(2,1)}, u32[]{:S(2)}, u32[]{:S(2)}) collective-permute-start(bf16[96,768]{1,0:T(8,128)(2,1)} %get-tuple-element.239), channel_id=1, source_target_pairs={{0,0},{1,8},{2,16},{3,24},{4,4},{5,12},{6,20},{7,28},{8,1},{9,9},{... | collective-permute-start | bytes 442376 | tf_op jit(solution)/shard_map/ppermute | solution.py:47
  590.4 28.1 %collective-permute-start.120 = (bf16[2,24,768]{2,1,0:T(8,128)(2,1)S(1)}, bf16[2,24,768]{2,1,0:T(8,128)(2,1)S(1)}, u32[]{:S(2)}, u32[]{:S(2)}) collective-permute-start(bf16[2,24,768]{2,1,0:T(8,128)(2,1)S(1)} %get-tuple-element.265), channel_id=1, source_target_pairs={{0,1},{1,0},{2,3},{3,2},{4,5},{5,4},{6,7},{7,6},{8,9},{9,8},{10,11... | collective-permute-start | bytes 221192 | tf_op jit(solution)/shard_map/ppermute | solution.py:30
  591.2 35.4 %collective-permute-start.125 = (bf16[96,768]{1,0:T(8,128)(2,1)}, bf16[96,768]{1,0:T(8,128)(2,1)}, u32[]{:S(2)}, u32[]{:S(2)}) collective-permute-start(bf16[96,768]{1,0:T(8,128)(2,1)} %get-tuple-element.237), channel_id=1, source_target_pairs={{0,0},{1,8},{2,16},{3,24},{4,4},{5,12},{6,20},{7,28},{8,1},{9,9},{... | collective-permute-start | bytes 442376 | tf_op jit(solution)/shard_map/ppermute | solution.py:47
  602.5 11.1 %collective-permute-start.86 = (bf16[144,1024]{1,0:T(8,128)(2,1)S(1)}, bf16[144,1024]{1,0:T(8,128)(2,1)S(1)}, u32[]{:S(2)}, u32[]{:S(2)}) collective-permute-start(bf16[144,1024]{1,0:T(8,128)(2,1)S(1)} %fusion.175), channel_id=1, source_target_pairs={{0,1},{1,0},{2,3},{3,2},{4,5},{5,4},{6,7},{7,6},{8,9},{9,8},{10,11... | collective-permute-start | bytes 884744 | tf_op jit(solution)/shard_map/ppermute | solution.py:30
  613.6 19.4 %collective-permute-start.129 = (bf16[4,64,1024]{2,1,0:T(8,128)(2,1)}, bf16[4,64,1024]{2,1,0:T(8,128)(2,1)}, u32[]{:S(2)}, u32[]{:S(2)}) collective-permute-start(bf16[4,64,1024]{2,1,0:T(8,128)(2,1)} %pad_maximum_fusion.26), channel_id=1, source_target_pairs={{0,4},{4,0},{1,5},{5,1},{2,6},{6,2},{3,7},{7,3},{8,12},{12,8},{9,1... | collective-permute-start | bytes 1572872 | tf_op jit(solution)/shard_map/ppermute | solution.py:33
  642.5 13.9 %collective-permute-start.89 = (bf16[2,144,1024]{2,1,0:T(8,128)(2,1)S(1)}, bf16[2,144,1024]{2,1,0:T(8,128)(2,1)S(1)}, u32[]{:S(2)}, u32[]{:S(2)}) collective-permute-start(bf16[2,144,1024]{2,1,0:T(8,128)(2,1)S(1)} %slice.1305), channel_id=1, source_target_pairs={{0,2},{2,0},{1,3},{3,1},{4,6},{6,4},{5,7},{7,5},{8,10},{10,8},{9,1... | collective-permute-start | bytes 1769480 | tf_op jit(solution)/shard_map/ppermute | solution.py:27
  642.7 11.3 %collective-permute-start.132 = (bf16[64,1024]{1,0:T(8,128)(2,1)S(1)}, bf16[64,1024]{1,0:T(8,128)(2,1)S(1)}, u32[]{:S(2)}, u32[]{:S(2)}) collective-permute-start(bf16[64,1024]{1,0:T(8,128)(2,1)S(1)} %get-tuple-element.196), channel_id=1, source_target_pairs={{0,24},{8,0},{16,8},{24,16},{1,25},{9,1},{17,9},{25,17},{2,26},{10... | collective-permute-start | bytes 393224 | tf_op jit(solution)/shard_map/ppermute | solution.py:36
  669.5 31.6 %collective-permute-start.113 = (bf16[4,248,768]{2,1,0:T(8,128)(2,1)}, bf16[4,248,768]{2,1,0:T(8,128)(2,1)}, u32[]{:S(2)}, u32[]{:S(2)}) collective-permute-start(bf16[4,248,768]{2,1,0:T(8,128)(2,1)} %pad_maximum_fusion.1), channel_id=1, source_target_pairs={{0,4},{4,0},{1,5},{5,1},{2,6},{6,2},{3,7},{7,3},{8,12},{12,8},{9,1... | collective-permute-start | bytes 4571144 | tf_op jit(solution)/shard_map/ppermute | solution.py:33
  680.3 24.0 %collective-permute-start.93 = (bf16[2,144,1024]{2,1,0:T(8,128)(2,1)}, bf16[2,144,1024]{2,1,0:T(8,128)(2,1)}, u32[]{:S(2)}, u32[]{:S(2)}) collective-permute-start(bf16[2,144,1024]{2,1,0:T(8,128)(2,1)} %slice.1304), channel_id=1, source_target_pairs={{0,2},{2,0},{1,3},{3,1},{4,6},{6,4},{5,7},{7,5},{8,10},{10,8},{9,1... | collective-permute-start | bytes 1769480 | tf_op jit(solution)/shard_map/ppermute | solution.py:27
  730.9 12.8 %collective-permute-start.97 = (bf16[2,64,768]{2,1,0:T(8,128)(2,1)S(1)}, bf16[2,64,768]{2,1,0:T(8,128)(2,1)S(1)}, u32[]{:S(2)}, u32[]{:S(2)}) collective-permute-start(bf16[2,64,768]{2,1,0:T(8,128)(2,1)S(1)} %slice.1311), channel_id=1, source_target_pairs={{0,2},{2,0},{1,3},{3,1},{4,6},{6,4},{5,7},{7,5},{8,10},{10,8},{9,1... | collective-permute-start | bytes 589832 | tf_op jit(solution)/shard_map/ppermute | solution.py:27
  738.3 26.3 %collective-permute-start.108 = (bf16[4,128,1024]{2,1,0:T(8,128)(2,1)}, bf16[4,128,1024]{2,1,0:T(8,128)(2,1)}, u32[]{:S(2)}, u32[]{:S(2)}) collective-permute-start(bf16[4,128,1024]{2,1,0:T(8,128)(2,1)} %pad_maximum_fusion.13), channel_id=1, source_target_pairs={{0,4},{4,0},{1,5},{5,1},{2,6},{6,2},{3,7},{7,3},{8,12},{12,8},{9,1... | collective-permute-start | bytes 3145736 | tf_op jit(solution)/shard_map/ppermute | solution.py:33
  747.6 60.1 %collective-permute-start.101 = (bf16[4,272,768]{2,1,0:T(8,128)(2,1)}, bf16[4,272,768]{2,1,0:T(8,128)(2,1)}, u32[]{:S(2)}, u32[]{:S(2)}) collective-permute-start(bf16[4,272,768]{2,1,0:T(8,128)(2,1)} %pad_maximum_fusion), channel_id=1, source_target_pairs={{0,4},{4,0},{1,5},{5,1},{2,6},{6,2},{3,7},{7,3},{8,12},{12,8},{9,1... | collective-permute-start | bytes 5013512 | tf_op jit(solution)/shard_map/ppermute | solution.py:33
  756.6 12.7 %collective-permute-start.116 = (bf16[24,768]{1,0:T(8,128)(2,1)S(1)}, bf16[24,768]{1,0:T(8,128)(2,1)S(1)}, u32[]{:S(2)}, u32[]{:S(2)}) collective-permute-start(bf16[24,768]{1,0:T(8,128)(2,1)S(1)} %slice_bitcast_fusion.58), channel_id=1, source_target_pairs={{0,0},{1,8},{2,16},{3,24},{4,4},{5,12},{6,20},{7,28},{8,1},{9,9},{... | collective-permute-start | bytes 110600 | tf_op jit(solution)/shard_map/ppermute | solution.py:47
  758.5 13.2 %collective-permute-start.114 = (bf16[2,24,576]{2,1,0:T(8,128)(2,1)S(1)}, bf16[2,24,576]{2,1,0:T(8,128)(2,1)S(1)}, u32[]{:S(2)}, u32[]{:S(2)}) collective-permute-start(bf16[2,24,576]{2,1,0:T(8,128)(2,1)S(1)} %get-tuple-element.289), channel_id=1, source_target_pairs={{0,1},{1,0},{2,3},{3,2},{4,5},{5,4},{6,7},{7,6},{8,9},{9,8},{10,11... | collective-permute-start | bytes 165896 | tf_op jit(solution)/shard_map/ppermute | solution.py:30
  767.2 11.4 %collective-permute-start.109 = (bf16[128,1024]{1,0:T(8,128)(2,1)}, bf16[128,1024]{1,0:T(8,128)(2,1)}, u32[]{:S(2)}, u32[]{:S(2)}) collective-permute-start(bf16[128,1024]{1,0:T(8,128)(2,1)} %get-tuple-element.153), channel_id=1, source_target_pairs={{0,8},{8,16},{16,24},{24,0},{1,9},{9,17},{17,25},{25,1},{2,10},{10... | collective-permute-start | bytes 786440 | tf_op jit(solution)/shard_map/ppermute | solution.py:36
  769.3 15.0 %collective-permute-start.111 = (bf16[128,1024]{1,0:T(8,128)(2,1)}, bf16[128,1024]{1,0:T(8,128)(2,1)}, u32[]{:S(2)}, u32[]{:S(2)}) collective-permute-start(bf16[128,1024]{1,0:T(8,128)(2,1)} %get-tuple-element.154), channel_id=1, source_target_pairs={{0,24},{8,0},{16,8},{24,16},{1,25},{9,1},{17,9},{25,17},{2,26},{10... | collective-permute-start | bytes 786440 | tf_op jit(solution)/shard_map/ppermute | solution.py:36
  771.7 21.7 %collective-permute-start.110 = (bf16[128,1024]{1,0:T(8,128)(2,1)}, bf16[128,1024]{1,0:T(8,128)(2,1)}, u32[]{:S(2)}, u32[]{:S(2)}) collective-permute-start(bf16[128,1024]{1,0:T(8,128)(2,1)} %get-tuple-element.155), channel_id=1, source_target_pairs={{0,16},{8,24},{16,0},{24,8},{1,17},{9,25},{17,1},{25,9},{2,18},{10... | collective-permute-start | bytes 786440 | tf_op jit(solution)/shard_map/ppermute | solution.py:36
  774.3 23.7 %collective-permute-start.133 = (bf16[2,32,256]{2,1,0:T(8,128)(2,1)}, bf16[2,32,256]{2,1,0:T(8,128)(2,1)}, u32[]{:S(2)}, u32[]{:S(2)}) collective-permute-start(bf16[2,32,256]{2,1,0:T(8,128)(2,1)} %get-tuple-element.301), channel_id=1, source_target_pairs={{0,1},{1,0},{2,3},{3,2},{4,5},{5,4},{6,7},{7,6},{8,9},{9,8},{10,11... | collective-permute-start | bytes 98312 | tf_op jit(solution)/shard_map/ppermute | solution.py:30
  778.6 18.4 %collective-permute-start.118 = (bf16[2,32,768]{2,1,0:T(8,128)(2,1)}, bf16[2,32,768]{2,1,0:T(8,128)(2,1)}, u32[]{:S(2)}, u32[]{:S(2)}) collective-permute-start(bf16[2,32,768]{2,1,0:T(8,128)(2,1)} %get-tuple-element.252), channel_id=1, source_target_pairs={{0,2},{2,0},{1,3},{3,1},{4,6},{6,4},{5,7},{7,5},{8,10},{10,8},{9,1... | collective-permute-start | bytes 294920 | tf_op jit(solution)/shard_map/ppermute | solution.py:27
  803.0 11.5 %collective-permute-start.112 = (bf16[96,1024]{1,0:T(8,128)(2,1)}, bf16[96,1024]{1,0:T(8,128)(2,1)}, u32[]{:S(2)}, u32[]{:S(2)}) collective-permute-start(bf16[96,1024]{1,0:T(8,128)(2,1)} %slice.1041), channel_id=1, source_target_pairs={{0,0},{1,8},{2,16},{3,24},{4,4},{5,12},{6,20},{7,28},{8,1},{9,9},{... | collective-permute-start | bytes 589832 | tf_op jit(solution)/shard_map/ppermute | solution.py:47
  809.7 14.5 %collective-permute-start.102 = (bf16[272,768]{1,0:T(8,128)(2,1)S(1)}, bf16[272,768]{1,0:T(8,128)(2,1)}, u32[]{:S(2)}, u32[]{:S(2)}) collective-permute-start(bf16[272,768]{1,0:T(8,128)(2,1)S(1)} %get-tuple-element.122), channel_id=1, source_target_pairs={{0,8},{8,16},{16,24},{24,0},{1,9},{9,17},{17,25},{25,1},{2,10},{10... | collective-permute-start | bytes 1253384 | tf_op jit(solution)/shard_map/ppermute | solution.py:36
  811.0 22.5 %collective-permute-start.104 = (bf16[272,768]{1,0:T(8,128)(2,1)S(1)}, bf16[272,768]{1,0:T(8,128)(2,1)}, u32[]{:S(2)}, u32[]{:S(2)}) collective-permute-start(bf16[272,768]{1,0:T(8,128)(2,1)S(1)} %get-tuple-element.123), channel_id=1, source_target_pairs={{0,24},{8,0},{16,8},{24,16},{1,25},{9,1},{17,9},{25,17},{2,26},{10... | collective-permute-start | bytes 1253384 | tf_op jit(solution)/shard_map/ppermute | solution.py:36
  813.6 35.9 %collective-permute-start.103 = (bf16[272,768]{1,0:T(8,128)(2,1)S(1)}, bf16[272,768]{1,0:T(8,128)(2,1)}, u32[]{:S(2)}, u32[]{:S(2)}) collective-permute-start(bf16[272,768]{1,0:T(8,128)(2,1)S(1)} %get-tuple-element.124), channel_id=1, source_target_pairs={{0,16},{8,24},{16,0},{24,8},{1,17},{9,25},{17,1},{25,9},{2,18},{10... | collective-permute-start | bytes 1253384 | tf_op jit(solution)/shard_map/ppermute | solution.py:36
  (408 other events, 2541.2 us)
Sparse Core Ops, SparseCore 0:
  39.7 61.4 all-gather.10
  103.3 52.7 all-gather.8
  158.2 32.6 all-gather.6
  513.2 28.8 reduce-scatter.7
  558.4 30.2 reduce-scatter.5
  704.4 36.4 reduce-scatter.3

commit v3 on v2

v3 whole, which is shorter than its diff:
```python
from functools import partial

import jax
import jax.numpy as jnp
from jax import lax
from jax.experimental import pallas as pl
from jax.experimental.pallas import tpu as pltpu
from jax.sharding import Mesh, PartitionSpec as P

HT = 12
HI = 8
HC = 8
REGIONS = 36
EPS = 1e-06
F32 = jnp.float32
BF16 = jnp.bfloat16
ALL = ("z", "y", "core", "x")
FLIP = ((0, 1), (1, 0))
TEAM = 4
PIECE = 8


class Grid:
    def __init__(self, depth):
        self.depth, self.rest = depth, depth // 4
        self.y, self.core, self.x = (lax.axis_index(name) for name in ALL[1:])
        z = lax.axis_index("z")
        self.near = z // self.rest % 2
        self.column = z // (2 * self.rest) * self.rest + z % self.rest

    def split(self, z):
        return z // (2 * self.rest), z // self.rest % 2, z % self.rest

    def join(self, far, near, low):
        return (far * 2 + near) * self.rest + low

    def to_core(self, value):
        return lax.ppermute(value, "core", FLIP)

    def to_x(self, value):
        return lax.ppermute(value, "x", FLIP)

    def to_y(self, value):
        return lax.ppermute(value, "y", FLIP)

    def to_near(self, value):
        pairs = []
        for z in range(self.depth):
            far, near, low = self.split(z)
            pairs.append((z, self.join(far, 1 - near, low)))
        return lax.ppermute(value, "z", pairs)

    def to_column(self, value, step):
        pairs = []
        for z in range(self.depth):
            far, near, low = self.split(z)
            column = (far * self.rest + low + step) % (2 * self.rest)
            pairs.append((z, self.join(column // self.rest, near, column % self.rest)))
        return lax.ppermute(value, "z", pairs)

    def swap_far(self, value):
        pairs = []
        for z in range(self.depth):
            far, near, low = self.split(z)
            for y in range(2):
                for core in range(2):
                    for x in range(2):
                        there = ((self.join(core, near, low) * 2 + y) * 2 + far) * 2 + x
                        pairs.append((((z * 2 + y) * 2 + core) * 2 + x, there))
        return lax.ppermute(value, ALL, pairs)


def pick(value, index, axis):
    return lax.dynamic_index_in_dim(value, index, axis, keepdims=False)


def paired(own, other, index, axis):
    own, other = jnp.expand_dims(own, axis), jnp.expand_dims(other, axis)
    shape = list(own.shape)
    shape[axis] = 2
    place = lax.broadcasted_iota(jnp.int32, shape, axis)
    return jnp.where(place == index, own, other)


def joined(values, axis):
    return jnp.concatenate(values, axis) if len(values) > 1 else values[0]


def widen(value, width):
    lack = width - value.shape[-1]
    return jnp.pad(value, [(0, 0)] * (value.ndim - 1) + [(0, lack)]) if lack else value


GROUPS = {"tci": 3, "ici": 3, "tsi": 3, "isi": 3, "tu0": 1, "tu1": 1, "iu0": 1, "iu1": 1}
WIDE = 256


def quarters(w, groups):
    r, n = w.shape
    wide = n // groups // TEAM
    parts = widen(w.reshape(r, groups, TEAM, wide), -(-wide // WIDE) * WIDE)
    return parts.transpose(2, 0, 1, 3).reshape(2, 2, r, groups * parts.shape[3])


def from_quarters(parts, groups, n):
    _, _, r, c = parts.shape
    parts = parts.reshape(TEAM, r, groups, c // groups)[..., : n // groups // TEAM]
    return parts.transpose(1, 2, 0, 3).reshape(r, n)


def team_trade(grid, parts):
    got = grid.to_near(pick(parts, 1 - grid.near, 1))
    parts = paired(pick(parts, grid.near, 1), got, grid.near, 1)
    got = grid.to_core(pick(parts, 1 - grid.core, 0))
    return paired(pick(parts, grid.core, 0), got, grid.core, 0)


def trade_ins(grid, parts):
    width = max(p.shape[3] for p in parts)
    lines = team_trade(grid, joined([widen(p, width) for p in parts], 2))
    out, at = [], 0
    for p in parts:
        r, c = p.shape[2:]
        out.append(lines[:, :, at : at + r, :c])
        at += r
    return out


class Bundle:
    def __init__(self, names, width):
        self.names, self.width = names, width

    def flat(self, value):
        p, r, c = value.shape[-3:]
        lead = value.shape[:-3]
        if p * c == self.width and p > 1:
            value = jnp.concatenate([value[..., k, :, :] for k in range(p)], -1)
        else:
            value = value.reshape(lead + (p * r, c))
        lack = -value.shape[-2] % PIECE
        if lack:
            value = jnp.pad(value, [(0, 0)] * len(lead) + [(0, lack), (0, 0)])
        return value.reshape(lead + (-1, PIECE, self.width))

    def count(self, shape):
        p, r, c = shape
        return -(-(r if p * c == self.width else p * r) // PIECE)

    def unflat(self, lines, shape):
        p, r, c = shape
        lead = lines.shape[:-3]
        lines = lines.reshape(lead + (-1, self.width))
        if p * c == self.width and p > 1:
            return jnp.stack([lines[..., :r, k * c : (k + 1) * c] for k in range(p)], -3)
        return lines[..., : p * r, :].reshape(lead + (p, r, c))


class Gather:
    def __init__(self, grid, bundles, parts):
        self.grid, self.bundles, self.parts = grid, bundles, parts
        self.blocks, self.sides, self.corners = {}, {}, {}
        self.gate = ()

    def chunk(self, i):
        bundle = self.bundles[i]
        return joined([bundle.flat(self.parts[n]) for n in bundle.names], 0)

    def round(self, moves, also=()):
        grid, columns = self.grid, 2 * self.grid.rest
        sends = []
        for kind, i in moves:
            if kind == "z":
                sends.append(self.chunk(i))
            elif kind == "xy":
                sends.append(self.blocks[i])
            else:
                by_x, by_y = self.sides[i]
                cut = by_x.shape[1] // 2
                sends.append((by_x[:, :cut], by_y[:, cut:]))
        if self.gate or also:
            sends, _ = lax.optimization_barrier((sends, (self.gate, also)))
        self.gate = ()
        for (kind, i), value in zip(moves, sends):
            if kind == "c":
                got = self.corners[i] = (grid.to_y(value[0]), grid.to_x(value[1]))
            elif kind == "xy":
                self.blocks[i] = value
                got = self.sides[i] = (grid.to_x(value), grid.to_y(value))
            else:
                got = tuple(grid.to_column(value, k) for k in range(1, columns))
                order = (value, *got)
                places = []
                for place in range(columns):
                    here = order[0]
                    for k in range(1, columns):
                        here = jnp.where((grid.column - place) % columns == k, order[k], here)
                    places.append(here)
                self.blocks[i] = jnp.stack(places)
            self.gate += got

    def full(self, i):
        grid, bundle, parts = self.grid, self.bundles[i], self.parts
        corner = jnp.concatenate(self.corners[i], 1)
        full, at = {}, 0
        for name in bundle.names:
            shape = parts[name].shape
            p, r, c = shape
            n = bundle.count(shape)
            cut = [bundle.unflat(b[:, at : at + n], shape) for b in (self.blocks[i], *self.sides[i], corner)]
            at += n
            if p == TEAM:
                cut = [b.reshape(2, grid.rest, 2, 2, r, c).transpose(0, 3, 1, 2, 4, 5) for b in cut]
                cut = [b[:, :, :, None, :, None] for b in cut]
                place = (3, 5)
            else:
                cut = [b.reshape(2, grid.rest, r, c).swapaxes(0, 1)[:, None, :, None] for b in cut]
                place = (1, 3)
            size = list(cut[0].shape)
            size[place[0]] = size[place[1]] = 2
            here_y = lax.broadcasted_iota(jnp.int32, size, place[0]) == grid.y
            here_x = lax.broadcasted_iota(jnp.int32, size, place[1]) == grid.x
            own, ox, oy, oxy = cut
            value = jnp.where(here_y, jnp.where(here_x, own, ox), jnp.where(here_x, oy, oxy))
            full[name] = lax.optimization_barrier(value).reshape(-1, c)
        return full


def plus(a, *more):
    total = a.astype(F32)
    for b in more:
        total = total + b.astype(F32)
    return total.astype(BF16)


def after(gate, value):
    return lax.optimization_barrier((value, gate))[0]


class Give:
    def __init__(self, grid, bundle, grads, widths):
        self.grid, self.bundle, self.widths, self.step = grid, bundle, widths, 0
        rest = grid.rest
        self.views, self.shapes = [], []
        for name in bundle.names:
            k, c = grads[name].shape
            if name in GROUPS:
                r = k // (rest * 32)
                self.views.append(grads[name].reshape(2, 2, rest, 2, 2, 2, r, c))
                self.shapes.append((TEAM, r, c))
            else:
                r = k // (rest * 8)
                self.views.append(grads[name].reshape(rest, 2, 2, 2, r, c))
                self.shapes.append((1, r, c))
        self.next()

    def block(self, y, x):
        pieces = []
        for view, (p, r, c) in zip(self.views, self.shapes):
            if p == TEAM:
                value = pick(pick(view, x, 5), y, 3).transpose(0, 2, 3, 1, 4, 5)
            else:
                value = pick(pick(view, x, 3), y, 1).swapaxes(0, 1)
            pieces.append(self.bundle.flat(value.reshape(2 * self.grid.rest, p, r, c)))
        return joined(pieces, 1)

    def next(self, gate=None):
        if gate is not None:
            self.got = after(gate, self.got)
        step, self.step = self.step, self.step + 1
        (self.corner, self.side, self.column, self.team, self.core, self.finish)[step]()

    def corner(self):
        grid = self.grid
        corner = self.block(1 - grid.y, 1 - grid.x)
        self.cut = corner.shape[1] // 2
        self.got = grid.to_y(corner[:, : self.cut]), grid.to_x(corner[:, self.cut :])

    def side(self):
        grid, cut, (by_y, by_x) = self.grid, self.cut, self.got
        x = self.block(grid.y, 1 - grid.x)
        y = self.block(1 - grid.y, grid.x)
        x = jnp.concatenate([plus(x[:, :cut], by_y), x[:, cut:]], 1)
        y = jnp.concatenate([y[:, :cut], plus(y[:, cut:], by_x)], 1)
        self.got = grid.to_x(x), grid.to_y(y)

    def column(self):
        grid, columns = self.grid, 2 * self.grid.rest
        chunk = plus(self.block(grid.y, grid.x), *self.got)
        mine = pick(chunk, grid.column, 0)
        sent = [grid.to_column(pick(chunk, (grid.column + k) % columns, 0), k) for k in range(1, columns)]
        self.got = mine, *sent

    def team(self):
        grid, bundle = self.grid, self.bundle
        total = plus(*self.got)
        self.quads, outs, at = [], [], 0
        for name, shape in zip(bundle.names, self.shapes):
            n = bundle.count(shape)
            part = bundle.unflat(total[at : at + n], shape)
            if name in GROUPS:
                self.quads.append((name, part.reshape((2, 2) + part.shape[1:])))
            else:
                outs.append(part[0])
            at += n
        self.got = ()
        if self.quads:
            width = max(q.shape[3] for _, q in self.quads)
            lines = joined([widen(q, width) for _, q in self.quads], 2)
            self.got += (pick(lines, grid.near, 1), grid.to_near(pick(lines, 1 - grid.near, 1)))
        if outs:
            self.got += (grid.swap_far(joined(outs, 0)),)

    def core(self):
        grid = self.grid
        if self.quads:
            mine, came, *outs = self.got
            lines = paired(mine, came, grid.near, 1)
            self.got = (pick(lines, grid.core, 0), grid.to_core(pick(lines, 1 - grid.core, 0)), *outs)

    def finish(self):
        grid, outs, self.done = self.grid, self.got, {}
        if self.quads:
            mine, came, *outs = self.got
            lines, at = paired(mine, came, grid.core, 0), 0
            for name, quad in self.quads:
                r, c = quad.shape[2:]
                part = lines[:, :, at : at + r, :c]
                self.done[name] = from_quarters(part, GROUPS[name], self.widths[name]).astype(F32)
                at += r
        at = 0
        for name, (p, r, c) in zip(self.bundle.names, self.shapes):
            if p == 1:
                self.done[name] = outs[0][at : at + r].astype(F32)
                at += r

    def end(self):
        while self.step < 6:
            self.next()
        return self.done


class Sizes:
    def __init__(self, lt, kt, li, ki):
        self.lt, self.kt, self.li, self.ki = lt, kt, li, ki
        self.third, self.tall, self.left = kt // 3, lt * 3 // 4, lt // 4
        self.rows = li + 2 * self.tall
        self.wide_rows = self.rows + li

    def text(self, ref, r, base=None):
        base = (self.li if base is None else base) + r * self.tall
        top = ref[pl.ds(base, self.tall), : self.kt]
        last = [ref[pl.ds(base + j * self.left, self.left), self.kt :] for j in range(3)]
        return jnp.concatenate([top, jnp.concatenate(last, 1)], 0)

    def put_text(self, ref, r, text):
        base = self.li + r * self.tall
        text = text.astype(ref.dtype)
        ref[pl.ds(base, self.tall), : self.kt] = text[: self.tall]
        for j in range(3):
            block = text[self.tall :, j * self.third : (j + 1) * self.third]
            ref[pl.ds(base + j * self.left, self.left), self.kt :] = block

    def image(self, ref, r=0):
        return ref[pl.ds(r * self.rows, self.li), :]

    def put_image(self, ref, image, r=0):
        ref[pl.ds(r * self.rows, self.li), :] = image.astype(ref.dtype)

    def pack_rows(self, text, image):
        last = text[self.tall :]
        last = [last[:, j * self.third : (j + 1) * self.third] for j in range(3)]
        return jnp.concatenate([image, jnp.concatenate([text[: self.tall], jnp.concatenate(last, 0)], 1)], 0)

    def unpack_text(self, rows):
        rows = rows[self.li : self.li + self.tall]
        last = [rows[j * self.left : (j + 1) * self.left, self.kt :] for j in range(3)]
        return jnp.concatenate([rows[:, : self.kt], jnp.concatenate(last, 1)], 0)

    def both(self, near, far, wide=False):
        text = [self.text(ref, r) for ref in (near, far) for r in range(2)]
        image = [self.image(ref, r) for ref in (near, far) for r in range(2 if wide else 1)]
        return jnp.concatenate(text, 0), jnp.concatenate(image, 0)

    def put_sums(self, home, away, text, image):
        for r in range(TEAM):
            self.put_text((home, away)[r // 2], r % 2, text[r * self.lt : (r + 1) * self.lt])
        count = image.shape[0] // self.li
        for r in range(count):
            part = image[r * self.li : (r + 1) * self.li]
            self.put_image((home, away)[r * 2 // count], part, r % (count // 2))

    def sums(self, wide=False):
        shape = (self.wide_rows if wide else self.rows, self.ki)
        return [(shape, F32), (shape, BF16)]


def kernel(body, outs, args, flops, scratch=()):
    outs = [jax.ShapeDtypeStruct(shape, kind) for shape, kind in outs]
    size = sum(a.size * a.dtype.itemsize for a in (*args, *outs))
    return pl.pallas_call(
        body,
        out_shape=outs,
        scratch_shapes=[pltpu.VMEM(shape, kind) for shape, kind in scratch],
        compiler_params=pltpu.CompilerParams(vmem_limit_bytes=int(1.25 * size) + (14 << 20)),
        cost_estimate=pl.CostEstimate(flops=flops, bytes_accessed=size, transcendentals=0),
    )(*args)


def mm(a, b):
    return jnp.dot(a, b, preferred_element_type=F32)


def mm_bt(a, b):
    return lax.dot_general(a, b, (((1,), (1,)), ((), ())), preferred_element_type=F32)


def mm_at(a, b):
    return lax.dot_general(a, b, (((0,), (0,)), ((), ())), preferred_element_type=F32)


def gelu(v):
    return 0.5 * v * (1.0 + lax.erf(v * (0.5**0.5)))


def gelu_slope(v):
    return 0.5 * (1.0 + lax.erf(v * (0.5**0.5))) + v * jnp.exp(-0.5 * v * v) * (0.5 / jnp.pi) ** 0.5


def ffn_kernel(near, far, ut, dt, ui, di, uj, dj, before_t, hidden_t, before_i, hidden_i, home, away, *, s):
    text, image = s.both(near, far)
    pre = mm(text, ut[...])
    before_t[...] = pre
    act = gelu(pre).astype(BF16)
    hidden_t[...] = act
    text_sums, image_sums = mm(act, dt[...]), 0.0
    f = ui.shape[1]
    for part, (up, down) in enumerate(((ui, di), (uj, dj))):
        at = pl.ds(part * f, f)
        pre = mm(image, up[...])
        before_i[:, at] = pre
        act = gelu(pre).astype(BF16)
        hidden_i[:, at] = act
        image_sums = image_sums + mm(act, down[...])
    s.put_sums(home, away, text_sums, image_sums)


def ffn(s, low, ut, dt, *image_w):
    ft, fi = ut.shape[1], 2 * image_w[0].shape[1]
    outs = []
    for length, f in ((TEAM * s.lt, ft), (2 * s.li, fi)):
        outs += [((length, f), F32), ((length, f), BF16)]
    flops = 16 * (s.lt * s.kt * ft + s.li * s.ki * fi)
    return kernel(partial(ffn_kernel, s=s), outs + s.sums(), (*low, ut, dt, *image_w), flops)


def ffn_back_kernel(near, far, before_t, before_i, ut, dt, ui, di, uj, dj, bg_t, bg_i, home, away, *, s):
    text, image = s.both(near, far)
    grad = (mm_bt(text, dt[...]) * gelu_slope(before_t[...])).astype(BF16)
    bg_t[...] = grad
    text_sums, image_sums = mm_bt(grad, ut[...]), 0.0
    f = ui.shape[1]
    for part, (up, down) in enumerate(((ui, di), (uj, dj))):
        at = pl.ds(part * f, f)
        grad = (mm_bt(image, down[...]) * gelu_slope(before_i[:, at])).astype(BF16)
        bg_i[:, at] = grad
        image_sums = image_sums + mm_bt(grad, up[...])
    s.put_sums(home, away, text_sums, image_sums)


def ffn_back(s, out, before_t, before_i, ut, dt, *image_w):
    ft, fi = ut.shape[1], 2 * image_w[0].shape[1]
    outs = [((TEAM * s.lt, ft), BF16), ((2 * s.li, fi), BF16)] + s.sums()
    flops = 16 * (s.lt * s.kt * ft + s.li * s.ki * fi)
    args = (*out, before_t, before_i, ut, dt, *image_w)
    return kernel(partial(ffn_back_kernel, s=s), outs, args, flops)


def softmax_of(q, k, allowed, factor):
    scores = jnp.where(allowed, mm_bt(q, k) * factor, -1e30)
    exponent = jnp.exp(scores - jnp.max(scores, -1, keepdims=True))
    return exponent / jnp.sum(exponent, -1, keepdims=True)


def head_back(q, k, v, grad, allowed, factor):
    probs = softmax_of(q, k, allowed, factor)
    dv = mm_at(probs.astype(BF16), grad)
    dp = mm_bt(grad, v)
    ds = (probs * (dp - jnp.sum(dp * probs, -1, keepdims=True))).astype(BF16)
    return mm(ds, k) * factor, mm_at(ds, q) * factor, dv


LANES = 128


def lane_part(size, sub):
    lane = lax.broadcasted_iota(jnp.int32, (1, LANES), 1)
    return jnp.logical_and(lane >= sub * size, lane < (sub + 1) * size)


def half_ids(length):
    col = lax.broadcasted_iota(jnp.int32, (length, 1), 0) >= length // 2
    row = lax.broadcasted_iota(jnp.int32, (1, length), 1) >= length // 2
    return col, row


def thirds(tile, wide):
    return [pl.ds(i * wide + tile * LANES, LANES) for i in range(3)]


def image_places(s):
    for r in range(TEAM):
        yield pl.ds(r * s.li, s.li)


def self_kernel(near, far, wt, wot, wi, woi, col, row, qkv_t, ctx_t, qkv_i, ctx_i, home, away, *, s, size, heads):
    text, image = s.both(near, far, True)
    qkv_t[...] = mm(text, wt[...]).astype(BF16)
    qkv_i[...] = mm(image, wi[...]).astype(BF16)
    wide = ctx_t.shape[1]
    allowed = col[...] == row[...]
    for tile in range(wide // LANES):
        q, k, v = (qkv_t[:, at] for at in thirds(tile, wide))
        total = jnp.zeros(q.shape, F32)
        for sub in range(min(LANES // size, heads - tile * (LANES // size))):
            lanes = lane_part(size, sub)
            probs = softmax_of(jnp.where(lanes, q, 0), k, allowed, size**-0.5)
            total = total + jnp.where(lanes, mm(probs.astype(BF16), v), 0.0)
        ctx_t[:, pl.ds(tile * LANES, LANES)] = total.astype(BF16)
    wide = ctx_i.shape[1]
    own, other = half_ids(s.li)
    for at in image_places(s):
        for tile in range(wide // LANES):
            q, k, v = (qkv_i[at, lanes] for lanes in thirds(tile, wide))
            probs = softmax_of(q, k, own == other, LANES**-0.5)
            ctx_i[at, pl.ds(tile * LANES, LANES)] = mm(probs.astype(BF16), v).astype(BF16)
    s.put_sums(home, away, mm(ctx_t[...], wot[...]), mm(ctx_i[...], woi[...]))


def attention_outs(s, wt, wi):
    outs = []
    for length, n in ((s.lt, wt.shape[1]), (s.li, wi.shape[1])):
        outs += [((TEAM * length, n), BF16), ((TEAM * length, n // 3), BF16)]
    return outs


def attention_flops(s, wt, wi):
    return 12 * (s.lt * s.kt * wt.shape[1] + s.li * s.ki * wi.shape[1])


def self_attention(s, low, wt, wot, wi, woi, col, row, size, heads):
    outs = attention_outs(s, wt, wi) + s.sums(True)
    args = (*low, wt, wot, wi, woi, col, row)
    return kernel(partial(self_kernel, s=s, size=size, heads=heads), outs, args, attention_flops(s, wt, wi))


def self_back_kernel(
    near, far, wt, wot, wi, woi, col, row, qkv_t, qkv_i, dqkv_t, dqkv_i, home, away, dctx_t, dctx_i, *, s, size, heads
):
    text, image = s.both(near, far, True)
    dctx_t[...] = mm_bt(text, wot[...]).astype(BF16)
    dctx_i[...] = mm_bt(image, woi[...]).astype(BF16)
    wide = dctx_t.shape[1]
    allowed = col[...] == row[...]
    for tile in range(wide // LANES):
        q, k, v = (qkv_t[:, at] for at in thirds(tile, wide))
        grad = dctx_t[:, pl.ds(tile * LANES, LANES)]
        totals = [jnp.zeros(q.shape, F32) for _ in range(3)]
        for sub in range(min(LANES // size, heads - tile * (LANES // size))):
            lanes = lane_part(size, sub)
            dq, dk, dv = head_back(
                jnp.where(lanes, q, 0), k, v, jnp.where(lanes, grad, 0), allowed, size**-0.5
            )
            totals = [totals[0] + jnp.where(lanes, dq, 0.0), totals[1] + dk, totals[2] + dv]
        for at, total in zip(thirds(tile, wide), totals):
            dqkv_t[:, at] = total.astype(BF16)
    wide = dctx_i.shape[1]
    own, other = half_ids(s.li)
    for at in image_places(s):
        for tile in range(wide // LANES):
            columns = thirds(tile, wide)
            q, k, v = (qkv_i[at, lanes] for lanes in columns)
            grad = dctx_i[at, pl.ds(tile * LANES, LANES)]
            grads = head_back(q, k, v, grad, own == other, LANES**-0.5)
            for lanes, value in zip(columns, grads):
                dqkv_i[at, lanes] = value.astype(BF16)
    s.put_sums(home, away, mm_bt(dqkv_t[...], wt[...]), mm_bt(dqkv_i[...], wi[...]))


def back_outs(s, wt, wi):
    outs = [((TEAM * s.lt, wt.shape[1]), BF16), ((TEAM * s.li, wi.shape[1]), BF16)] + s.sums(True)
    scratch = [((TEAM * s.lt, wt.shape[1] // 3), BF16), ((TEAM * s.li, wi.shape[1] // 3), BF16)]
    return outs, scratch


def self_back(s, out, wt, wot, wi, woi, col, row, qkv_t, qkv_i, size, heads):
    outs, scratch = back_outs(s, wt, wi)
    args = (*out, wt, wot, wi, woi, col, row, qkv_t, qkv_i)
    body = partial(self_back_kernel, s=s, size=size, heads=heads)
    return kernel(body, outs, args, attention_flops(s, wt, wi), scratch)


def co_places(s, seg_col, seg_row):
    col, row = half_ids(s.li)
    for r in range(TEAM):
        text, image = pl.ds(r * s.lt, s.lt), pl.ds(r * s.li, s.li)
        text_col = seg_col[text, :] > 0.5
        text_row = seg_row[pl.ds(r, 1), :] > 0.5
        yield text, image, text_col == row, col == text_row


def co_kernel(
    near, far, wt, wot, wi, woi, seg_col, seg_row, qkv_t, ctx_t, qkv_i, ctx_i, home, away, *, s
):
    text, image = s.both(near, far, True)
    qkv_t[...] = mm(text, wt[...]).astype(BF16)
    qkv_i[...] = mm(image, wi[...]).astype(BF16)
    wide = ctx_t.shape[1]
    for text, image, cross, back in co_places(s, seg_col, seg_row):
        for tile in range(wide // LANES):
            q, k, v = thirds(tile, wide)
            probs = softmax_of(qkv_t[text, q], qkv_i[image, k], cross, LANES**-0.5)
            ctx_t[text, q] = mm(probs.astype(BF16), qkv_i[image, v]).astype(BF16)
            probs = softmax_of(qkv_i[image, q], qkv_t[text, k], back, LANES**-0.5)
            ctx_i[image, q] = mm(probs.astype(BF16), qkv_t[text, v]).astype(BF16)
    s.put_sums(home, away, mm(ctx_t[...], wot[...]), mm(ctx_i[...], woi[...]))


def co_attention(s, low, wt, wot, wi, woi, seg_col, seg_row):
    outs = attention_outs(s, wt, wi) + s.sums(True)
    args = (*low, wt, wot, wi, woi, seg_col, seg_row)
    return kernel(partial(co_kernel, s=s), outs, args, attention_flops(s, wt, wi))


def co_back_kernel(
    near, far, wt, wot, wi, woi, seg_col, seg_row, qkv_t, qkv_i, dqkv_t, dqkv_i, home, away, dctx_t, dctx_i, *, s
):
    text, image = s.both(near, far, True)
    dctx_t[...] = mm_bt(text, wot[...]).astype(BF16)
    dctx_i[...] = mm_bt(image, woi[...]).astype(BF16)
    wide = dctx_t.shape[1]
    for text, image, cross, back in co_places(s, seg_col, seg_row):
        for tile in range(wide // LANES):
            q, k, v = thirds(tile, wide)
            dq, dk, dv = head_back(
                qkv_t[text, q], qkv_i[image, k], qkv_i[image, v], dctx_t[text, q], cross, LANES**-0.5
            )
            dqkv_t[text, q] = dq.astype(BF16)
            dqkv_i[image, k] = dk.astype(BF16)
            dqkv_i[image, v] = dv.astype(BF16)
            dq, dk, dv = head_back(
                qkv_i[image, q], qkv_t[text, k], qkv_t[text, v], dctx_i[image, q], back, LANES**-0.5
            )
            dqkv_i[image, q] = dq.astype(BF16)
            dqkv_t[text, k] = dk.astype(BF16)
            dqkv_t[text, v] = dv.astype(BF16)
    s.put_sums(home, away, mm_bt(dqkv_t[...], wt[...]), mm_bt(dqkv_i[...], wi[...]))


def co_back(s, out, wt, wot, wi, woi, seg_col, seg_row, qkv_t, qkv_i):
    outs, scratch = back_outs(s, wt, wi)
    args = (*out, wt, wot, wi, woi, seg_col, seg_row, qkv_t, qkv_i)
    return kernel(partial(co_back_kernel, s=s), outs, args, attention_flops(s, wt, wi), scratch)


def weight_kernel(near, far, out_near, out_far, mid_t, grad_t, mid_i, grad_i, *outs, s, wide, parts):
    text, image = s.both(near, far, wide)
    text_out, image_out = s.both(out_near, out_far, wide)
    outs[0][...] = mm_at(text, grad_t[...]).astype(BF16)
    outs[1][...] = mm_at(mid_t[...], text_out).astype(BF16)
    grad, mid = grad_i.shape[1] // parts, mid_i.shape[1] // parts
    for part in range(parts):
        at = grad_i[:, pl.ds(part * grad, grad)]
        outs[2 + 2 * part][...] = mm_at(image, at).astype(BF16)
        at = mid_i[:, pl.ds(part * mid, mid)]
        outs[3 + 2 * part][...] = mm_at(at, image_out).astype(BF16)


def weight_grads(s, low, out, mid_t, grad_t, mid_i, grad_i, parts):
    outs = [((s.kt, grad_t.shape[1]), BF16), ((mid_t.shape[1], s.kt), BF16)]
    for _ in range(parts):
        outs += [((s.ki, grad_i.shape[1] // parts), BF16), ((mid_i.shape[1] // parts, s.ki), BF16)]
    flops = sum(8 * s.lt * shape[0] * shape[1] for shape, _ in outs)
    args = (*low, *out, mid_t, grad_t, mid_i, grad_i)
    return kernel(partial(weight_kernel, s=s, wide=parts == 1, parts=parts), outs, args, flops)


def fold_kernel(home, got, out, *, s):
    text = pl.ds(s.li, 2 * s.tall)
    sums = (home[text, :] + got[text, :].astype(F32)).astype(BF16)
    if out.shape[0] == 2 * s.tall:
        out[...] = sums
    else:
        out[pl.ds(0, s.li), :] = (s.image(home, 1) + s.image(got, 1).astype(F32)).astype(BF16)
        out[text, :] = sums


def fold(s, home, got):
    rows = s.rows if home.shape[0] > s.rows else 2 * s.tall
    body = partial(fold_kernel, s=s)
    return kernel(body, [((rows, s.ki), BF16)], (home, got), home.size)[0]


def settled_text(s, base, home, got, other, r):
    start = s.li if other.shape[0] == s.rows else 0
    value = s.text(base, r).astype(F32) + s.text(home, r) + s.text(got, r).astype(F32)
    return value + s.text(other, 1 - r, start).astype(F32)


def settled_image(s, base, home, got, other):
    value = s.image(base).astype(F32) + s.image(home) + s.image(got).astype(F32)
    return value + s.image(other).astype(F32) if other.shape[0] == s.rows else value


def norm_kernel(values, home, got, other, params, out, low, normed, inverse, *, s, i):
    def one(v, gain, shift, start):
        centred = v - jnp.mean(v, -1, keepdims=True)
        inv = lax.rsqrt(jnp.mean(centred * centred, -1, keepdims=True) + EPS)
        n = centred * inv
        inverse[pl.ds(start, v.shape[0]), :] = inv
        return n, n * gain + shift

    param = lambda k, width: params[pl.ds(4 * k + i, 1), :width]
    for r in range(2):
        v = settled_text(s, values, home, got, other, r)
        n, y = one(v, param(0, s.kt), param(1, s.kt), s.li + r * s.lt)
        for ref, value in ((normed, n), (out, y), (low, y)):
            s.put_text(ref, r, value)
    v = settled_image(s, values, home, got, other)
    n, y = one(v, param(2, s.ki), param(3, s.ki), 0)
    for ref, value in ((normed, n), (out, y), (low, y)):
        s.put_image(ref, value)


def norm(s, values, sums, params, i):
    pack = (s.rows, s.ki)
    outs = [(pack, F32), (pack, BF16), (pack, F32), ((s.li + 2 * s.lt, 1), F32)]
    y, low, *stored = kernel(partial(norm_kernel, s=s, i=i), outs, (values, *sums, params), 32 * s.rows * s.ki)
    return y, low, stored


def norm_back_kernel(*refs, s, i, first):
    if first:
        up, normed, inverse, params, grad, low, sums = refs
    else:
        up, home, got, other, normed, inverse, params, grad, low, sums = refs

    def one(u, n, gain, start):
        scaled = u * gain
        return inverse[pl.ds(start, u.shape[0]), :] * (
            scaled - jnp.mean(scaled, -1, keepdims=True) - n * jnp.mean(scaled * n, -1, keepdims=True)
        )

    def keep(k, u, n):
        width = u.shape[1]
        sums[pl.ds(k, 1), :width] = jnp.sum(u * n, axis=0, keepdims=True)
        sums[pl.ds(k + 1, 1), :width] = jnp.sum(u, axis=0, keepdims=True)

    sums[...] = jnp.zeros(sums.shape, F32)
    for r in range(2):
        u = s.text(up, r).astype(F32) if first else settled_text(s, up, home, got, other, r)
        n = s.text(normed, r)
        value = one(u, n, params[pl.ds(i, 1), : s.kt], s.li + r * s.lt)
        s.put_text(grad, r, value)
        s.put_text(low, r, value)
        if r == 0:
            keep(0, u, n)
    u = s.image(up).astype(F32) if first else settled_image(s, up, home, got, other)
    n = s.image(normed)
    value = one(u, n, params[pl.ds(8 + i, 1), :], 0)
    s.put_image(grad, value)
    s.put_image(low, value)
    keep(2, u, n)


def norm_back(s, upstream, sums, stored, params, i):
    pack = (s.rows, s.ki)
    outs = [(pack, F32), (pack, BF16), ((4, s.ki), F32)]
    body = partial(norm_back_kernel, s=s, i=i, first=sums is None)
    return kernel(body, outs, (upstream, *(sums or ()), *stored, params), 32 * s.rows * s.ki)


def sum_all(grid, value):
    value = value + grid.to_core(value)
    value = value + grid.to_x(value)
    value = value + grid.to_y(value)
    value = value + grid.to_near(value)
    return sum((grid.to_column(value, k) for k in range(1, 2 * grid.rest)), value)


FETCH = (
    Bundle(["tci", "ici", "tco", "icoa", "icob"], 768),
    Bundle(["id0", "iu0", "iso"], 1024),
    Bundle(["tu0", "td0"], 768),
    Bundle(["tsi", "isi", "tso"], 768),
    Bundle(["id1", "iu1"], 1024),
    Bundle(["tu1", "td1"], 768),
)


def shards(
    text_in,
    image_in,
    text_segments,
    text_co_in,
    text_co_out,
    image_co_in,
    image_co_out,
    text_self_in,
    text_self_out,
    image_self_in,
    image_self_out,
    text_up,
    text_down,
    image_up,
    image_down,
    text_gains,
    text_shifts,
    image_gains,
    image_shifts,
    grad_text_out,
    grad_image_out,
    depth,
):
    grid = Grid(depth)
    tw, iw = text_gains.shape[2], image_gains.shape[2]
    s = Sizes(*text_in.shape[1:], *image_in.shape[1:])
    weights = {
        "tci": text_co_in[0],
        "tco": text_co_out[0],
        "ici": image_co_in[0],
        "ico": image_co_out[0],
        "tsi": text_self_in[0],
        "tso": text_self_out[0],
        "isi": image_self_in[0],
        "iso": image_self_out[0],
        "tu0": text_up[0, 0],
        "tu1": text_up[0, 1],
        "td0": text_down[0, 0],
        "td1": text_down[0, 1],
        "iu0": image_up[0, 0],
        "iu1": image_up[0, 1],
        "id0": image_down[0, 0],
        "id1": image_down[0, 1],
    }

    weights["icoa"] = image_co_out[0][:, : FETCH[0].width]
    weights["icob"] = widen(image_co_out[0][:, FETCH[0].width :], FETCH[0].width)
    place = ((lax.axis_index("z") * 2 + grid.y) * 2 + grid.core) * 2 + grid.x
    params = jnp.zeros((16, s.ki), F32)
    for at, k, kinds in ((0, tw, (text_gains, text_shifts)), (8, iw, (image_gains, image_shifts))):
        own = jnp.concatenate([a[0] for a in kinds]).astype(F32)
        params = lax.dynamic_update_slice(params, own, (at, place * k))
    width = FETCH[0].width
    widths = {name: weights[name].shape[1] for name in GROUPS}
    quads = {name: quarters(weights[name], groups) for name, groups in GROUPS.items()}
    early = ("tci", "ici")
    late = ("tu0", "tsi", "isi", "tu1", "iu0", "iu1")
    parts = {}

    def trade(names):
        for n, q in zip(names, trade_ins(grid, [quads[n] for n in names])):
            parts[n] = q.reshape((TEAM,) + q.shape[2:])

    def swap(names):
        swapped, at = grid.swap_far(joined([weights[n] for n in names], 0)), 0
        for n in names:
            r = weights[n].shape[0]
            parts[n] = swapped[at : at + r][None]
            at += r

    trade(early)
    swap(("tco", "icoa", "icob"))
    fetch = Gather(grid, FETCH, parts)
    fetch.round([("z", 0)])
    names = ("td0", "tso", "td1", "id0", "iso", "id1")
    inputs = (text_in, image_in, text_segments, grad_text_out, grad_image_out, params)
    later = {n: quads[n] for n in late}, {n: weights[n] for n in names}, inputs
    quarters_later, weights_later, inputs = after(parts["ici"], later)
    quads.update(quarters_later)
    weights.update(weights_later)
    text_in, image_in, text_segments, grad_text_out, grad_image_out, params = inputs
    trade(late)
    swap(("id0", "iso", "id1"))
    swap(("td0", "tso", "td1"))
    fetch.round([("xy", 0)])
    params = sum_all(grid, params)

    def pair(own):
        return own, grid.to_core(own)

    segments = text_segments.astype(F32)
    segments = jnp.concatenate(pair(jnp.concatenate([segments, grid.to_near(segments)])))
    seg_col = segments.reshape(-1, 1)
    ids = segments + 2.0 * jnp.arange(TEAM, dtype=F32)[:, None]
    id_col, id_row = ids.reshape(-1, 1), ids.reshape(1, -1)
    size, heads = s.kt // HT, HT // TEAM
    own = s.pack_rows(text_in[0], image_in[0])
    got = grid.to_near(own)
    values = jnp.concatenate([own, got[s.li :], got[: s.li]])
    low0 = pair(values)
    own = s.pack_rows(grad_text_out[0], grad_image_out[0])
    upstream = jnp.concatenate([own, grid.to_near(own[s.li :])])

    def settle(home, away):
        got = grid.to_core(away)
        return home, got, grid.to_near(fold(s, home, got))

    def normal(values, sums, i):
        return norm(s, values, sums, params, i)

    def widened(low):
        return jnp.concatenate([low, grid.to_near(low[: s.li])])

    def near_pairs(*names):
        for name in names:
            yield full[name]
        for name in names:
            yield grid.to_near(full[name])

    fetch.round([("c", 0), ("z", 1)])
    full = fetch.full(0)
    full["ico"] = jnp.concatenate([full["icoa"], full["icob"][:, : s.ki - width]], 1)
    co_w = [full[n] for n in ("tci", "tco", "ici", "ico")]
    fetch.round([("xy", 1), ("z", 2)])
    qkv_t, ctx_t, qkv_i, ctx_i, home, away = co_attention(s, low0, *co_w, seg_col, segments)
    fetch.round([("c", 1), ("xy", 2), ("z", 3)], away)
    full.update(fetch.full(1))
    sums = settle(home, away)
    y, low, stored0 = normal(values, sums, 0)
    low1 = pair(low)
    fetch.round([("c", 2), ("xy", 3), ("z", 4)], sums[1])
    full.update(fetch.full(2))
    ffn_w = [[full["tu0"], full["td0"], *near_pairs("iu0", "id0")]]
    fetch.round([("c", 3), ("xy", 4), ("z", 5)], low)
    full.update(fetch.full(3))
    full["tso"] = jnp.pad(full["tso"], ((0, full["tsi"].shape[1] // 3 - full["tso"].shape[0]), (0, 0)))
    self_w = [full[n] for n in ("tsi", "tso", "isi", "iso")]
    before_t0, hidden_t0, before_i0, hidden_i0, home, away = ffn(s, low1, *ffn_w[0])
    fetch.round([("c", 4), ("xy", 5)], away)
    full.update(fetch.full(4))
    y, low, stored1 = normal(y, settle(home, away), 1)
    fetch.round([("c", 5)], low)
    full.update(fetch.full(5))
    low2 = pair(widened(low))
    ffn_w.append([full["tu1"], full["td1"], *near_pairs("iu1", "id1")])
    sqkv_t, sctx_t, sqkv_i, sctx_i, home, away = self_attention(s, low2, *self_w, id_col, id_row, size, heads)
    y, low, stored2 = normal(y, settle(home, away), 2)
    low3 = pair(low)
    before_t1, hidden_t1, before_i1, hidden_i1, home, away = ffn(s, low3, *ffn_w[1])
    _, last, stored3 = normal(y, settle(home, away), 3)

    grads, norm_grads = {}, [None] * 4

    def normal_back(upstream, sums, stored, i):
        grad, low, norm_grads[i] = norm_back(s, upstream, sums, stored, params, i)
        return grad, low

    def weigh(names, home, away, low, out, *mids, parts=1):
        got = grid.to_core(away)
        folded = fold(s, home, got)
        low, out, mids = after(folded, (low, out, mids))
        values = weight_grads(s, low, out, *mids, parts)
        grads.update(zip(names, values))
        return (home, got, grid.to_near(folded)), folded, values[4:]

    def give(names, wide, *gate):
        return Give(grid, Bundle(names, wide), grads, widths)

    def join_near(names, values, gate):
        values = after(gate, values)
        for name, value in zip(names, values):
            grads[name] = plus(grads[name], grid.to_near(value))

    g, low = normal_back(upstream, None, stored3, 3)
    out = pair(low)
    bg_t, bg_i, home, away = ffn_back(s, out, before_t1, before_i1, *ffn_w[1])
    sums, folded, others = weigh(
        ("tu1", "td1", "iu1", "id1"), home, away, low3, out, hidden_t1, bg_t, hidden_i1, bg_i, parts=2
    )
    text3 = give(["tu1", "td1"], width)

    g, low = normal_back(g, sums, stored2, 2)
    out = pair(widened(low))
    text3.next(low)
    dqkv_t, dqkv_i, home, away = self_back(s, out, *self_w, id_col, id_row, sqkv_t, sqkv_i, size, heads)
    join_near(("iu1", "id1"), others, away)
    sums, folded, _ = weigh(
        ("tsi", "tso", "isi", "iso"), home, away, low2, out, sctx_t, dqkv_t, sctx_i, dqkv_i
    )
    text3.next(folded)
    grads["tso"] = grads["tso"][: size * heads]
    text2 = give(["tsi", "isi", "tso"], width)

    g, low = normal_back(g, sums, stored1, 1)
    out = pair(low)
    text2.next(low)
    text3.next(low)
    image3 = give(["id1", "iu1", "iso"], s.ki)
    bg_t, bg_i, home, away = ffn_back(s, out, before_t0, before_i0, *ffn_w[0])
    sums, folded, others = weigh(
        ("tu0", "td0", "iu0", "id0"), home, away, low1, out, hidden_t0, bg_t, hidden_i0, bg_i, parts=2
    )
    image3.next(folded)
    text2.next(folded)
    text3.next(folded)
    text1 = give(["tu0", "td0"], width)

    g, low = normal_back(g, sums, stored0, 0)
    out = pair(widened(low))
    text1.next(low)
    image3.next(low)
    text2.next(low)
    join_near(("iu0", "id0"), others, out[1])
    dqkv_t, dqkv_i, home, away = co_back(s, out, *co_w, seg_col, segments, qkv_t, qkv_i)
    image1 = give(["id0", "iu0"], s.ki)
    sums, folded, _ = weigh(
        ("tci", "tco", "ici", "ico"), home, away, low0, out, ctx_t, dqkv_t, ctx_i, dqkv_i
    )
    grads["icoa"] = grads["ico"][:, :width]
    grads["icob"] = widen(grads["ico"][:, width:], width)
    text0 = give(["tci", "ici", "tco", "icoa", "icob"], width)
    for each in (text1, image3, text2, image1):
        each.next(folded)
    norm_sums = sum_all(grid, after(folded, jnp.concatenate(norm_grads))).reshape(4, 4, s.ki)
    home, got, other = sums
    mine = slice(0, s.li + s.tall)
    sums = g[mine] + home[mine] + got[mine].astype(F32)
    sums = sums + jnp.concatenate([other[: s.li], other[s.li + s.tall :]]).astype(F32)

    done = {}
    for each in (text3, text2, image3, text1, image1, text0):
        done.update(each.end())
    done["ico"] = jnp.concatenate([done["icoa"], done["icob"][:, : s.ki - width]], 1)
    norm_outs = [
        lax.dynamic_slice(norm_sums[:, i], (0, place * k), (4, k))[None]
        for i, k in enumerate((tw, tw, iw, iw))
    ]

    def both(first, second):
        return jnp.stack([done[first], done[second]])[None]

    return (
        s.unpack_text(last)[None],
        last[: s.li][None],
        s.unpack_text(sums)[None],
        sums[: s.li][None],
        *(done[n][None] for n in ("tci", "tco", "ici", "ico", "tsi", "tso", "isi", "iso")),
        both("tu0", "tu1"),
        both("td0", "td1"),
        both("iu0", "iu1"),
        both("id0", "id1"),
        *norm_outs,
    )


def solution(mesh):
    depth = mesh.shape["wide"] // 4
    fine = Mesh(mesh.devices.reshape(depth, 2, 2, mesh.shape["narrow"]), ALL)
    rows = P(ALL, None, None)
    weight = P(None, ALL, None)
    pair = P(None, None, ALL, None)
    norm = P(None, None, ALL)
    return jax.shard_map(
        partial(shards, depth=depth),
        mesh=fine,
        in_specs=(rows, rows, P(ALL, None), *[weight] * 8, *[pair] * 4, *[norm] * 4, rows, rows),
        out_specs=(rows, rows, rows, rows, *[weight] * 8, *[pair] * 4, *[norm] * 4),
        check_vma=False,
    )
```

time: 884 us -> 658 us (0.74)
  matrix products: 85.3 us -> 0 us
  local copies, waits for them, and re-layouts: 140 us -> 63.7 us
  other arithmetic: 107 us -> 38.8 us
  Pallas kernels: 0 us -> 49.8 us
  starting transfers between devices: 157 us -> 127 us
  between operations: 20.1 us -> 5.83 us
    ppermute x28 -> x55, waiting for transfers between devices: 134 us -> 241 us  [the longest x32 130 us: to_near(): return lax.ppermute(value, 'z', pairs)]
    dot_general x68 -> x0, matrix products: 81.3 us -> none  [the longest x16 23.5 us: dot(): return jnp.einsum('rlk,km->rlm', a, b, preferred_element_type=F32)]
    ppermute x12 -> x26, waiting for transfers between devices: 118 us -> 54 us  [to_y(): return lax.ppermute(value, 'y', FLIP)]
    pallas_call x0 -> x28, Pallas kernels: none -> 49.8 us  [kernel(): pl.pallas_call(body, out_shape=outs, scratch_shapes=[pltpu.VMEM(shape, ki...]
    ppermute x49 -> x26, waiting for transfers between devices: 99 us -> 60.4 us  [to_x(): return lax.ppermute(value, 'x', FLIP)]
    ppermute x49 -> x26, starting transfers between devices: 65.3 us -> 27.7 us  [to_x(): return lax.ppermute(value, 'x', FLIP)]
    slice x66 -> x64, local copies, waits for them, and re-layouts: 37.7 us -> 4.86 us  [the longest x22 1.35 us: full(): b[:, at:at + n]]
    convert_element_type x42 -> x39, other arithmetic: 37.5 us -> 10.5 us  [the longest x28 8.04 us: plus(): return total.astype(BF16)]
  transfers between devices with their start and end apart: 144 -> 134, of which waited for: 59 -> 62; matrix products, arithmetic and copies ran while one was open for 32% -> 12% of each run, Pallas kernels for 0% -> 5%
where the time goes in v3:
time: 658 us; the launch traced here: 649 us
  waiting for transfers between devices  364 us (55%)
  starting transfers between devices  127 us (19%)
  local copies, waits for them, and re-layouts  63.7 us (10%)
  Pallas kernels  49.8 us (8%)
  other arithmetic  38.8 us (6%)
    ppermute x32, waiting for transfers between devices, to_near(): return lax.ppermute(value, 'z', pairs)  130 us
    ppermute x14, waiting for transfers between devices, to_column(): return lax.ppermute(value, 'z', pairs)  111 us
    ppermute x26, waiting for transfers between devices, to_x(): return lax.ppermute(value, 'x', FLIP)  60.4 us
    ppermute x26, waiting for transfers between devices, to_y(): return lax.ppermute(value, 'y', FLIP)  54 us
    pallas_call x28, Pallas kernels, kernel(): pl.pallas_call(body, out_shape=outs, scratch_shapes=[pltpu.VMEM(shape, ki...  49.8 us
    ppermute x26, starting transfers between devices, to_y(): return lax.ppermute(value, 'y', FLIP)  28.5 us
    ppermute x26, starting transfers between devices, to_x(): return lax.ppermute(value, 'x', FLIP)  27.7 us
    ppermute x32, starting transfers between devices, to_near(): return lax.ppermute(value, 'z', pairs)  25.4 us
  transfers between devices with their start and end apart: 134, of which 62 were waited for; matrix products, arithmetic and copies ran while one was open for 12% of the time, Pallas kernels for 5%

profile of v3, /device:TPU:0, one launch (start us, length us, event | category | flops | bytes accessed | tf_op | source)
XLA Modules:
  0.0 648.9 jit_solution(13884309913021078126)
XLA Ops:
  5.9 3.2 collective-permute-start.9
  12.1 4.3 collective-permute-start.24
  19.1 6.4 collective-permute-done.13
  26.5 2.1 collective-permute-start.2
  36.4 2.6 collective-permute-done.19
  39.8 3.6 collective-permute-done.20
  44.1 3.9 collective-permute-start.21
  48.0 6.6 %collective-permute-done.21 = f32[16,1024]{1,0:T(8,128)S(1)} collective-permute-done((f32[16,1024]{1,0:T(8,128)S(1)}, f32[16,1024]{1,0:T(8,128)S(1)}, u32[]{:S(2)}, u32[]{:S(2)}) %collective-permute-start.21) | collective-permute-done | bytes 65568 | tf_op jit(solution)/shard_map/ppermute | solution.py:59
  57.1 3.1 collective-permute-start.5
  63.1 19.4 %collective-permute-done.5 = bf16[40,8,768]{2,1,0:T(8,128)(2,1)S(1)} collective-permute-done((bf16[40,8,768]{2,1,0:T(8,128)(2,1)S(1)}, bf16[40,8,768]{2,1,0:T(8,128)(2,1)S(1)}, u32[]{:S(2)}, u32[]{:S(2)}) %collective-permute-start.5) | collective-permute-done | bytes 491552 | tf_op jit(solution)/shard_map/ppermute | solution.py:59
  86.4 19.8 %collective-permute-done.6 = bf16[2,40,8,768]{3,2,1,0:T(8,128)(2,1)S(1)} collective-permute-done((bf16[2,40,8,768]{3,2,1,0:T(8,128)(2,1)S(1)}, bf16[2,40,8,768]{3,2,1,0:T(8,128)(2,1)S(1)}, u32[]{:S(2)}, u32[]{:S(2)}) %collective-permute-start.6) | collective-permute-done | bytes 983072 | tf_op jit(solution)/shard_map/ppermute | solution.py:41
  109.9 6.7 %collective-permute-done.23 = bf16[12,8,1024]{2,1,0:T(8,128)(2,1)S(1)} collective-permute-done((bf16[12,8,1024]{2,1,0:T(8,128)(2,1)S(1)}, bf16[12,8,1024]{2,1,0:T(8,128)(2,1)S(1)}, u32[]{:S(2)}, u32[]{:S(2)}) %collective-permute-start.23) | collective-permute-done | bytes 196640 | tf_op jit(solution)/shard_map/ppermute | solution.py:59
  116.7 2.7 collective-permute-done.11
  121.7 2.5 collective-permute-start.27
  127.0 4.9 shard_map.356
  132.1 2.9 collective-permute-done.27
  139.7 14.5 %collective-permute-done.31 = bf16[2,6,8,1024]{3,2,1,0:T(8,128)(2,1)S(1)} collective-permute-done((bf16[2,6,8,1024]{3,2,1,0:T(8,128)(2,1)S(1)}, bf16[2,6,8,1024]{3,2,1,0:T(8,128)(2,1)S(1)}, u32[]{:S(2)}, u32[]{:S(2)}) %collective-permute-start.31) | collective-permute-done | bytes 196640 | tf_op jit(solution)/shard_map/ppermute | solution.py:44
  156.2 13.8 %collective-permute-done.30 = bf16[31,8,768]{2,1,0:T(8,128)(2,1)S(1)} collective-permute-done((bf16[31,8,768]{2,1,0:T(8,128)(2,1)S(1)}, bf16[31,8,768]{2,1,0:T(8,128)(2,1)S(1)}, u32[]{:S(2)}, u32[]{:S(2)}) %collective-permute-start.30) | collective-permute-done | bytes 380960 | tf_op jit(solution)/shard_map/ppermute | solution.py:59
  170.7 3.2 collective-permute-start.43
  176.0 9.9 %collective-permute-done.43 = bf16[8,8,1024]{2,1,0:T(8,128)(2,1)S(1)} collective-permute-done((bf16[8,8,1024]{2,1,0:T(8,128)(2,1)S(1)}, bf16[8,8,1024]{2,1,0:T(8,128)(2,1)S(1)}, u32[]{:S(2)}, u32[]{:S(2)}) %collective-permute-start.43) | collective-permute-done | bytes 131104 | tf_op jit(solution)/shard_map/ppermute | solution.py:59
  187.0 6.2 collective-permute-done.34
  198.5 11.7 %collective-permute-done.41 = bf16[2,31,8,768]{3,2,1,0:T(8,128)(2,1)S(1)} collective-permute-done((bf16[2,31,8,768]{3,2,1,0:T(8,128)(2,1)S(1)}, bf16[2,31,8,768]{3,2,1,0:T(8,128)(2,1)S(1)}, u32[]{:S(2)}, u32[]{:S(2)}) %collective-permute-start.41) | collective-permute-done | bytes 761888 | tf_op jit(solution)/shard_map/ppermute | solution.py:41
  212.6 3.7 collective-permute-start.51
  221.2 4.6 collective-permute-done.51
  232.7 4.1 collective-permute-done.38.other
  237.3 2.5 collective-permute-start.39
  245.6 5.8 collective-permute-done.56
  252.4 3.6 shard_map.362
  256.3 2.1 collective-permute-done.46.got
  261.6 11.1 %collective-permute-done.47.other = bf16[240,1024]{1,0:T(8,128)(2,1)S(1)} collective-permute-done((bf16[240,1024]{1,0:T(8,128)(2,1)S(1)}, bf16[240,1024]{1,0:T(8,128)(2,1)S(1)}, u32[]{:S(2)}, u32[]{:S(2)}) %collective-permute-start.47) | collective-permute-done | bytes 491552 | tf_op jit(solution)/shard_map/ppermute | solution.py:51
  273.8 10.1 %collective-permute-done.58.uj = bf16[1024,256]{1,0:T(8,128)(2,1)S(1)} collective-permute-done((bf16[1024,256]{1,0:T(8,128)(2,1)S(1)}, bf16[1024,256]{1,0:T(8,128)(2,1)S(1)}, u32[]{:S(2)}, u32[]{:S(2)}) %collective-permute-start.58) | collective-permute-done | bytes 524320 | tf_op jit(solution)/shard_map/ppermute | solution.py:51
  283.9 10.4 %collective-permute-done.59.dj = bf16[256,1024]{1,0:T(8,128)(2,1)S(1)} collective-permute-done((bf16[256,1024]{1,0:T(8,128)(2,1)S(1)}, bf16[256,1024]{1,0:T(8,128)(2,1)S(1)}, u32[]{:S(2)}, u32[]{:S(2)}) %collective-permute-start.59) | collective-permute-done | bytes 524320 | tf_op jit(solution)/shard_map/ppermute | solution.py:51
  298.3 3.5 collective-permute-done.62
  301.9 3.7 collective-permute-done.61.other
  316.5 6.8 %collective-permute-done.65.refs_3_ = bf16[96,1024]{1,0:T(8,128)(2,1)} collective-permute-done((bf16[96,1024]{1,0:T(8,128)(2,1)}, bf16[96,1024]{1,0:T(8,128)(2,1)}, u32[]{:S(2)}, u32[]{:S(2)}) %collective-permute-start.65) | collective-permute-done | bytes 196640 | tf_op jit(solution)/shard_map/ppermute | solution.py:51
  331.8 7.2 %collective-permute-done.66 = bf16[144,1024]{1,0:T(8,128)(2,1)S(1)} collective-permute-done((bf16[144,1024]{1,0:T(8,128)(2,1)S(1)}, bf16[144,1024]{1,0:T(8,128)(2,1)S(1)}, u32[]{:S(2)}, u32[]{:S(2)}) %collective-permute-start.66) | collective-permute-done | bytes 294944 | tf_op jit(solution)/shard_map/ppermute | solution.py:51
  343.3 7.4 %collective-permute-done.108 = bf16[2,12,8,768]{3,2,1,0:T(8,128)(2,1)S(1)} collective-permute-done((bf16[2,12,8,768]{3,2,1,0:T(8,128)(2,1)S(1)}, bf16[2,12,8,768]{3,2,1,0:T(8,128)(2,1)S(1)}, u32[]{:S(2)}, u32[]{:S(2)}) %collective-permute-start.108) | collective-permute-done | bytes 294944 | tf_op jit(solution)/shard_map/ppermute | solution.py:44
  351.2 7.7 %shard_map.372 = (bf16[256,768]{1,0:T(8,128)(2,1)S(1)}, bf16[576,768]{1,0:T(8,128)(2,1)S(1)}, f32[384,1024]{1,0:T(8,128)S(1)}, bf16[384,1024]{1,0:T(8,128)(2,1)S(1)}) custom-call(bf16[384,1024]{1,0:T(8,128)(2,1)S(1)} %constant_dynamic-update-slice_fusion.13.near.out_near, bf16[384,1024]{1,0:T(8,128)(2,1)S(1)} %collective-permute-done.67.far.out_far, ...), custom_call_target="tpu_custom_call" | custom-call | flops 1811939328 | bytes 10160128 | tf_op jit(solution)/shard_map/pallas_call | solution.py:400
  363.4 10.5 %collective-permute-done.94 = bf16[1024,256]{1,0:T(8,128)(2,1)S(1)} collective-permute-done((bf16[1024,256]{1,0:T(8,128)(2,1)S(1)}, bf16[1024,256]{1,0:T(8,128)(2,1)S(1)}, u32[]{:S(2)}, u32[]{:S(2)}) %collective-permute-start.94) | collective-permute-done | bytes 524320 | tf_op jit(solution)/shard_map/ppermute | solution.py:51
  374.2 9.2 %collective-permute-done.93 = bf16[256,1024]{1,0:T(8,128)(2,1)S(1)} collective-permute-done((bf16[256,1024]{1,0:T(8,128)(2,1)S(1)}, bf16[256,1024]{1,0:T(8,128)(2,1)S(1)}, u32[]{:S(2)}, u32[]{:S(2)}) %collective-permute-start.93) | collective-permute-done | bytes 524320 | tf_op jit(solution)/shard_map/ppermute | solution.py:51
  386.0 2.2 shard_map.381
  391.8 10.4 %collective-permute-done.69.refs_3_ = bf16[240,1024]{1,0:T(8,128)(2,1)S(1)} collective-permute-done((bf16[240,1024]{1,0:T(8,128)(2,1)S(1)}, bf16[240,1024]{1,0:T(8,128)(2,1)S(1)}, u32[]{:S(2)}, u32[]{:S(2)}) %collective-permute-start.69) | collective-permute-done | bytes 491552 | tf_op jit(solution)/shard_map/ppermute | solution.py:51
  411.4 2.1 collective-permute-start.72
  415.7 7.5 %collective-permute-done.88 = bf16[2,31,8,768]{3,2,1,0:T(8,128)(2,1)S(1)} collective-permute-done((bf16[2,31,8,768]{3,2,1,0:T(8,128)(2,1)S(1)}, bf16[2,31,8,768]{3,2,1,0:T(8,128)(2,1)S(1)}, u32[]{:S(2)}, u32[]{:S(2)}) %collective-permute-start.88) | collective-permute-done | bytes 761888 | tf_op jit(solution)/shard_map/ppermute | solution.py:44
  429.3 3.8 collective-permute-done.101
  435.7 11.8 %collective-permute-done.73 = bf16[144,1024]{1,0:T(8,128)(2,1)S(1)} collective-permute-done((bf16[144,1024]{1,0:T(8,128)(2,1)S(1)}, bf16[144,1024]{1,0:T(8,128)(2,1)S(1)}, u32[]{:S(2)}, u32[]{:S(2)}) %collective-permute-start.73) | collective-permute-done | bytes 294944 | tf_op jit(solution)/shard_map/ppermute | solution.py:51
  451.8 9.3 %shard_map.378 = (bf16[256,768]{1,0:T(8,128)(2,1)S(1)}, bf16[576,768]{1,0:T(8,128)(2,1)S(1)}, f32[384,1024]{1,0:T(8,128)S(1)}, bf16[384,1024]{1,0:T(8,128)(2,1)S(1)}) custom-call(bf16[384,1024]{1,0:T(8,128)(2,1)S(1)} %constant_dynamic-update-slice_fusion.15.near.out_near, bf16[384,1024]{1,0:T(8,128)(2,1)S(1)} %collective-permute-done.74.far.out_far, ...), custom_call_target="tpu_custom_call" | custom-call | flops 1811939328 | bytes 10160128 | tf_op jit(solution)/shard_map/pallas_call | solution.py:400
  462.2 2.3 collective-permute-done.118
  466.3 9.4 %collective-permute-done.117 = bf16[256,1024]{1,0:T(8,128)(2,1)S(1)} collective-permute-done((bf16[256,1024]{1,0:T(8,128)(2,1)S(1)}, bf16[256,1024]{1,0:T(8,128)(2,1)S(1)}, u32[]{:S(2)}, u32[]{:S(2)}) %collective-permute-start.117) | collective-permute-done | bytes 524320 | tf_op jit(solution)/shard_map/ppermute | solution.py:51
  481.0 2.1 collective-permute-start.99
  483.2 10.1 %collective-permute-done.99 = bf16[12,8,1024]{2,1,0:T(8,128)(2,1)S(1)} collective-permute-done((bf16[12,8,1024]{2,1,0:T(8,128)(2,1)S(1)}, bf16[12,8,1024]{2,1,0:T(8,128)(2,1)S(1)}, u32[]{:S(2)}, u32[]{:S(2)}) %collective-permute-start.99) | collective-permute-done | bytes 196640 | tf_op jit(solution)/shard_map/ppermute | solution.py:59
  493.4 2.2 shard_map.380
  503.4 3.3 collective-permute-done.130
  511.5 2.1 collective-permute-start.126
  514.4 3.6 collective-permute-done.132
  518.0 3.8 collective-permute-start.105
  525.1 8.0 %collective-permute-done.105 = bf16[24,8,768]{2,1,0:T(8,128)(2,1)S(1)} collective-permute-done((bf16[24,8,768]{2,1,0:T(8,128)(2,1)S(1)}, bf16[24,8,768]{2,1,0:T(8,128)(2,1)S(1)}, u32[]{:S(2)}, u32[]{:S(2)}) %collective-permute-start.105) | collective-permute-done | bytes 294944 | tf_op jit(solution)/shard_map/ppermute | solution.py:59
  534.5 3.7 collective-permute-done.133
  545.2 4.9 collective-permute-done.123
  563.8 2.8 collective-permute-start.116
  596.1 10.7 %collective-permute-done.78 = bf16[2,40,8,768]{3,2,1,0:T(8,128)(2,1)} collective-permute-done((bf16[2,40,8,768]{3,2,1,0:T(8,128)(2,1)}, bf16[2,40,8,768]{3,2,1,0:T(8,128)(2,1)}, u32[]{:S(2)}, u32[]{:S(2)}) %collective-permute-start.78) | collective-permute-done | bytes 983072 | tf_op jit(solution)/shard_map/ppermute | solution.py:41
  606.8 3.0 collective-permute-done.80
  615.0 20.3 %collective-permute-done.81 = bf16[40,8,768]{2,1,0:T(8,128)(2,1)S(1)} collective-permute-done((bf16[40,8,768]{2,1,0:T(8,128)(2,1)S(1)}, bf16[40,8,768]{2,1,0:T(8,128)(2,1)S(1)}, u32[]{:S(2)}, u32[]{:S(2)}) %collective-permute-start.81) | collective-permute-done | bytes 491552 | tf_op jit(solution)/shard_map/ppermute | solution.py:59
  636.5 4.5 collective-permute-done.82
  (950 shorter events, 230.7 us)
Async XLA Ops:
  5.9 54.7 %collective-permute-start.9 = (bf16[2,168,768]{2,1,0:T(8,128)(2,1)}, bf16[2,168,768]{2,1,0:T(8,128)(2,1)S(1)}, u32[]{:S(2)}, u32[]{:S(2)}) collective-permute-start(bf16[2,168,768]{2,1,0:T(8,128)(2,1)} %get-tuple-element.448), channel_id=1, source_target_pairs={{0,8},{8,0},{16,24},{24,16},{1,9},{9,1},{17,25},{25,17},{2,10},{10... | collective-permute-start | bytes 1548296 | tf_op jit(solution)/shard_map/ppermute | solution.py:51
  9.8 34.3 %collective-permute-start.8 = (bf16[96,1024]{1,0:T(8,128)(2,1)}, bf16[96,1024]{1,0:T(8,128)(2,1)S(1)}, u32[]{:S(2)}, u32[]{:S(2)}) collective-permute-start(bf16[96,1024]{1,0:T(8,128)(2,1)} %pad_maximum_fusion.48), channel_id=1, source_target_pairs={{0,0},{1,1},{2,16},{3,17},{4,4},{5,5},{6,20},{7,21},{8,8},{9,9},{1... | collective-permute-start | bytes 589832 | tf_op jit(solution)/shard_map/ppermute | solution.py:70
  12.1 43.0 %collective-permute-start.24 = (bf16[216,768]{1,0:T(8,128)(2,1)}, bf16[216,768]{1,0:T(8,128)(2,1)}, u32[]{:S(2)}, u32[]{:S(2)}) collective-permute-start(bf16[216,768]{1,0:T(8,128)(2,1)} %pad_maximum_fusion.27), channel_id=1, source_target_pairs={{0,0},{1,1},{2,16},{3,17},{4,4},{5,5},{6,20},{7,21},{8,8},{9,9},{1... | collective-permute-start | bytes 995336 | tf_op jit(solution)/shard_map/ppermute | solution.py:70
  33.0 24.1 %collective-permute-start.4 = (bf16[96,768]{1,0:T(8,128)(2,1)}, bf16[96,768]{1,0:T(8,128)(2,1)S(1)}, u32[]{:S(2)}, u32[]{:S(2)}) collective-permute-start(bf16[96,768]{1,0:T(8,128)(2,1)} %fusion.51), channel_id=1, source_target_pairs={{0,0},{1,1},{2,16},{3,17},{4,4},{5,5},{6,20},{7,21},{8,8},{9,9},{1... | collective-permute-start | bytes 442376 | tf_op jit(solution)/shard_map/ppermute | solution.py:70
  43.4 16.9 %collective-permute-start = (bf16[192,1024]{1,0:T(8,128)(2,1)S(1)}, bf16[192,1024]{1,0:T(8,128)(2,1)S(1)}, u32[]{:S(2)}, u32[]{:S(2)}) collective-permute-start(bf16[192,1024]{1,0:T(8,128)(2,1)S(1)} %maximum_maximum_fusion), channel_id=1, source_target_pairs={{0,8},{8,0},{16,24},{24,16},{1,9},{9,1},{17,25},{25,17},{2,10},{10... | collective-permute-start | bytes 1179656 | tf_op jit(solution)/shard_map/ppermute | solution.py:51
  57.1 25.4 %collective-permute-start.5 = (bf16[40,8,768]{2,1,0:T(8,128)(2,1)S(1)}, bf16[40,8,768]{2,1,0:T(8,128)(2,1)S(1)}, u32[]{:S(2)}, u32[]{:S(2)}) collective-permute-start(bf16[40,8,768]{2,1,0:T(8,128)(2,1)S(1)} %constant_dynamic-update-slice_fusion.2), channel_id=1, source_target_pairs={{0,16},{8,24},{16,0},{24,8},{1,17},{9,25},{17,1},{25,9},{2,18},{10... | collective-permute-start | bytes 1474568 | tf_op jit(solution)/shard_map/ppermute | solution.py:59
  60.4 66.6 %collective-permute-start.1 = (bf16[384,1024]{1,0:T(8,128)(2,1)S(1)}, bf16[384,1024]{1,0:T(8,128)(2,1)S(1)}, u32[]{:S(2)}, u32[]{:S(2)}) collective-permute-start(bf16[384,1024]{1,0:T(8,128)(2,1)S(1)} %pad_maximum_fusion.1.near.values), channel_id=1, source_target_pairs={{0,2},{2,0},{1,3},{3,1},{4,6},{6,4},{5,7},{7,5},{8,10},{10,8},{9,1... | collective-permute-start | bytes 2359304 | tf_op jit(solution)/shard_map/ppermute | solution.py:38
  62.6 23.4 %collective-permute-start.10 = (bf16[2,168,768]{2,1,0:T(8,128)(2,1)S(1)}, bf16[2,168,768]{2,1,0:T(8,128)(2,1)S(1)}, u32[]{:S(2)}, u32[]{:S(2)}) collective-permute-start(bf16[2,168,768]{2,1,0:T(8,128)(2,1)S(1)} %get-tuple-element.446), channel_id=1, source_target_pairs={{0,2},{2,0},{1,3},{3,1},{4,6},{6,4},{5,7},{7,5},{8,10},{10,8},{9,1... | collective-permute-start | bytes 1548296 | tf_op jit(solution)/shard_map/ppermute | solution.py:38
  82.7 23.5 %collective-permute-start.6 = (bf16[2,40,8,768]{3,2,1,0:T(8,128)(2,1)S(1)}, bf16[2,40,8,768]{3,2,1,0:T(8,128)(2,1)S(1)}, u32[]{:S(2)}, u32[]{:S(2)}) collective-permute-start(bf16[2,40,8,768]{3,2,1,0:T(8,128)(2,1)S(1)} %pad_maximum_fusion), channel_id=1, source_target_pairs={{0,1},{1,0},{2,3},{3,2},{4,5},{5,4},{6,7},{7,6},{8,9},{9,8},{10,11... | collective-permute-start | bytes 2949128 | tf_op jit(solution)/shard_map/ppermute | solution.py:41
  84.3 23.2 %collective-permute-start.7 = (bf16[2,40,8,768]{3,2,1,0:T(8,128)(2,1)S(1)}, bf16[2,40,8,768]{3,2,1,0:T(8,128)(2,1)S(1)}, u32[]{:S(2)}, u32[]{:S(2)}) collective-permute-start(bf16[2,40,8,768]{3,2,1,0:T(8,128)(2,1)S(1)} %pad_maximum_fusion), channel_id=1, source_target_pairs={{0,4},{4,0},{1,5},{5,1},{2,6},{6,2},{3,7},{7,3},{8,12},{12,8},{9,1... | collective-permute-start | bytes 2949128 | tf_op jit(solution)/shard_map/ppermute | solution.py:44
  132.0 38.2 %collective-permute-start.15 = (bf16[384,1024]{1,0:T(8,128)(2,1)S(1)}, bf16[384,1024]{1,0:T(8,128)(2,1)S(1)}, u32[]{:S(2)}, u32[]{:S(2)}) collective-permute-start(bf16[384,1024]{1,0:T(8,128)(2,1)S(1)} %get-tuple-element.231), channel_id=1, source_target_pairs={{0,2},{2,0},{1,3},{3,1},{4,6},{6,4},{5,7},{7,5},{8,10},{10,8},{9,1... | collective-permute-start | bytes 2359304 | tf_op jit(solution)/shard_map/ppermute | solution.py:38
  135.3 35.1 %collective-permute-start.29 = (bf16[2,24,8,768]{3,2,1,0:T(8,128)(2,1)S(1)}, bf16[2,24,8,768]{3,2,1,0:T(8,128)(2,1)S(1)}, u32[]{:S(2)}, u32[]{:S(2)}) collective-permute-start(bf16[2,24,8,768]{3,2,1,0:T(8,128)(2,1)S(1)} %pad_maximum_fusion.3), channel_id=1, source_target_pairs={{0,4},{4,0},{1,5},{5,1},{2,6},{6,2},{3,7},{7,3},{8,12},{12,8},{9,1... | collective-permute-start | bytes 1769480 | tf_op jit(solution)/shard_map/ppermute | solution.py:44
  136.8 33.7 %collective-permute-start.28 = (bf16[2,24,8,768]{3,2,1,0:T(8,128)(2,1)S(1)}, bf16[2,24,8,768]{3,2,1,0:T(8,128)(2,1)S(1)}, u32[]{:S(2)}, u32[]{:S(2)}) collective-permute-start(bf16[2,24,8,768]{3,2,1,0:T(8,128)(2,1)S(1)} %pad_maximum_fusion.3), channel_id=1, source_target_pairs={{0,1},{1,0},{2,3},{3,2},{4,5},{5,4},{6,7},{7,6},{8,9},{9,8},{10,11... | collective-permute-start | bytes 1769480 | tf_op jit(solution)/shard_map/ppermute | solution.py:41
  138.1 16.1 %collective-permute-start.31 = (bf16[2,6,8,1024]{3,2,1,0:T(8,128)(2,1)S(1)}, bf16[2,6,8,1024]{3,2,1,0:T(8,128)(2,1)S(1)}, u32[]{:S(2)}, u32[]{:S(2)}) collective-permute-start(bf16[2,6,8,1024]{3,2,1,0:T(8,128)(2,1)S(1)} %slice.1123), channel_id=1, source_target_pairs={{0,4},{4,0},{1,5},{5,1},{2,6},{6,2},{3,7},{7,3},{8,12},{12,8},{9,1... | collective-permute-start | bytes 589832 | tf_op jit(solution)/shard_map/ppermute | solution.py:44
  138.7 16.5 %collective-permute-start.32 = (bf16[2,6,8,1024]{3,2,1,0:T(8,128)(2,1)S(1)}, bf16[2,6,8,1024]{3,2,1,0:T(8,128)(2,1)S(1)}, u32[]{:S(2)}, u32[]{:S(2)}) collective-permute-start(bf16[2,6,8,1024]{3,2,1,0:T(8,128)(2,1)S(1)} %slice.1124), channel_id=1, source_target_pairs={{0,1},{1,0},{2,3},{3,2},{4,5},{5,4},{6,7},{7,6},{8,9},{9,8},{10,11... | collective-permute-start | bytes 589832 | tf_op jit(solution)/shard_map/ppermute | solution.py:41
  154.2 15.8 %collective-permute-start.30 = (bf16[31,8,768]{2,1,0:T(8,128)(2,1)S(1)}, bf16[31,8,768]{2,1,0:T(8,128)(2,1)S(1)}, u32[]{:S(2)}, u32[]{:S(2)}) collective-permute-start(bf16[31,8,768]{2,1,0:T(8,128)(2,1)S(1)} %pad_maximum_fusion.24), channel_id=1, source_target_pairs={{0,16},{8,24},{16,0},{24,8},{1,17},{9,25},{17,1},{25,9},{2,18},{10... | collective-permute-start | bytes 1142792 | tf_op jit(solution)/shard_map/ppermute | solution.py:59
  155.4 57.2 %collective-permute-start.36 = (bf16[256,1024]{1,0:T(8,128)(2,1)S(1)}, bf16[256,1024]{1,0:T(8,128)(2,1)S(1)}, u32[]{:S(2)}, u32[]{:S(2)}) collective-permute-start(bf16[256,1024]{1,0:T(8,128)(2,1)S(1)} %bitcast.1113), channel_id=1, source_target_pairs={{0,8},{8,0},{16,24},{24,16},{1,9},{9,1},{17,25},{25,17},{2,10},{10... | collective-permute-start | bytes 1572872 | tf_op jit(solution)/shard_map/ppermute | solution.py:51
  170.3 27.4 %collective-permute-start.16 = (bf16[240,1024]{1,0:T(8,128)(2,1)S(1)}, bf16[240,1024]{1,0:T(8,128)(2,1)S(1)}, u32[]{:S(2)}, u32[]{:S(2)}) collective-permute-start(bf16[240,1024]{1,0:T(8,128)(2,1)S(1)} %shard_map.357), channel_id=1, source_target_pairs={{0,8},{8,0},{16,24},{24,16},{1,9},{9,1},{17,25},{25,17},{2,10},{10... | collective-permute-start | bytes 1474568 | tf_op jit(solution)/shard_map/ppermute | solution.py:51
  170.5 27.9 %collective-permute-start.42 = (bf16[2,31,8,768]{3,2,1,0:T(8,128)(2,1)S(1)}, bf16[2,31,8,768]{3,2,1,0:T(8,128)(2,1)S(1)}, u32[]{:S(2)}, u32[]{:S(2)}) collective-permute-start(bf16[2,31,8,768]{3,2,1,0:T(8,128)(2,1)S(1)} %pad_maximum_fusion.2), channel_id=1, source_target_pairs={{0,4},{4,0},{1,5},{5,1},{2,6},{6,2},{3,7},{7,3},{8,12},{12,8},{9,1... | collective-permute-start | bytes 2285576 | tf_op jit(solution)/shard_map/ppermute | solution.py:44
  170.7 15.2 %collective-permute-start.43 = (bf16[8,8,1024]{2,1,0:T(8,128)(2,1)S(1)}, bf16[8,8,1024]{2,1,0:T(8,128)(2,1)S(1)}, u32[]{:S(2)}, u32[]{:S(2)}) collective-permute-start(bf16[8,8,1024]{2,1,0:T(8,128)(2,1)S(1)} %maximum_maximum_fusion.2), channel_id=1, source_target_pairs={{0,16},{8,24},{16,0},{24,8},{1,17},{9,25},{17,1},{25,9},{2,18},{10... | collective-permute-start | bytes 393224 | tf_op jit(solution)/shard_map/ppermute | solution.py:59
  173.9 21.9 %collective-permute-start.33 = (bf16[2,12,8,768]{3,2,1,0:T(8,128)(2,1)S(1)}, bf16[2,12,8,768]{3,2,1,0:T(8,128)(2,1)S(1)}, u32[]{:S(2)}, u32[]{:S(2)}) collective-permute-start(bf16[2,12,8,768]{3,2,1,0:T(8,128)(2,1)S(1)} %get-tuple-element.245), channel_id=1, source_target_pairs={{0,4},{4,0},{1,5},{5,1},{2,6},{6,2},{3,7},{7,3},{8,12},{12,8},{9,1... | collective-permute-start | bytes 884744 | tf_op jit(solution)/shard_map/ppermute | solution.py:44
  193.2 17.0 %collective-permute-start.41 = (bf16[2,31,8,768]{3,2,1,0:T(8,128)(2,1)S(1)}, bf16[2,31,8,768]{3,2,1,0:T(8,128)(2,1)S(1)}, u32[]{:S(2)}, u32[]{:S(2)}) collective-permute-start(bf16[2,31,8,768]{3,2,1,0:T(8,128)(2,1)S(1)} %pad_maximum_fusion.2), channel_id=1, source_target_pairs={{0,1},{1,0},{2,3},{3,2},{4,5},{5,4},{6,7},{7,6},{8,9},{9,8},{10,11... | collective-permute-start | bytes 2285576 | tf_op jit(solution)/shard_map/ppermute | solution.py:41
  195.8 20.6 %collective-permute-start.35 = (bf16[1024,256]{1,0:T(8,128)(2,1)S(1)}, bf16[1024,256]{1,0:T(8,128)(2,1)S(1)}, u32[]{:S(2)}, u32[]{:S(2)}) collective-permute-start(bf16[1024,256]{1,0:T(8,128)(2,1)S(1)} %bitcast.1116), channel_id=1, source_target_pairs={{0,8},{8,0},{16,24},{24,16},{1,9},{9,1},{17,25},{25,17},{2,10},{10... | collective-permute-start | bytes 1572872 | tf_op jit(solution)/shard_map/ppermute | solution.py:51
  198.3 18.9 %collective-permute-start.22 = (bf16[240,1024]{1,0:T(8,128)(2,1)S(1)}, bf16[240,1024]{1,0:T(8,128)(2,1)S(1)}, u32[]{:S(2)}, u32[]{:S(2)}) collective-permute-start(bf16[240,1024]{1,0:T(8,128)(2,1)S(1)} %get-tuple-element.372.near), channel_id=1, source_target_pairs={{0,2},{2,0},{1,3},{3,1},{4,6},{6,4},{5,7},{7,5},{8,10},{10,8},{9,1... | collective-permute-start | bytes 1474568 | tf_op jit(solution)/shard_map/ppermute | solution.py:38
  226.0 15.7 %collective-permute-start.53 = (bf16[2,24,8,768]{3,2,1,0:T(8,128)(2,1)S(1)}, bf16[2,24,8,768]{3,2,1,0:T(8,128)(2,1)S(1)}, u32[]{:S(2)}, u32[]{:S(2)}) collective-permute-start(bf16[2,24,8,768]{3,2,1,0:T(8,128)(2,1)S(1)} %pad_maximum_fusion.4), channel_id=1, source_target_pairs={{0,4},{4,0},{1,5},{5,1},{2,6},{6,2},{3,7},{7,3},{8,12},{12,8},{9,1... | collective-permute-start | bytes 1769480 | tf_op jit(solution)/shard_map/ppermute | solution.py:44
  227.8 15.4 %collective-permute-start.52 = (bf16[2,24,8,768]{3,2,1,0:T(8,128)(2,1)S(1)}, bf16[2,24,8,768]{3,2,1,0:T(8,128)(2,1)S(1)}, u32[]{:S(2)}, u32[]{:S(2)}) collective-permute-start(bf16[2,24,8,768]{3,2,1,0:T(8,128)(2,1)S(1)} %pad_maximum_fusion.4), channel_id=1, source_target_pairs={{0,1},{1,0},{2,3},{3,2},{4,5},{5,4},{6,7},{7,6},{8,9},{9,8},{10,11... | collective-permute-start | bytes 1769480 | tf_op jit(solution)/shard_map/ppermute | solution.py:41
  228.2 16.4 %collective-permute-start.55 = (bf16[2,4,8,1024]{3,2,1,0:T(8,128)(2,1)S(1)}, bf16[2,4,8,1024]{3,2,1,0:T(8,128)(2,1)S(1)}, u32[]{:S(2)}, u32[]{:S(2)}) collective-permute-start(bf16[2,4,8,1024]{3,2,1,0:T(8,128)(2,1)S(1)} %get-tuple-element.263), channel_id=1, source_target_pairs={{0,1},{1,0},{2,3},{3,2},{4,5},{5,4},{6,7},{7,6},{8,9},{9,8},{10,11... | collective-permute-start | bytes 393224 | tf_op jit(solution)/shard_map/ppermute | solution.py:41
  259.5 24.4 %collective-permute-start.58 = (bf16[1024,256]{1,0:T(8,128)(2,1)S(1)}, bf16[1024,256]{1,0:T(8,128)(2,1)S(1)}, u32[]{:S(2)}, u32[]{:S(2)}) collective-permute-start(bf16[1024,256]{1,0:T(8,128)(2,1)S(1)} %bitcast.1119), channel_id=1, source_target_pairs={{0,8},{8,0},{16,24},{24,16},{1,9},{9,1},{17,25},{25,17},{2,10},{10... | collective-permute-start | bytes 1572872 | tf_op jit(solution)/shard_map/ppermute | solution.py:51
  261.5 32.8 %collective-permute-start.59 = (bf16[256,1024]{1,0:T(8,128)(2,1)S(1)}, bf16[256,1024]{1,0:T(8,128)(2,1)S(1)}, u32[]{:S(2)}, u32[]{:S(2)}) collective-permute-start(bf16[256,1024]{1,0:T(8,128)(2,1)S(1)} %bitcast.1122), channel_id=1, source_target_pairs={{0,8},{8,0},{16,24},{24,16},{1,9},{9,1},{17,25},{25,17},{2,10},{10... | collective-permute-start | bytes 1572872 | tf_op jit(solution)/shard_map/ppermute | solution.py:51
  273.2 21.1 %collective-permute-start.48 = (bf16[240,1024]{1,0:T(8,128)(2,1)S(1)}, bf16[240,1024]{1,0:T(8,128)(2,1)S(1)}, u32[]{:S(2)}, u32[]{:S(2)}) collective-permute-start(bf16[240,1024]{1,0:T(8,128)(2,1)S(1)} %get-tuple-element.347.near), channel_id=1, source_target_pairs={{0,2},{2,0},{1,3},{3,1},{4,6},{6,4},{5,7},{7,5},{8,10},{10,8},{9,1... | collective-permute-start | bytes 1474568 | tf_op jit(solution)/shard_map/ppermute | solution.py:38
  358.9 14.9 %collective-permute-start.94 = (bf16[1024,256]{1,0:T(8,128)(2,1)S(1)}, bf16[1024,256]{1,0:T(8,128)(2,1)S(1)}, u32[]{:S(2)}, u32[]{:S(2)}) collective-permute-start(bf16[1024,256]{1,0:T(8,128)(2,1)S(1)} %get-tuple-element.360), channel_id=1, source_target_pairs={{0,8},{8,0},{16,24},{24,16},{1,9},{9,1},{17,25},{25,17},{2,10},{10... | collective-permute-start | bytes 1572872 | tf_op jit(solution)/shard_map/ppermute | solution.py:51
  359.4 25.1 %collective-permute-start.111 = (bf16[2,24,8,768]{3,2,1,0:T(8,128)(2,1)S(1)}, bf16[2,24,8,768]{3,2,1,0:T(8,128)(2,1)S(1)}, u32[]{:S(2)}, u32[]{:S(2)}) collective-permute-start(bf16[2,24,8,768]{3,2,1,0:T(8,128)(2,1)S(1)} %pad_maximum_fusion.8), channel_id=1, source_target_pairs={{0,4},{4,0},{1,5},{5,1},{2,6},{6,2},{3,7},{7,3},{8,12},{12,8},{9,1... | collective-permute-start | bytes 1769480 | tf_op jit(solution)/shard_map/ppermute | solution.py:44
  361.1 23.4 %collective-permute-start.110 = (bf16[2,24,8,768]{3,2,1,0:T(8,128)(2,1)S(1)}, bf16[2,24,8,768]{3,2,1,0:T(8,128)(2,1)S(1)}, u32[]{:S(2)}, u32[]{:S(2)}) collective-permute-start(bf16[2,24,8,768]{3,2,1,0:T(8,128)(2,1)S(1)} %pad_maximum_fusion.7), channel_id=1, source_target_pairs={{0,1},{1,0},{2,3},{3,2},{4,5},{5,4},{6,7},{7,6},{8,9},{9,8},{10,11... | collective-permute-start | bytes 1769480 | tf_op jit(solution)/shard_map/ppermute | solution.py:41
  361.7 22.0 %collective-permute-start.68 = (bf16[384,1024]{1,0:T(8,128)(2,1)S(1)}, bf16[384,1024]{1,0:T(8,128)(2,1)S(1)}, u32[]{:S(2)}, u32[]{:S(2)}) collective-permute-start(bf16[384,1024]{1,0:T(8,128)(2,1)S(1)} %get-tuple-element.286), channel_id=1, source_target_pairs={{0,2},{2,0},{1,3},{3,1},{4,6},{6,4},{5,7},{7,5},{8,10},{10,8},{9,1... | collective-permute-start | bytes 2359304 | tf_op jit(solution)/shard_map/ppermute | solution.py:38
  361.7 21.8 %collective-permute-start.93 = (bf16[256,1024]{1,0:T(8,128)(2,1)S(1)}, bf16[256,1024]{1,0:T(8,128)(2,1)S(1)}, u32[]{:S(2)}, u32[]{:S(2)}) collective-permute-start(bf16[256,1024]{1,0:T(8,128)(2,1)S(1)} %get-tuple-element.358), channel_id=1, source_target_pairs={{0,8},{8,0},{16,24},{24,16},{1,9},{9,1},{17,25},{25,17},{2,10},{10... | collective-permute-start | bytes 1572872 | tf_op jit(solution)/shard_map/ppermute | solution.py:51
  384.2 18.0 %collective-permute-start.69 = (bf16[240,1024]{1,0:T(8,128)(2,1)S(1)}, bf16[240,1024]{1,0:T(8,128)(2,1)S(1)}, u32[]{:S(2)}, u32[]{:S(2)}) collective-permute-start(bf16[240,1024]{1,0:T(8,128)(2,1)S(1)} %shard_map.373), channel_id=1, source_target_pairs={{0,8},{8,0},{16,24},{24,16},{1,9},{9,1},{17,25},{25,17},{2,10},{10... | collective-permute-start | bytes 1474568 | tf_op jit(solution)/shard_map/ppermute | solution.py:51
  384.8 18.5 %collective-permute-start.112 = (bf16[24,8,768]{2,1,0:T(8,128)(2,1)S(1)}, bf16[24,8,768]{2,1,0:T(8,128)(2,1)S(1)}, u32[]{:S(2)}, u32[]{:S(2)}) collective-permute-start(bf16[24,8,768]{2,1,0:T(8,128)(2,1)S(1)} %get-tuple-element.469), channel_id=1, source_target_pairs={{0,16},{8,24},{16,0},{24,8},{1,17},{9,25},{17,1},{25,9},{2,18},{10... | collective-permute-start | bytes 884744 | tf_op jit(solution)/shard_map/ppermute | solution.py:59
  388.5 14.9 %collective-permute-start.86 = (bf16[2,16,8,768]{3,2,1,0:T(8,128)(2,1)S(1)}, bf16[2,16,8,768]{3,2,1,0:T(8,128)(2,1)S(1)}, u32[]{:S(2)}, u32[]{:S(2)}) collective-permute-start(bf16[2,16,8,768]{3,2,1,0:T(8,128)(2,1)S(1)} %pad_maximum_fusion.20), channel_id=1, source_target_pairs={{0,1},{1,0},{2,3},{3,2},{4,5},{5,4},{6,7},{7,6},{8,9},{9,8},{10,11... | collective-permute-start | bytes 1179656 | tf_op jit(solution)/shard_map/ppermute | solution.py:41
  390.9 19.8 %collective-permute-start.95 = (bf16[2,6,8,1024]{3,2,1,0:T(8,128)(2,1)S(1)}, bf16[2,6,8,1024]{3,2,1,0:T(8,128)(2,1)S(1)}, u32[]{:S(2)}, u32[]{:S(2)}) collective-permute-start(bf16[2,6,8,1024]{3,2,1,0:T(8,128)(2,1)S(1)} %get-tuple-element.625), channel_id=1, source_target_pairs={{0,4},{4,0},{1,5},{5,1},{2,6},{6,2},{3,7},{7,3},{8,12},{12,8},{9,1... | collective-permute-start | bytes 589832 | tf_op jit(solution)/shard_map/ppermute | solution.py:44
  403.7 19.5 %collective-permute-start.88 = (bf16[2,31,8,768]{3,2,1,0:T(8,128)(2,1)S(1)}, bf16[2,31,8,768]{3,2,1,0:T(8,128)(2,1)S(1)}, u32[]{:S(2)}, u32[]{:S(2)}) collective-permute-start(bf16[2,31,8,768]{3,2,1,0:T(8,128)(2,1)S(1)} %fusion.20), channel_id=1, source_target_pairs={{0,4},{4,0},{1,5},{5,1},{2,6},{6,2},{3,7},{7,3},{8,12},{12,8},{9,1... | collective-permute-start | bytes 2285576 | tf_op jit(solution)/shard_map/ppermute | solution.py:44
  405.4 19.3 %collective-permute-start.87 = (bf16[2,31,8,768]{3,2,1,0:T(8,128)(2,1)S(1)}, bf16[2,31,8,768]{3,2,1,0:T(8,128)(2,1)S(1)}, u32[]{:S(2)}, u32[]{:S(2)}) collective-permute-start(bf16[2,31,8,768]{3,2,1,0:T(8,128)(2,1)S(1)} %fusion.22), channel_id=1, source_target_pairs={{0,1},{1,0},{2,3},{3,2},{4,5},{5,4},{6,7},{7,6},{8,9},{9,8},{10,11... | collective-permute-start | bytes 2285576 | tf_op jit(solution)/shard_map/ppermute | solution.py:41
  410.7 16.1 %collective-permute-start.113 = (bf16[2,24,768]{2,1,0:T(8,128)(2,1)S(1)}, bf16[2,24,768]{2,1,0:T(8,128)(2,1)S(1)}, u32[]{:S(2)}, u32[]{:S(2)}) collective-permute-start(bf16[2,24,768]{2,1,0:T(8,128)(2,1)S(1)} %get-tuple-element.592), channel_id=1, source_target_pairs={{0,8},{8,0},{16,24},{24,16},{1,9},{9,1},{17,25},{25,17},{2,10},{10... | collective-permute-start | bytes 221192 | tf_op jit(solution)/shard_map/ppermute | solution.py:51
  410.7 16.7 %collective-permute-start.114 = (bf16[96,768]{1,0:T(8,128)(2,1)S(1)}, bf16[96,768]{1,0:T(8,128)(2,1)S(1)}, u32[]{:S(2)}, u32[]{:S(2)}) collective-permute-start(bf16[96,768]{1,0:T(8,128)(2,1)S(1)} %get-tuple-element.557), channel_id=1, source_target_pairs={{0,0},{1,1},{2,16},{3,17},{4,4},{5,5},{6,20},{7,21},{8,8},{9,9},{1... | collective-permute-start | bytes 442376 | tf_op jit(solution)/shard_map/ppermute | solution.py:70
  411.4 17.0 %collective-permute-start.72 = (bf16[96,1024]{1,0:T(8,128)(2,1)S(1)}, bf16[96,1024]{1,0:T(8,128)(2,1)S(1)}, u32[]{:S(2)}, u32[]{:S(2)}) collective-permute-start(bf16[96,1024]{1,0:T(8,128)(2,1)S(1)} %shard_map.376), channel_id=1, source_target_pairs={{0,8},{8,0},{16,24},{24,16},{1,9},{9,1},{17,25},{25,17},{2,10},{10... | collective-permute-start | bytes 589832 | tf_op jit(solution)/shard_map/ppermute | solution.py:51
  426.8 23.5 %collective-permute-start.98 = (bf16[2,12,8,1024]{3,2,1,0:T(8,128)(2,1)S(1)}, bf16[2,12,8,1024]{3,2,1,0:T(8,128)(2,1)S(1)}, u32[]{:S(2)}, u32[]{:S(2)}) collective-permute-start(bf16[2,12,8,1024]{3,2,1,0:T(8,128)(2,1)S(1)} %fusion.35), channel_id=1, source_target_pairs={{0,4},{4,0},{1,5},{5,1},{2,6},{6,2},{3,7},{7,3},{8,12},{12,8},{9,1... | collective-permute-start | bytes 1179656 | tf_op jit(solution)/shard_map/ppermute | solution.py:44
  427.4 22.9 %collective-permute-start.97 = (bf16[2,12,8,1024]{3,2,1,0:T(8,128)(2,1)S(1)}, bf16[2,12,8,1024]{3,2,1,0:T(8,128)(2,1)S(1)}, u32[]{:S(2)}, u32[]{:S(2)}) collective-permute-start(bf16[2,12,8,1024]{3,2,1,0:T(8,128)(2,1)S(1)} %fusion.30), channel_id=1, source_target_pairs={{0,1},{1,0},{2,3},{3,2},{4,5},{5,4},{6,7},{7,6},{8,9},{9,8},{10,11... | collective-permute-start | bytes 1179656 | tf_op jit(solution)/shard_map/ppermute | solution.py:41
  428.4 19.4 %collective-permute-start.89 = (bf16[31,8,768]{2,1,0:T(8,128)(2,1)S(1)}, bf16[31,8,768]{2,1,0:T(8,128)(2,1)S(1)}, u32[]{:S(2)}, u32[]{:S(2)}) collective-permute-start(bf16[31,8,768]{2,1,0:T(8,128)(2,1)S(1)} %get-tuple-element.463), channel_id=1, source_target_pairs={{0,16},{8,24},{16,0},{24,8},{1,17},{9,25},{17,1},{25,9},{2,18},{10... | collective-permute-start | bytes 1142792 | tf_op jit(solution)/shard_map/ppermute | solution.py:59
  434.8 61.0 %collective-permute-start.104 = (bf16[2,24,8,768]{3,2,1,0:T(8,128)(2,1)S(1)}, bf16[2,24,8,768]{3,2,1,0:T(8,128)(2,1)S(1)}, u32[]{:S(2)}, u32[]{:S(2)}) collective-permute-start(bf16[2,24,8,768]{3,2,1,0:T(8,128)(2,1)S(1)} %pad_maximum_fusion.6), channel_id=1, source_target_pairs={{0,4},{4,0},{1,5},{5,1},{2,6},{6,2},{3,7},{7,3},{8,12},{12,8},{9,1... | collective-permute-start | bytes 1769480 | tf_op jit(solution)/shard_map/ppermute | solution.py:44
  447.8 48.1 %collective-permute-start.103 = (bf16[2,24,8,768]{3,2,1,0:T(8,128)(2,1)S(1)}, bf16[2,24,8,768]{3,2,1,0:T(8,128)(2,1)S(1)}, u32[]{:S(2)}, u32[]{:S(2)}) collective-permute-start(bf16[2,24,8,768]{3,2,1,0:T(8,128)(2,1)S(1)} %pad_maximum_fusion.5), channel_id=1, source_target_pairs={{0,1},{1,0},{2,3},{3,2},{4,5},{5,4},{6,7},{7,6},{8,9},{9,8},{10,11... | collective-permute-start | bytes 1769480 | tf_op jit(solution)/shard_map/ppermute | solution.py:41
  461.2 16.4 %collective-permute-start.75 = (bf16[384,1024]{1,0:T(8,128)(2,1)S(1)}, bf16[384,1024]{1,0:T(8,128)(2,1)S(1)}, u32[]{:S(2)}, u32[]{:S(2)}) collective-permute-start(bf16[384,1024]{1,0:T(8,128)(2,1)S(1)} %get-tuple-element.302), channel_id=1, source_target_pairs={{0,2},{2,0},{1,3},{3,1},{4,6},{6,4},{5,7},{7,5},{8,10},{10,8},{9,1... | collective-permute-start | bytes 2359304 | tf_op jit(solution)/shard_map/ppermute | solution.py:38
  477.6 22.4 %collective-permute-start.90 = (bf16[2,56,768]{2,1,0:T(8,128)(2,1)S(1)}, bf16[2,56,768]{2,1,0:T(8,128)(2,1)S(1)}, u32[]{:S(2)}, u32[]{:S(2)}) collective-permute-start(bf16[2,56,768]{2,1,0:T(8,128)(2,1)S(1)} %get-tuple-element.543), channel_id=1, source_target_pairs={{0,8},{8,0},{16,24},{24,16},{1,9},{9,1},{17,25},{25,17},{2,10},{10... | collective-permute-start | bytes 516104 | tf_op jit(solution)/shard_map/ppermute | solution.py:51
  479.3 20.0 %collective-permute-start.91 = (bf16[24,768]{1,0:T(8,128)(2,1)S(1)}, bf16[24,768]{1,0:T(8,128)(2,1)S(1)}, u32[]{:S(2)}, u32[]{:S(2)}) collective-permute-start(bf16[24,768]{1,0:T(8,128)(2,1)S(1)} %slice_bitcast_fusion.64), channel_id=1, source_target_pairs={{0,0},{1,1},{2,16},{3,17},{4,4},{5,5},{6,20},{7,21},{8,8},{9,9},{1... | collective-permute-start | bytes 110600 | tf_op jit(solution)/shard_map/ppermute | solution.py:70
  493.3 99.5 %collective-permute-start.76 = (bf16[240,1024]{1,0:T(8,128)(2,1)}, bf16[240,1024]{1,0:T(8,128)(2,1)}, u32[]{:S(2)}, u32[]{:S(2)}) collective-permute-start(bf16[240,1024]{1,0:T(8,128)(2,1)} %shard_map.379), channel_id=1, source_target_pairs={{0,8},{8,0},{16,24},{24,16},{1,9},{9,1},{17,25},{25,17},{2,10},{10... | collective-permute-start | bytes 1474568 | tf_op jit(solution)/shard_map/ppermute | solution.py:51
  495.9 25.9 %collective-permute-start.121 = (bf16[2,8,8,1024]{3,2,1,0:T(8,128)(2,1)S(1)}, bf16[2,8,8,1024]{3,2,1,0:T(8,128)(2,1)S(1)}, u32[]{:S(2)}, u32[]{:S(2)}) collective-permute-start(bf16[2,8,8,1024]{3,2,1,0:T(8,128)(2,1)S(1)} %maximum_maximum_fusion.1), channel_id=1, source_target_pairs={{0,1},{1,0},{2,3},{3,2},{4,5},{5,4},{6,7},{7,6},{8,9},{9,8},{10,11... | collective-permute-start | bytes 786440 | tf_op jit(solution)/shard_map/ppermute | solution.py:41
  499.4 23.9 %collective-permute-start.122 = (bf16[2,8,8,1024]{3,2,1,0:T(8,128)(2,1)S(1)}, bf16[2,8,8,1024]{3,2,1,0:T(8,128)(2,1)S(1)}, u32[]{:S(2)}, u32[]{:S(2)}) collective-permute-start(bf16[2,8,8,1024]{3,2,1,0:T(8,128)(2,1)S(1)} %pad_maximum_fusion.31), channel_id=1, source_target_pairs={{0,4},{4,0},{1,5},{5,1},{2,6},{6,2},{3,7},{7,3},{8,12},{12,8},{9,1... | collective-permute-start | bytes 786440 | tf_op jit(solution)/shard_map/ppermute | solution.py:44
  511.5 47.2 %collective-permute-start.126 = (bf16[2,32,256]{2,1,0:T(8,128)(2,1)}, bf16[2,32,256]{2,1,0:T(8,128)(2,1)}, u32[]{:S(2)}, u32[]{:S(2)}) collective-permute-start(bf16[2,32,256]{2,1,0:T(8,128)(2,1)} %get-tuple-element.685), channel_id=1, source_target_pairs={{0,8},{8,0},{16,24},{24,16},{1,9},{9,1},{17,25},{25,17},{2,10},{10... | collective-permute-start | bytes 98312 | tf_op jit(solution)/shard_map/ppermute | solution.py:51
  518.0 15.1 %collective-permute-start.105 = (bf16[24,8,768]{2,1,0:T(8,128)(2,1)S(1)}, bf16[24,8,768]{2,1,0:T(8,128)(2,1)S(1)}, u32[]{:S(2)}, u32[]{:S(2)}) collective-permute-start(bf16[24,8,768]{2,1,0:T(8,128)(2,1)S(1)} %dynamic-slice_bitcast_fusion.19), channel_id=1, source_target_pairs={{0,16},{8,24},{16,0},{24,8},{1,17},{9,25},{17,1},{25,9},{2,18},{10... | collective-permute-start | bytes 884744 | tf_op jit(solution)/shard_map/ppermute | solution.py:59
  521.8 57.8 %collective-permute-start.77 = (bf16[2,20,8,768]{3,2,1,0:T(8,128)(2,1)}, bf16[2,20,8,768]{3,2,1,0:T(8,128)(2,1)}, u32[]{:S(2)}, u32[]{:S(2)}) collective-permute-start(bf16[2,20,8,768]{3,2,1,0:T(8,128)(2,1)} %get-tuple-element.519), channel_id=1, source_target_pairs={{0,4},{4,0},{1,5},{5,1},{2,6},{6,2},{3,7},{7,3},{8,12},{12,8},{9,1... | collective-permute-start | bytes 1474568 | tf_op jit(solution)/shard_map/ppermute | solution.py:44
  523.3 60.6 %collective-permute-start.79 = (bf16[2,20,8,768]{3,2,1,0:T(8,128)(2,1)}, bf16[2,20,8,768]{3,2,1,0:T(8,128)(2,1)}, u32[]{:S(2)}, u32[]{:S(2)}) collective-permute-start(bf16[2,20,8,768]{3,2,1,0:T(8,128)(2,1)} %get-tuple-element.520), channel_id=1, source_target_pairs={{0,1},{1,0},{2,3},{3,2},{4,5},{5,4},{6,7},{7,6},{8,9},{9,8},{10,11... | collective-permute-start | bytes 1474568 | tf_op jit(solution)/shard_map/ppermute | solution.py:41
  563.8 24.6 %collective-permute-start.116 = (bf16[96,768]{1,0:T(8,128)(2,1)}, bf16[96,768]{1,0:T(8,128)(2,1)}, u32[]{:S(2)}, u32[]{:S(2)}) collective-permute-start(bf16[96,768]{1,0:T(8,128)(2,1)} %get-tuple-element.555), channel_id=1, source_target_pairs={{0,0},{1,1},{2,16},{3,17},{4,4},{5,5},{6,20},{7,21},{8,8},{9,9},{1... | collective-permute-start | bytes 442376 | tf_op jit(solution)/shard_map/ppermute | solution.py:70
  569.9 20.4 %collective-permute-start.127 = (bf16[2,32,256]{2,0,1:T(2,128)(2,1)}, bf16[2,32,256]{2,0,1:T(2,128)(2,1)S(1)}, u32[]{:S(2)}, u32[]{:S(2)}) collective-permute-start(bf16[2,32,256]{2,0,1:T(2,128)(2,1)} %get-tuple-element.682), channel_id=1, source_target_pairs={{0,2},{2,0},{1,3},{3,1},{4,6},{6,4},{5,7},{7,5},{8,10},{10,8},{9,1... | collective-permute-start | bytes 98312 | tf_op jit(solution)/shard_map/ppermute | solution.py:38
  582.9 24.0 %collective-permute-start.78 = (bf16[2,40,8,768]{3,2,1,0:T(8,128)(2,1)}, bf16[2,40,8,768]{3,2,1,0:T(8,128)(2,1)}, u32[]{:S(2)}, u32[]{:S(2)}) collective-permute-start(bf16[2,40,8,768]{3,2,1,0:T(8,128)(2,1)} %fusion.9), channel_id=1, source_target_pairs={{0,1},{1,0},{2,3},{3,2},{4,5},{5,4},{6,7},{7,6},{8,9},{9,8},{10,11... | collective-permute-start | bytes 2949128 | tf_op jit(solution)/shard_map/ppermute | solution.py:41
  586.2 23.7 %collective-permute-start.80 = (bf16[2,40,8,768]{3,2,1,0:T(8,128)(2,1)}, bf16[2,40,8,768]{3,2,1,0:T(8,128)(2,1)}, u32[]{:S(2)}, u32[]{:S(2)}) collective-permute-start(bf16[2,40,8,768]{3,2,1,0:T(8,128)(2,1)} %fusion.5), channel_id=1, source_target_pairs={{0,4},{4,0},{1,5},{5,1},{2,6},{6,2},{3,7},{7,3},{8,12},{12,8},{9,1... | collective-permute-start | bytes 2949128 | tf_op jit(solution)/shard_map/ppermute | solution.py:44
  611.8 23.5 %collective-permute-start.81 = (bf16[40,8,768]{2,1,0:T(8,128)(2,1)S(1)}, bf16[40,8,768]{2,1,0:T(8,128)(2,1)S(1)}, u32[]{:S(2)}, u32[]{:S(2)}) collective-permute-start(bf16[40,8,768]{2,1,0:T(8,128)(2,1)S(1)} %dynamic-slice_bitcast_fusion.4), channel_id=1, source_target_pairs={{0,16},{8,24},{16,0},{24,8},{1,17},{9,25},{17,1},{25,9},{2,18},{10... | collective-permute-start | bytes 1474568 | tf_op jit(solution)/shard_map/ppermute | solution.py:59
  (221 other events, 1634.0 us)

commit v4 on v3

--- a/solution.py
+++ b/solution.py
@@ -108,27 +108,24 @@
     return parts.transpose(1, 2, 0, 3).reshape(r, n)
 
 
-def team_trade(grid, parts):
-    got = grid.to_near(pick(parts, 1 - grid.near, 1))
-    parts = paired(pick(parts, grid.near, 1), got, grid.near, 1)
-    got = grid.to_core(pick(parts, 1 - grid.core, 0))
-    return paired(pick(parts, grid.core, 0), got, grid.core, 0)
-
-
 def trade_ins(grid, parts):
     width = max(p.shape[3] for p in parts)
-    lines = team_trade(grid, joined([widen(p, width) for p in parts], 2))
+    lines = joined([widen(p, width) for p in parts], 2)
+    got = grid.to_near(pick(lines, 1 - grid.near, 1))
+    lines = paired(pick(lines, grid.near, 1), got, grid.near, 1)
+    came = grid.to_core(pick(lines, 1 - grid.core, 0))
+    lines = paired(pick(lines, grid.core, 0), came, grid.core, 0)
     out, at = [], 0
     for p in parts:
         r, c = p.shape[2:]
         out.append(lines[:, :, at : at + r, :c])
         at += r
-    return out
+    return out, (got, came)
 
 
 class Bundle:
-    def __init__(self, names, width):
-        self.names, self.width = names, width
+    def __init__(self, names, width, turn="both"):
+        self.names, self.width, self.turn = names, width, turn
 
     def flat(self, value):
         p, r, c = value.shape[-3:]
@@ -165,6 +162,9 @@
         bundle = self.bundles[i]
         return joined([bundle.flat(self.parts[n]) for n in bundle.names], 0)
 
+    def cut(self, i, n):
+        return {"both": n // 2, "x": n, "y": 0}[self.bundles[i].turn]
+
     def round(self, moves, also=()):
         grid, columns = self.grid, 2 * self.grid.rest
         sends = []
@@ -175,14 +175,19 @@
                 sends.append(self.blocks[i])
             else:
                 by_x, by_y = self.sides[i]
-                cut = by_x.shape[1] // 2
+                cut = self.cut(i, by_x.shape[1])
                 sends.append((by_x[:, :cut], by_y[:, cut:]))
         if self.gate or also:
             sends, _ = lax.optimization_barrier((sends, (self.gate, also)))
         self.gate = ()
         for (kind, i), value in zip(moves, sends):
             if kind == "c":
-                got = self.corners[i] = (grid.to_y(value[0]), grid.to_x(value[1]))
+                got = ()
+                if value[0].shape[1]:
+                    got += (grid.to_y(value[0]),)
+                if value[1].shape[1]:
+                    got += (grid.to_x(value[1]),)
+                self.corners[i] = got
             elif kind == "xy":
                 self.blocks[i] = value
                 got = self.sides[i] = (grid.to_x(value), grid.to_y(value))
@@ -200,7 +205,7 @@
 
     def full(self, i):
         grid, bundle, parts = self.grid, self.bundles[i], self.parts
-        corner = jnp.concatenate(self.corners[i], 1)
+        corner = joined(self.corners[i], 1)
         full, at = {}, 0
         for name in bundle.names:
             shape = parts[name].shape
@@ -232,13 +237,46 @@
     return total.astype(BF16)
 
 
+def lay_kernel(core, mine, came, *outs, shapes):
+    first = core[0] == 0
+    at = 0
+    for (r, c, groups, n), out in zip(shapes, outs):
+        wide = n // groups // TEAM
+        step = c // groups
+        for near in range(2):
+            a = mine[near, pl.ds(at, r), :].astype(F32)
+            b = came[near, pl.ds(at, r), :].astype(F32)
+            for k, value in enumerate((jnp.where(first, a, b), jnp.where(first, b, a))):
+                for g in range(groups):
+                    to = g * (n // groups) + (2 * k + near) * wide
+                    out[:, to : to + wide] = value[:, g * step : g * step + wide]
+        at += r
+
+
+def lay_out(core, mine, came, shapes):
+    if any(r % 8 for r, _, _, _ in shapes):
+        lines, at, outs = paired(mine, came, core, 0), 0, []
+        for r, c, groups, n in shapes:
+            outs.append(from_quarters(lines[:, :, at : at + r, :c], groups, n).astype(F32))
+            at += r
+        return outs
+    size = 4 * mine.size + sum(4 * r * n for r, _, _, n in shapes)
+    return pl.pallas_call(
+        partial(lay_kernel, shapes=shapes),
+        out_shape=[jax.ShapeDtypeStruct((r, n), F32) for r, _, _, n in shapes],
+        in_specs=[pl.BlockSpec(memory_space=pltpu.SMEM)] + [pl.BlockSpec(memory_space=pltpu.VMEM)] * 2,
+        compiler_params=pltpu.CompilerParams(vmem_limit_bytes=2 * size + (8 << 20)),
+        cost_estimate=pl.CostEstimate(flops=size, bytes_accessed=size, transcendentals=0),
+    )(core.astype(jnp.int32).reshape(1), mine, came)
+
+
 def after(gate, value):
     return lax.optimization_barrier((value, gate))[0]
 
 
 class Give:
-    def __init__(self, grid, bundle, grads, widths):
-        self.grid, self.bundle, self.widths, self.step = grid, bundle, widths, 0
+    def __init__(self, grid, bundle, grads):
+        self.grid, self.bundle, self.step = grid, bundle, 0
         rest = grid.rest
         self.views, self.shapes = [], []
         for name in bundle.names:
@@ -267,76 +305,83 @@
         if gate is not None:
             self.got = after(gate, self.got)
         step, self.step = self.step, self.step + 1
-        (self.corner, self.side, self.column, self.team, self.core, self.finish)[step]()
+        (self.corner, self.side, self.column)[step]()
 
     def corner(self):
         grid = self.grid
         corner = self.block(1 - grid.y, 1 - grid.x)
-        self.cut = corner.shape[1] // 2
-        self.got = grid.to_y(corner[:, : self.cut]), grid.to_x(corner[:, self.cut :])
+        n = corner.shape[1]
+        self.cut = {"both": n // 2, "x": 0, "y": n}[self.bundle.turn]
+        self.got = ()
+        if self.cut:
+            self.got += (grid.to_y(corner[:, : self.cut]),)
+        if self.cut < n:
+            self.got += (grid.to_x(corner[:, self.cut :]),)
 
     def side(self):
-        grid, cut, (by_y, by_x) = self.grid, self.cut, self.got
+        grid, cut, got = self.grid, self.cut, list(self.got)
         x = self.block(grid.y, 1 - grid.x)
         y = self.block(1 - grid.y, grid.x)
-        x = jnp.concatenate([plus(x[:, :cut], by_y), x[:, cut:]], 1)
-        y = jnp.concatenate([y[:, :cut], plus(y[:, cut:], by_x)], 1)
+        n = x.shape[1]
+        if cut == n:
+            x = plus(x, got[0])
+        elif cut == 0:
+            y = plus(y, got[0])
+        else:
+            x = jnp.concatenate([plus(x[:, :cut], got[0]), x[:, cut:]], 1)
+            y = jnp.concatenate([y[:, :cut], plus(y[:, cut:], got[1])], 1)
         self.got = grid.to_x(x), grid.to_y(y)
 
     def column(self):
         grid, columns = self.grid, 2 * self.grid.rest
         chunk = plus(self.block(grid.y, grid.x), *self.got)
-        mine = pick(chunk, grid.column, 0)
-        sent = [grid.to_column(pick(chunk, (grid.column + k) % columns, 0), k) for k in range(1, columns)]
-        self.got = mine, *sent
-
-    def team(self):
-        grid, bundle = self.grid, self.bundle
-        total = plus(*self.got)
-        self.quads, outs, at = [], [], 0
-        for name, shape in zip(bundle.names, self.shapes):
-            n = bundle.count(shape)
-            part = bundle.unflat(total[at : at + n], shape)
-            if name in GROUPS:
-                self.quads.append((name, part.reshape((2, 2) + part.shape[1:])))
-            else:
-                outs.append(part[0])
-            at += n
-        self.got = ()
-        if self.quads:
-            width = max(q.shape[3] for _, q in self.quads)
-            lines = joined([widen(q, width) for _, q in self.quads], 2)
-            self.got += (pick(lines, grid.near, 1), grid.to_near(pick(lines, 1 - grid.near, 1)))
-        if outs:
-            self.got += (grid.swap_far(joined(outs, 0)),)
-
-    def core(self):
+        self.mine = pick(chunk, grid.column, 0)
+        self.got = tuple(
+            grid.to_column(pick(chunk, (grid.column + k) % columns, 0), k) for k in range(1, columns)
+        )
+
+
+class Deliver:
+    def __init__(self, grid, gives, widths, gate=None):
+        self.grid, self.widths = grid, widths
+        self.quads, self.outs = [], []
+        for give in gives:
+            got = give.got if gate is None else after(gate, give.got)
+            total, at = plus(give.mine, *got), 0
+            for name, shape in zip(give.bundle.names, give.shapes):
+                n = give.bundle.count(shape)
+                part = give.bundle.unflat(total[at : at + n], shape)
+                if name in GROUPS:
+                    self.quads.append((name, part.reshape((2, 2) + part.shape[1:])))
+                else:
+                    self.outs.append((name, part[0]))
+                at += n
+        width = max(q.shape[3] for _, q in self.quads)
+        lines = joined([widen(q, width) for _, q in self.quads], 2)
+        self.mine, self.came = pick(lines, grid.near, 1), grid.to_near(pick(lines, 1 - grid.near, 1))
+        width = max(o.shape[1] for _, o in self.outs)
+        self.swapped = grid.swap_far(joined([widen(o, width) for _, o in self.outs], 0))
+        self.got = self.came
+
+    def core(self, gate=None):
         grid = self.grid
-        if self.quads:
-            mine, came, *outs = self.got
-            lines = paired(mine, came, grid.near, 1)
-            self.got = (pick(lines, grid.core, 0), grid.to_core(pick(lines, 1 - grid.core, 0)), *outs)
-
-    def finish(self):
-        grid, outs, self.done = self.grid, self.got, {}
-        if self.quads:
-            mine, came, *outs = self.got
-            lines, at = paired(mine, came, grid.core, 0), 0
-            for name, quad in self.quads:
-                r, c = quad.shape[2:]
-                part = lines[:, :, at : at + r, :c]
-                self.done[name] = from_quarters(part, GROUPS[name], self.widths[name]).astype(F32)
-                at += r
+        came = self.came if gate is None else after(gate, self.came)
+        lines = paired(self.mine, came, grid.near, 1)
+        self.mine, self.came = pick(lines, grid.core, 0), grid.to_core(pick(lines, 1 - grid.core, 0))
+        self.got = self.came
+
+    def finish(self, gate=None):
+        came, swapped = self.came, self.swapped
+        if gate is not None:
+            came, swapped = after(gate, (came, swapped))
+        shapes = [(*quad.shape[2:], GROUPS[name], self.widths[name]) for name, quad in self.quads]
+        done = dict(zip((n for n, _ in self.quads), lay_out(self.grid.core, self.mine, came, shapes)))
         at = 0
-        for name, (p, r, c) in zip(self.bundle.names, self.shapes):
-            if p == 1:
-                self.done[name] = outs[0][at : at + r].astype(F32)
-                at += r
-
-    def end(self):
-        while self.step < 6:
-            self.next()
-        return self.done
+        for name, out in self.outs:
+            r, c = out.shape
+            done[name] = swapped[at : at + r, :c].astype(F32)
+            at += r
+        return done
 
 
 class Sizes:
@@ -779,21 +824,13 @@
     return kernel(body, outs, (upstream, *(sums or ()), *stored, params), 32 * s.rows * s.ki)
 
 
-def sum_all(grid, value):
-    value = value + grid.to_core(value)
-    value = value + grid.to_x(value)
-    value = value + grid.to_y(value)
-    value = value + grid.to_near(value)
-    return sum((grid.to_column(value, k) for k in range(1, 2 * grid.rest)), value)
-
-
 FETCH = (
     Bundle(["tci", "ici", "tco", "icoa", "icob"], 768),
-    Bundle(["id0", "iu0", "iso"], 1024),
-    Bundle(["tu0", "td0"], 768),
-    Bundle(["tsi", "isi", "tso"], 768),
-    Bundle(["id1", "iu1"], 1024),
-    Bundle(["tu1", "td1"], 768),
+    Bundle(["id0", "iu0", "iso"], 1024, "x"),
+    Bundle(["tu0", "td0"], 768, "y"),
+    Bundle(["tsi", "isi", "tso"], 768, "x"),
+    Bundle(["id1", "iu1"], 1024, "y"),
+    Bundle(["tu1", "td1"], 768, "y"),
 )
 
 
@@ -822,6 +859,7 @@
     depth,
 ):
     grid = Grid(depth)
+    rest = grid.rest
     tw, iw = text_gains.shape[2], image_gains.shape[2]
     s = Sizes(*text_in.shape[1:], *image_in.shape[1:])
     weights = {
@@ -858,8 +896,10 @@
     parts = {}
 
     def trade(names):
-        for n, q in zip(names, trade_ins(grid, [quads[n] for n in names])):
+        got, arrived = trade_ins(grid, [quads[n] for n in names])
+        for n, q in zip(names, got):
             parts[n] = q.reshape((TEAM,) + q.shape[2:])
+        return arrived
 
     def swap(names):
         swapped, at = grid.swap_far(joined([weights[n] for n in names], 0)), 0
@@ -875,7 +915,7 @@
     names = ("td0", "tso", "td1", "id0", "iso", "id1")
     inputs = (text_in, image_in, text_segments, grad_text_out, grad_image_out, params)
     later = {n: quads[n] for n in late}, {n: weights[n] for n in names}, inputs
-    quarters_later, weights_later, inputs = after(parts["ici"], later)
+    quarters_later, weights_later, inputs = after(fetch.gate, later)
     quads.update(quarters_later)
     weights.update(weights_later)
     text_in, image_in, text_segments, grad_text_out, grad_image_out, params = inputs
@@ -883,7 +923,12 @@
     swap(("id0", "iso", "id1"))
     swap(("td0", "tso", "td1"))
     fetch.round([("xy", 0)])
-    params = sum_all(grid, params)
+    moved = grid.to_core(params)
+
+    def more(move):
+        nonlocal params, moved
+        params = params + after(fetch.gate, moved)
+        moved = move(params)
 
     def pair(own):
         return own, grid.to_core(own)
@@ -917,15 +962,20 @@
         for name in names:
             yield grid.to_near(full[name])
 
+    more(grid.to_x)
     fetch.round([("c", 0), ("z", 1)])
     full = fetch.full(0)
     full["ico"] = jnp.concatenate([full["icoa"], full["icob"][:, : s.ki - width]], 1)
     co_w = [full[n] for n in ("tci", "tco", "ici", "ico")]
+    more(grid.to_y)
     fetch.round([("xy", 1), ("z", 2)])
     qkv_t, ctx_t, qkv_i, ctx_i, home, away = co_attention(s, low0, *co_w, seg_col, segments)
+    more(grid.to_near)
     fetch.round([("c", 1), ("xy", 2), ("z", 3)], away)
     full.update(fetch.full(1))
     sums = settle(home, away)
+    more(lambda value: sum((grid.to_column(value, k) for k in range(2, 2 * rest)), grid.to_column(value, 1)))
+    params = params + moved
     y, low, stored0 = normal(values, sums, 0)
     low1 = pair(low)
     fetch.round([("c", 2), ("xy", 3), ("z", 4)], sums[1])
@@ -951,86 +1001,110 @@
 
     grads, norm_grads = {}, [None] * 4
 
-    def normal_back(upstream, sums, stored, i):
+    def normal_back(upstream, sums, stored, i, due=None):
         grad, low, norm_grads[i] = norm_back(s, upstream, sums, stored, params, i)
-        return grad, low
-
-    def weigh(names, home, away, low, out, *mids, parts=1):
+        return grad, low if due is None else after(due, low)
+
+    def weigh(names, home, away, low, out, *mids, parts=1, due=None):
         got = grid.to_core(away)
+        if due is not None:
+            got = after(due, got)
         folded = fold(s, home, got)
         low, out, mids = after(folded, (low, out, mids))
         values = weight_grads(s, low, out, *mids, parts)
         grads.update(zip(names, values))
-        return (home, got, grid.to_near(folded)), folded, values[4:]
-
-    def give(names, wide, *gate):
-        return Give(grid, Bundle(names, wide), grads, widths)
-
-    def join_near(names, values, gate):
-        values = after(gate, values)
-        for name, value in zip(names, values):
-            grads[name] = plus(grads[name], grid.to_near(value))
+        return (home, got, grid.to_near(folded)), values[0], values[4:]
+
+    def give(names, wide, turn="both"):
+        return Give(grid, Bundle(names, wide, turn), grads)
+
+    def send_near(values, gate):
+        return [grid.to_near(v) for v in after(gate, values)]
+
+    def join_near(names, came, gate):
+        for name, value in zip(names, after(gate, came)):
+            grads[name] = plus(grads[name], value)
 
     g, low = normal_back(upstream, None, stored3, 3)
     out = pair(low)
     bg_t, bg_i, home, away = ffn_back(s, out, before_t1, before_i1, *ffn_w[1])
-    sums, folded, others = weigh(
+    sums, weighed, others = weigh(
         ("tu1", "td1", "iu1", "id1"), home, away, low3, out, hidden_t1, bg_t, hidden_i1, bg_i, parts=2
     )
-    text3 = give(["tu1", "td1"], width)
-
-    g, low = normal_back(g, sums, stored2, 2)
-    out = pair(widened(low))
-    text3.next(low)
+    text3 = give(["tu1", "td1"], width, "y")
+
+    g, low = normal_back(g, sums, stored2, 2, weighed)
+    across = grid.to_near(low[: s.li])
+    came = send_near(others, across)
+    out = pair(jnp.concatenate([low, across]))
     dqkv_t, dqkv_i, home, away = self_back(s, out, *self_w, id_col, id_row, sqkv_t, sqkv_i, size, heads)
-    join_near(("iu1", "id1"), others, away)
-    sums, folded, _ = weigh(
-        ("tsi", "tso", "isi", "iso"), home, away, low2, out, sctx_t, dqkv_t, sctx_i, dqkv_i
+    sums, weighed, _ = weigh(
+        ("tsi", "tso", "isi", "iso"), home, away, low2, out, sctx_t, dqkv_t, sctx_i, dqkv_i, due=text3.got
     )
-    text3.next(folded)
+    text3.next(away)
     grads["tso"] = grads["tso"][: size * heads]
-    text2 = give(["tsi", "isi", "tso"], width)
-
-    g, low = normal_back(g, sums, stored1, 1)
+    text2 = give(["tsi", "isi", "tso"], width, "x")
+
+    g, low = normal_back(g, sums, stored1, 1, (weighed, came))
+    join_near(("iu1", "id1"), came, low)
+    image3 = give(["id1", "iu1", "iso"], s.ki, "y")
     out = pair(low)
-    text2.next(low)
-    text3.next(low)
-    image3 = give(["id1", "iu1", "iso"], s.ki)
     bg_t, bg_i, home, away = ffn_back(s, out, before_t0, before_i0, *ffn_w[0])
-    sums, folded, others = weigh(
-        ("tu0", "td0", "iu0", "id0"), home, away, low1, out, hidden_t0, bg_t, hidden_i0, bg_i, parts=2
+    sums, weighed, others = weigh(
+        ("tu0", "td0", "iu0", "id0"), home, away, low1, out, hidden_t0, bg_t, hidden_i0, bg_i,
+        parts=2, due=(text3.got, text2.got),
     )
-    image3.next(folded)
-    text2.next(folded)
-    text3.next(folded)
-    text1 = give(["tu0", "td0"], width)
-
-    g, low = normal_back(g, sums, stored0, 0)
-    out = pair(widened(low))
-    text1.next(low)
+    text3.next(away)
+    text2.next(away)
+    text1 = give(["tu0", "td0"], width, "x")
+
+    g, low = normal_back(g, sums, stored0, 0, (weighed, image3.got))
+    across = grid.to_near(low[: s.li])
+    came = send_near(others, across)
+    out = pair(jnp.concatenate([low, across]))
     image3.next(low)
-    text2.next(low)
-    join_near(("iu0", "id0"), others, out[1])
+    norm_sums = jnp.concatenate(norm_grads)
+    moved = grid.to_core(norm_sums)
     dqkv_t, dqkv_i, home, away = co_back(s, out, *co_w, seg_col, segments, qkv_t, qkv_i)
-    image1 = give(["id0", "iu0"], s.ki)
-    sums, folded, _ = weigh(
-        ("tci", "tco", "ici", "ico"), home, away, low0, out, ctx_t, dqkv_t, ctx_i, dqkv_i
+    norm_sums = norm_sums + after(away, moved)
+    moved = grid.to_x(norm_sums)
+    sums, weighed, _ = weigh(
+        ("tci", "tco", "ici", "ico"), home, away, low0, out, ctx_t, dqkv_t, ctx_i, dqkv_i,
+        due=(text2.got, text1.got, image3.got),
     )
-    grads["icoa"] = grads["ico"][:, :width]
-    grads["icob"] = widen(grads["ico"][:, width:], width)
-    text0 = give(["tci", "ici", "tco", "icoa", "icob"], width)
-    for each in (text1, image3, text2, image1):
-        each.next(folded)
-    norm_sums = sum_all(grid, after(folded, jnp.concatenate(norm_grads))).reshape(4, 4, s.ki)
+    text0 = give(["tci", "ici", "tco"], width)
+    text2.next(away)
+    text1.next(away)
+    image3.next(away)
     home, got, other = sums
+
+    gate = text0.got
+    text0.next()
+    join_near(("iu0", "id0"), came, gate)
+    image1 = give(["id0", "iu0", "ico"], s.ki)
+    text1.next(gate)
+    first = Deliver(grid, [text3, text2, image3], widths, gate)
+    norm_sums = norm_sums + after(gate, moved)
+    moved = grid.to_y(norm_sums)
+    gate = text0.got
+    text0.next()
+    image1.next(gate)
+    first.core(gate)
+    norm_sums = norm_sums + after(gate, moved)
+    moved = grid.to_near(norm_sums)
     mine = slice(0, s.li + s.tall)
+    other = after(gate, other)
     sums = g[mine] + home[mine] + got[mine].astype(F32)
     sums = sums + jnp.concatenate([other[: s.li], other[s.li + s.tall :]]).astype(F32)
-
-    done = {}
-    for each in (text3, text2, image3, text1, image1, text0):
-        done.update(each.end())
-    done["ico"] = jnp.concatenate([done["icoa"], done["icob"][:, : s.ki - width]], 1)
+    gate = text0.got
+    image1.next(gate)
+    norm_sums = norm_sums + after(gate, moved)
+    moved = [grid.to_column(norm_sums, k) for k in range(1, 2 * rest)]
+    done = first.finish(gate)
+    last_two = Deliver(grid, [text0, text1, image1], widths)
+    norm_sums = sum(after(last_two.got, moved), norm_sums).reshape(4, 4, s.ki)
+    last_two.core()
+    done.update(last_two.finish())
     norm_outs = [
         lax.dynamic_slice(norm_sums[:, i], (0, place * k), (4, k))[None]
         for i, k in enumerate((tw, tw, iw, iw))

time: 658 us -> 574 us (0.87)
  waiting for transfers between devices: 364 us -> 323 us
  other arithmetic: 38.8 us -> 20.2 us
  local copies, waits for them, and re-layouts: 63.7 us -> 45.3 us
  starting transfers between devices: 127 us -> 120 us
    ppermute x26 -> x21, waiting for transfers between devices: 54 us -> 24.2 us  [to_y(): return lax.ppermute(value, 'y', FLIP)]
    broadcast_in_dim x25 -> x6, local copies, waits for them, and re-layouts: 16.7 us -> 1.14 us  [paired(): return jnp.where(place == index, own, other)]
    ppermute x14, waiting for transfers between devices: 111 us -> 98 us  [to_column(): return lax.ppermute(value, 'z', pairs)]
    ppermute x32 -> x28, starting transfers between devices: 25.4 us -> 37.5 us  [to_near(): return lax.ppermute(value, 'z', pairs)]
    ppermute x26 -> x22, waiting for transfers between devices: 60.4 us -> 71.3 us  [to_x(): return lax.ppermute(value, 'x', FLIP)]
    ppermute x9 -> x5, starting transfers between devices: 14.1 us -> 5.25 us  [swap_far(): return lax.ppermute(value, ALL, pairs)]
    ppermute x32 -> x28, waiting for transfers between devices: 130 us -> 121 us  [to_near(): return lax.ppermute(value, 'z', pairs)]
    convert_element_type x15 -> x0, local copies, waits for them, and re-layouts: 8.49 us -> none  [finish(): from_quarters(part, GROUPS[name], self.widths[name]).astype(F32)]
  transfers between devices with their start and end apart: 134 -> 113, of which waited for: 62 -> 50; matrix products, arithmetic and copies ran while one was open for 12% -> 9% of each run, Pallas kernels for 5% -> 7%
where the time goes in v4:
time: 574 us; the launch traced here: 566 us
  waiting for transfers between devices  323 us (56%)
  starting transfers between devices  120 us (21%)
  Pallas kernels  52 us (9%)
  local copies, waits for them, and re-layouts  45.3 us (8%)
  other arithmetic  20.2 us (4%)
    ppermute x28, waiting for transfers between devices, to_near(): return lax.ppermute(value, 'z', pairs)  121 us
    ppermute x14, waiting for transfers between devices, to_column(): return lax.ppermute(value, 'z', pairs)  98 us
    ppermute x22, waiting for transfers between devices, to_x(): return lax.ppermute(value, 'x', FLIP)  71.3 us
    pallas_call x28, Pallas kernels, kernel(): pl.pallas_call(body, out_shape=outs, scratch_shapes=[pltpu.VMEM(shape, ki...  50.2 us
    ppermute x28, starting transfers between devices, to_near(): return lax.ppermute(value, 'z', pairs)  37.5 us
    ppermute x21, waiting for transfers between devices, to_y(): return lax.ppermute(value, 'y', FLIP)  24.2 us
    ppermute x22, starting transfers between devices, to_x(): return lax.ppermute(value, 'x', FLIP)  22.5 us
    ppermute x21, starting transfers between devices, to_y(): return lax.ppermute(value, 'y', FLIP)  21.8 us
  transfers between devices with their start and end apart: 113, of which 50 were waited for; matrix products, arithmetic and copies ran while one was open for 9% of the time, Pallas kernels for 7%

profile of v4, /device:TPU:0, one launch (start us, length us, event | category | flops | bytes accessed | tf_op | source)
XLA Modules:
  0.0 566.0 jit_solution(5085490906539687230)
XLA Ops:
  2.7 3.1 collective-permute-start
  6.7 3.4 collective-permute-done
  12.2 3.8 collective-permute-start.3
  19.0 2.6 dynamic_update_slice.6
  23.0 15.4 %collective-permute-done.3 = bf16[40,8,768]{2,1,0:T(8,128)(2,1)S(1)} collective-permute-done((bf16[40,8,768]{2,1,0:T(8,128)(2,1)S(1)}, bf16[40,8,768]{2,1,0:T(8,128)(2,1)S(1)}, u32[]{:S(2)}, u32[]{:S(2)}) %collective-permute-start.3) | collective-permute-done | bytes 491552 | tf_op jit(solution)/shard_map/ppermute | solution.py:59
  44.8 2.0 collective-permute-start.13
  46.9 12.2 %collective-permute-done.13 = f32[1,64]{1,0:T(1,128)S(1)} collective-permute-done((f32[1,64]{1,0:T(1,128)S(1)}, f32[1,64]{1,0:T(1,128)S(1)}, u32[]{:S(2)}, u32[]{:S(2)}) %collective-permute-start.13) | collective-permute-done | bytes 288 | tf_op jit(solution)/shard_map/ppermute | solution.py:51
  60.7 1.9 collective-permute-start.21
  65.1 8.6 %collective-permute-start.17 = (f32[16,1024]{1,0:T(8,128)}, f32[16,1024]{1,0:T(8,128)S(1)}, u32[]{:S(2)}, u32[]{:S(2)}) collective-permute-start(f32[16,1024]{1,0:T(8,128)} %dynamic_update_slice.7), channel_id=1, source_target_pairs={{0,2},{2,0},{1,3},{3,1},{4,6},{6,4},{5,7},{7,5},{8,10},{10,8},{9,1... | collective-permute-start | bytes 196616 | tf_op jit(solution)/shard_map/ppermute | solution.py:38
  75.5 3.6 collective-permute-done.4
  93.9 8.8 %collective-permute-done.19 = bf16[12,8,1024]{2,1,0:T(8,128)(2,1)S(1)} collective-permute-done((bf16[12,8,1024]{2,1,0:T(8,128)(2,1)S(1)}, bf16[12,8,1024]{2,1,0:T(8,128)(2,1)S(1)}, u32[]{:S(2)}, u32[]{:S(2)}) %collective-permute-start.19) | collective-permute-done | bytes 196640 | tf_op jit(solution)/shard_map/ppermute | solution.py:59
  102.8 2.1 collective-permute-done.11
  108.2 2.6 collective-permute-start.24
  113.5 4.9 shard_map.356
  119.2 3.5 collective-permute-done.24
  125.9 14.6 %collective-permute-done.29 = bf16[31,8,768]{2,1,0:T(8,128)(2,1)S(1)} collective-permute-done((bf16[31,8,768]{2,1,0:T(8,128)(2,1)S(1)}, bf16[31,8,768]{2,1,0:T(8,128)(2,1)S(1)}, u32[]{:S(2)}, u32[]{:S(2)}) %collective-permute-start.29) | collective-permute-done | bytes 380960 | tf_op jit(solution)/shard_map/ppermute | solution.py:59
  140.7 2.1 collective-permute-start.16
  142.8 2.7 collective-permute-done.26
  151.0 17.7 %collective-permute-done.30 = f32[16,1024]{1,0:T(8,128)S(1)} collective-permute-done((f32[16,1024]{1,0:T(8,128)S(1)}, f32[16,1024]{1,0:T(8,128)S(1)}, u32[]{:S(2)}, u32[]{:S(2)}) %collective-permute-start.30) | collective-permute-done | bytes 65568 | tf_op jit(solution)/shard_map/ppermute | solution.py:59
  168.7 3.4 collective-permute-start.33
  177.0 12.4 %collective-permute-done.39 = bf16[2,31,8,768]{3,2,1,0:T(8,128)(2,1)S(1)} collective-permute-done((bf16[2,31,8,768]{3,2,1,0:T(8,128)(2,1)S(1)}, bf16[2,31,8,768]{3,2,1,0:T(8,128)(2,1)S(1)}, u32[]{:S(2)}, u32[]{:S(2)}) %collective-permute-start.39) | collective-permute-done | bytes 761888 | tf_op jit(solution)/shard_map/ppermute | solution.py:41
  197.1 3.2 collective-permute-done.46
  200.4 5.2 collective-permute-done.47
  205.8 4.0 collective-permute-done.36.other
  210.5 2.3 collective-permute-done.42
  217.1 2.2 collective-permute-done.37
  219.5 12.0 %collective-permute-done.51 = bf16[2,8,8,1024]{3,2,1,0:T(8,128)(2,1)S(1)} collective-permute-done((bf16[2,8,8,1024]{3,2,1,0:T(8,128)(2,1)S(1)}, bf16[2,8,8,1024]{3,2,1,0:T(8,128)(2,1)S(1)}, u32[]{:S(2)}, u32[]{:S(2)}) %collective-permute-start.51) | collective-permute-done | bytes 262176 | tf_op jit(solution)/shard_map/ppermute | solution.py:41
  233.5 10.8 %collective-permute-done.52 = bf16[2,24,8,768]{3,2,1,0:T(8,128)(2,1)S(1)} collective-permute-done((bf16[2,24,8,768]{3,2,1,0:T(8,128)(2,1)S(1)}, bf16[2,24,8,768]{3,2,1,0:T(8,128)(2,1)S(1)}, u32[]{:S(2)}, u32[]{:S(2)}) %collective-permute-start.52) | collective-permute-done | bytes 589856 | tf_op jit(solution)/shard_map/ppermute | solution.py:41
  245.4 3.6 shard_map.362
  249.2 2.1 collective-permute-done.43.got
  251.5 2.6 collective-permute-start.44
  254.4 2.0 collective-permute-start.54
  256.5 9.6 %collective-permute-done.44.other = bf16[240,1024]{1,0:T(8,128)(2,1)S(1)} collective-permute-done((bf16[240,1024]{1,0:T(8,128)(2,1)S(1)}, bf16[240,1024]{1,0:T(8,128)(2,1)S(1)}, u32[]{:S(2)}, u32[]{:S(2)}) %collective-permute-start.44) | collective-permute-done | bytes 491552 | tf_op jit(solution)/shard_map/ppermute | solution.py:51
  267.2 10.1 %collective-permute-done.53.uj = bf16[1024,256]{1,0:T(8,128)(2,1)S(1)} collective-permute-done((bf16[1024,256]{1,0:T(8,128)(2,1)S(1)}, bf16[1024,256]{1,0:T(8,128)(2,1)S(1)}, u32[]{:S(2)}, u32[]{:S(2)}) %collective-permute-start.53) | collective-permute-done | bytes 524320 | tf_op jit(solution)/shard_map/ppermute | solution.py:51
  277.3 10.8 %collective-permute-done.54.dj = bf16[256,1024]{1,0:T(8,128)(2,1)S(1)} collective-permute-done((bf16[256,1024]{1,0:T(8,128)(2,1)S(1)}, bf16[256,1024]{1,0:T(8,128)(2,1)S(1)}, u32[]{:S(2)}, u32[]{:S(2)}) %collective-permute-start.54) | collective-permute-done | bytes 524320 | tf_op jit(solution)/shard_map/ppermute | solution.py:51
  293.5 2.0 collective-permute-done.57
  295.6 3.8 collective-permute-done.56.other
  308.9 1.9 shard_map.372
  311.9 2.2 collective-permute-done.60.refs_3_
  317.5 5.6 collective-permute-done.61
  327.5 9.1 %shard_map.373 = (bf16[256,768]{1,0:T(8,128)(2,1)S(1)}, bf16[576,768]{1,0:T(8,128)(2,1)S(1)}, f32[384,1024]{1,0:T(8,128)S(1)}, bf16[384,1024]{1,0:T(8,128)(2,1)S(1)}) custom-call(bf16[384,1024]{1,0:T(8,128)(2,1)} %constant_dynamic-update-slice_fusion.10.near.out_near, bf16[384,1024]{1,0:T(8,128)(2,1)} %collective-permute-done.62.far.out_far, ...), custom_call_target="tpu_custom_call" | custom-call | flops 1811939328 | bytes 10160128 | tf_op jit(solution)/shard_map/pallas_call | solution.py:445
  345.6 4.1 shard_map.376
  350.6 24.7 %collective-permute-done.65.refs_3_ = bf16[240,1024]{1,0:T(8,128)(2,1)S(1)} collective-permute-done((bf16[240,1024]{1,0:T(8,128)(2,1)S(1)}, bf16[240,1024]{1,0:T(8,128)(2,1)S(1)}, u32[]{:S(2)}, u32[]{:S(2)}) %collective-permute-start.65) | collective-permute-done | bytes 491552 | tf_op jit(solution)/shard_map/ppermute | solution.py:51
  383.2 10.2 %collective-permute-done.72 = bf16[2,31,8,768]{3,2,1,0:T(8,128)(2,1)S(1)} collective-permute-done((bf16[2,31,8,768]{3,2,1,0:T(8,128)(2,1)S(1)}, bf16[2,31,8,768]{3,2,1,0:T(8,128)(2,1)S(1)}, u32[]{:S(2)}, u32[]{:S(2)}) %collective-permute-start.72) | collective-permute-done | bytes 761888 | tf_op jit(solution)/shard_map/ppermute | solution.py:41
  399.3 1.9 shard_map.380
  404.4 4.7 collective-permute-done.75
  412.1 9.5 %shard_map.381 = (bf16[256,768]{1,0:T(8,128)(2,1)S(1)}, bf16[576,768]{1,0:T(8,128)(2,1)S(1)}, f32[384,1024]{1,0:T(8,128)S(1)}, bf16[384,1024]{1,0:T(8,128)(2,1)S(1)}) custom-call(bf16[384,1024]{1,0:T(8,128)(2,1)S(1)} %constant_dynamic-update-slice_fusion.12.near.out_near, bf16[384,1024]{1,0:T(8,128)(2,1)S(1)} %collective-permute-done.76.far.out_far, ...), custom_call_target="tpu_custom_call" | custom-call | flops 1811939328 | bytes 10160128 | tf_op jit(solution)/shard_map/pallas_call | solution.py:445
  421.6 4.1 collective-permute-done.80
  426.6 2.7 collective-permute-start.103
  429.4 17.0 %collective-permute-done.81 = bf16[2,12,8,1024]{3,2,1,0:T(8,128)(2,1)S(1)} collective-permute-done((bf16[2,12,8,1024]{3,2,1,0:T(8,128)(2,1)S(1)}, bf16[2,12,8,1024]{3,2,1,0:T(8,128)(2,1)S(1)}, u32[]{:S(2)}, u32[]{:S(2)}) %collective-permute-start.81) | collective-permute-done | bytes 393248 | tf_op jit(solution)/shard_map/ppermute | solution.py:41
  447.9 2.3 shard_map.383
  453.4 2.1 collective-permute-start.92
  455.5 7.2 %collective-permute-done.84 = bf16[2,16,8,768]{3,2,1,0:T(8,128)(2,1)S(1)} collective-permute-done((bf16[2,16,8,768]{3,2,1,0:T(8,128)(2,1)S(1)}, bf16[2,16,8,768]{3,2,1,0:T(8,128)(2,1)S(1)}, u32[]{:S(2)}, u32[]{:S(2)}) %collective-permute-start.84) | collective-permute-done | bytes 393248 | tf_op jit(solution)/shard_map/ppermute | solution.py:44
  465.2 3.5 collective-permute-done.109
  469.7 2.1 collective-permute-start.104
  471.7 2.3 collective-permute-done.90
  477.3 12.8 %collective-permute-done.93 = bf16[256,1024]{1,0:T(8,128)(2,1)S(1)} collective-permute-done((bf16[256,1024]{1,0:T(8,128)(2,1)S(1)}, bf16[256,1024]{1,0:T(8,128)(2,1)S(1)}, u32[]{:S(2)}, u32[]{:S(2)}) %collective-permute-start.93) | collective-permute-done | bytes 524320 | tf_op jit(solution)/shard_map/ppermute | solution.py:51
  495.5 12.6 %collective-permute-done.91 = bf16[24,8,768]{2,1,0:T(8,128)(2,1)S(1)} collective-permute-done((bf16[24,8,768]{2,1,0:T(8,128)(2,1)S(1)}, bf16[24,8,768]{2,1,0:T(8,128)(2,1)S(1)}, u32[]{:S(2)}, u32[]{:S(2)}) %collective-permute-start.91) | collective-permute-done | bytes 294944 | tf_op jit(solution)/shard_map/ppermute | solution.py:59
  510.8 1.9 collective-permute-start.88
  512.7 2.8 collective-permute-done.94
  523.5 13.4 %collective-permute-done.88 = bf16[32,8,768]{2,1,0:T(8,128)(2,1)S(1)} collective-permute-done((bf16[32,8,768]{2,1,0:T(8,128)(2,1)S(1)}, bf16[32,8,768]{2,1,0:T(8,128)(2,1)S(1)}, u32[]{:S(2)}, u32[]{:S(2)}) %collective-permute-start.88) | collective-permute-done | bytes 393248 | tf_op jit(solution)/shard_map/ppermute | solution.py:59
  537.4 3.0 collective-permute-start.112
  540.4 6.7 %collective-permute-done.98 = bf16[12,8,1024]{2,1,0:T(8,128)(2,1)S(1)} collective-permute-done((bf16[12,8,1024]{2,1,0:T(8,128)(2,1)S(1)}, bf16[12,8,1024]{2,1,0:T(8,128)(2,1)S(1)}, u32[]{:S(2)}, u32[]{:S(2)}) %collective-permute-start.98) | collective-permute-done | bytes 196640 | tf_op jit(solution)/shard_map/ppermute | solution.py:59
  548.1 7.7 %collective-permute-done.99 = bf16[2,112,768]{2,1,0:T(8,128)(2,1)S(1)} collective-permute-done((bf16[2,112,768]{2,1,0:T(8,128)(2,1)S(1)}, bf16[2,112,768]{2,1,0:T(8,128)(2,1)S(1)}, u32[]{:S(2)}, u32[]{:S(2)}) %collective-permute-start.99) | collective-permute-done | bytes 344096 | tf_op jit(solution)/shard_map/ppermute | solution.py:51
  (803 shorter events, 165.2 us)
Async XLA Ops:
  12.2 26.3 %collective-permute-start.3 = (bf16[40,8,768]{2,1,0:T(8,128)(2,1)S(1)}, bf16[40,8,768]{2,1,0:T(8,128)(2,1)S(1)}, u32[]{:S(2)}, u32[]{:S(2)}) collective-permute-start(bf16[40,8,768]{2,1,0:T(8,128)(2,1)S(1)} %fusion.52), channel_id=1, source_target_pairs={{0,16},{8,24},{16,0},{24,8},{1,17},{9,25},{17,1},{25,9},{2,18},{10... | collective-permute-start | bytes 1474568 | tf_op jit(solution)/shard_map/ppermute | solution.py:59
  38.6 42.9 %collective-permute-start.6 = (bf16[2,40,8,768]{3,2,1,0:T(8,128)(2,1)S(1)}, bf16[2,40,8,768]{3,2,1,0:T(8,128)(2,1)}, u32[]{:S(2)}, u32[]{:S(2)}) collective-permute-start(bf16[2,40,8,768]{3,2,1,0:T(8,128)(2,1)S(1)} %pad_maximum_fusion), channel_id=1, source_target_pairs={{0,1},{1,0},{2,3},{3,2},{4,5},{5,4},{6,7},{7,6},{8,9},{9,8},{10,11... | collective-permute-start | bytes 2949128 | tf_op jit(solution)/shard_map/ppermute | solution.py:41
  40.2 41.4 %collective-permute-start.7 = (bf16[2,40,8,768]{3,2,1,0:T(8,128)(2,1)S(1)}, bf16[2,40,8,768]{3,2,1,0:T(8,128)(2,1)}, u32[]{:S(2)}, u32[]{:S(2)}) collective-permute-start(bf16[2,40,8,768]{3,2,1,0:T(8,128)(2,1)S(1)} %pad_maximum_fusion), channel_id=1, source_target_pairs={{0,4},{4,0},{1,5},{5,1},{2,6},{6,2},{3,7},{7,3},{8,12},{12,8},{9,1... | collective-permute-start | bytes 2949128 | tf_op jit(solution)/shard_map/ppermute | solution.py:44
  43.5 35.6 %collective-permute-start.9 = (bf16[2,168,768]{2,1,0:T(8,128)(2,1)}, bf16[2,168,768]{2,1,0:T(8,128)(2,1)}, u32[]{:S(2)}, u32[]{:S(2)}) collective-permute-start(bf16[2,168,768]{2,1,0:T(8,128)(2,1)} %get-tuple-element.478), channel_id=1, source_target_pairs={{0,8},{8,0},{16,24},{24,16},{1,9},{9,1},{17,25},{25,17},{2,10},{10... | collective-permute-start | bytes 1548296 | tf_op jit(solution)/shard_map/ppermute | solution.py:51
  43.5 20.3 %collective-permute-start.8 = (bf16[96,1024]{1,0:T(8,128)(2,1)S(1)}, bf16[96,1024]{1,0:T(8,128)(2,1)}, u32[]{:S(2)}, u32[]{:S(2)}) collective-permute-start(bf16[96,1024]{1,0:T(8,128)(2,1)S(1)} %pad_maximum_fusion.42), channel_id=1, source_target_pairs={{0,0},{1,1},{2,16},{3,17},{4,4},{5,5},{6,20},{7,21},{8,8},{9,9},{1... | collective-permute-start | bytes 589832 | tf_op jit(solution)/shard_map/ppermute | solution.py:70
  63.8 15.2 %collective-permute-start.4 = (bf16[192,1024]{1,0:T(8,128)(2,1)S(1)}, bf16[192,1024]{1,0:T(8,128)(2,1)S(1)}, u32[]{:S(2)}, u32[]{:S(2)}) collective-permute-start(bf16[192,1024]{1,0:T(8,128)(2,1)S(1)} %maximum_maximum_fusion), channel_id=1, source_target_pairs={{0,8},{8,0},{16,24},{24,16},{1,9},{9,1},{17,25},{25,17},{2,10},{10... | collective-permute-start | bytes 1179656 | tf_op jit(solution)/shard_map/ppermute | solution.py:51
  65.1 16.4 %collective-permute-start.17 = (f32[16,1024]{1,0:T(8,128)}, f32[16,1024]{1,0:T(8,128)S(1)}, u32[]{:S(2)}, u32[]{:S(2)}) collective-permute-start(f32[16,1024]{1,0:T(8,128)} %dynamic_update_slice.7), channel_id=1, source_target_pairs={{0,2},{2,0},{1,3},{3,1},{4,6},{6,4},{5,7},{7,5},{8,10},{10,8},{9,1... | collective-permute-start | bytes 196616 | tf_op jit(solution)/shard_map/ppermute | solution.py:38
  81.4 32.0 %collective-permute-start.5 = (bf16[384,1024]{1,0:T(8,128)(2,1)S(1)}, bf16[384,1024]{1,0:T(8,128)(2,1)S(1)}, u32[]{:S(2)}, u32[]{:S(2)}) collective-permute-start(bf16[384,1024]{1,0:T(8,128)(2,1)S(1)} %pad_maximum_fusion.1.near.values), channel_id=1, source_target_pairs={{0,2},{2,0},{1,3},{3,1},{4,6},{6,4},{5,7},{7,5},{8,10},{10,8},{9,1... | collective-permute-start | bytes 2359304 | tf_op jit(solution)/shard_map/ppermute | solution.py:38
  82.4 36.1 %collective-permute-start.18 = (f32[16,1024]{1,0:T(8,128)S(1)}, f32[16,1024]{1,0:T(8,128)S(1)}, u32[]{:S(2)}, u32[]{:S(2)}) collective-permute-start(f32[16,1024]{1,0:T(8,128)S(1)} %add.906), channel_id=1, source_target_pairs={{0,1},{1,0},{2,3},{3,2},{4,5},{5,4},{6,7},{7,6},{8,9},{9,8},{10,11... | collective-permute-start | bytes 196616 | tf_op jit(solution)/shard_map/ppermute | solution.py:41
  105.2 17.7 %collective-permute-start.22 = (bf16[2,12,8,1024]{3,2,1,0:T(8,128)(2,1)S(1)}, bf16[2,12,8,1024]{3,2,1,0:T(8,128)(2,1)S(1)}, u32[]{:S(2)}, u32[]{:S(2)}) collective-permute-start(bf16[2,12,8,1024]{3,2,1,0:T(8,128)(2,1)S(1)} %pad_maximum_fusion.18), channel_id=1, source_target_pairs={{0,1},{1,0},{2,3},{3,2},{4,5},{5,4},{6,7},{7,6},{8,9},{9,8},{10,11... | collective-permute-start | bytes 1179656 | tf_op jit(solution)/shard_map/ppermute | solution.py:41
  106.7 16.2 %collective-permute-start.23 = (bf16[2,12,8,1024]{3,2,1,0:T(8,128)(2,1)S(1)}, bf16[2,12,8,1024]{3,2,1,0:T(8,128)(2,1)S(1)}, u32[]{:S(2)}, u32[]{:S(2)}) collective-permute-start(bf16[2,12,8,1024]{3,2,1,0:T(8,128)(2,1)S(1)} %pad_maximum_fusion.18), channel_id=1, source_target_pairs={{0,4},{4,0},{1,5},{5,1},{2,6},{6,2},{3,7},{7,3},{8,12},{12,8},{9,1... | collective-permute-start | bytes 1179656 | tf_op jit(solution)/shard_map/ppermute | solution.py:44
  118.5 22.2 %collective-permute-start.15 = (bf16[384,1024]{1,0:T(8,128)(2,1)S(1)}, bf16[384,1024]{1,0:T(8,128)(2,1)S(1)}, u32[]{:S(2)}, u32[]{:S(2)}) collective-permute-start(bf16[384,1024]{1,0:T(8,128)(2,1)S(1)} %get-tuple-element.245), channel_id=1, source_target_pairs={{0,2},{2,0},{1,3},{3,1},{4,6},{6,4},{5,7},{7,5},{8,10},{10,8},{9,1... | collective-permute-start | bytes 2359304 | tf_op jit(solution)/shard_map/ppermute | solution.py:38
  122.8 23.3 %collective-permute-start.27 = (bf16[2,24,8,768]{3,2,1,0:T(8,128)(2,1)S(1)}, bf16[2,24,8,768]{3,2,1,0:T(8,128)(2,1)S(1)}, u32[]{:S(2)}, u32[]{:S(2)}) collective-permute-start(bf16[2,24,8,768]{3,2,1,0:T(8,128)(2,1)S(1)} %pad_maximum_fusion.5), channel_id=1, source_target_pairs={{0,1},{1,0},{2,3},{3,2},{4,5},{5,4},{6,7},{7,6},{8,9},{9,8},{10,11... | collective-permute-start | bytes 1769480 | tf_op jit(solution)/shard_map/ppermute | solution.py:41
  123.4 22.7 %collective-permute-start.28 = (bf16[2,24,8,768]{3,2,1,0:T(8,128)(2,1)S(1)}, bf16[2,24,8,768]{3,2,1,0:T(8,128)(2,1)S(1)}, u32[]{:S(2)}, u32[]{:S(2)}) collective-permute-start(bf16[2,24,8,768]{3,2,1,0:T(8,128)(2,1)S(1)} %pad_maximum_fusion.5), channel_id=1, source_target_pairs={{0,4},{4,0},{1,5},{5,1},{2,6},{6,2},{3,7},{7,3},{8,12},{12,8},{9,1... | collective-permute-start | bytes 1769480 | tf_op jit(solution)/shard_map/ppermute | solution.py:44
  124.1 16.4 %collective-permute-start.29 = (bf16[31,8,768]{2,1,0:T(8,128)(2,1)S(1)}, bf16[31,8,768]{2,1,0:T(8,128)(2,1)S(1)}, u32[]{:S(2)}, u32[]{:S(2)}) collective-permute-start(bf16[31,8,768]{2,1,0:T(8,128)(2,1)S(1)} %pad_maximum_fusion.21), channel_id=1, source_target_pairs={{0,16},{8,24},{16,0},{24,8},{1,17},{9,25},{17,1},{25,9},{2,18},{10... | collective-permute-start | bytes 1142792 | tf_op jit(solution)/shard_map/ppermute | solution.py:59
  124.3 21.3 %collective-permute-start.26 = (bf16[2,12,8,1024]{3,2,1,0:T(8,128)(2,1)S(1)}, bf16[2,12,8,1024]{3,2,1,0:T(8,128)(2,1)S(1)}, u32[]{:S(2)}, u32[]{:S(2)}) collective-permute-start(bf16[2,12,8,1024]{3,2,1,0:T(8,128)(2,1)S(1)} %collective-permute-done.22), channel_id=1, source_target_pairs={{0,4},{4,0},{1,5},{5,1},{2,6},{6,2},{3,7},{7,3},{8,12},{12,8},{9,1... | collective-permute-start | bytes 1179656 | tf_op jit(solution)/shard_map/ppermute | solution.py:44
  140.7 33.0 %collective-permute-start.16 = (bf16[240,1024]{1,0:T(8,128)(2,1)S(1)}, bf16[240,1024]{1,0:T(8,128)(2,1)S(1)}, u32[]{:S(2)}, u32[]{:S(2)}) collective-permute-start(bf16[240,1024]{1,0:T(8,128)(2,1)S(1)} %shard_map.357), channel_id=1, source_target_pairs={{0,8},{8,0},{16,24},{24,16},{1,9},{9,1},{17,25},{25,17},{2,10},{10... | collective-permute-start | bytes 1474568 | tf_op jit(solution)/shard_map/ppermute | solution.py:51
  145.8 47.2 %collective-permute-start.34 = (bf16[256,1024]{1,0:T(8,128)(2,1)S(1)}, bf16[256,1024]{1,0:T(8,128)(2,1)S(1)}, u32[]{:S(2)}, u32[]{:S(2)}) collective-permute-start(bf16[256,1024]{1,0:T(8,128)(2,1)S(1)} %bitcast.1047), channel_id=1, source_target_pairs={{0,8},{8,0},{16,24},{24,16},{1,9},{9,1},{17,25},{25,17},{2,10},{10... | collective-permute-start | bytes 1572872 | tf_op jit(solution)/shard_map/ppermute | solution.py:51
  146.2 25.9 %collective-permute-start.41 = (bf16[8,8,1024]{2,1,0:T(8,128)(2,1)S(1)}, bf16[8,8,1024]{2,1,0:T(8,128)(2,1)S(1)}, u32[]{:S(2)}, u32[]{:S(2)}) collective-permute-start(bf16[8,8,1024]{2,1,0:T(8,128)(2,1)S(1)} %maximum_maximum_fusion.1), channel_id=1, source_target_pairs={{0,16},{8,24},{16,0},{24,8},{1,17},{9,25},{17,1},{25,9},{2,18},{10... | collective-permute-start | bytes 393224 | tf_op jit(solution)/shard_map/ppermute | solution.py:59
  147.8 28.1 %collective-permute-start.32 = (bf16[2,24,8,768]{3,2,1,0:T(8,128)(2,1)S(1)}, bf16[2,24,8,768]{3,2,1,0:T(8,128)(2,1)S(1)}, u32[]{:S(2)}, u32[]{:S(2)}) collective-permute-start(bf16[2,24,8,768]{3,2,1,0:T(8,128)(2,1)S(1)} %collective-permute-done.28), channel_id=1, source_target_pairs={{0,1},{1,0},{2,3},{3,2},{4,5},{5,4},{6,7},{7,6},{8,9},{9,8},{10,11... | collective-permute-start | bytes 1769480 | tf_op jit(solution)/shard_map/ppermute | solution.py:41
  149.3 19.4 %collective-permute-start.30 = (f32[16,1024]{1,0:T(8,128)S(1)}, f32[16,1024]{1,0:T(8,128)S(1)}, u32[]{:S(2)}, u32[]{:S(2)}) collective-permute-start(f32[16,1024]{1,0:T(8,128)S(1)} %add.909), channel_id=1, source_target_pairs={{0,16},{8,24},{16,0},{24,8},{1,17},{9,25},{17,1},{25,9},{2,18},{10... | collective-permute-start | bytes 196616 | tf_op jit(solution)/shard_map/ppermute | solution.py:59
  168.7 24.7 %collective-permute-start.33 = (bf16[1024,256]{1,0:T(8,128)(2,1)S(1)}, bf16[1024,256]{1,0:T(8,128)(2,1)S(1)}, u32[]{:S(2)}, u32[]{:S(2)}) collective-permute-start(bf16[1024,256]{1,0:T(8,128)(2,1)S(1)} %bitcast.1050), channel_id=1, source_target_pairs={{0,8},{8,0},{16,24},{24,16},{1,9},{9,1},{17,25},{25,17},{2,10},{10... | collective-permute-start | bytes 1572872 | tf_op jit(solution)/shard_map/ppermute | solution.py:51
  172.1 17.3 %collective-permute-start.39 = (bf16[2,31,8,768]{3,2,1,0:T(8,128)(2,1)S(1)}, bf16[2,31,8,768]{3,2,1,0:T(8,128)(2,1)S(1)}, u32[]{:S(2)}, u32[]{:S(2)}) collective-permute-start(bf16[2,31,8,768]{3,2,1,0:T(8,128)(2,1)S(1)} %pad_maximum_fusion.2), channel_id=1, source_target_pairs={{0,1},{1,0},{2,3},{3,2},{4,5},{5,4},{6,7},{7,6},{8,9},{9,8},{10,11... | collective-permute-start | bytes 2285576 | tf_op jit(solution)/shard_map/ppermute | solution.py:41
  173.8 17.2 %collective-permute-start.40 = (bf16[2,31,8,768]{3,2,1,0:T(8,128)(2,1)S(1)}, bf16[2,31,8,768]{3,2,1,0:T(8,128)(2,1)S(1)}, u32[]{:S(2)}, u32[]{:S(2)}) collective-permute-start(bf16[2,31,8,768]{3,2,1,0:T(8,128)(2,1)S(1)} %pad_maximum_fusion.2), channel_id=1, source_target_pairs={{0,4},{4,0},{1,5},{5,1},{2,6},{6,2},{3,7},{7,3},{8,12},{12,8},{9,1... | collective-permute-start | bytes 2285576 | tf_op jit(solution)/shard_map/ppermute | solution.py:44
  175.9 18.1 %collective-permute-start.31 = (bf16[240,1024]{1,0:T(8,128)(2,1)S(1)}, bf16[240,1024]{1,0:T(8,128)(2,1)S(1)}, u32[]{:S(2)}, u32[]{:S(2)}) collective-permute-start(bf16[240,1024]{1,0:T(8,128)(2,1)S(1)} %get-tuple-element.354.near), channel_id=1, source_target_pairs={{0,2},{2,0},{1,3},{3,1},{4,6},{6,4},{5,7},{7,5},{8,10},{10,8},{9,1... | collective-permute-start | bytes 1474568 | tf_op jit(solution)/shard_map/ppermute | solution.py:38
  193.4 19.4 %collective-permute-start.42 = (bf16[2,31,8,768]{3,2,1,0:T(8,128)(2,1)S(1)}, bf16[2,31,8,768]{3,2,1,0:T(8,128)(2,1)S(1)}, u32[]{:S(2)}, u32[]{:S(2)}) collective-permute-start(bf16[2,31,8,768]{3,2,1,0:T(8,128)(2,1)S(1)} %collective-permute-done.39), channel_id=1, source_target_pairs={{0,4},{4,0},{1,5},{5,1},{2,6},{6,2},{3,7},{7,3},{8,12},{12,8},{9,1... | collective-permute-start | bytes 2285576 | tf_op jit(solution)/shard_map/ppermute | solution.py:44
  212.7 18.7 %collective-permute-start.49 = (bf16[2,24,8,768]{3,2,1,0:T(8,128)(2,1)S(1)}, bf16[2,24,8,768]{3,2,1,0:T(8,128)(2,1)S(1)}, u32[]{:S(2)}, u32[]{:S(2)}) collective-permute-start(bf16[2,24,8,768]{3,2,1,0:T(8,128)(2,1)S(1)} %pad_maximum_fusion.6), channel_id=1, source_target_pairs={{0,1},{1,0},{2,3},{3,2},{4,5},{5,4},{6,7},{7,6},{8,9},{9,8},{10,11... | collective-permute-start | bytes 1769480 | tf_op jit(solution)/shard_map/ppermute | solution.py:41
  213.4 18.1 %collective-permute-start.50 = (bf16[2,24,8,768]{3,2,1,0:T(8,128)(2,1)S(1)}, bf16[2,24,8,768]{3,2,1,0:T(8,128)(2,1)S(1)}, u32[]{:S(2)}, u32[]{:S(2)}) collective-permute-start(bf16[2,24,8,768]{3,2,1,0:T(8,128)(2,1)S(1)} %pad_maximum_fusion.6), channel_id=1, source_target_pairs={{0,4},{4,0},{1,5},{5,1},{2,6},{6,2},{3,7},{7,3},{8,12},{12,8},{9,1... | collective-permute-start | bytes 1769480 | tf_op jit(solution)/shard_map/ppermute | solution.py:44
  214.7 16.7 %collective-permute-start.51 = (bf16[2,8,8,1024]{3,2,1,0:T(8,128)(2,1)S(1)}, bf16[2,8,8,1024]{3,2,1,0:T(8,128)(2,1)S(1)}, u32[]{:S(2)}, u32[]{:S(2)}) collective-permute-start(bf16[2,8,8,1024]{3,2,1,0:T(8,128)(2,1)S(1)} %collective-permute-done.46), channel_id=1, source_target_pairs={{0,1},{1,0},{2,3},{3,2},{4,5},{5,4},{6,7},{7,6},{8,9},{9,8},{10,11... | collective-permute-start | bytes 786440 | tf_op jit(solution)/shard_map/ppermute | solution.py:41
  219.4 25.9 %collective-permute-start.38 = (bf16[384,1024]{1,0:T(8,128)(2,1)S(1)}, bf16[384,1024]{1,0:T(8,128)(2,1)S(1)}, u32[]{:S(2)}, u32[]{:S(2)}) collective-permute-start(bf16[384,1024]{1,0:T(8,128)(2,1)S(1)} %constant_dynamic-update-slice_fusion.8.near), channel_id=1, source_target_pairs={{0,2},{2,0},{1,3},{3,1},{4,6},{6,4},{5,7},{7,5},{8,10},{10,8},{9,1... | collective-permute-start | bytes 2359304 | tf_op jit(solution)/shard_map/ppermute | solution.py:38
  254.4 23.0 %collective-permute-start.53 = (bf16[1024,256]{1,0:T(8,128)(2,1)S(1)}, bf16[1024,256]{1,0:T(8,128)(2,1)S(1)}, u32[]{:S(2)}, u32[]{:S(2)}) collective-permute-start(bf16[1024,256]{1,0:T(8,128)(2,1)S(1)} %bitcast.1053), channel_id=1, source_target_pairs={{0,8},{8,0},{16,24},{24,16},{1,9},{9,1},{17,25},{25,17},{2,10},{10... | collective-permute-start | bytes 1572872 | tf_op jit(solution)/shard_map/ppermute | solution.py:51
  254.4 33.6 %collective-permute-start.54 = (bf16[256,1024]{1,0:T(8,128)(2,1)S(1)}, bf16[256,1024]{1,0:T(8,128)(2,1)S(1)}, u32[]{:S(2)}, u32[]{:S(2)}) collective-permute-start(bf16[256,1024]{1,0:T(8,128)(2,1)S(1)} %bitcast.1056), channel_id=1, source_target_pairs={{0,8},{8,0},{16,24},{24,16},{1,9},{9,1},{17,25},{25,17},{2,10},{10... | collective-permute-start | bytes 1572872 | tf_op jit(solution)/shard_map/ppermute | solution.py:51
  266.6 21.5 %collective-permute-start.45 = (bf16[240,1024]{1,0:T(8,128)(2,1)S(1)}, bf16[240,1024]{1,0:T(8,128)(2,1)S(1)}, u32[]{:S(2)}, u32[]{:S(2)}) collective-permute-start(bf16[240,1024]{1,0:T(8,128)(2,1)S(1)} %get-tuple-element.300.near), channel_id=1, source_target_pairs={{0,2},{2,0},{1,3},{3,1},{4,6},{6,4},{5,7},{7,5},{8,10},{10,8},{9,1... | collective-permute-start | bytes 1474568 | tf_op jit(solution)/shard_map/ppermute | solution.py:38
  325.7 16.0 %collective-permute-start.64 = (bf16[2,24,8,768]{3,2,1,0:T(8,128)(2,1)S(1)}, bf16[2,24,8,768]{3,2,1,0:T(8,128)(2,1)S(1)}, u32[]{:S(2)}, u32[]{:S(2)}) collective-permute-start(bf16[2,24,8,768]{3,2,1,0:T(8,128)(2,1)S(1)} %pad_maximum_fusion.7), channel_id=1, source_target_pairs={{0,4},{4,0},{1,5},{5,1},{2,6},{6,2},{3,7},{7,3},{8,12},{12,8},{9,1... | collective-permute-start | bytes 1769480 | tf_op jit(solution)/shard_map/ppermute | solution.py:44
  338.6 56.5 %collective-permute-start.71 = (bf16[2,24,8,768]{3,2,1,0:T(8,128)(2,1)S(1)}, bf16[2,24,8,768]{3,2,1,0:T(8,128)(2,1)S(1)}, u32[]{:S(2)}, u32[]{:S(2)}) collective-permute-start(bf16[2,24,8,768]{3,2,1,0:T(8,128)(2,1)S(1)} %pad_maximum_fusion.8), channel_id=1, source_target_pairs={{0,4},{4,0},{1,5},{5,1},{2,6},{6,2},{3,7},{7,3},{8,12},{12,8},{9,1... | collective-permute-start | bytes 1769480 | tf_op jit(solution)/shard_map/ppermute | solution.py:44
  339.6 38.1 %collective-permute-start.66 = (bf16[1024,256]{1,0:T(8,128)(2,1)S(1)}, bf16[1024,256]{1,0:T(8,128)(2,1)S(1)}, u32[]{:S(2)}, u32[]{:S(2)}) collective-permute-start(bf16[1024,256]{1,0:T(8,128)(2,1)S(1)} %copy-done.66), channel_id=1, source_target_pairs={{0,8},{8,0},{16,24},{24,16},{1,9},{9,1},{17,25},{25,17},{2,10},{10... | collective-permute-start | bytes 1572872 | tf_op jit(solution)/shard_map/ppermute | solution.py:51
  341.4 36.4 %collective-permute-start.67 = (bf16[256,1024]{1,0:T(8,128)(2,1)S(1)}, bf16[256,1024]{1,0:T(8,128)(2,1)S(1)}, u32[]{:S(2)}, u32[]{:S(2)}) collective-permute-start(bf16[256,1024]{1,0:T(8,128)(2,1)S(1)} %copy-done.64), channel_id=1, source_target_pairs={{0,8},{8,0},{16,24},{24,16},{1,9},{9,1},{17,25},{25,17},{2,10},{10... | collective-permute-start | bytes 1572872 | tf_op jit(solution)/shard_map/ppermute | solution.py:51
  341.8 54.0 %collective-permute-start.70 = (bf16[2,24,8,768]{3,2,1,0:T(8,128)(2,1)S(1)}, bf16[2,24,8,768]{3,2,1,0:T(8,128)(2,1)S(1)}, u32[]{:S(2)}, u32[]{:S(2)}) collective-permute-start(bf16[2,24,8,768]{3,2,1,0:T(8,128)(2,1)S(1)} %add_convert_fusion.6), channel_id=1, source_target_pairs={{0,1},{1,0},{2,3},{3,2},{4,5},{5,4},{6,7},{7,6},{8,9},{9,8},{10,11... | collective-permute-start | bytes 1769480 | tf_op jit(solution)/shard_map/ppermute | solution.py:41
  343.8 31.5 %collective-permute-start.65 = (bf16[240,1024]{1,0:T(8,128)(2,1)S(1)}, bf16[240,1024]{1,0:T(8,128)(2,1)S(1)}, u32[]{:S(2)}, u32[]{:S(2)}) collective-permute-start(bf16[240,1024]{1,0:T(8,128)(2,1)S(1)} %shard_map.374), channel_id=1, source_target_pairs={{0,8},{8,0},{16,24},{24,16},{1,9},{9,1},{17,25},{25,17},{2,10},{10... | collective-permute-start | bytes 1474568 | tf_op jit(solution)/shard_map/ppermute | solution.py:51
  375.3 18.1 %collective-permute-start.72 = (bf16[2,31,8,768]{3,2,1,0:T(8,128)(2,1)S(1)}, bf16[2,31,8,768]{3,2,1,0:T(8,128)(2,1)S(1)}, u32[]{:S(2)}, u32[]{:S(2)}) collective-permute-start(bf16[2,31,8,768]{3,2,1,0:T(8,128)(2,1)S(1)} %pad_maximum_fusion.3), channel_id=1, source_target_pairs={{0,1},{1,0},{2,3},{3,2},{4,5},{5,4},{6,7},{7,6},{8,9},{9,8},{10,11... | collective-permute-start | bytes 2285576 | tf_op jit(solution)/shard_map/ppermute | solution.py:41
  379.5 22.8 %collective-permute-start.74 = (bf16[2,12,8,1024]{3,2,1,0:T(8,128)(2,1)S(1)}, bf16[2,12,8,1024]{3,2,1,0:T(8,128)(2,1)S(1)}, u32[]{:S(2)}, u32[]{:S(2)}) collective-permute-start(bf16[2,12,8,1024]{3,2,1,0:T(8,128)(2,1)S(1)} %pad_maximum_fusion.19), channel_id=1, source_target_pairs={{0,4},{4,0},{1,5},{5,1},{2,6},{6,2},{3,7},{7,3},{8,12},{12,8},{9,1... | collective-permute-start | bytes 1179656 | tf_op jit(solution)/shard_map/ppermute | solution.py:44
  393.4 32.3 %collective-permute-start.78 = (bf16[2,31,8,768]{3,2,1,0:T(8,128)(2,1)S(1)}, bf16[2,31,8,768]{3,2,1,0:T(8,128)(2,1)S(1)}, u32[]{:S(2)}, u32[]{:S(2)}) collective-permute-start(bf16[2,31,8,768]{3,2,1,0:T(8,128)(2,1)S(1)} %pad_maximum_fusion.4), channel_id=1, source_target_pairs={{0,1},{1,0},{2,3},{3,2},{4,5},{5,4},{6,7},{7,6},{8,9},{9,8},{10,11... | collective-permute-start | bytes 2285576 | tf_op jit(solution)/shard_map/ppermute | solution.py:41
  395.1 31.5 %collective-permute-start.82 = (bf16[2,12,8,1024]{3,2,1,0:T(8,128)(2,1)S(1)}, bf16[2,12,8,1024]{3,2,1,0:T(8,128)(2,1)S(1)}, u32[]{:S(2)}, u32[]{:S(2)}) collective-permute-start(bf16[2,12,8,1024]{3,2,1,0:T(8,128)(2,1)S(1)} %pad_maximum_fusion.20), channel_id=1, source_target_pairs={{0,4},{4,0},{1,5},{5,1},{2,6},{6,2},{3,7},{7,3},{8,12},{12,8},{9,1... | collective-permute-start | bytes 1179656 | tf_op jit(solution)/shard_map/ppermute | solution.py:44
  397.9 28.2 %collective-permute-start.79 = (bf16[2,31,8,768]{3,2,1,0:T(8,128)(2,1)S(1)}, bf16[2,31,8,768]{3,2,1,0:T(8,128)(2,1)S(1)}, u32[]{:S(2)}, u32[]{:S(2)}) collective-permute-start(bf16[2,31,8,768]{3,2,1,0:T(8,128)(2,1)S(1)} %add_convert_fusion.2), channel_id=1, source_target_pairs={{0,4},{4,0},{1,5},{5,1},{2,6},{6,2},{3,7},{7,3},{8,12},{12,8},{9,1... | collective-permute-start | bytes 2285576 | tf_op jit(solution)/shard_map/ppermute | solution.py:44
  409.5 16.2 %collective-permute-start.80 = (bf16[2,24,8,768]{3,2,1,0:T(8,128)(2,1)S(1)}, bf16[2,24,8,768]{3,2,1,0:T(8,128)(2,1)S(1)}, u32[]{:S(2)}, u32[]{:S(2)}) collective-permute-start(bf16[2,24,8,768]{3,2,1,0:T(8,128)(2,1)S(1)} %pad_maximum_fusion.9), channel_id=1, source_target_pairs={{0,1},{1,0},{2,3},{3,2},{4,5},{5,4},{6,7},{7,6},{8,9},{9,8},{10,11... | collective-permute-start | bytes 1769480 | tf_op jit(solution)/shard_map/ppermute | solution.py:41
  411.5 58.2 %collective-permute-start.89 = (bf16[2,24,8,768]{3,2,1,0:T(8,128)(2,1)S(1)}, bf16[2,24,8,768]{3,2,1,0:T(8,128)(2,1)S(1)}, u32[]{:S(2)}, u32[]{:S(2)}) collective-permute-start(bf16[2,24,8,768]{3,2,1,0:T(8,128)(2,1)S(1)} %pad_maximum_fusion.10), channel_id=1, source_target_pairs={{0,1},{1,0},{2,3},{3,2},{4,5},{5,4},{6,7},{7,6},{8,9},{9,8},{10,11... | collective-permute-start | bytes 1769480 | tf_op jit(solution)/shard_map/ppermute | solution.py:41
  425.7 26.6 %collective-permute-start.108 = (f32[16,1024]{1,0:T(8,128)S(1)}, f32[16,1024]{1,0:T(8,128)S(1)}, u32[]{:S(2)}, u32[]{:S(2)}) collective-permute-start(f32[16,1024]{1,0:T(8,128)S(1)} %pad_maximum_fusion.54), channel_id=1, source_target_pairs={{0,2},{2,0},{1,3},{3,1},{4,6},{6,4},{5,7},{7,5},{8,10},{10,8},{9,1... | collective-permute-start | bytes 196616 | tf_op jit(solution)/shard_map/ppermute | solution.py:38
  425.7 20.6 %collective-permute-start.81 = (bf16[2,12,8,1024]{3,2,1,0:T(8,128)(2,1)S(1)}, bf16[2,12,8,1024]{3,2,1,0:T(8,128)(2,1)S(1)}, u32[]{:S(2)}, u32[]{:S(2)}) collective-permute-start(bf16[2,12,8,1024]{3,2,1,0:T(8,128)(2,1)S(1)} %add_convert_fusion.15), channel_id=1, source_target_pairs={{0,1},{1,0},{2,3},{3,2},{4,5},{5,4},{6,7},{7,6},{8,9},{9,8},{10,11... | collective-permute-start | bytes 1179656 | tf_op jit(solution)/shard_map/ppermute | solution.py:41
  426.1 20.7 %collective-permute-start.77 = (bf16[384,1024]{1,0:T(8,128)(2,1)S(1)}, bf16[384,1024]{1,0:T(8,128)(2,1)S(1)}, u32[]{:S(2)}, u32[]{:S(2)}) collective-permute-start(bf16[384,1024]{1,0:T(8,128)(2,1)S(1)} %get-tuple-element.372), channel_id=1, source_target_pairs={{0,2},{2,0},{1,3},{3,1},{4,6},{6,4},{5,7},{7,5},{8,10},{10,8},{9,1... | collective-permute-start | bytes 2359304 | tf_op jit(solution)/shard_map/ppermute | solution.py:38
  426.6 26.7 %collective-permute-start.103 = (bf16[31,8,768]{2,1,0:T(8,128)(2,1)S(1)}, bf16[31,8,768]{2,1,0:T(8,128)(2,1)S(1)}, u32[]{:S(2)}, u32[]{:S(2)}) collective-permute-start(bf16[31,8,768]{2,1,0:T(8,128)(2,1)S(1)} %dynamic-slice_bitcast_fusion.13), channel_id=1, source_target_pairs={{0,16},{8,24},{16,0},{24,8},{1,17},{9,25},{17,1},{25,9},{2,18},{10... | collective-permute-start | bytes 1142792 | tf_op jit(solution)/shard_map/ppermute | solution.py:59
  452.3 21.7 %collective-permute-start.90 = (bf16[2,24,8,768]{3,2,1,0:T(8,128)(2,1)S(1)}, bf16[2,24,8,768]{3,2,1,0:T(8,128)(2,1)S(1)}, u32[]{:S(2)}, u32[]{:S(2)}) collective-permute-start(bf16[2,24,8,768]{3,2,1,0:T(8,128)(2,1)S(1)} %add_convert_fusion.5), channel_id=1, source_target_pairs={{0,4},{4,0},{1,5},{5,1},{2,6},{6,2},{3,7},{7,3},{8,12},{12,8},{9,1... | collective-permute-start | bytes 1769480 | tf_op jit(solution)/shard_map/ppermute | solution.py:44
  453.4 22.5 %collective-permute-start.92 = (bf16[1024,256]{1,0:T(8,128)(2,1)S(1)}, bf16[1024,256]{1,0:T(8,128)(2,1)S(1)}, u32[]{:S(2)}, u32[]{:S(2)}) collective-permute-start(bf16[1024,256]{1,0:T(8,128)(2,1)S(1)} %get-tuple-element.399), channel_id=1, source_target_pairs={{0,8},{8,0},{16,24},{24,16},{1,9},{9,1},{17,25},{25,17},{2,10},{10... | collective-permute-start | bytes 1572872 | tf_op jit(solution)/shard_map/ppermute | solution.py:51
  462.7 27.4 %collective-permute-start.93 = (bf16[256,1024]{1,0:T(8,128)(2,1)S(1)}, bf16[256,1024]{1,0:T(8,128)(2,1)S(1)}, u32[]{:S(2)}, u32[]{:S(2)}) collective-permute-start(bf16[256,1024]{1,0:T(8,128)(2,1)S(1)} %get-tuple-element.400), channel_id=1, source_target_pairs={{0,8},{8,0},{16,24},{24,16},{1,9},{9,1},{17,25},{25,17},{2,10},{10... | collective-permute-start | bytes 1572872 | tf_op jit(solution)/shard_map/ppermute | solution.py:51
  468.7 23.7 %collective-permute-start.102 = (bf16[24,8,768]{2,1,0:T(8,128)(2,1)S(1)}, bf16[24,8,768]{2,1,0:T(8,128)(2,1)S(1)}, u32[]{:S(2)}, u32[]{:S(2)}) collective-permute-start(bf16[24,8,768]{2,1,0:T(8,128)(2,1)S(1)} %dynamic-slice_bitcast_fusion.23), channel_id=1, source_target_pairs={{0,16},{8,24},{16,0},{24,8},{1,17},{9,25},{17,1},{25,9},{2,18},{10... | collective-permute-start | bytes 884744 | tf_op jit(solution)/shard_map/ppermute | solution.py:59
  469.7 24.7 %collective-permute-start.104 = (bf16[12,8,1024]{2,1,0:T(8,128)(2,1)S(1)}, bf16[12,8,1024]{2,1,0:T(8,128)(2,1)S(1)}, u32[]{:S(2)}, u32[]{:S(2)}) collective-permute-start(bf16[12,8,1024]{2,1,0:T(8,128)(2,1)S(1)} %dynamic-slice_bitcast_fusion.48), channel_id=1, source_target_pairs={{0,16},{8,24},{16,0},{24,8},{1,17},{9,25},{17,1},{25,9},{2,18},{10... | collective-permute-start | bytes 589832 | tf_op jit(solution)/shard_map/ppermute | solution.py:59
  474.0 36.7 %collective-permute-start.83 = (bf16[240,1024]{1,0:T(8,128)(2,1)S(1)}, bf16[240,1024]{1,0:T(8,128)(2,1)S(1)}, u32[]{:S(2)}, u32[]{:S(2)}) collective-permute-start(bf16[240,1024]{1,0:T(8,128)(2,1)S(1)} %shard_map.382), channel_id=1, source_target_pairs={{0,8},{8,0},{16,24},{24,16},{1,9},{9,1},{17,25},{25,17},{2,10},{10... | collective-permute-start | bytes 1474568 | tf_op jit(solution)/shard_map/ppermute | solution.py:51
  475.9 43.5 %collective-permute-start.110 = (f32[16,1024]{1,0:T(8,128)S(1)}, f32[16,1024]{1,0:T(8,128)S(1)}, u32[]{:S(2)}, u32[]{:S(2)}) collective-permute-start(f32[16,1024]{1,0:T(8,128)S(1)} %add.958), channel_id=1, source_target_pairs={{0,4},{4,0},{1,5},{5,1},{2,6},{6,2},{3,7},{7,3},{8,12},{12,8},{9,1... | collective-permute-start | bytes 196616 | tf_op jit(solution)/shard_map/ppermute | solution.py:44
  490.1 19.0 %collective-permute-start.87 = (bf16[2,32,8,768]{3,2,1,0:T(8,128)(2,1)S(1)}, bf16[2,32,8,768]{3,2,1,0:T(8,128)(2,1)S(1)}, u32[]{:S(2)}, u32[]{:S(2)}) collective-permute-start(bf16[2,32,8,768]{3,2,1,0:T(8,128)(2,1)S(1)} %fusion.5), channel_id=1, source_target_pairs={{0,4},{4,0},{1,5},{5,1},{2,6},{6,2},{3,7},{7,3},{8,12},{12,8},{9,1... | collective-permute-start | bytes 2359304 | tf_op jit(solution)/shard_map/ppermute | solution.py:44
  492.4 16.8 %collective-permute-start.85 = (bf16[2,32,8,768]{3,2,1,0:T(8,128)(2,1)S(1)}, bf16[2,32,8,768]{3,2,1,0:T(8,128)(2,1)S(1)}, u32[]{:S(2)}, u32[]{:S(2)}) collective-permute-start(bf16[2,32,8,768]{3,2,1,0:T(8,128)(2,1)S(1)} %fusion.7), channel_id=1, source_target_pairs={{0,1},{1,0},{2,3},{3,2},{4,5},{5,4},{6,7},{7,6},{8,9},{9,8},{10,11... | collective-permute-start | bytes 2359304 | tf_op jit(solution)/shard_map/ppermute | solution.py:41
  510.8 26.1 %collective-permute-start.88 = (bf16[32,8,768]{2,1,0:T(8,128)(2,1)S(1)}, bf16[32,8,768]{2,1,0:T(8,128)(2,1)S(1)}, u32[]{:S(2)}, u32[]{:S(2)}) collective-permute-start(bf16[32,8,768]{2,1,0:T(8,128)(2,1)S(1)} %dynamic-slice_bitcast_fusion.5), channel_id=1, source_target_pairs={{0,16},{8,24},{16,0},{24,8},{1,17},{9,25},{17,1},{25,9},{2,18},{10... | collective-permute-start | bytes 1179656 | tf_op jit(solution)/shard_map/ppermute | solution.py:59
  516.6 20.3 %collective-permute-start.97 = (bf16[2,12,8,1024]{3,2,1,0:T(8,128)(2,1)S(1)}, bf16[2,12,8,1024]{3,2,1,0:T(8,128)(2,1)S(1)}, u32[]{:S(2)}, u32[]{:S(2)}) collective-permute-start(bf16[2,12,8,1024]{3,2,1,0:T(8,128)(2,1)S(1)} %fusion.40), channel_id=1, source_target_pairs={{0,4},{4,0},{1,5},{5,1},{2,6},{6,2},{3,7},{7,3},{8,12},{12,8},{9,1... | collective-permute-start | bytes 1179656 | tf_op jit(solution)/shard_map/ppermute | solution.py:44
  518.3 18.6 %collective-permute-start.96 = (bf16[2,12,8,1024]{3,2,1,0:T(8,128)(2,1)S(1)}, bf16[2,12,8,1024]{3,2,1,0:T(8,128)(2,1)S(1)}, u32[]{:S(2)}, u32[]{:S(2)}) collective-permute-start(bf16[2,12,8,1024]{3,2,1,0:T(8,128)(2,1)S(1)} %fusion.35), channel_id=1, source_target_pairs={{0,1},{1,0},{2,3},{3,2},{4,5},{5,4},{6,7},{7,6},{8,9},{9,8},{10,11... | collective-permute-start | bytes 1179656 | tf_op jit(solution)/shard_map/ppermute | solution.py:41
  519.5 40.1 %collective-permute-start.107 = (bf16[184,1024]{1,0:T(8,128)(2,1)S(1)}, bf16[184,1024]{1,0:T(8,128)(2,1)S(1)}, u32[]{:S(2)}, u32[]{:S(2)}) collective-permute-start(bf16[184,1024]{1,0:T(8,128)(2,1)S(1)} %fusion.45), channel_id=1, source_target_pairs={{0,0},{1,1},{2,16},{3,17},{4,4},{5,5},{6,20},{7,21},{8,8},{9,9},{1... | collective-permute-start | bytes 1130504 | tf_op jit(solution)/shard_map/ppermute | solution.py:70
  522.0 15.4 %collective-permute-start.111 = (f32[16,1024]{1,0:T(8,128)S(1)}, f32[16,1024]{1,0:T(8,128)S(1)}, u32[]{:S(2)}, u32[]{:S(2)}) collective-permute-start(f32[16,1024]{1,0:T(8,128)S(1)} %add.959), channel_id=1, source_target_pairs={{0,8},{8,0},{16,24},{24,16},{1,9},{9,1},{17,25},{25,17},{2,10},{10... | collective-permute-start | bytes 196616 | tf_op jit(solution)/shard_map/ppermute | solution.py:51
  (177 other events, 1180.5 us)

commit v5 on v4

--- a/solution.py
+++ b/solution.py
@@ -14,25 +14,17 @@
 EPS = 1e-06
 F32 = jnp.float32
 BF16 = jnp.bfloat16
-ALL = ("z", "y", "core", "x")
+ALL = ("far", "near", "low", "y", "core", "x")
 FLIP = ((0, 1), (1, 0))
 TEAM = 4
 PIECE = 8
 
 
 class Grid:
-    def __init__(self, depth):
-        self.depth, self.rest = depth, depth // 4
-        self.y, self.core, self.x = (lax.axis_index(name) for name in ALL[1:])
-        z = lax.axis_index("z")
-        self.near = z // self.rest % 2
-        self.column = z // (2 * self.rest) * self.rest + z % self.rest
-
-    def split(self, z):
-        return z // (2 * self.rest), z // self.rest % 2, z % self.rest
-
-    def join(self, far, near, low):
-        return (far * 2 + near) * self.rest + low
+    def __init__(self, rest):
+        self.rest = rest
+        self.far, self.near, self.low, self.y, self.core, self.x = (lax.axis_index(name) for name in ALL)
+        self.column = self.far * rest + self.low
 
     def to_core(self, value):
         return lax.ppermute(value, "core", FLIP)
@@ -44,30 +36,14 @@
         return lax.ppermute(value, "y", FLIP)
 
     def to_near(self, value):
-        pairs = []
-        for z in range(self.depth):
-            far, near, low = self.split(z)
-            pairs.append((z, self.join(far, 1 - near, low)))
-        return lax.ppermute(value, "z", pairs)
+        return lax.ppermute(value, "near", FLIP)
 
     def to_column(self, value, step):
-        pairs = []
-        for z in range(self.depth):
-            far, near, low = self.split(z)
-            column = (far * self.rest + low + step) % (2 * self.rest)
-            pairs.append((z, self.join(column // self.rest, near, column % self.rest)))
-        return lax.ppermute(value, "z", pairs)
+        columns = 2 * self.rest
+        return lax.ppermute(value, ("far", "low"), [(c, (c + step) % columns) for c in range(columns)])
 
     def swap_far(self, value):
-        pairs = []
-        for z in range(self.depth):
-            far, near, low = self.split(z)
-            for y in range(2):
-                for core in range(2):
-                    for x in range(2):
-                        there = ((self.join(core, near, low) * 2 + y) * 2 + far) * 2 + x
-                        pairs.append((((z * 2 + y) * 2 + core) * 2 + x, there))
-        return lax.ppermute(value, ALL, pairs)
+        return lax.ppermute(value, ("far", "core"), ((0, 0), (1, 2), (2, 1), (3, 3)))
 
 
 def pick(value, index, axis):
@@ -203,9 +179,9 @@
                 self.blocks[i] = jnp.stack(places)
             self.gate += got
 
-    def full(self, i):
+    def full(self, i, gate=None):
         grid, bundle, parts = self.grid, self.bundles[i], self.parts
-        corner = joined(self.corners[i], 1)
+        corner = joined(self.corners[i] if gate is None else after(gate, self.corners[i]), 1)
         full, at = {}, 0
         for name in bundle.names:
             shape = parts[name].shape
@@ -289,7 +265,7 @@
                 r = k // (rest * 8)
                 self.views.append(grads[name].reshape(rest, 2, 2, 2, r, c))
                 self.shapes.append((1, r, c))
-        self.next()
+        self.names = list(bundle.names)
 
     def block(self, y, x):
         pieces = []
@@ -301,9 +277,11 @@
             pieces.append(self.bundle.flat(value.reshape(2 * self.grid.rest, p, r, c)))
         return joined(pieces, 1)
 
-    def next(self, gate=None):
-        if gate is not None:
+    def next(self, gate):
+        if self.step:
             self.got = after(gate, self.got)
+        else:
+            self.views = after(gate, self.views)
         step, self.step = self.step, self.step + 1
         (self.corner, self.side, self.column)[step]()
 
@@ -348,7 +326,7 @@
         for give in gives:
             got = give.got if gate is None else after(gate, give.got)
             total, at = plus(give.mine, *got), 0
-            for name, shape in zip(give.bundle.names, give.shapes):
+            for name, shape in zip(give.names, give.shapes):
                 n = give.bundle.count(shape)
                 part = give.bundle.unflat(total[at : at + n], shape)
                 if name in GROUPS:
@@ -388,11 +366,11 @@
     def __init__(self, lt, kt, li, ki):
         self.lt, self.kt, self.li, self.ki = lt, kt, li, ki
         self.third, self.tall, self.left = kt // 3, lt * 3 // 4, lt // 4
-        self.rows = li + 2 * self.tall
-        self.wide_rows = self.rows + li
-
-    def text(self, ref, r, base=None):
-        base = (self.li if base is None else base) + r * self.tall
+        self.below = li + 2 * self.tall
+        self.rows = self.below + li
+
+    def text(self, ref, r):
+        base = self.li + r * self.tall
         top = ref[pl.ds(base, self.tall), : self.kt]
         last = [ref[pl.ds(base + j * self.left, self.left), self.kt :] for j in range(3)]
         return jnp.concatenate([top, jnp.concatenate(last, 1)], 0)
@@ -406,10 +384,10 @@
             ref[pl.ds(base + j * self.left, self.left), self.kt :] = block
 
     def image(self, ref, r=0):
-        return ref[pl.ds(r * self.rows, self.li), :]
+        return ref[pl.ds(r * self.below, self.li), :]
 
     def put_image(self, ref, image, r=0):
-        ref[pl.ds(r * self.rows, self.li), :] = image.astype(ref.dtype)
+        ref[pl.ds(r * self.below, self.li), :] = image.astype(ref.dtype)
 
     def pack_rows(self, text, image):
         last = text[self.tall :]
@@ -421,21 +399,19 @@
         last = [rows[j * self.left : (j + 1) * self.left, self.kt :] for j in range(3)]
         return jnp.concatenate([rows[:, : self.kt], jnp.concatenate(last, 1)], 0)
 
-    def both(self, near, far, wide=False):
+    def both(self, near, far):
         text = [self.text(ref, r) for ref in (near, far) for r in range(2)]
-        image = [self.image(ref, r) for ref in (near, far) for r in range(2 if wide else 1)]
+        image = [self.image(ref, r) for ref in (near, far) for r in range(2)]
         return jnp.concatenate(text, 0), jnp.concatenate(image, 0)
 
     def put_sums(self, home, away, text, image):
         for r in range(TEAM):
-            self.put_text((home, away)[r // 2], r % 2, text[r * self.lt : (r + 1) * self.lt])
-        count = image.shape[0] // self.li
-        for r in range(count):
-            part = image[r * self.li : (r + 1) * self.li]
-            self.put_image((home, away)[r * 2 // count], part, r % (count // 2))
-
-    def sums(self, wide=False):
-        shape = (self.wide_rows if wide else self.rows, self.ki)
+            ref = (home, away)[r // 2]
+            self.put_text(ref, r % 2, text[r * self.lt : (r + 1) * self.lt])
+            self.put_image(ref, image[r * self.li : (r + 1) * self.li], r % 2)
+
+    def sums(self):
+        shape = (self.rows, self.ki)
         return [(shape, F32), (shape, BF16)]
 
 
@@ -471,52 +447,48 @@
     return 0.5 * (1.0 + lax.erf(v * (0.5**0.5))) + v * jnp.exp(-0.5 * v * v) * (0.5 / jnp.pi) ** 0.5
 
 
-def ffn_kernel(near, far, ut, dt, ui, di, uj, dj, before_t, hidden_t, before_i, hidden_i, home, away, *, s):
+def ffn_kernel(near, far, ut, dt, ui, di, before_t, hidden_t, before_i, hidden_i, home, away, *, s):
     text, image = s.both(near, far)
-    pre = mm(text, ut[...])
-    before_t[...] = pre
-    act = gelu(pre).astype(BF16)
-    hidden_t[...] = act
-    text_sums, image_sums = mm(act, dt[...]), 0.0
-    f = ui.shape[1]
-    for part, (up, down) in enumerate(((ui, di), (uj, dj))):
-        at = pl.ds(part * f, f)
-        pre = mm(image, up[...])
-        before_i[:, at] = pre
+    sums = []
+    for low, up, down, before, hidden in (
+        (text, ut, dt, before_t, hidden_t),
+        (image, ui, di, before_i, hidden_i),
+    ):
+        pre = mm(low, up[...])
+        before[...] = pre
         act = gelu(pre).astype(BF16)
-        hidden_i[:, at] = act
-        image_sums = image_sums + mm(act, down[...])
-    s.put_sums(home, away, text_sums, image_sums)
-
-
-def ffn(s, low, ut, dt, *image_w):
-    ft, fi = ut.shape[1], 2 * image_w[0].shape[1]
+        hidden[...] = act
+        sums.append(mm(act, down[...]))
+    s.put_sums(home, away, *sums)
+
+
+def ffn(s, low, ut, dt, ui, di):
+    ft, fi = ut.shape[1], ui.shape[1]
     outs = []
-    for length, f in ((TEAM * s.lt, ft), (2 * s.li, fi)):
+    for length, f in ((TEAM * s.lt, ft), (TEAM * s.li, fi)):
         outs += [((length, f), F32), ((length, f), BF16)]
     flops = 16 * (s.lt * s.kt * ft + s.li * s.ki * fi)
-    return kernel(partial(ffn_kernel, s=s), outs + s.sums(), (*low, ut, dt, *image_w), flops)
-
-
-def ffn_back_kernel(near, far, before_t, before_i, ut, dt, ui, di, uj, dj, bg_t, bg_i, home, away, *, s):
+    return kernel(partial(ffn_kernel, s=s), outs + s.sums(), (*low, ut, dt, ui, di), flops)
+
+
+def ffn_back_kernel(near, far, before_t, before_i, ut, dt, ui, di, bg_t, bg_i, home, away, *, s):
     text, image = s.both(near, far)
-    grad = (mm_bt(text, dt[...]) * gelu_slope(before_t[...])).astype(BF16)
-    bg_t[...] = grad
-    text_sums, image_sums = mm_bt(grad, ut[...]), 0.0
-    f = ui.shape[1]
-    for part, (up, down) in enumerate(((ui, di), (uj, dj))):
-        at = pl.ds(part * f, f)
-        grad = (mm_bt(image, down[...]) * gelu_slope(before_i[:, at])).astype(BF16)
-        bg_i[:, at] = grad
-        image_sums = image_sums + mm_bt(grad, up[...])
-    s.put_sums(home, away, text_sums, image_sums)
-
-
-def ffn_back(s, out, before_t, before_i, ut, dt, *image_w):
-    ft, fi = ut.shape[1], 2 * image_w[0].shape[1]
-    outs = [((TEAM * s.lt, ft), BF16), ((2 * s.li, fi), BF16)] + s.sums()
+    sums = []
+    for out, before, up, down, bg in (
+        (text, before_t, ut, dt, bg_t),
+        (image, before_i, ui, di, bg_i),
+    ):
+        grad = (mm_bt(out, down[...]) * gelu_slope(before[...])).astype(BF16)
+        bg[...] = grad
+        sums.append(mm_bt(grad, up[...]))
+    s.put_sums(home, away, *sums)
+
+
+def ffn_back(s, out, before_t, before_i, ut, dt, ui, di):
+    ft, fi = ut.shape[1], ui.shape[1]
+    outs = [((TEAM * s.lt, ft), BF16), ((TEAM * s.li, fi), BF16)] + s.sums()
     flops = 16 * (s.lt * s.kt * ft + s.li * s.ki * fi)
-    args = (*out, before_t, before_i, ut, dt, *image_w)
+    args = (*out, before_t, before_i, ut, dt, ui, di)
     return kernel(partial(ffn_back_kernel, s=s), outs, args, flops)
 
 
@@ -558,7 +530,7 @@
 
 
 def self_kernel(near, far, wt, wot, wi, woi, col, row, qkv_t, ctx_t, qkv_i, ctx_i, home, away, *, s, size, heads):
-    text, image = s.both(near, far, True)
+    text, image = s.both(near, far)
     qkv_t[...] = mm(text, wt[...]).astype(BF16)
     qkv_i[...] = mm(image, wi[...]).astype(BF16)
     wide = ctx_t.shape[1]
@@ -593,7 +565,7 @@
 
 
 def self_attention(s, low, wt, wot, wi, woi, col, row, size, heads):
-    outs = attention_outs(s, wt, wi) + s.sums(True)
+    outs = attention_outs(s, wt, wi) + s.sums()
     args = (*low, wt, wot, wi, woi, col, row)
     return kernel(partial(self_kernel, s=s, size=size, heads=heads), outs, args, attention_flops(s, wt, wi))
 
@@ -601,7 +573,7 @@
 def self_back_kernel(
     near, far, wt, wot, wi, woi, col, row, qkv_t, qkv_i, dqkv_t, dqkv_i, home, away, dctx_t, dctx_i, *, s, size, heads
 ):
-    text, image = s.both(near, far, True)
+    text, image = s.both(near, far)
     dctx_t[...] = mm_bt(text, wot[...]).astype(BF16)
     dctx_i[...] = mm_bt(image, woi[...]).astype(BF16)
     wide = dctx_t.shape[1]
@@ -632,7 +604,7 @@
 
 
 def back_outs(s, wt, wi):
-    outs = [((TEAM * s.lt, wt.shape[1]), BF16), ((TEAM * s.li, wi.shape[1]), BF16)] + s.sums(True)
+    outs = [((TEAM * s.lt, wt.shape[1]), BF16), ((TEAM * s.li, wi.shape[1]), BF16)] + s.sums()
     scratch = [((TEAM * s.lt, wt.shape[1] // 3), BF16), ((TEAM * s.li, wi.shape[1] // 3), BF16)]
     return outs, scratch
 
@@ -656,7 +628,7 @@
 def co_kernel(
     near, far, wt, wot, wi, woi, seg_col, seg_row, qkv_t, ctx_t, qkv_i, ctx_i, home, away, *, s
 ):
-    text, image = s.both(near, far, True)
+    text, image = s.both(near, far)
     qkv_t[...] = mm(text, wt[...]).astype(BF16)
     qkv_i[...] = mm(image, wi[...]).astype(BF16)
     wide = ctx_t.shape[1]
@@ -671,7 +643,7 @@
 
 
 def co_attention(s, low, wt, wot, wi, woi, seg_col, seg_row):
-    outs = attention_outs(s, wt, wi) + s.sums(True)
+    outs = attention_outs(s, wt, wi) + s.sums()
     args = (*low, wt, wot, wi, woi, seg_col, seg_row)
     return kernel(partial(co_kernel, s=s), outs, args, attention_flops(s, wt, wi))
 
@@ -679,7 +651,7 @@
 def co_back_kernel(
     near, far, wt, wot, wi, woi, seg_col, seg_row, qkv_t, qkv_i, dqkv_t, dqkv_i, home, away, dctx_t, dctx_i, *, s
 ):
-    text, image = s.both(near, far, True)
+    text, image = s.both(near, far)
     dctx_t[...] = mm_bt(text, wot[...]).astype(BF16)
     dctx_i[...] = mm_bt(image, woi[...]).astype(BF16)
     wide = dctx_t.shape[1]
@@ -707,78 +679,59 @@
     return kernel(partial(co_back_kernel, s=s), outs, args, attention_flops(s, wt, wi), scratch)
 
 
-def weight_kernel(near, far, out_near, out_far, mid_t, grad_t, mid_i, grad_i, *outs, s, wide, parts):
-    text, image = s.both(near, far, wide)
-    text_out, image_out = s.both(out_near, out_far, wide)
-    outs[0][...] = mm_at(text, grad_t[...]).astype(BF16)
-    outs[1][...] = mm_at(mid_t[...], text_out).astype(BF16)
-    grad, mid = grad_i.shape[1] // parts, mid_i.shape[1] // parts
-    for part in range(parts):
-        at = grad_i[:, pl.ds(part * grad, grad)]
-        outs[2 + 2 * part][...] = mm_at(image, at).astype(BF16)
-        at = mid_i[:, pl.ds(part * mid, mid)]
-        outs[3 + 2 * part][...] = mm_at(at, image_out).astype(BF16)
-
-
-def weight_grads(s, low, out, mid_t, grad_t, mid_i, grad_i, parts):
-    outs = [((s.kt, grad_t.shape[1]), BF16), ((mid_t.shape[1], s.kt), BF16)]
-    for _ in range(parts):
-        outs += [((s.ki, grad_i.shape[1] // parts), BF16), ((mid_i.shape[1] // parts, s.ki), BF16)]
+def weight_kernel(near, far, out_near, out_far, mid_t, grad_t, mid_i, grad_i, in_t, out_t, in_i, out_i, *, s):
+    text, image = s.both(near, far)
+    in_t[...] = mm_at(text, grad_t[...]).astype(BF16)
+    in_i[...] = mm_at(image, grad_i[...]).astype(BF16)
+    text, image = s.both(out_near, out_far)
+    out_t[...] = mm_at(mid_t[...], text).astype(BF16)
+    out_i[...] = mm_at(mid_i[...], image).astype(BF16)
+
+
+def weight_grads(s, low, out, mid_t, grad_t, mid_i, grad_i):
+    outs = []
+    for k, mid, grad in ((s.kt, mid_t, grad_t), (s.ki, mid_i, grad_i)):
+        outs += [((k, grad.shape[1]), BF16), ((mid.shape[1], k), BF16)]
     flops = sum(8 * s.lt * shape[0] * shape[1] for shape, _ in outs)
     args = (*low, *out, mid_t, grad_t, mid_i, grad_i)
-    return kernel(partial(weight_kernel, s=s, wide=parts == 1, parts=parts), outs, args, flops)
-
-
-def fold_kernel(home, got, out, *, s):
-    text = pl.ds(s.li, 2 * s.tall)
-    sums = (home[text, :] + got[text, :].astype(F32)).astype(BF16)
-    if out.shape[0] == 2 * s.tall:
-        out[...] = sums
-    else:
-        out[pl.ds(0, s.li), :] = (s.image(home, 1) + s.image(got, 1).astype(F32)).astype(BF16)
-        out[text, :] = sums
+    return kernel(partial(weight_kernel, s=s), outs, args, flops)
+
+
+def fold_kernel(home, got, out):
+    out[...] = (home[...] + got[...].astype(F32)).astype(BF16)
 
 
 def fold(s, home, got):
-    rows = s.rows if home.shape[0] > s.rows else 2 * s.tall
-    body = partial(fold_kernel, s=s)
-    return kernel(body, [((rows, s.ki), BF16)], (home, got), home.size)[0]
-
-
-def settled_text(s, base, home, got, other, r):
-    start = s.li if other.shape[0] == s.rows else 0
-    value = s.text(base, r).astype(F32) + s.text(home, r) + s.text(got, r).astype(F32)
-    return value + s.text(other, 1 - r, start).astype(F32)
-
-
-def settled_image(s, base, home, got, other):
-    value = s.image(base).astype(F32) + s.image(home) + s.image(got).astype(F32)
-    return value + s.image(other).astype(F32) if other.shape[0] == s.rows else value
+    return kernel(fold_kernel, [((s.rows, s.ki), BF16)], (home, got), home.size)[0]
+
+
+def settled(read, base, home, got, other, r):
+    return read(base, r).astype(F32) + read(home, r) + read(got, r).astype(F32) + read(other, 1 - r).astype(F32)
+
+
+def streams(s, params, i, k):
+    return (
+        (s.text, lambda ref, r, v: s.put_text(ref, r, v), params[pl.ds(4 * k + i, 1), : s.kt], 2 * s.li, s.lt),
+        (s.image, lambda ref, r, v: s.put_image(ref, v, r), params[pl.ds(8 + 4 * k + i, 1), :], 0, s.li),
+    )
 
 
 def norm_kernel(values, home, got, other, params, out, low, normed, inverse, *, s, i):
-    def one(v, gain, shift, start):
-        centred = v - jnp.mean(v, -1, keepdims=True)
-        inv = lax.rsqrt(jnp.mean(centred * centred, -1, keepdims=True) + EPS)
-        n = centred * inv
-        inverse[pl.ds(start, v.shape[0]), :] = inv
-        return n, n * gain + shift
-
-    param = lambda k, width: params[pl.ds(4 * k + i, 1), :width]
-    for r in range(2):
-        v = settled_text(s, values, home, got, other, r)
-        n, y = one(v, param(0, s.kt), param(1, s.kt), s.li + r * s.lt)
-        for ref, value in ((normed, n), (out, y), (low, y)):
-            s.put_text(ref, r, value)
-    v = settled_image(s, values, home, got, other)
-    n, y = one(v, param(2, s.ki), param(3, s.ki), 0)
-    for ref, value in ((normed, n), (out, y), (low, y)):
-        s.put_image(ref, value)
+    for (read, put, gain, start, length), (_, _, shift, _, _) in zip(streams(s, params, i, 0), streams(s, params, i, 1)):
+        for r in range(2):
+            v = settled(read, values, home, got, other, r)
+            centred = v - jnp.mean(v, -1, keepdims=True)
+            inv = lax.rsqrt(jnp.mean(centred * centred, -1, keepdims=True) + EPS)
+            n = centred * inv
+            inverse[pl.ds(start + r * length, length), :] = inv
+            y = n * gain + shift
+            for ref, value in ((normed, n), (out, y), (low, y)):
+                put(ref, r, value)
 
 
 def norm(s, values, sums, params, i):
     pack = (s.rows, s.ki)
-    outs = [(pack, F32), (pack, BF16), (pack, F32), ((s.li + 2 * s.lt, 1), F32)]
+    outs = [(pack, F32), (pack, BF16), (pack, F32), ((2 * s.li + 2 * s.lt, 1), F32)]
     y, low, *stored = kernel(partial(norm_kernel, s=s, i=i), outs, (values, *sums, params), 32 * s.rows * s.ki)
     return y, low, stored
 
@@ -788,33 +741,21 @@
         up, normed, inverse, params, grad, low, sums = refs
     else:
         up, home, got, other, normed, inverse, params, grad, low, sums = refs
-
-    def one(u, n, gain, start):
-        scaled = u * gain
-        return inverse[pl.ds(start, u.shape[0]), :] * (
-            scaled - jnp.mean(scaled, -1, keepdims=True) - n * jnp.mean(scaled * n, -1, keepdims=True)
-        )
-
-    def keep(k, u, n):
-        width = u.shape[1]
-        sums[pl.ds(k, 1), :width] = jnp.sum(u * n, axis=0, keepdims=True)
-        sums[pl.ds(k + 1, 1), :width] = jnp.sum(u, axis=0, keepdims=True)
-
     sums[...] = jnp.zeros(sums.shape, F32)
-    for r in range(2):
-        u = s.text(up, r).astype(F32) if first else settled_text(s, up, home, got, other, r)
-        n = s.text(normed, r)
-        value = one(u, n, params[pl.ds(i, 1), : s.kt], s.li + r * s.lt)
-        s.put_text(grad, r, value)
-        s.put_text(low, r, value)
-        if r == 0:
-            keep(0, u, n)
-    u = s.image(up).astype(F32) if first else settled_image(s, up, home, got, other)
-    n = s.image(normed)
-    value = one(u, n, params[pl.ds(8 + i, 1), :], 0)
-    s.put_image(grad, value)
-    s.put_image(low, value)
-    keep(2, u, n)
+    for stream, (read, put, gain, start, length) in enumerate(streams(s, params, i, 0)):
+        for r in range(2):
+            u = read(up, r).astype(F32) if first else settled(read, up, home, got, other, r)
+            n = read(normed, r)
+            scaled = u * gain
+            value = inverse[pl.ds(start + r * length, length), :] * (
+                scaled - jnp.mean(scaled, -1, keepdims=True) - n * jnp.mean(scaled * n, -1, keepdims=True)
+            )
+            put(grad, r, value)
+            put(low, r, value)
+            if r == 0:
+                width = u.shape[1]
+                sums[pl.ds(2 * stream, 1), :width] = jnp.sum(u * n, axis=0, keepdims=True)
+                sums[pl.ds(2 * stream + 1, 1), :width] = jnp.sum(u, axis=0, keepdims=True)
 
 
 def norm_back(s, upstream, sums, stored, params, i):
@@ -856,10 +797,9 @@
     image_shifts,
     grad_text_out,
     grad_image_out,
-    depth,
+    rest,
 ):
-    grid = Grid(depth)
-    rest = grid.rest
+    grid = Grid(rest)
     tw, iw = text_gains.shape[2], image_gains.shape[2]
     s = Sizes(*text_in.shape[1:], *image_in.shape[1:])
     weights = {
@@ -883,23 +823,20 @@
 
     weights["icoa"] = image_co_out[0][:, : FETCH[0].width]
     weights["icob"] = widen(image_co_out[0][:, FETCH[0].width :], FETCH[0].width)
-    place = ((lax.axis_index("z") * 2 + grid.y) * 2 + grid.core) * 2 + grid.x
-    params = jnp.zeros((16, s.ki), F32)
+    place = ((((grid.far * 2 + grid.near) * rest + grid.low) * 2 + grid.y) * 2 + grid.core) * 2 + grid.x
+    params = jnp.zeros((16, s.ki), BF16)
     for at, k, kinds in ((0, tw, (text_gains, text_shifts)), (8, iw, (image_gains, image_shifts))):
-        own = jnp.concatenate([a[0] for a in kinds]).astype(F32)
+        own = jnp.concatenate([a[0] for a in kinds])
         params = lax.dynamic_update_slice(params, own, (at, place * k))
     width = FETCH[0].width
     widths = {name: weights[name].shape[1] for name in GROUPS}
     quads = {name: quarters(weights[name], groups) for name, groups in GROUPS.items()}
-    early = ("tci", "ici")
-    late = ("tu0", "tsi", "isi", "tu1", "iu0", "iu1")
     parts = {}
 
     def trade(names):
-        got, arrived = trade_ins(grid, [quads[n] for n in names])
+        got, _ = trade_ins(grid, [quads[n] for n in names])
         for n, q in zip(names, got):
             parts[n] = q.reshape((TEAM,) + q.shape[2:])
-        return arrived
 
     def swap(names):
         swapped, at = grid.swap_far(joined([weights[n] for n in names], 0)), 0
@@ -908,43 +845,49 @@
             parts[n] = swapped[at : at + r][None]
             at += r
 
-    trade(early)
+    def pair(own):
+        return own, grid.to_core(own)
+
+    trade(("tci", "ici"))
     swap(("tco", "icoa", "icob"))
-    fetch = Gather(grid, FETCH, parts)
-    fetch.round([("z", 0)])
-    names = ("td0", "tso", "td1", "id0", "iso", "id1")
-    inputs = (text_in, image_in, text_segments, grad_text_out, grad_image_out, params)
-    later = {n: quads[n] for n in late}, {n: weights[n] for n in names}, inputs
-    quarters_later, weights_later, inputs = after(fetch.gate, later)
-    quads.update(quarters_later)
-    weights.update(weights_later)
-    text_in, image_in, text_segments, grad_text_out, grad_image_out, params = inputs
-    trade(late)
-    swap(("id0", "iso", "id1"))
-    swap(("td0", "tso", "td1"))
-    fetch.round([("xy", 0)])
-    moved = grid.to_core(params)
+    segments = text_segments.astype(F32)
+    segments = jnp.concatenate(pair(jnp.concatenate([segments, grid.to_near(segments)])))
+    params = params + grid.to_x(params)
+    params = params + grid.to_y(params)
+    params = params + grid.to_core(params)
 
     def more(move):
         nonlocal params, moved
         params = params + after(fetch.gate, moved)
         moved = move(params)
 
-    def pair(own):
-        return own, grid.to_core(own)
-
-    segments = text_segments.astype(F32)
-    segments = jnp.concatenate(pair(jnp.concatenate([segments, grid.to_near(segments)])))
+    fetch = Gather(grid, FETCH, parts)
+    moved = grid.to_near(params)
+    fetch.round([("z", 0)])
+
+    def later(ins, outs, *inputs):
+        new = {n: quads[n] for n in ins}, {n: weights[n] for n in sum(outs, ())}, inputs
+        new_quads, new_weights, inputs = after(fetch.gate, new)
+        quads.update(new_quads)
+        weights.update(new_weights)
+        trade(ins)
+        for names in outs:
+            swap(names)
+        return inputs
+
+    text_in, image_in = later(
+        ("iu0", "tu0", "tsi", "isi", "iu1", "tu1"), (("id0", "iso", "id1"), ("td0", "tso", "td1")), text_in, image_in
+    )
+    own = s.pack_rows(text_in[0], image_in[0])
+    got = grid.to_near(own)
+    values = jnp.concatenate([own, got[s.li :], got[: s.li]])
+    low0 = pair(values)
+    fetch.round([("xy", 0)])
+
     seg_col = segments.reshape(-1, 1)
     ids = segments + 2.0 * jnp.arange(TEAM, dtype=F32)[:, None]
     id_col, id_row = ids.reshape(-1, 1), ids.reshape(1, -1)
     size, heads = s.kt // HT, HT // TEAM
-    own = s.pack_rows(text_in[0], image_in[0])
-    got = grid.to_near(own)
-    values = jnp.concatenate([own, got[s.li :], got[: s.li]])
-    low0 = pair(values)
-    own = s.pack_rows(grad_text_out[0], grad_image_out[0])
-    upstream = jnp.concatenate([own, grid.to_near(own[s.li :])])
 
     def settle(home, away):
         got = grid.to_core(away)
@@ -953,48 +896,41 @@
     def normal(values, sums, i):
         return norm(s, values, sums, params, i)
 
-    def widened(low):
-        return jnp.concatenate([low, grid.to_near(low[: s.li])])
-
-    def near_pairs(*names):
-        for name in names:
-            yield full[name]
-        for name in names:
-            yield grid.to_near(full[name])
-
-    more(grid.to_x)
+    more(lambda value: sum((grid.to_column(value, k) for k in range(2, 2 * rest)), grid.to_column(value, 1)))
     fetch.round([("c", 0), ("z", 1)])
+    params = (params + after(fetch.gate, moved)).astype(F32)
+    grad_text_out, grad_image_out = after(fetch.gate, (grad_text_out, grad_image_out))
+    own = s.pack_rows(grad_text_out[0], grad_image_out[0])
+    got = grid.to_near(own)
+    upstream = jnp.concatenate([own, got[s.li :], got[: s.li]])
     full = fetch.full(0)
     full["ico"] = jnp.concatenate([full["icoa"], full["icob"][:, : s.ki - width]], 1)
     co_w = [full[n] for n in ("tci", "tco", "ici", "ico")]
-    more(grid.to_y)
     fetch.round([("xy", 1), ("z", 2)])
     qkv_t, ctx_t, qkv_i, ctx_i, home, away = co_attention(s, low0, *co_w, seg_col, segments)
-    more(grid.to_near)
     fetch.round([("c", 1), ("xy", 2), ("z", 3)], away)
-    full.update(fetch.full(1))
     sums = settle(home, away)
-    more(lambda value: sum((grid.to_column(value, k) for k in range(2, 2 * rest)), grid.to_column(value, 1)))
-    params = params + moved
+    full.update(fetch.full(1, sums[1]))
     y, low, stored0 = normal(values, sums, 0)
     low1 = pair(low)
     fetch.round([("c", 2), ("xy", 3), ("z", 4)], sums[1])
-    full.update(fetch.full(2))
-    ffn_w = [[full["tu0"], full["td0"], *near_pairs("iu0", "id0")]]
+    full.update(fetch.full(2, low))
+    ffn_w = [[full["tu0"], full["td0"], full["iu0"], full["id0"]]]
+    before_t0, hidden_t0, before_i0, hidden_i0, home, away = ffn(s, low1, *ffn_w[0])
     fetch.round([("c", 3), ("xy", 4), ("z", 5)], low)
-    full.update(fetch.full(3))
+    full.update(fetch.full(3, away))
     full["tso"] = jnp.pad(full["tso"], ((0, full["tsi"].shape[1] // 3 - full["tso"].shape[0]), (0, 0)))
     self_w = [full[n] for n in ("tsi", "tso", "isi", "iso")]
-    before_t0, hidden_t0, before_i0, hidden_i0, home, away = ffn(s, low1, *ffn_w[0])
     fetch.round([("c", 4), ("xy", 5)], away)
-    full.update(fetch.full(4))
     y, low, stored1 = normal(y, settle(home, away), 1)
+    low2 = pair(low)
+    sqkv_t, sctx_t, sqkv_i, sctx_i, home, away = self_attention(s, low2, *self_w, id_col, id_row, size, heads)
     fetch.round([("c", 5)], low)
-    full.update(fetch.full(5))
-    low2 = pair(widened(low))
-    ffn_w.append([full["tu1"], full["td1"], *near_pairs("iu1", "id1")])
-    sqkv_t, sctx_t, sqkv_i, sctx_i, home, away = self_attention(s, low2, *self_w, id_col, id_row, size, heads)
-    y, low, stored2 = normal(y, settle(home, away), 2)
+    full.update(fetch.full(4, away))
+    sums = settle(home, away)
+    full.update(fetch.full(5, sums[1]))
+    ffn_w.append([full["tu1"], full["td1"], full["iu1"], full["id1"]])
+    y, low, stored2 = normal(y, sums, 2)
     low3 = pair(low)
     before_t1, hidden_t1, before_i1, hidden_i1, home, away = ffn(s, low3, *ffn_w[1])
     _, last, stored3 = normal(y, settle(home, away), 3)
@@ -1005,106 +941,100 @@
         grad, low, norm_grads[i] = norm_back(s, upstream, sums, stored, params, i)
         return grad, low if due is None else after(due, low)
 
-    def weigh(names, home, away, low, out, *mids, parts=1, due=None):
+    def weigh(names, home, away, low, out, *mids, due=None):
         got = grid.to_core(away)
         if due is not None:
             got = after(due, got)
         folded = fold(s, home, got)
         low, out, mids = after(folded, (low, out, mids))
-        values = weight_grads(s, low, out, *mids, parts)
+        values = weight_grads(s, low, out, *mids)
         grads.update(zip(names, values))
-        return (home, got, grid.to_near(folded)), values[0], values[4:]
+        return home, got, folded, values[0]
 
     def give(names, wide, turn="both"):
         return Give(grid, Bundle(names, wide, turn), grads)
 
-    def send_near(values, gate):
-        return [grid.to_near(v) for v in after(gate, values)]
-
-    def join_near(names, came, gate):
-        for name, value in zip(names, after(gate, came)):
-            grads[name] = plus(grads[name], value)
+    arrived = ()
+
+    def steps(*gives, also=()):
+        nonlocal arrived
+        gate = arrived, also
+        for each in gives:
+            each.next(gate)
+        arrived = tuple(each.got for each in gives)
 
     g, low = normal_back(upstream, None, stored3, 3)
     out = pair(low)
     bg_t, bg_i, home, away = ffn_back(s, out, before_t1, before_i1, *ffn_w[1])
-    sums, weighed, others = weigh(
-        ("tu1", "td1", "iu1", "id1"), home, away, low3, out, hidden_t1, bg_t, hidden_i1, bg_i, parts=2
+    home, got, folded, weighed = weigh(
+        ("tu1", "td1", "iu1", "id1"), home, away, low3, out, hidden_t1, bg_t, hidden_i1, bg_i
     )
+    other = grid.to_near(folded)
+
     text3 = give(["tu1", "td1"], width, "y")
-
-    g, low = normal_back(g, sums, stored2, 2, weighed)
-    across = grid.to_near(low[: s.li])
-    came = send_near(others, across)
-    out = pair(jnp.concatenate([low, across]))
+    steps(text3, also=weighed)
+
+    g, low = normal_back(g, (home, got, other), stored2, 2, (weighed, text3.got))
+    out = pair(low)
     dqkv_t, dqkv_i, home, away = self_back(s, out, *self_w, id_col, id_row, sqkv_t, sqkv_i, size, heads)
-    sums, weighed, _ = weigh(
-        ("tsi", "tso", "isi", "iso"), home, away, low2, out, sctx_t, dqkv_t, sctx_i, dqkv_i, due=text3.got
+    home, got, folded, weighed = weigh(
+        ("tsi", "tso", "isi", "iso"), home, away, low2, out, sctx_t, dqkv_t, sctx_i, dqkv_i
     )
-    text3.next(away)
+    other = grid.to_near(folded)
     grads["tso"] = grads["tso"][: size * heads]
     text2 = give(["tsi", "isi", "tso"], width, "x")
-
-    g, low = normal_back(g, sums, stored1, 1, (weighed, came))
-    join_near(("iu1", "id1"), came, low)
+    text3.next(folded)
+    text2.next(weighed)
+
+    g, low = normal_back(g, (home, got, other), stored1, 1, (weighed, text3.got))
     image3 = give(["id1", "iu1", "iso"], s.ki, "y")
+    text3.next(low)
+    image3.next(low)
     out = pair(low)
     bg_t, bg_i, home, away = ffn_back(s, out, before_t0, before_i0, *ffn_w[0])
-    sums, weighed, others = weigh(
-        ("tu0", "td0", "iu0", "id0"), home, away, low1, out, hidden_t0, bg_t, hidden_i0, bg_i,
-        parts=2, due=(text3.got, text2.got),
+    home, got, folded, weighed = weigh(
+        ("tu0", "td0", "iu0", "id0"), home, away, low1, out, hidden_t0, bg_t, hidden_i0, bg_i
     )
-    text3.next(away)
-    text2.next(away)
-    text1 = give(["tu0", "td0"], width, "x")
-
-    g, low = normal_back(g, sums, stored0, 0, (weighed, image3.got))
-    across = grid.to_near(low[: s.li])
-    came = send_near(others, across)
-    out = pair(jnp.concatenate([low, across]))
-    image3.next(low)
+    other = grid.to_near(folded)
+    text1 = give(["tu0", "td0"], width, "y")
+    text1.next(weighed)
+
+    g, low = normal_back(g, (home, got, other), stored0, 0, (weighed, text3.got, text2.got, image3.got, text1.got))
+    steps(text2, image3, also=low)
+    out = pair(low)
     norm_sums = jnp.concatenate(norm_grads)
     moved = grid.to_core(norm_sums)
     dqkv_t, dqkv_i, home, away = co_back(s, out, *co_w, seg_col, segments, qkv_t, qkv_i)
     norm_sums = norm_sums + after(away, moved)
     moved = grid.to_x(norm_sums)
-    sums, weighed, _ = weigh(
-        ("tci", "tco", "ici", "ico"), home, away, low0, out, ctx_t, dqkv_t, ctx_i, dqkv_i,
-        due=(text2.got, text1.got, image3.got),
+    home, got, folded, weighed = weigh(
+        ("tci", "tco", "ici", "ico"), home, away, low0, out, ctx_t, dqkv_t, ctx_i, dqkv_i
     )
     text0 = give(["tci", "ici", "tco"], width)
-    text2.next(away)
-    text1.next(away)
-    image3.next(away)
-    home, got, other = sums
-
-    gate = text0.got
-    text0.next()
-    join_near(("iu0", "id0"), came, gate)
-    image1 = give(["id0", "iu0", "ico"], s.ki)
-    text1.next(gate)
-    first = Deliver(grid, [text3, text2, image3], widths, gate)
-    norm_sums = norm_sums + after(gate, moved)
-    moved = grid.to_y(norm_sums)
-    gate = text0.got
-    text0.next()
-    image1.next(gate)
-    first.core(gate)
-    norm_sums = norm_sums + after(gate, moved)
+    image1 = give(["id0", "iu0", "ico"], s.ki, "y")
+
+    other = grid.to_near(after(weighed, folded))
+    steps(text0, text2, text1, image1, also=weighed)
+    arrived = arrived, other
+    norm_sums = norm_sums + after(arrived, moved)
+    steps(text0, image1, image3, text1)
+    moved = grid.to_y(after(arrived, norm_sums))
+    first = Deliver(grid, [text3, text2, image3], widths, arrived)
+    steps(text0, image1)
+    first.core(arrived)
+    norm_sums = norm_sums + after(arrived, moved)
     moved = grid.to_near(norm_sums)
+    second = Deliver(grid, [text0, text1, image1], widths, arrived)
+    done = first.finish(second.got)
+    norm_sums = norm_sums + after(second.got, moved)
+    moved = [grid.to_column(norm_sums, k) for k in range(1, 2 * rest)]
+    other = after(second.got, other)
     mine = slice(0, s.li + s.tall)
-    other = after(gate, other)
     sums = g[mine] + home[mine] + got[mine].astype(F32)
-    sums = sums + jnp.concatenate([other[: s.li], other[s.li + s.tall :]]).astype(F32)
-    gate = text0.got
-    image1.next(gate)
-    norm_sums = norm_sums + after(gate, moved)
-    moved = [grid.to_column(norm_sums, k) for k in range(1, 2 * rest)]
-    done = first.finish(gate)
-    last_two = Deliver(grid, [text0, text1, image1], widths)
-    norm_sums = sum(after(last_two.got, moved), norm_sums).reshape(4, 4, s.ki)
-    last_two.core()
-    done.update(last_two.finish())
+    sums = sums + jnp.concatenate([other[s.below :], other[s.li + s.tall : s.below]]).astype(F32)
+    second.core()
+    norm_sums = sum(after(second.got, moved), norm_sums).reshape(4, 4, s.ki)
+    done.update(second.finish())
     norm_outs = [
         lax.dynamic_slice(norm_sums[:, i], (0, place * k), (4, k))[None]
         for i, k in enumerate((tw, tw, iw, iw))
@@ -1128,14 +1058,14 @@
 
 
 def solution(mesh):
-    depth = mesh.shape["wide"] // 4
-    fine = Mesh(mesh.devices.reshape(depth, 2, 2, mesh.shape["narrow"]), ALL)
+    rest = mesh.shape["wide"] // 16
+    fine = Mesh(mesh.devices.reshape(2, 2, rest, 2, 2, mesh.shape["narrow"]), ALL)
     rows = P(ALL, None, None)
     weight = P(None, ALL, None)
     pair = P(None, None, ALL, None)
     norm = P(None, None, ALL)
     return jax.shard_map(
-        partial(shards, depth=depth),
+        partial(shards, rest=rest),
         mesh=fine,
         in_specs=(rows, rows, P(ALL, None), *[weight] * 8, *[pair] * 4, *[norm] * 4, rows, rows),
         out_specs=(rows, rows, rows, rows, *[weight] * 8, *[pair] * 4, *[norm] * 4),

time: 574 us -> 539 us (0.939)
  starting transfers between devices: 120 us -> 84.2 us
  waiting for transfers between devices: 323 us -> 314 us
  Pallas kernels: 52 us -> 59.9 us
    ppermute x47 -> x36, starting transfers between devices: 63.6 us -> 30.8 us  [the longest x17 16.3 us: to_near(): return lax.ppermute(value, 'near', FLIP)]
    ppermute x22 -> x20, waiting for transfers between devices: 71.3 us -> 43.4 us  [to_x(): return lax.ppermute(value, 'x', FLIP)]
    ppermute x21 -> x22, waiting for transfers between devices: 24.2 us -> 42.3 us  [to_y(): return lax.ppermute(value, 'y', FLIP)]
    unnamed x257 -> x296, local copies, waits for them, and re-layouts: 10.8 us -> 27.1 us
    pallas_call x28, Pallas kernels: 50.2 us -> 58.1 us  [kernel(): pl.pallas_call(body, out_shape=outs, scratch_shapes=[pltpu.VMEM(shape, ki...]
    ppermute x23, waiting for transfers between devices: 8.38 us -> 14.2 us  [to_core(): return lax.ppermute(value, 'core', FLIP)]
    ppermute x47 -> x36, waiting for transfers between devices: 220 us -> 214 us  [the longest x17 108 us: to_near(): return lax.ppermute(value, 'near', FLIP)]
    ppermute x22 -> x20, starting transfers between devices: 22.5 us -> 23 us  [to_x(): return lax.ppermute(value, 'x', FLIP)]
  transfers between devices with their start and end apart: 113 -> 101, of which waited for: 50 -> 45; matrix products, arithmetic and copies ran while one was open for 9% -> 6% of each run, Pallas kernels for 7% -> 7%
where the time goes in v5:
time: 539 us; the launch traced here: 534 us
  waiting for transfers between devices  314 us (58%)
  starting transfers between devices  84.2 us (16%)
  Pallas kernels  59.9 us (11%)
  local copies, waits for them, and re-layouts  50.8 us (9%)
  other arithmetic  20.4 us (4%)
    ppermute x17, waiting for transfers between devices, to_near(): return lax.ppermute(value, 'near', FLIP)  108 us
    ppermute x14, waiting for transfers between devices, to_column(): lax.ppermute(value, ('far', 'low'), [(c, (c + step) % columns) for c in r...  105 us
    pallas_call x28, Pallas kernels, kernel(): pl.pallas_call(body, out_shape=outs, scratch_shapes=[pltpu.VMEM(shape, ki...  58.1 us
    ppermute x20, waiting for transfers between devices, to_x(): return lax.ppermute(value, 'x', FLIP)  43.4 us
    ppermute x22, waiting for transfers between devices, to_y(): return lax.ppermute(value, 'y', FLIP)  42.3 us
    unnamed x296, local copies, waits for them, and re-layouts  27.1 us
    ppermute x20, starting transfers between devices, to_x(): return lax.ppermute(value, 'x', FLIP)  23 us
    ppermute x22, starting transfers between devices, to_y(): return lax.ppermute(value, 'y', FLIP)  22.1 us
  transfers between devices with their start and end apart: 101, of which 45 were waited for; matrix products, arithmetic and copies ran while one was open for 6% of the time, Pallas kernels for 7%

profile of v5, /device:TPU:0, one launch (start us, length us, event | category | flops | bytes accessed | tf_op | source)
XLA Modules:
  0.0 534.1 jit_solution(3708155438131168907)
XLA Ops:
  2.7 3.1 collective-permute-start
  7.4 2.4 collective-permute-start.17
  11.4 3.4 collective-permute-start.1
  20.6 2.1 collective-permute-done.18
  24.7 1.6 collective-permute-start.20
  26.3 14.8 %collective-permute-done.3 = bf16[40,8,768]{2,1,0:T(8,128)(2,1)S(1)} collective-permute-done((bf16[40,8,768]{2,1,0:T(8,128)(2,1)S(1)}, bf16[40,8,768]{2,1,0:T(8,128)(2,1)S(1)}, u32[]{:S(2)}, u32[]{:S(2)}) %collective-permute-start.3) | collective-permute-done | bytes 491552 | tf_op jit(solution)/shard_map/ppermute | solution.py:43
  46.8 2.1 collective-permute-start.4
  48.9 23.4 %collective-permute-done.4 = bf16[192,1024]{1,0:T(8,128)(2,1)S(1)} collective-permute-done((bf16[192,1024]{1,0:T(8,128)(2,1)S(1)}, bf16[192,1024]{1,0:T(8,128)(2,1)S(1)}, u32[]{:S(2)}, u32[]{:S(2)}) %collective-permute-start.4) | collective-permute-done | bytes 393248 | tf_op jit(solution)/shard_map/ppermute | solution.py:39
  72.7 2.2 collective-permute-start.10
  78.8 2.4 collective-permute-start.22
  81.3 9.3 %collective-permute-done.22 = bf16[12,8,1024]{2,1,0:T(8,128)(2,1)S(1)} collective-permute-done((bf16[12,8,1024]{2,1,0:T(8,128)(2,1)S(1)}, bf16[12,8,1024]{2,1,0:T(8,128)(2,1)S(1)}, u32[]{:S(2)}, u32[]{:S(2)}) %collective-permute-start.22) | collective-permute-done | bytes 196640 | tf_op jit(solution)/shard_map/ppermute | solution.py:43
  93.6 2.1 collective-permute-start.26
  99.3 4.9 shard_map.356
  104.5 3.5 collective-permute-done.26
  111.0 15.1 %collective-permute-done.30 = bf16[31,8,768]{2,1,0:T(8,128)(2,1)S(1)} collective-permute-done((bf16[31,8,768]{2,1,0:T(8,128)(2,1)S(1)}, bf16[31,8,768]{2,1,0:T(8,128)(2,1)S(1)}, u32[]{:S(2)}, u32[]{:S(2)}) %collective-permute-start.30) | collective-permute-done | bytes 380960 | tf_op jit(solution)/shard_map/ppermute | solution.py:43
  126.5 5.5 %collective-permute-done.31 = bf16[2,12,8,1024]{3,2,1,0:T(8,128)(2,1)S(1)} collective-permute-done((bf16[2,12,8,1024]{3,2,1,0:T(8,128)(2,1)S(1)}, bf16[2,12,8,1024]{3,2,1,0:T(8,128)(2,1)S(1)}, u32[]{:S(2)}, u32[]{:S(2)}) %collective-permute-start.31) | collective-permute-done | bytes 393248 | tf_op jit(solution)/shard_map/ppermute | solution.py:36
  132.5 1.7 collective-permute-start.36
  135.8 10.7 %collective-permute-done.38 = bf16[8,8,1024]{2,1,0:T(8,128)(2,1)S(1)} collective-permute-done((bf16[8,8,1024]{2,1,0:T(8,128)(2,1)S(1)}, bf16[8,8,1024]{2,1,0:T(8,128)(2,1)S(1)}, u32[]{:S(2)}, u32[]{:S(2)}) %collective-permute-start.38) | collective-permute-done | bytes 131104 | tf_op jit(solution)/shard_map/ppermute | solution.py:43
  146.6 2.1 collective-permute-done.16.other
  149.7 13.3 %collective-permute-done.32 = bf16[2,24,8,768]{3,2,1,0:T(8,128)(2,1)S(1)} collective-permute-done((bf16[2,24,8,768]{3,2,1,0:T(8,128)(2,1)S(1)}, bf16[2,24,8,768]{3,2,1,0:T(8,128)(2,1)S(1)}, u32[]{:S(2)}, u32[]{:S(2)}) %collective-permute-start.32) | collective-permute-done | bytes 589856 | tf_op jit(solution)/shard_map/ppermute | solution.py:33
  167.5 2.2 shard_map.359
  173.9 4.1 collective-permute-done.44
  178.1 8.0 %collective-permute-done.39 = bf16[2,31,8,768]{3,2,1,0:T(8,128)(2,1)S(1)} collective-permute-done((bf16[2,31,8,768]{3,2,1,0:T(8,128)(2,1)S(1)}, bf16[2,31,8,768]{3,2,1,0:T(8,128)(2,1)S(1)}, u32[]{:S(2)}, u32[]{:S(2)}) %collective-permute-start.39) | collective-permute-done | bytes 761888 | tf_op jit(solution)/shard_map/ppermute | solution.py:36
  186.2 1.9 collective-permute-start.46
  188.5 6.2 %collective-permute-done.34.other = bf16[384,1024]{1,0:T(8,128)(2,1)S(1)} collective-permute-done((bf16[384,1024]{1,0:T(8,128)(2,1)S(1)}, bf16[384,1024]{1,0:T(8,128)(2,1)S(1)}, u32[]{:S(2)}, u32[]{:S(2)}) %collective-permute-start.34) | collective-permute-done | bytes 786464 | tf_op jit(solution)/shard_map/ppermute | solution.py:39
  198.7 3.6 shard_map.362
  203.6 7.7 %collective-permute-done.48 = bf16[2,8,8,1024]{3,2,1,0:T(8,128)(2,1)S(1)} collective-permute-done((bf16[2,8,8,1024]{3,2,1,0:T(8,128)(2,1)S(1)}, bf16[2,8,8,1024]{3,2,1,0:T(8,128)(2,1)S(1)}, u32[]{:S(2)}, u32[]{:S(2)}) %collective-permute-start.48) | collective-permute-done | bytes 262176 | tf_op jit(solution)/shard_map/ppermute | solution.py:33
  212.5 13.7 %collective-permute-done.49 = bf16[2,24,8,768]{3,2,1,0:T(8,128)(2,1)S(1)} collective-permute-done((bf16[2,24,8,768]{3,2,1,0:T(8,128)(2,1)S(1)}, bf16[2,24,8,768]{3,2,1,0:T(8,128)(2,1)S(1)}, u32[]{:S(2)}, u32[]{:S(2)}) %collective-permute-start.49) | collective-permute-done | bytes 589856 | tf_op jit(solution)/shard_map/ppermute | solution.py:33
  226.2 4.7 collective-permute-done.41.other
  234.1 2.0 shard_map.365
  237.7 2.1 collective-permute-done.50.got
  242.2 25.9 %collective-permute-done.52 = bf16[192,1024]{1,0:T(8,128)(2,1)S(1)} collective-permute-done((bf16[192,1024]{1,0:T(8,128)(2,1)S(1)}, bf16[192,1024]{1,0:T(8,128)(2,1)S(1)}, u32[]{:S(2)}, u32[]{:S(2)}) %collective-permute-start.52) | collective-permute-done | bytes 393248 | tf_op jit(solution)/shard_map/ppermute | solution.py:39
  268.2 2.0 shard_map.367
  271.4 2.3 collective-permute-done.53.far.out_far
  273.7 3.0 shard_map.369
  279.4 2.5 collective-permute-done.54.got.refs_2_
  289.3 1.6 shard_map.372
  293.2 11.3 %collective-permute-done.55.refs_3_ = bf16[384,1024]{1,0:T(8,128)(2,1)S(1)} collective-permute-done((bf16[384,1024]{1,0:T(8,128)(2,1)S(1)}, bf16[384,1024]{1,0:T(8,128)(2,1)S(1)}, u32[]{:S(2)}, u32[]{:S(2)}) %collective-permute-start.55) | collective-permute-done | bytes 786464 | tf_op jit(solution)/shard_map/ppermute | solution.py:39
  304.5 2.4 shard_map.371
  308.2 2.3 collective-permute-done.57.far.out_far
  310.5 7.7 %shard_map.373 = (bf16[256,768]{1,0:T(8,128)(2,1)S(1)}, bf16[576,768]{1,0:T(8,128)(2,1)S(1)}, f32[384,1024]{1,0:T(8,128)S(1)}, bf16[384,1024]{1,0:T(8,128)(2,1)S(1)}) custom-call(bf16[384,1024]{1,0:T(8,128)(2,1)S(1)} %get-tuple-element.338.near.out_near, bf16[384,1024]{1,0:T(8,128)(2,1)S(1)} %collective-permute-done.57.far.out_far, ...), custom_call_target="tpu_custom_call" | custom-call | flops 1811939328 | bytes 10160128 | tf_op jit(solution)/shard_map/pallas_call | solution.py:421
  325.8 1.8 slice_bitcast_fusion.5
  336.1 2.3 shard_map.376
  338.4 3.7 collective-permute-done.59.refs_3_
  342.1 2.3 shard_map.375
  346.8 2.1 shard_map.377
  353.7 1.6 shard_map.380
  360.6 17.5 %collective-permute-done.64.refs_3_ = bf16[384,1024]{1,0:T(8,128)(2,1)S(1)} collective-permute-done((bf16[384,1024]{1,0:T(8,128)(2,1)S(1)}, bf16[384,1024]{1,0:T(8,128)(2,1)S(1)}, u32[]{:S(2)}, u32[]{:S(2)}) %collective-permute-start.64) | collective-permute-done | bytes 786464 | tf_op jit(solution)/shard_map/ppermute | solution.py:39
  383.9 9.5 %shard_map.381 = (bf16[256,768]{1,0:T(8,128)(2,1)S(1)}, bf16[576,768]{1,0:T(8,128)(2,1)S(1)}, f32[384,1024]{1,0:T(8,128)S(1)}, bf16[384,1024]{1,0:T(8,128)(2,1)S(1)}) custom-call(bf16[384,1024]{1,0:T(8,128)(2,1)S(1)} %get-tuple-element.395.near.out_near, bf16[384,1024]{1,0:T(8,128)(2,1)S(1)} %collective-permute-done.69.far.out_far, ...), custom_call_target="tpu_custom_call" | custom-call | flops 1811939328 | bytes 10160128 | tf_op jit(solution)/shard_map/pallas_call | solution.py:421
  399.2 2.2 shard_map.383
  401.5 6.1 %collective-permute-done.74 = bf16[2,12,8,1024]{3,2,1,0:T(8,128)(2,1)S(1)} collective-permute-done((bf16[2,12,8,1024]{3,2,1,0:T(8,128)(2,1)S(1)}, bf16[2,12,8,1024]{3,2,1,0:T(8,128)(2,1)S(1)}, u32[]{:S(2)}, u32[]{:S(2)}) %collective-permute-start.74) | collective-permute-done | bytes 393248 | tf_op jit(solution)/shard_map/ppermute | solution.py:33
  407.5 6.3 %collective-permute-done.73 = bf16[2,31,8,768]{3,2,1,0:T(8,128)(2,1)S(1)} collective-permute-done((bf16[2,31,8,768]{3,2,1,0:T(8,128)(2,1)S(1)}, bf16[2,31,8,768]{3,2,1,0:T(8,128)(2,1)S(1)}, u32[]{:S(2)}, u32[]{:S(2)}) %collective-permute-start.73) | collective-permute-done | bytes 761888 | tf_op jit(solution)/shard_map/ppermute | solution.py:36
  416.8 2.4 collective-permute-start.71
  419.3 7.1 %collective-permute-done.80 = bf16[2,24,8,768]{3,2,1,0:T(8,128)(2,1)S(1)} collective-permute-done((bf16[2,24,8,768]{3,2,1,0:T(8,128)(2,1)S(1)}, bf16[2,24,8,768]{3,2,1,0:T(8,128)(2,1)S(1)}, u32[]{:S(2)}, u32[]{:S(2)}) %collective-permute-start.80) | collective-permute-done | bytes 589856 | tf_op jit(solution)/shard_map/ppermute | solution.py:36
  427.0 5.8 %collective-permute-done.78 = bf16[31,8,768]{2,1,0:T(8,128)(2,1)S(1)} collective-permute-done((bf16[31,8,768]{2,1,0:T(8,128)(2,1)S(1)}, bf16[31,8,768]{2,1,0:T(8,128)(2,1)S(1)}, u32[]{:S(2)}, u32[]{:S(2)}) %collective-permute-start.78) | collective-permute-done | bytes 380960 | tf_op jit(solution)/shard_map/ppermute | solution.py:43
  437.5 7.3 %collective-permute-done.81 = bf16[2,12,8,1024]{3,2,1,0:T(8,128)(2,1)S(1)} collective-permute-done((bf16[2,12,8,1024]{3,2,1,0:T(8,128)(2,1)S(1)}, bf16[2,12,8,1024]{3,2,1,0:T(8,128)(2,1)S(1)}, u32[]{:S(2)}, u32[]{:S(2)}) %collective-permute-start.81) | collective-permute-done | bytes 393248 | tf_op jit(solution)/shard_map/ppermute | solution.py:36
  446.1 1.7 collective-permute-start.82
  449.0 4.1 collective-permute-done.85
  453.2 16.7 %collective-permute-done.86 = bf16[12,8,1024]{2,1,0:T(8,128)(2,1)S(1)} collective-permute-done((bf16[12,8,1024]{2,1,0:T(8,128)(2,1)S(1)}, bf16[12,8,1024]{2,1,0:T(8,128)(2,1)S(1)}, u32[]{:S(2)}, u32[]{:S(2)}) %collective-permute-start.86) | collective-permute-done | bytes 196640 | tf_op jit(solution)/shard_map/ppermute | solution.py:43
  470.0 1.9 collective-permute-done.84
  473.6 3.0 collective-permute-start.89
  477.9 25.3 %collective-permute-done.89 = bf16[12,8,1024]{2,1,0:T(8,128)(2,1)S(1)} collective-permute-done((bf16[12,8,1024]{2,1,0:T(8,128)(2,1)S(1)}, bf16[12,8,1024]{2,1,0:T(8,128)(2,1)S(1)}, u32[]{:S(2)}, u32[]{:S(2)}) %collective-permute-start.89) | collective-permute-done | bytes 196640 | tf_op jit(solution)/shard_map/ppermute | solution.py:43
  503.9 2.1 collective-permute-start.90
  506.7 13.6 %collective-permute-done.90 = bf16[2,112,768]{2,1,0:T(8,128)(2,1)S(1)} collective-permute-done((bf16[2,112,768]{2,1,0:T(8,128)(2,1)S(1)}, bf16[2,112,768]{2,1,0:T(8,128)(2,1)S(1)}, u32[]{:S(2)}, u32[]{:S(2)}) %collective-permute-start.90) | collective-permute-done | bytes 344096 | tf_op jit(solution)/shard_map/ppermute | solution.py:39
  (811 shorter events, 139.8 us)
Async XLA Ops:
  6.5 13.8 %collective-permute-start.13 = (f32[1,64]{1,0:T(1,128)S(1)}, f32[1,64]{1,0:T(1,128)S(1)}, u32[]{:S(2)}, u32[]{:S(2)}) collective-permute-start(f32[1,64]{1,0:T(1,128)S(1)} %convert_element_type.245), channel_id=1, source_target_pairs={{0,8},{8,0},{1,9},{9,1},{2,10},{10,2},{3,11},{11,3},{4,12},{12,4},... | collective-permute-start | bytes 776 | tf_op jit(solution)/shard_map/ppermute | solution.py:39
  16.2 25.0 %collective-permute-start.3 = (bf16[40,8,768]{2,1,0:T(8,128)(2,1)S(1)}, bf16[40,8,768]{2,1,0:T(8,128)(2,1)S(1)}, u32[]{:S(2)}, u32[]{:S(2)}) collective-permute-start(bf16[40,8,768]{2,1,0:T(8,128)(2,1)S(1)} %fusion.34), channel_id=1, source_target_pairs={{0,16},{16,0},{1,17},{17,1},{2,18},{18,2},{3,19},{19,3},{4,20},{20... | collective-permute-start | bytes 1474568 | tf_op jit(solution)/shard_map/ppermute | solution.py:43
  24.7 50.3 %collective-permute-start.20 = (bf16[16,1024]{1,0:T(8,128)(2,1)S(1)}, bf16[16,1024]{1,0:T(8,128)(2,1)S(1)}, u32[]{:S(2)}, u32[]{:S(2)}) collective-permute-start(bf16[16,1024]{1,0:T(8,128)(2,1)S(1)} %add.891), channel_id=1, source_target_pairs={{0,8},{8,0},{1,9},{9,1},{2,10},{10,2},{3,11},{11,3},{4,12},{12,4},... | collective-permute-start | bytes 98312 | tf_op jit(solution)/shard_map/ppermute | solution.py:39
  41.4 33.6 %collective-permute-start.6 = (bf16[2,40,8,768]{3,2,1,0:T(8,128)(2,1)S(1)}, bf16[2,40,8,768]{3,2,1,0:T(8,128)(2,1)S(1)}, u32[]{:S(2)}, u32[]{:S(2)}) collective-permute-start(bf16[2,40,8,768]{3,2,1,0:T(8,128)(2,1)S(1)} %pad_maximum_fusion), channel_id=1, source_target_pairs={{0,1},{1,0},{2,3},{3,2},{4,5},{5,4},{6,7},{7,6},{8,9},{9,8},{10,11... | collective-permute-start | bytes 2949128 | tf_op jit(solution)/shard_map/ppermute | solution.py:33
  42.0 33.0 %collective-permute-start.7 = (bf16[2,40,8,768]{3,2,1,0:T(8,128)(2,1)S(1)}, bf16[2,40,8,768]{3,2,1,0:T(8,128)(2,1)S(1)}, u32[]{:S(2)}, u32[]{:S(2)}) collective-permute-start(bf16[2,40,8,768]{3,2,1,0:T(8,128)(2,1)S(1)} %pad_maximum_fusion), channel_id=1, source_target_pairs={{0,4},{4,0},{1,5},{5,1},{2,6},{6,2},{3,7},{7,3},{8,12},{12,8},{9,1... | collective-permute-start | bytes 2949128 | tf_op jit(solution)/shard_map/ppermute | solution.py:36
  46.7 25.7 %collective-permute-start.9 = (bf16[2,168,768]{2,1,0:T(8,128)(2,1)S(1)}, bf16[2,168,768]{2,1,0:T(8,128)(2,1)S(1)}, u32[]{:S(2)}, u32[]{:S(2)}) collective-permute-start(bf16[2,168,768]{2,1,0:T(8,128)(2,1)S(1)} %get-tuple-element.498), channel_id=1, source_target_pairs={{0,8},{8,0},{1,9},{9,1},{2,10},{10,2},{3,11},{11,3},{4,12},{12,4},... | collective-permute-start | bytes 1548296 | tf_op jit(solution)/shard_map/ppermute | solution.py:39
  46.8 25.5 %collective-permute-start.4 = (bf16[192,1024]{1,0:T(8,128)(2,1)S(1)}, bf16[192,1024]{1,0:T(8,128)(2,1)S(1)}, u32[]{:S(2)}, u32[]{:S(2)}) collective-permute-start(bf16[192,1024]{1,0:T(8,128)(2,1)S(1)} %maximum_maximum_fusion), channel_id=1, source_target_pairs={{0,8},{8,0},{1,9},{9,1},{2,10},{10,2},{3,11},{11,3},{4,12},{12,4},... | collective-permute-start | bytes 1179656 | tf_op jit(solution)/shard_map/ppermute | solution.py:39
  74.9 23.4 %collective-permute-start.5 = (bf16[384,1024]{1,0:T(8,128)(2,1)S(1)}, bf16[384,1024]{1,0:T(8,128)(2,1)S(1)}, u32[]{:S(2)}, u32[]{:S(2)}) collective-permute-start(bf16[384,1024]{1,0:T(8,128)(2,1)S(1)} %pad_maximum_fusion.1.near.values), channel_id=1, source_target_pairs={{0,2},{2,0},{1,3},{3,1},{4,6},{6,4},{5,7},{7,5},{8,10},{10,8},{9,1... | collective-permute-start | bytes 2359304 | tf_op jit(solution)/shard_map/ppermute | solution.py:30
  75.1 29.3 %collective-permute-start.21 = (bf16[16,1024]{1,0:T(8,128)(2,1)S(1)}, bf16[16,1024]{1,0:T(8,128)(2,1)S(1)}, u32[]{:S(2)}, u32[]{:S(2)}) collective-permute-start(bf16[16,1024]{1,0:T(8,128)(2,1)S(1)} %add.892), channel_id=1, source_target_pairs={{0,16},{16,0},{1,17},{17,1},{2,18},{18,2},{3,19},{19,3},{4,20},{20... | collective-permute-start | bytes 98312 | tf_op jit(solution)/shard_map/ppermute | solution.py:43
  76.7 14.0 %collective-permute-start.11 = (bf16[2,20,8,768]{3,2,1,0:T(8,128)(2,1)S(1)}, bf16[2,20,8,768]{3,2,1,0:T(8,128)(2,1)S(1)}, u32[]{:S(2)}, u32[]{:S(2)}) collective-permute-start(bf16[2,20,8,768]{3,2,1,0:T(8,128)(2,1)S(1)} %slice.1014), channel_id=1, source_target_pairs={{0,4},{4,0},{1,5},{5,1},{2,6},{6,2},{3,7},{7,3},{8,12},{12,8},{9,1... | collective-permute-start | bytes 1474568 | tf_op jit(solution)/shard_map/ppermute | solution.py:36
  90.7 17.4 %collective-permute-start.25 = (bf16[2,12,8,1024]{3,2,1,0:T(8,128)(2,1)S(1)}, bf16[2,12,8,1024]{3,2,1,0:T(8,128)(2,1)S(1)}, u32[]{:S(2)}, u32[]{:S(2)}) collective-permute-start(bf16[2,12,8,1024]{3,2,1,0:T(8,128)(2,1)S(1)} %pad_maximum_fusion.18), channel_id=1, source_target_pairs={{0,1},{1,0},{2,3},{3,2},{4,5},{5,4},{6,7},{7,6},{8,9},{9,8},{10,11... | collective-permute-start | bytes 1179656 | tf_op jit(solution)/shard_map/ppermute | solution.py:33
  92.1 16.0 %collective-permute-start.27 = (bf16[2,12,8,1024]{3,2,1,0:T(8,128)(2,1)S(1)}, bf16[2,12,8,1024]{3,2,1,0:T(8,128)(2,1)S(1)}, u32[]{:S(2)}, u32[]{:S(2)}) collective-permute-start(bf16[2,12,8,1024]{3,2,1,0:T(8,128)(2,1)S(1)} %pad_maximum_fusion.18), channel_id=1, source_target_pairs={{0,4},{4,0},{1,5},{5,1},{2,6},{6,2},{3,7},{7,3},{8,12},{12,8},{9,1... | collective-permute-start | bytes 1179656 | tf_op jit(solution)/shard_map/ppermute | solution.py:36
  93.6 14.3 %collective-permute-start.26 = (bf16[24,8,768]{2,1,0:T(8,128)(2,1)S(1)}, bf16[24,8,768]{2,1,0:T(8,128)(2,1)S(1)}, u32[]{:S(2)}, u32[]{:S(2)}) collective-permute-start(bf16[24,8,768]{2,1,0:T(8,128)(2,1)S(1)} %pad_maximum_fusion.25), channel_id=1, source_target_pairs={{0,16},{16,0},{1,17},{17,1},{2,18},{18,2},{3,19},{19,3},{4,20},{20... | collective-permute-start | bytes 884744 | tf_op jit(solution)/shard_map/ppermute | solution.py:43
  104.3 21.9 %collective-permute-start.15 = (bf16[384,1024]{1,0:T(8,128)(2,1)S(1)}, bf16[384,1024]{1,0:T(8,128)(2,1)S(1)}, u32[]{:S(2)}, u32[]{:S(2)}) collective-permute-start(bf16[384,1024]{1,0:T(8,128)(2,1)S(1)} %get-tuple-element.254), channel_id=1, source_target_pairs={{0,2},{2,0},{1,3},{3,1},{4,6},{6,4},{5,7},{7,5},{8,10},{10,8},{9,1... | collective-permute-start | bytes 2359304 | tf_op jit(solution)/shard_map/ppermute | solution.py:30
  108.1 24.4 %collective-permute-start.28 = (bf16[2,24,8,768]{3,2,1,0:T(8,128)(2,1)S(1)}, bf16[2,24,8,768]{3,2,1,0:T(8,128)(2,1)S(1)}, u32[]{:S(2)}, u32[]{:S(2)}) collective-permute-start(bf16[2,24,8,768]{3,2,1,0:T(8,128)(2,1)S(1)} %pad_maximum_fusion.6), channel_id=1, source_target_pairs={{0,1},{1,0},{2,3},{3,2},{4,5},{5,4},{6,7},{7,6},{8,9},{9,8},{10,11... | collective-permute-start | bytes 1769480 | tf_op jit(solution)/shard_map/ppermute | solution.py:33
  108.5 24.0 %collective-permute-start.29 = (bf16[2,24,8,768]{3,2,1,0:T(8,128)(2,1)S(1)}, bf16[2,24,8,768]{3,2,1,0:T(8,128)(2,1)S(1)}, u32[]{:S(2)}, u32[]{:S(2)}) collective-permute-start(bf16[2,24,8,768]{3,2,1,0:T(8,128)(2,1)S(1)} %pad_maximum_fusion.6), channel_id=1, source_target_pairs={{0,4},{4,0},{1,5},{5,1},{2,6},{6,2},{3,7},{7,3},{8,12},{12,8},{9,1... | collective-permute-start | bytes 1769480 | tf_op jit(solution)/shard_map/ppermute | solution.py:36
  109.4 16.6 %collective-permute-start.30 = (bf16[31,8,768]{2,1,0:T(8,128)(2,1)S(1)}, bf16[31,8,768]{2,1,0:T(8,128)(2,1)S(1)}, u32[]{:S(2)}, u32[]{:S(2)}) collective-permute-start(bf16[31,8,768]{2,1,0:T(8,128)(2,1)S(1)} %pad_maximum_fusion.23), channel_id=1, source_target_pairs={{0,16},{16,0},{1,17},{17,1},{2,18},{18,2},{3,19},{19,3},{4,20},{20... | collective-permute-start | bytes 1142792 | tf_op jit(solution)/shard_map/ppermute | solution.py:43
  109.5 22.4 %collective-permute-start.31 = (bf16[2,12,8,1024]{3,2,1,0:T(8,128)(2,1)S(1)}, bf16[2,12,8,1024]{3,2,1,0:T(8,128)(2,1)S(1)}, u32[]{:S(2)}, u32[]{:S(2)}) collective-permute-start(bf16[2,12,8,1024]{3,2,1,0:T(8,128)(2,1)S(1)} %collective-permute-done.25), channel_id=1, source_target_pairs={{0,4},{4,0},{1,5},{5,1},{2,6},{6,2},{3,7},{7,3},{8,12},{12,8},{9,1... | collective-permute-start | bytes 1179656 | tf_op jit(solution)/shard_map/ppermute | solution.py:36
  126.4 22.3 %collective-permute-start.16 = (bf16[384,1024]{1,0:T(8,128)(2,1)S(1)}, bf16[384,1024]{1,0:T(8,128)(2,1)S(1)}, u32[]{:S(2)}, u32[]{:S(2)}) collective-permute-start(bf16[384,1024]{1,0:T(8,128)(2,1)S(1)} %shard_map.357), channel_id=1, source_target_pairs={{0,8},{8,0},{1,9},{9,1},{2,10},{10,2},{3,11},{11,3},{4,12},{12,4},... | collective-permute-start | bytes 2359304 | tf_op jit(solution)/shard_map/ppermute | solution.py:39
  132.5 31.0 %collective-permute-start.36 = (bf16[2,31,8,768]{3,2,1,0:T(8,128)(2,1)S(1)}, bf16[2,31,8,768]{3,2,1,0:T(8,128)(2,1)S(1)}, u32[]{:S(2)}, u32[]{:S(2)}) collective-permute-start(bf16[2,31,8,768]{3,2,1,0:T(8,128)(2,1)S(1)} %pad_maximum_fusion.3), channel_id=1, source_target_pairs={{0,1},{1,0},{2,3},{3,2},{4,5},{5,4},{6,7},{7,6},{8,9},{9,8},{10,11... | collective-permute-start | bytes 2285576 | tf_op jit(solution)/shard_map/ppermute | solution.py:33
  134.3 29.3 %collective-permute-start.37 = (bf16[2,31,8,768]{3,2,1,0:T(8,128)(2,1)S(1)}, bf16[2,31,8,768]{3,2,1,0:T(8,128)(2,1)S(1)}, u32[]{:S(2)}, u32[]{:S(2)}) collective-permute-start(bf16[2,31,8,768]{3,2,1,0:T(8,128)(2,1)S(1)} %pad_maximum_fusion.3), channel_id=1, source_target_pairs={{0,4},{4,0},{1,5},{5,1},{2,6},{6,2},{3,7},{7,3},{8,12},{12,8},{9,1... | collective-permute-start | bytes 2285576 | tf_op jit(solution)/shard_map/ppermute | solution.py:36
  135.0 28.0 %collective-permute-start.32 = (bf16[2,24,8,768]{3,2,1,0:T(8,128)(2,1)S(1)}, bf16[2,24,8,768]{3,2,1,0:T(8,128)(2,1)S(1)}, u32[]{:S(2)}, u32[]{:S(2)}) collective-permute-start(bf16[2,24,8,768]{3,2,1,0:T(8,128)(2,1)S(1)} %collective-permute-done.29), channel_id=1, source_target_pairs={{0,1},{1,0},{2,3},{3,2},{4,5},{5,4},{6,7},{7,6},{8,9},{9,8},{10,11... | collective-permute-start | bytes 1769480 | tf_op jit(solution)/shard_map/ppermute | solution.py:33
  149.6 17.9 %collective-permute-start.23 = (bf16[384,1024]{1,0:T(8,128)(2,1)S(1)}, bf16[384,1024]{1,0:T(8,128)(2,1)S(1)}, u32[]{:S(2)}, u32[]{:S(2)}) collective-permute-start(bf16[384,1024]{1,0:T(8,128)(2,1)S(1)} %get-tuple-element.359.near), channel_id=1, source_target_pairs={{0,2},{2,0},{1,3},{3,1},{4,6},{6,4},{5,7},{7,5},{8,10},{10,8},{9,1... | collective-permute-start | bytes 2359304 | tf_op jit(solution)/shard_map/ppermute | solution.py:30
  165.9 20.2 %collective-permute-start.39 = (bf16[2,31,8,768]{3,2,1,0:T(8,128)(2,1)S(1)}, bf16[2,31,8,768]{3,2,1,0:T(8,128)(2,1)S(1)}, u32[]{:S(2)}, u32[]{:S(2)}) collective-permute-start(bf16[2,31,8,768]{3,2,1,0:T(8,128)(2,1)S(1)} %collective-permute-done.36), channel_id=1, source_target_pairs={{0,4},{4,0},{1,5},{5,1},{2,6},{6,2},{3,7},{7,3},{8,12},{12,8},{9,1... | collective-permute-start | bytes 2285576 | tf_op jit(solution)/shard_map/ppermute | solution.py:36
  173.7 21.0 %collective-permute-start.34 = (bf16[384,1024]{1,0:T(8,128)(2,1)S(1)}, bf16[384,1024]{1,0:T(8,128)(2,1)S(1)}, u32[]{:S(2)}, u32[]{:S(2)}) collective-permute-start(bf16[384,1024]{1,0:T(8,128)(2,1)S(1)} %shard_map.360), channel_id=1, source_target_pairs={{0,8},{8,0},{1,9},{9,1},{2,10},{10,2},{3,11},{11,3},{4,12},{12,4},... | collective-permute-start | bytes 2359304 | tf_op jit(solution)/shard_map/ppermute | solution.py:39
  186.2 17.4 %collective-permute-start.46 = (bf16[2,24,8,768]{3,2,1,0:T(8,128)(2,1)S(1)}, bf16[2,24,8,768]{3,2,1,0:T(8,128)(2,1)S(1)}, u32[]{:S(2)}, u32[]{:S(2)}) collective-permute-start(bf16[2,24,8,768]{3,2,1,0:T(8,128)(2,1)S(1)} %pad_maximum_fusion.7), channel_id=1, source_target_pairs={{0,1},{1,0},{2,3},{3,2},{4,5},{5,4},{6,7},{7,6},{8,9},{9,8},{10,11... | collective-permute-start | bytes 1769480 | tf_op jit(solution)/shard_map/ppermute | solution.py:33
  188.0 15.1 %collective-permute-start.47 = (bf16[2,24,8,768]{3,2,1,0:T(8,128)(2,1)S(1)}, bf16[2,24,8,768]{3,2,1,0:T(8,128)(2,1)S(1)}, u32[]{:S(2)}, u32[]{:S(2)}) collective-permute-start(bf16[2,24,8,768]{3,2,1,0:T(8,128)(2,1)S(1)} %pad_maximum_fusion.7), channel_id=1, source_target_pairs={{0,4},{4,0},{1,5},{5,1},{2,6},{6,2},{3,7},{7,3},{8,12},{12,8},{9,1... | collective-permute-start | bytes 1769480 | tf_op jit(solution)/shard_map/ppermute | solution.py:36
  211.2 14.9 %collective-permute-start.49 = (bf16[2,24,8,768]{3,2,1,0:T(8,128)(2,1)S(1)}, bf16[2,24,8,768]{3,2,1,0:T(8,128)(2,1)S(1)}, u32[]{:S(2)}, u32[]{:S(2)}) collective-permute-start(bf16[2,24,8,768]{3,2,1,0:T(8,128)(2,1)S(1)} %collective-permute-done.47), channel_id=1, source_target_pairs={{0,1},{1,0},{2,3},{3,2},{4,5},{5,4},{6,7},{7,6},{8,9},{9,8},{10,11... | collective-permute-start | bytes 1769480 | tf_op jit(solution)/shard_map/ppermute | solution.py:33
  212.0 18.9 %collective-permute-start.41 = (bf16[384,1024]{1,0:T(8,128)(2,1)S(1)}, bf16[384,1024]{1,0:T(8,128)(2,1)S(1)}, u32[]{:S(2)}, u32[]{:S(2)}) collective-permute-start(bf16[384,1024]{1,0:T(8,128)(2,1)S(1)} %shard_map.363), channel_id=1, source_target_pairs={{0,8},{8,0},{1,9},{9,1},{2,10},{10,2},{3,11},{11,3},{4,12},{12,4},... | collective-permute-start | bytes 2359304 | tf_op jit(solution)/shard_map/ppermute | solution.py:39
  240.0 28.2 %collective-permute-start.51 = (bf16[384,1024]{1,0:T(8,128)(2,1)S(1)}, bf16[384,1024]{1,0:T(8,128)(2,1)S(1)}, u32[]{:S(2)}, u32[]{:S(2)}) collective-permute-start(bf16[384,1024]{1,0:T(8,128)(2,1)S(1)} %shard_map.366), channel_id=1, source_target_pairs={{0,8},{8,0},{1,9},{9,1},{2,10},{10,2},{3,11},{11,3},{4,12},{12,4},... | collective-permute-start | bytes 2359304 | tf_op jit(solution)/shard_map/ppermute | solution.py:39
  240.9 27.2 %collective-permute-start.52 = (bf16[192,1024]{1,0:T(8,128)(2,1)S(1)}, bf16[192,1024]{1,0:T(8,128)(2,1)S(1)}, u32[]{:S(2)}, u32[]{:S(2)}) collective-permute-start(bf16[192,1024]{1,0:T(8,128)(2,1)S(1)} %maximum_maximum_fusion.1), channel_id=1, source_target_pairs={{0,8},{8,0},{1,9},{9,1},{2,10},{10,2},{3,11},{11,3},{4,12},{12,4},... | collective-permute-start | bytes 1179656 | tf_op jit(solution)/shard_map/ppermute | solution.py:39
  284.8 19.6 %collective-permute-start.55 = (bf16[384,1024]{1,0:T(8,128)(2,1)S(1)}, bf16[384,1024]{1,0:T(8,128)(2,1)S(1)}, u32[]{:S(2)}, u32[]{:S(2)}) collective-permute-start(bf16[384,1024]{1,0:T(8,128)(2,1)S(1)} %shard_map.370), channel_id=1, source_target_pairs={{0,8},{8,0},{1,9},{9,1},{2,10},{10,2},{3,11},{11,3},{4,12},{12,4},... | collective-permute-start | bytes 2359304 | tf_op jit(solution)/shard_map/ppermute | solution.py:39
  292.7 15.4 %collective-permute-start.56 = (bf16[2,24,8,768]{3,2,1,0:T(8,128)(2,1)S(1)}, bf16[2,24,8,768]{3,2,1,0:T(8,128)(2,1)S(1)}, u32[]{:S(2)}, u32[]{:S(2)}) collective-permute-start(bf16[2,24,8,768]{3,2,1,0:T(8,128)(2,1)S(1)} %pad_maximum_fusion.8), channel_id=1, source_target_pairs={{0,4},{4,0},{1,5},{5,1},{2,6},{6,2},{3,7},{7,3},{8,12},{12,8},{9,1... | collective-permute-start | bytes 1769480 | tf_op jit(solution)/shard_map/ppermute | solution.py:36
  319.6 24.9 %collective-permute-start.61 = (bf16[2,24,8,768]{3,2,1,0:T(8,128)(2,1)}, bf16[2,24,8,768]{3,2,1,0:T(8,128)(2,1)}, u32[]{:S(2)}, u32[]{:S(2)}) collective-permute-start(bf16[2,24,8,768]{3,2,1,0:T(8,128)(2,1)} %pad_maximum_fusion.9), channel_id=1, source_target_pairs={{0,4},{4,0},{1,5},{5,1},{2,6},{6,2},{3,7},{7,3},{8,12},{12,8},{9,1... | collective-permute-start | bytes 1769480 | tf_op jit(solution)/shard_map/ppermute | solution.py:36
  322.1 20.0 %collective-permute-start.59 = (bf16[384,1024]{1,0:T(8,128)(2,1)}, bf16[384,1024]{1,0:T(8,128)(2,1)}, u32[]{:S(2)}, u32[]{:S(2)}) collective-permute-start(bf16[384,1024]{1,0:T(8,128)(2,1)} %shard_map.374), channel_id=1, source_target_pairs={{0,8},{8,0},{1,9},{9,1},{2,10},{10,2},{3,11},{11,3},{4,12},{12,4},... | collective-permute-start | bytes 2359304 | tf_op jit(solution)/shard_map/ppermute | solution.py:39
  324.3 20.1 %collective-permute-start.60 = (bf16[2,24,8,768]{3,2,1,0:T(8,128)(2,1)}, bf16[2,24,8,768]{3,2,1,0:T(8,128)(2,1)}, u32[]{:S(2)}, u32[]{:S(2)}) collective-permute-start(bf16[2,24,8,768]{3,2,1,0:T(8,128)(2,1)} %add_convert_fusion.6), channel_id=1, source_target_pairs={{0,1},{1,0},{2,3},{3,2},{4,5},{5,4},{6,7},{7,6},{8,9},{9,8},{10,11... | collective-permute-start | bytes 1769480 | tf_op jit(solution)/shard_map/ppermute | solution.py:33
  345.0 35.8 %collective-permute-start.66 = (bf16[2,31,8,768]{3,2,1,0:T(8,128)(2,1)S(1)}, bf16[2,31,8,768]{3,2,1,0:T(8,128)(2,1)S(1)}, u32[]{:S(2)}, u32[]{:S(2)}) collective-permute-start(bf16[2,31,8,768]{3,2,1,0:T(8,128)(2,1)S(1)} %pad_maximum_fusion.4), channel_id=1, source_target_pairs={{0,1},{1,0},{2,3},{3,2},{4,5},{5,4},{6,7},{7,6},{8,9},{9,8},{10,11... | collective-permute-start | bytes 2285576 | tf_op jit(solution)/shard_map/ppermute | solution.py:33
  349.4 31.5 %collective-permute-start.67 = (bf16[2,12,8,1024]{3,2,1,0:T(8,128)(2,1)S(1)}, bf16[2,12,8,1024]{3,2,1,0:T(8,128)(2,1)S(1)}, u32[]{:S(2)}, u32[]{:S(2)}) collective-permute-start(bf16[2,12,8,1024]{3,2,1,0:T(8,128)(2,1)S(1)} %pad_maximum_fusion.19), channel_id=1, source_target_pairs={{0,4},{4,0},{1,5},{5,1},{2,6},{6,2},{3,7},{7,3},{8,12},{12,8},{9,1... | collective-permute-start | bytes 1179656 | tf_op jit(solution)/shard_map/ppermute | solution.py:36
  352.4 25.8 %collective-permute-start.64 = (bf16[384,1024]{1,0:T(8,128)(2,1)S(1)}, bf16[384,1024]{1,0:T(8,128)(2,1)S(1)}, u32[]{:S(2)}, u32[]{:S(2)}) collective-permute-start(bf16[384,1024]{1,0:T(8,128)(2,1)S(1)} %shard_map.378), channel_id=1, source_target_pairs={{0,8},{8,0},{1,9},{9,1},{2,10},{10,2},{3,11},{11,3},{4,12},{12,4},... | collective-permute-start | bytes 2359304 | tf_op jit(solution)/shard_map/ppermute | solution.py:39
  355.7 25.2 %collective-permute-start.68 = (bf16[2,24,8,768]{3,2,1,0:T(8,128)(2,1)S(1)}, bf16[2,24,8,768]{3,2,1,0:T(8,128)(2,1)S(1)}, u32[]{:S(2)}, u32[]{:S(2)}) collective-permute-start(bf16[2,24,8,768]{3,2,1,0:T(8,128)(2,1)S(1)} %pad_maximum_fusion.10), channel_id=1, source_target_pairs={{0,4},{4,0},{1,5},{5,1},{2,6},{6,2},{3,7},{7,3},{8,12},{12,8},{9,1... | collective-permute-start | bytes 1769480 | tf_op jit(solution)/shard_map/ppermute | solution.py:36
  356.6 24.3 %collective-permute-start.65 = (bf16[24,8,768]{2,1,0:T(8,128)(2,1)S(1)}, bf16[24,8,768]{2,1,0:T(8,128)(2,1)S(1)}, u32[]{:S(2)}, u32[]{:S(2)}) collective-permute-start(bf16[24,8,768]{2,1,0:T(8,128)(2,1)S(1)} %dynamic-slice_bitcast_fusion.39), channel_id=1, source_target_pairs={{0,16},{16,0},{1,17},{17,1},{2,18},{18,2},{3,19},{19,3},{4,20},{20... | collective-permute-start | bytes 884744 | tf_op jit(solution)/shard_map/ppermute | solution.py:43
  378.2 23.3 %collective-permute-start.72 = (bf16[2,31,8,768]{3,2,1,0:T(8,128)(2,1)S(1)}, bf16[2,31,8,768]{3,2,1,0:T(8,128)(2,1)S(1)}, u32[]{:S(2)}, u32[]{:S(2)}) collective-permute-start(bf16[2,31,8,768]{3,2,1,0:T(8,128)(2,1)S(1)} %pad_maximum_fusion.5), channel_id=1, source_target_pairs={{0,1},{1,0},{2,3},{3,2},{4,5},{5,4},{6,7},{7,6},{8,9},{9,8},{10,11... | collective-permute-start | bytes 2285576 | tf_op jit(solution)/shard_map/ppermute | solution.py:33
  381.1 20.4 %collective-permute-start.75 = (bf16[2,12,8,1024]{3,2,1,0:T(8,128)(2,1)S(1)}, bf16[2,12,8,1024]{3,2,1,0:T(8,128)(2,1)S(1)}, u32[]{:S(2)}, u32[]{:S(2)}) collective-permute-start(bf16[2,12,8,1024]{3,2,1,0:T(8,128)(2,1)S(1)} %pad_maximum_fusion.20), channel_id=1, source_target_pairs={{0,4},{4,0},{1,5},{5,1},{2,6},{6,2},{3,7},{7,3},{8,12},{12,8},{9,1... | collective-permute-start | bytes 1179656 | tf_op jit(solution)/shard_map/ppermute | solution.py:36
  393.9 19.9 %collective-permute-start.73 = (bf16[2,31,8,768]{3,2,1,0:T(8,128)(2,1)S(1)}, bf16[2,31,8,768]{3,2,1,0:T(8,128)(2,1)S(1)}, u32[]{:S(2)}, u32[]{:S(2)}) collective-permute-start(bf16[2,31,8,768]{3,2,1,0:T(8,128)(2,1)S(1)} %add_convert_fusion.2), channel_id=1, source_target_pairs={{0,4},{4,0},{1,5},{5,1},{2,6},{6,2},{3,7},{7,3},{8,12},{12,8},{9,1... | collective-permute-start | bytes 2285576 | tf_op jit(solution)/shard_map/ppermute | solution.py:36
  397.0 29.5 %collective-permute-start.80 = (bf16[2,24,8,768]{3,2,1,0:T(8,128)(2,1)S(1)}, bf16[2,24,8,768]{3,2,1,0:T(8,128)(2,1)S(1)}, u32[]{:S(2)}, u32[]{:S(2)}) collective-permute-start(bf16[2,24,8,768]{3,2,1,0:T(8,128)(2,1)S(1)} %pad_maximum_fusion.11), channel_id=1, source_target_pairs={{0,4},{4,0},{1,5},{5,1},{2,6},{6,2},{3,7},{7,3},{8,12},{12,8},{9,1... | collective-permute-start | bytes 1769480 | tf_op jit(solution)/shard_map/ppermute | solution.py:36
  414.0 30.8 %collective-permute-start.79 = (bf16[2,24,8,768]{3,2,1,0:T(8,128)(2,1)S(1)}, bf16[2,24,8,768]{3,2,1,0:T(8,128)(2,1)S(1)}, u32[]{:S(2)}, u32[]{:S(2)}) collective-permute-start(bf16[2,24,8,768]{3,2,1,0:T(8,128)(2,1)S(1)} %add_convert_fusion.4), channel_id=1, source_target_pairs={{0,1},{1,0},{2,3},{3,2},{4,5},{5,4},{6,7},{7,6},{8,9},{9,8},{10,11... | collective-permute-start | bytes 1769480 | tf_op jit(solution)/shard_map/ppermute | solution.py:33
  414.9 17.9 %collective-permute-start.78 = (bf16[31,8,768]{2,1,0:T(8,128)(2,1)S(1)}, bf16[31,8,768]{2,1,0:T(8,128)(2,1)S(1)}, u32[]{:S(2)}, u32[]{:S(2)}) collective-permute-start(bf16[31,8,768]{2,1,0:T(8,128)(2,1)S(1)} %dynamic-slice_bitcast_fusion.13), channel_id=1, source_target_pairs={{0,16},{16,0},{1,17},{17,1},{2,18},{18,2},{3,19},{19,3},{4,20},{20... | collective-permute-start | bytes 1142792 | tf_op jit(solution)/shard_map/ppermute | solution.py:43
  415.7 18.6 %collective-permute-start.76 = (bf16[2,16,8,768]{3,2,1,0:T(8,128)(2,1)S(1)}, bf16[2,16,8,768]{3,2,1,0:T(8,128)(2,1)S(1)}, u32[]{:S(2)}, u32[]{:S(2)}) collective-permute-start(bf16[2,16,8,768]{3,2,1,0:T(8,128)(2,1)S(1)} %get-tuple-element.580), channel_id=1, source_target_pairs={{0,4},{4,0},{1,5},{5,1},{2,6},{6,2},{3,7},{7,3},{8,12},{12,8},{9,1... | collective-permute-start | bytes 1179656 | tf_op jit(solution)/shard_map/ppermute | solution.py:36
  416.8 27.9 %collective-permute-start.71 = (bf16[384,1024]{1,0:T(8,128)(2,1)S(1)}, bf16[384,1024]{1,0:T(8,128)(2,1)S(1)}, u32[]{:S(2)}, u32[]{:S(2)}) collective-permute-start(bf16[384,1024]{1,0:T(8,128)(2,1)S(1)} %shard_map.382), channel_id=1, source_target_pairs={{0,8},{8,0},{1,9},{9,1},{2,10},{10,2},{3,11},{11,3},{4,12},{12,4},... | collective-permute-start | bytes 2359304 | tf_op jit(solution)/shard_map/ppermute | solution.py:39
  434.2 14.7 %collective-permute-start.97 = (f32[16,1024]{1,0:T(8,128)S(1)}, f32[16,1024]{1,0:T(8,128)S(1)}, u32[]{:S(2)}, u32[]{:S(2)}) collective-permute-start(f32[16,1024]{1,0:T(8,128)S(1)} %fusion.37), channel_id=1, source_target_pairs={{0,1},{1,0},{2,3},{3,2},{4,5},{5,4},{6,7},{7,6},{8,9},{9,8},{10,11... | collective-permute-start | bytes 196616 | tf_op jit(solution)/shard_map/ppermute | solution.py:33
  436.5 16.7 %collective-permute-start.85 = (bf16[2,12,8,1024]{3,2,1,0:T(8,128)(2,1)S(1)}, bf16[2,12,8,1024]{3,2,1,0:T(8,128)(2,1)S(1)}, u32[]{:S(2)}, u32[]{:S(2)}) collective-permute-start(bf16[2,12,8,1024]{3,2,1,0:T(8,128)(2,1)S(1)} %pad_maximum_fusion.22), channel_id=1, source_target_pairs={{0,4},{4,0},{1,5},{5,1},{2,6},{6,2},{3,7},{7,3},{8,12},{12,8},{9,1... | collective-permute-start | bytes 1179656 | tf_op jit(solution)/shard_map/ppermute | solution.py:36
  444.9 27.0 %collective-permute-start.83 = (bf16[2,32,8,768]{3,2,1,0:T(8,128)(2,1)S(1)}, bf16[2,32,8,768]{3,2,1,0:T(8,128)(2,1)S(1)}, u32[]{:S(2)}, u32[]{:S(2)}) collective-permute-start(bf16[2,32,8,768]{3,2,1,0:T(8,128)(2,1)S(1)} %fusion.5), channel_id=1, source_target_pairs={{0,4},{4,0},{1,5},{5,1},{2,6},{6,2},{3,7},{7,3},{8,12},{12,8},{9,1... | collective-permute-start | bytes 2359304 | tf_op jit(solution)/shard_map/ppermute | solution.py:36
  446.1 25.8 %collective-permute-start.82 = (bf16[2,32,8,768]{3,2,1,0:T(8,128)(2,1)S(1)}, bf16[2,32,8,768]{3,2,1,0:T(8,128)(2,1)S(1)}, u32[]{:S(2)}, u32[]{:S(2)}) collective-permute-start(bf16[2,32,8,768]{3,2,1,0:T(8,128)(2,1)S(1)} %fusion.7), channel_id=1, source_target_pairs={{0,1},{1,0},{2,3},{3,2},{4,5},{5,4},{6,7},{7,6},{8,9},{9,8},{10,11... | collective-permute-start | bytes 2359304 | tf_op jit(solution)/shard_map/ppermute | solution.py:33
  448.0 23.9 %collective-permute-start.84 = (bf16[2,12,8,1024]{3,2,1,0:T(8,128)(2,1)S(1)}, bf16[2,12,8,1024]{3,2,1,0:T(8,128)(2,1)S(1)}, u32[]{:S(2)}, u32[]{:S(2)}) collective-permute-start(bf16[2,12,8,1024]{3,2,1,0:T(8,128)(2,1)S(1)} %add_convert_fusion.9), channel_id=1, source_target_pairs={{0,1},{1,0},{2,3},{3,2},{4,5},{5,4},{6,7},{7,6},{8,9},{9,8},{10,11... | collective-permute-start | bytes 1179656 | tf_op jit(solution)/shard_map/ppermute | solution.py:33
  448.9 21.0 %collective-permute-start.87 = (bf16[24,8,768]{2,1,0:T(8,128)(2,1)S(1)}, bf16[24,8,768]{2,1,0:T(8,128)(2,1)S(1)}, u32[]{:S(2)}, u32[]{:S(2)}) collective-permute-start(bf16[24,8,768]{2,1,0:T(8,128)(2,1)S(1)} %dynamic-slice_bitcast_fusion.22), channel_id=1, source_target_pairs={{0,16},{16,0},{1,17},{17,1},{2,18},{18,2},{3,19},{19,3},{4,20},{20... | collective-permute-start | bytes 884744 | tf_op jit(solution)/shard_map/ppermute | solution.py:43
  453.2 16.8 %collective-permute-start.86 = (bf16[12,8,1024]{2,1,0:T(8,128)(2,1)S(1)}, bf16[12,8,1024]{2,1,0:T(8,128)(2,1)S(1)}, u32[]{:S(2)}, u32[]{:S(2)}) collective-permute-start(bf16[12,8,1024]{2,1,0:T(8,128)(2,1)S(1)} %dynamic-slice_bitcast_fusion.49), channel_id=1, source_target_pairs={{0,16},{16,0},{1,17},{17,1},{2,18},{18,2},{3,19},{19,3},{4,20},{20... | collective-permute-start | bytes 589832 | tf_op jit(solution)/shard_map/ppermute | solution.py:43
  471.9 31.5 %collective-permute-start.98 = (f32[16,1024]{1,0:T(8,128)S(1)}, f32[16,1024]{1,0:T(8,128)S(1)}, u32[]{:S(2)}, u32[]{:S(2)}) collective-permute-start(f32[16,1024]{1,0:T(8,128)S(1)} %add.936), channel_id=1, source_target_pairs={{0,4},{4,0},{1,5},{5,1},{2,6},{6,2},{3,7},{7,3},{8,12},{12,8},{9,1... | collective-permute-start | bytes 196616 | tf_op jit(solution)/shard_map/ppermute | solution.py:36
  473.3 29.9 %collective-permute-start.88 = (bf16[32,8,768]{2,1,0:T(8,128)(2,1)S(1)}, bf16[32,8,768]{2,1,0:T(8,128)(2,1)S(1)}, u32[]{:S(2)}, u32[]{:S(2)}) collective-permute-start(bf16[32,8,768]{2,1,0:T(8,128)(2,1)S(1)} %dynamic-slice_bitcast_fusion.4), channel_id=1, source_target_pairs={{0,16},{16,0},{1,17},{17,1},{2,18},{18,2},{3,19},{19,3},{4,20},{20... | collective-permute-start | bytes 1179656 | tf_op jit(solution)/shard_map/ppermute | solution.py:43
  473.6 29.6 %collective-permute-start.89 = (bf16[12,8,1024]{2,1,0:T(8,128)(2,1)S(1)}, bf16[12,8,1024]{2,1,0:T(8,128)(2,1)S(1)}, u32[]{:S(2)}, u32[]{:S(2)}) collective-permute-start(bf16[12,8,1024]{2,1,0:T(8,128)(2,1)S(1)} %dynamic-slice_bitcast_fusion.48), channel_id=1, source_target_pairs={{0,16},{16,0},{1,17},{17,1},{2,18},{18,2},{3,19},{19,3},{4,20},{20... | collective-permute-start | bytes 589832 | tf_op jit(solution)/shard_map/ppermute | solution.py:43
  477.1 28.8 %collective-permute-start.93 = (bf16[2,112,768]{2,1,0:T(8,128)(2,1)S(1)}, bf16[2,112,768]{2,1,0:T(8,128)(2,1)S(1)}, u32[]{:S(2)}, u32[]{:S(2)}) collective-permute-start(bf16[2,112,768]{2,1,0:T(8,128)(2,1)S(1)} %get-tuple-element.521), channel_id=1, source_target_pairs={{0,8},{8,0},{1,9},{9,1},{2,10},{10,2},{3,11},{11,3},{4,12},{12,4},... | collective-permute-start | bytes 1032200 | tf_op jit(solution)/shard_map/ppermute | solution.py:39
  477.2 47.6 %collective-permute-start.95 = (bf16[184,1024]{1,0:T(8,128)(2,1)S(1)}, bf16[184,1024]{1,0:T(8,128)(2,1)S(1)}, u32[]{:S(2)}, u32[]{:S(2)}) collective-permute-start(bf16[184,1024]{1,0:T(8,128)(2,1)S(1)} %fusion.27), channel_id=1, source_target_pairs={{0,0},{2,16},{16,2},{18,18},{1,1},{3,17},{17,3},{19,19},{4,4},{6,2... | collective-permute-start | bytes 1130504 | tf_op jit(solution)/shard_map/ppermute | solution.py:46
  503.4 17.2 %collective-permute-start.99 = (f32[16,1024]{1,0:T(8,128)S(1)}, f32[16,1024]{1,0:T(8,128)S(1)}, u32[]{:S(2)}, u32[]{:S(2)}) collective-permute-start(f32[16,1024]{1,0:T(8,128)S(1)} %add.937), channel_id=1, source_target_pairs={{0,8},{8,0},{1,9},{9,1},{2,10},{10,2},{3,11},{11,3},{4,12},{12,4},... | collective-permute-start | bytes 196616 | tf_op jit(solution)/shard_map/ppermute | solution.py:39
  503.9 16.4 %collective-permute-start.90 = (bf16[2,112,768]{2,1,0:T(8,128)(2,1)S(1)}, bf16[2,112,768]{2,1,0:T(8,128)(2,1)S(1)}, u32[]{:S(2)}, u32[]{:S(2)}) collective-permute-start(bf16[2,112,768]{2,1,0:T(8,128)(2,1)S(1)} %get-tuple-element.525), channel_id=1, source_target_pairs={{0,8},{8,0},{1,9},{9,1},{2,10},{10,2},{3,11},{11,3},{4,12},{12,4},... | collective-permute-start | bytes 1032200 | tf_op jit(solution)/shard_map/ppermute | solution.py:39
  506.0 17.5 %collective-permute-start.92 = (bf16[192,1024]{1,0:T(8,128)(2,1)S(1)}, bf16[192,1024]{1,0:T(8,128)(2,1)S(1)}, u32[]{:S(2)}, u32[]{:S(2)}) collective-permute-start(bf16[192,1024]{1,0:T(8,128)(2,1)S(1)} %fusion.22), channel_id=1, source_target_pairs={{0,0},{2,16},{16,2},{18,18},{1,1},{3,17},{17,3},{19,19},{4,4},{6,2... | collective-permute-start | bytes 1179656 | tf_op jit(solution)/shard_map/ppermute | solution.py:46
  (187 other events, 945.1 us)

commit v6 on v5

--- a/solution.py
+++ b/solution.py
@@ -768,7 +768,7 @@
 FETCH = (
     Bundle(["tci", "ici", "tco", "icoa", "icob"], 768),
     Bundle(["id0", "iu0", "iso"], 1024, "x"),
-    Bundle(["tu0", "td0"], 768, "y"),
+    Bundle(["tu0", "td0"], 768),
     Bundle(["tsi", "isi", "tso"], 768, "x"),
     Bundle(["id1", "iu1"], 1024, "y"),
     Bundle(["tu1", "td1"], 768, "y"),

time: 539 us -> 534 us (level)
  waiting for transfers between devices: 314 us -> 305 us
    ppermute x20, waiting for transfers between devices: 43.4 us -> 27.4 us  [to_x(): return lax.ppermute(value, 'x', FLIP)]
    ppermute x22 -> x23, waiting for transfers between devices: 42.3 us -> 49 us  [to_y(): return lax.ppermute(value, 'y', FLIP)]
    ppermute x22 -> x23, starting transfers between devices: 22.1 us -> 23.8 us  [to_y(): return lax.ppermute(value, 'y', FLIP)]
  transfers between devices with their start and end apart: 101 -> 102, of which waited for: 45 -> 42; matrix products, arithmetic and copies ran while one was open for 6% -> 6% of each run, Pallas kernels for 7% -> 7%
where the time goes in v6:
time: 534 us; the launch traced here: 528 us
  waiting for transfers between devices  305 us (57%)
  starting transfers between devices  88.8 us (17%)
  Pallas kernels  59.4 us (11%)
  local copies, waits for them, and re-layouts  49.5 us (9%)
  other arithmetic  20.5 us (4%)
    ppermute x17, waiting for transfers between devices, to_near(): return lax.ppermute(value, 'near', FLIP)  108 us
    ppermute x14, waiting for transfers between devices, to_column(): lax.ppermute(value, ('far', 'low'), [(c, (c + step) % columns) for c in r...  105 us
    pallas_call x28, Pallas kernels, kernel(): pl.pallas_call(body, out_shape=outs, scratch_shapes=[pltpu.VMEM(shape, ki...  57.7 us
    ppermute x23, waiting for transfers between devices, to_y(): return lax.ppermute(value, 'y', FLIP)  49 us
    ppermute x20, waiting for transfers between devices, to_x(): return lax.ppermute(value, 'x', FLIP)  27.4 us
    unnamed x296, local copies, waits for them, and re-layouts  25.8 us
    ppermute x20, starting transfers between devices, to_x(): return lax.ppermute(value, 'x', FLIP)  25.1 us
    ppermute x23, starting transfers between devices, to_y(): return lax.ppermute(value, 'y', FLIP)  23.8 us
  transfers between devices with their start and end apart: 102, of which 42 were waited for; matrix products, arithmetic and copies ran while one was open for 6% of the time, Pallas kernels for 7%

profile of v6, /device:TPU:0, one launch (start us, length us, event | category | flops | bytes accessed | tf_op | source)
XLA Modules:
  0.0 528.3 jit_solution(3022423874411448296)
XLA Ops:
  2.7 3.1 collective-permute-start
  7.4 2.4 collective-permute-start.17
  11.4 3.4 collective-permute-start.1
  19.3 1.6 collective-permute-start.18
  21.2 2.1 collective-permute-done.18
  24.6 1.6 collective-permute-start.20
  26.3 14.8 %collective-permute-done.3 = bf16[40,8,768]{2,1,0:T(8,128)(2,1)S(1)} collective-permute-done((bf16[40,8,768]{2,1,0:T(8,128)(2,1)S(1)}, bf16[40,8,768]{2,1,0:T(8,128)(2,1)S(1)}, u32[]{:S(2)}, u32[]{:S(2)}) %collective-permute-start.3) | collective-permute-done | bytes 491552 | tf_op jit(solution)/shard_map/ppermute | solution.py:43
  46.8 2.1 collective-permute-start.4
  48.9 23.4 %collective-permute-done.4 = bf16[192,1024]{1,0:T(8,128)(2,1)S(1)} collective-permute-done((bf16[192,1024]{1,0:T(8,128)(2,1)S(1)}, bf16[192,1024]{1,0:T(8,128)(2,1)S(1)}, u32[]{:S(2)}, u32[]{:S(2)}) %collective-permute-start.4) | collective-permute-done | bytes 393248 | tf_op jit(solution)/shard_map/ppermute | solution.py:39
  72.6 2.2 collective-permute-start.10
  78.7 2.4 collective-permute-start.22
  81.3 9.3 %collective-permute-done.22 = bf16[12,8,1024]{2,1,0:T(8,128)(2,1)S(1)} collective-permute-done((bf16[12,8,1024]{2,1,0:T(8,128)(2,1)S(1)}, bf16[12,8,1024]{2,1,0:T(8,128)(2,1)S(1)}, u32[]{:S(2)}, u32[]{:S(2)}) %collective-permute-start.22) | collective-permute-done | bytes 196640 | tf_op jit(solution)/shard_map/ppermute | solution.py:43
  93.6 2.1 collective-permute-start.26
  98.4 4.9 shard_map.356
  103.5 4.4 collective-permute-done.26
  110.9 15.1 %collective-permute-done.30 = bf16[31,8,768]{2,1,0:T(8,128)(2,1)S(1)} collective-permute-done((bf16[31,8,768]{2,1,0:T(8,128)(2,1)S(1)}, bf16[31,8,768]{2,1,0:T(8,128)(2,1)S(1)}, u32[]{:S(2)}, u32[]{:S(2)}) %collective-permute-start.30) | collective-permute-done | bytes 380960 | tf_op jit(solution)/shard_map/ppermute | solution.py:43
  126.4 5.5 %collective-permute-done.31 = bf16[2,12,8,1024]{3,2,1,0:T(8,128)(2,1)S(1)} collective-permute-done((bf16[2,12,8,1024]{3,2,1,0:T(8,128)(2,1)S(1)}, bf16[2,12,8,1024]{3,2,1,0:T(8,128)(2,1)S(1)}, u32[]{:S(2)}, u32[]{:S(2)}) %collective-permute-start.31) | collective-permute-done | bytes 393248 | tf_op jit(solution)/shard_map/ppermute | solution.py:36
  135.3 11.2 %collective-permute-done.39 = bf16[8,8,1024]{2,1,0:T(8,128)(2,1)S(1)} collective-permute-done((bf16[8,8,1024]{2,1,0:T(8,128)(2,1)S(1)}, bf16[8,8,1024]{2,1,0:T(8,128)(2,1)S(1)}, u32[]{:S(2)}, u32[]{:S(2)}) %collective-permute-start.39) | collective-permute-done | bytes 131104 | tf_op jit(solution)/shard_map/ppermute | solution.py:43
  149.6 7.5 %collective-permute-done.32 = bf16[2,12,8,768]{3,2,1,0:T(8,128)(2,1)S(1)} collective-permute-done((bf16[2,12,8,768]{3,2,1,0:T(8,128)(2,1)S(1)}, bf16[2,12,8,768]{3,2,1,0:T(8,128)(2,1)S(1)}, u32[]{:S(2)}, u32[]{:S(2)}) %collective-permute-start.32) | collective-permute-done | bytes 294944 | tf_op jit(solution)/shard_map/ppermute | solution.py:36
  160.0 1.8 collective-permute-start.45
  162.5 2.2 shard_map.359
  166.3 2.2 collective-permute-done.34.got
  168.8 2.7 collective-permute-done.45
  171.6 8.8 %collective-permute-done.40 = bf16[2,31,8,768]{3,2,1,0:T(8,128)(2,1)S(1)} collective-permute-done((bf16[2,31,8,768]{3,2,1,0:T(8,128)(2,1)S(1)}, bf16[2,31,8,768]{3,2,1,0:T(8,128)(2,1)S(1)}, u32[]{:S(2)}, u32[]{:S(2)}) %collective-permute-start.40) | collective-permute-done | bytes 761888 | tf_op jit(solution)/shard_map/ppermute | solution.py:36
  182.6 5.7 %collective-permute-done.35.other = bf16[384,1024]{1,0:T(8,128)(2,1)S(1)} collective-permute-done((bf16[384,1024]{1,0:T(8,128)(2,1)S(1)}, bf16[384,1024]{1,0:T(8,128)(2,1)S(1)}, u32[]{:S(2)}, u32[]{:S(2)}) %collective-permute-start.35) | collective-permute-done | bytes 786464 | tf_op jit(solution)/shard_map/ppermute | solution.py:39
  192.2 3.6 shard_map.362
  197.8 7.0 %collective-permute-done.49 = bf16[2,8,8,1024]{3,2,1,0:T(8,128)(2,1)S(1)} collective-permute-done((bf16[2,8,8,1024]{3,2,1,0:T(8,128)(2,1)S(1)}, bf16[2,8,8,1024]{3,2,1,0:T(8,128)(2,1)S(1)}, u32[]{:S(2)}, u32[]{:S(2)}) %collective-permute-start.49) | collective-permute-done | bytes 262176 | tf_op jit(solution)/shard_map/ppermute | solution.py:33
  207.0 12.7 %collective-permute-done.50 = bf16[2,24,8,768]{3,2,1,0:T(8,128)(2,1)S(1)} collective-permute-done((bf16[2,24,8,768]{3,2,1,0:T(8,128)(2,1)S(1)}, bf16[2,24,8,768]{3,2,1,0:T(8,128)(2,1)S(1)}, u32[]{:S(2)}, u32[]{:S(2)}) %collective-permute-start.50) | collective-permute-done | bytes 589856 | tf_op jit(solution)/shard_map/ppermute | solution.py:33
  219.7 5.7 %collective-permute-done.42.other = bf16[384,1024]{1,0:T(8,128)(2,1)S(1)} collective-permute-done((bf16[384,1024]{1,0:T(8,128)(2,1)S(1)}, bf16[384,1024]{1,0:T(8,128)(2,1)S(1)}, u32[]{:S(2)}, u32[]{:S(2)}) %collective-permute-start.42) | collective-permute-done | bytes 786464 | tf_op jit(solution)/shard_map/ppermute | solution.py:39
  228.6 2.0 shard_map.365
  232.3 2.1 collective-permute-done.51.got
  236.8 25.9 %collective-permute-done.53 = bf16[192,1024]{1,0:T(8,128)(2,1)S(1)} collective-permute-done((bf16[192,1024]{1,0:T(8,128)(2,1)S(1)}, bf16[192,1024]{1,0:T(8,128)(2,1)S(1)}, u32[]{:S(2)}, u32[]{:S(2)}) %collective-permute-start.53) | collective-permute-done | bytes 393248 | tf_op jit(solution)/shard_map/ppermute | solution.py:39
  262.8 2.0 shard_map.367
  265.9 2.3 collective-permute-done.54.far.out_far
  268.2 3.0 shard_map.369
  274.0 2.5 collective-permute-done.55.got.refs_2_
  283.9 1.6 shard_map.372
  287.9 11.0 %collective-permute-done.56.refs_3_ = bf16[384,1024]{1,0:T(8,128)(2,1)S(1)} collective-permute-done((bf16[384,1024]{1,0:T(8,128)(2,1)S(1)}, bf16[384,1024]{1,0:T(8,128)(2,1)S(1)}, u32[]{:S(2)}, u32[]{:S(2)}) %collective-permute-start.56) | collective-permute-done | bytes 786464 | tf_op jit(solution)/shard_map/ppermute | solution.py:39
  299.1 2.4 shard_map.371
  302.7 2.3 collective-permute-done.58.far.out_far
  305.1 7.7 %shard_map.373 = (bf16[256,768]{1,0:T(8,128)(2,1)S(1)}, bf16[576,768]{1,0:T(8,128)(2,1)S(1)}, f32[384,1024]{1,0:T(8,128)S(1)}, bf16[384,1024]{1,0:T(8,128)(2,1)S(1)}) custom-call(bf16[384,1024]{1,0:T(8,128)(2,1)S(1)} %get-tuple-element.342.near.out_near, bf16[384,1024]{1,0:T(8,128)(2,1)S(1)} %collective-permute-done.58.far.out_far, ...), custom_call_target="tpu_custom_call" | custom-call | flops 1811939328 | bytes 10160128 | tf_op jit(solution)/shard_map/pallas_call | solution.py:421
  319.9 1.8 slice_bitcast_fusion.4
  330.2 2.3 shard_map.376
  332.5 3.9 collective-permute-done.60.refs_3_
  336.5 2.3 shard_map.375
  341.2 2.1 shard_map.377
  348.3 1.7 shard_map.380
  354.7 18.1 %collective-permute-done.65.refs_3_ = bf16[384,1024]{1,0:T(8,128)(2,1)S(1)} collective-permute-done((bf16[384,1024]{1,0:T(8,128)(2,1)S(1)}, bf16[384,1024]{1,0:T(8,128)(2,1)S(1)}, u32[]{:S(2)}, u32[]{:S(2)}) %collective-permute-start.65) | collective-permute-done | bytes 786464 | tf_op jit(solution)/shard_map/ppermute | solution.py:39
  377.9 9.5 %shard_map.381 = (bf16[256,768]{1,0:T(8,128)(2,1)S(1)}, bf16[576,768]{1,0:T(8,128)(2,1)S(1)}, f32[384,1024]{1,0:T(8,128)S(1)}, bf16[384,1024]{1,0:T(8,128)(2,1)S(1)}) custom-call(bf16[384,1024]{1,0:T(8,128)(2,1)S(1)} %get-tuple-element.399.near.out_near, bf16[384,1024]{1,0:T(8,128)(2,1)S(1)} %collective-permute-done.70.far.out_far, ...), custom_call_target="tpu_custom_call" | custom-call | flops 1811939328 | bytes 10160128 | tf_op jit(solution)/shard_map/pallas_call | solution.py:421
  393.9 2.2 shard_map.383
  396.1 5.5 %collective-permute-done.75 = bf16[2,12,8,1024]{3,2,1,0:T(8,128)(2,1)S(1)} collective-permute-done((bf16[2,12,8,1024]{3,2,1,0:T(8,128)(2,1)S(1)}, bf16[2,12,8,1024]{3,2,1,0:T(8,128)(2,1)S(1)}, u32[]{:S(2)}, u32[]{:S(2)}) %collective-permute-start.75) | collective-permute-done | bytes 393248 | tf_op jit(solution)/shard_map/ppermute | solution.py:33
  401.6 6.3 %collective-permute-done.74 = bf16[2,31,8,768]{3,2,1,0:T(8,128)(2,1)S(1)} collective-permute-done((bf16[2,31,8,768]{3,2,1,0:T(8,128)(2,1)S(1)}, bf16[2,31,8,768]{3,2,1,0:T(8,128)(2,1)S(1)}, u32[]{:S(2)}, u32[]{:S(2)}) %collective-permute-start.74) | collective-permute-done | bytes 761888 | tf_op jit(solution)/shard_map/ppermute | solution.py:36
  411.2 2.1 collective-permute-start.72
  413.5 7.1 %collective-permute-done.81 = bf16[2,24,8,768]{3,2,1,0:T(8,128)(2,1)S(1)} collective-permute-done((bf16[2,24,8,768]{3,2,1,0:T(8,128)(2,1)S(1)}, bf16[2,24,8,768]{3,2,1,0:T(8,128)(2,1)S(1)}, u32[]{:S(2)}, u32[]{:S(2)}) %collective-permute-start.81) | collective-permute-done | bytes 589856 | tf_op jit(solution)/shard_map/ppermute | solution.py:36
  421.7 5.4 %collective-permute-done.79 = bf16[31,8,768]{2,1,0:T(8,128)(2,1)S(1)} collective-permute-done((bf16[31,8,768]{2,1,0:T(8,128)(2,1)S(1)}, bf16[31,8,768]{2,1,0:T(8,128)(2,1)S(1)}, u32[]{:S(2)}, u32[]{:S(2)}) %collective-permute-start.79) | collective-permute-done | bytes 380960 | tf_op jit(solution)/shard_map/ppermute | solution.py:43
  428.3 1.6 collective-permute-start.98
  431.6 7.5 %collective-permute-done.82 = bf16[2,12,8,1024]{3,2,1,0:T(8,128)(2,1)S(1)} collective-permute-done((bf16[2,12,8,1024]{3,2,1,0:T(8,128)(2,1)S(1)}, bf16[2,12,8,1024]{3,2,1,0:T(8,128)(2,1)S(1)}, u32[]{:S(2)}, u32[]{:S(2)}) %collective-permute-start.82) | collective-permute-done | bytes 393248 | tf_op jit(solution)/shard_map/ppermute | solution.py:36
  440.4 1.6 collective-permute-start.83
  443.3 4.2 collective-permute-done.86
  447.5 17.1 %collective-permute-done.87 = bf16[12,8,1024]{2,1,0:T(8,128)(2,1)S(1)} collective-permute-done((bf16[12,8,1024]{2,1,0:T(8,128)(2,1)S(1)}, bf16[12,8,1024]{2,1,0:T(8,128)(2,1)S(1)}, u32[]{:S(2)}, u32[]{:S(2)}) %collective-permute-start.87) | collective-permute-done | bytes 196640 | tf_op jit(solution)/shard_map/ppermute | solution.py:43
  467.9 3.0 collective-permute-start.90
  472.2 25.3 %collective-permute-done.90 = bf16[12,8,1024]{2,1,0:T(8,128)(2,1)S(1)} collective-permute-done((bf16[12,8,1024]{2,1,0:T(8,128)(2,1)S(1)}, bf16[12,8,1024]{2,1,0:T(8,128)(2,1)S(1)}, u32[]{:S(2)}, u32[]{:S(2)}) %collective-permute-start.90) | collective-permute-done | bytes 196640 | tf_op jit(solution)/shard_map/ppermute | solution.py:43
  498.1 2.1 collective-permute-start.91
  501.0 13.6 %collective-permute-done.91 = bf16[2,112,768]{2,1,0:T(8,128)(2,1)S(1)} collective-permute-done((bf16[2,112,768]{2,1,0:T(8,128)(2,1)S(1)}, bf16[2,112,768]{2,1,0:T(8,128)(2,1)S(1)}, u32[]{:S(2)}, u32[]{:S(2)}) %collective-permute-start.91) | collective-permute-done | bytes 344096 | tf_op jit(solution)/shard_map/ppermute | solution.py:39
  (812 shorter events, 141.1 us)
Async XLA Ops:
  6.5 14.4 %collective-permute-start.13 = (f32[1,64]{1,0:T(1,128)S(1)}, f32[1,64]{1,0:T(1,128)S(1)}, u32[]{:S(2)}, u32[]{:S(2)}) collective-permute-start(f32[1,64]{1,0:T(1,128)S(1)} %convert_element_type.245), channel_id=1, source_target_pairs={{0,8},{8,0},{1,9},{9,1},{2,10},{10,2},{3,11},{11,3},{4,12},{12,4},... | collective-permute-start | bytes 776 | tf_op jit(solution)/shard_map/ppermute | solution.py:39
  16.1 25.0 %collective-permute-start.3 = (bf16[40,8,768]{2,1,0:T(8,128)(2,1)S(1)}, bf16[40,8,768]{2,1,0:T(8,128)(2,1)S(1)}, u32[]{:S(2)}, u32[]{:S(2)}) collective-permute-start(bf16[40,8,768]{2,1,0:T(8,128)(2,1)S(1)} %fusion.34), channel_id=1, source_target_pairs={{0,16},{16,0},{1,17},{17,1},{2,18},{18,2},{3,19},{19,3},{4,20},{20... | collective-permute-start | bytes 1474568 | tf_op jit(solution)/shard_map/ppermute | solution.py:43
  24.6 50.4 %collective-permute-start.20 = (bf16[16,1024]{1,0:T(8,128)(2,1)S(1)}, bf16[16,1024]{1,0:T(8,128)(2,1)S(1)}, u32[]{:S(2)}, u32[]{:S(2)}) collective-permute-start(bf16[16,1024]{1,0:T(8,128)(2,1)S(1)} %add.891), channel_id=1, source_target_pairs={{0,8},{8,0},{1,9},{9,1},{2,10},{10,2},{3,11},{11,3},{4,12},{12,4},... | collective-permute-start | bytes 98312 | tf_op jit(solution)/shard_map/ppermute | solution.py:39
  41.4 33.6 %collective-permute-start.6 = (bf16[2,40,8,768]{3,2,1,0:T(8,128)(2,1)S(1)}, bf16[2,40,8,768]{3,2,1,0:T(8,128)(2,1)S(1)}, u32[]{:S(2)}, u32[]{:S(2)}) collective-permute-start(bf16[2,40,8,768]{3,2,1,0:T(8,128)(2,1)S(1)} %pad_maximum_fusion), channel_id=1, source_target_pairs={{0,1},{1,0},{2,3},{3,2},{4,5},{5,4},{6,7},{7,6},{8,9},{9,8},{10,11... | collective-permute-start | bytes 2949128 | tf_op jit(solution)/shard_map/ppermute | solution.py:33
  42.0 33.1 %collective-permute-start.7 = (bf16[2,40,8,768]{3,2,1,0:T(8,128)(2,1)S(1)}, bf16[2,40,8,768]{3,2,1,0:T(8,128)(2,1)S(1)}, u32[]{:S(2)}, u32[]{:S(2)}) collective-permute-start(bf16[2,40,8,768]{3,2,1,0:T(8,128)(2,1)S(1)} %pad_maximum_fusion), channel_id=1, source_target_pairs={{0,4},{4,0},{1,5},{5,1},{2,6},{6,2},{3,7},{7,3},{8,12},{12,8},{9,1... | collective-permute-start | bytes 2949128 | tf_op jit(solution)/shard_map/ppermute | solution.py:36
  46.7 25.7 %collective-permute-start.9 = (bf16[2,168,768]{2,1,0:T(8,128)(2,1)S(1)}, bf16[2,168,768]{2,1,0:T(8,128)(2,1)S(1)}, u32[]{:S(2)}, u32[]{:S(2)}) collective-permute-start(bf16[2,168,768]{2,1,0:T(8,128)(2,1)S(1)} %get-tuple-element.502), channel_id=1, source_target_pairs={{0,8},{8,0},{1,9},{9,1},{2,10},{10,2},{3,11},{11,3},{4,12},{12,4},... | collective-permute-start | bytes 1548296 | tf_op jit(solution)/shard_map/ppermute | solution.py:39
  46.8 25.5 %collective-permute-start.4 = (bf16[192,1024]{1,0:T(8,128)(2,1)S(1)}, bf16[192,1024]{1,0:T(8,128)(2,1)S(1)}, u32[]{:S(2)}, u32[]{:S(2)}) collective-permute-start(bf16[192,1024]{1,0:T(8,128)(2,1)S(1)} %maximum_maximum_fusion), channel_id=1, source_target_pairs={{0,8},{8,0},{1,9},{9,1},{2,10},{10,2},{3,11},{11,3},{4,12},{12,4},... | collective-permute-start | bytes 1179656 | tf_op jit(solution)/shard_map/ppermute | solution.py:39
  74.9 23.4 %collective-permute-start.5 = (bf16[384,1024]{1,0:T(8,128)(2,1)S(1)}, bf16[384,1024]{1,0:T(8,128)(2,1)S(1)}, u32[]{:S(2)}, u32[]{:S(2)}) collective-permute-start(bf16[384,1024]{1,0:T(8,128)(2,1)S(1)} %pad_maximum_fusion.1.near.values), channel_id=1, source_target_pairs={{0,2},{2,0},{1,3},{3,1},{4,6},{6,4},{5,7},{7,5},{8,10},{10,8},{9,1... | collective-permute-start | bytes 2359304 | tf_op jit(solution)/shard_map/ppermute | solution.py:30
  75.0 28.4 %collective-permute-start.21 = (bf16[16,1024]{1,0:T(8,128)(2,1)S(1)}, bf16[16,1024]{1,0:T(8,128)(2,1)S(1)}, u32[]{:S(2)}, u32[]{:S(2)}) collective-permute-start(bf16[16,1024]{1,0:T(8,128)(2,1)S(1)} %add.892), channel_id=1, source_target_pairs={{0,16},{16,0},{1,17},{17,1},{2,18},{18,2},{3,19},{19,3},{4,20},{20... | collective-permute-start | bytes 98312 | tf_op jit(solution)/shard_map/ppermute | solution.py:43
  76.7 14.0 %collective-permute-start.11 = (bf16[2,20,8,768]{3,2,1,0:T(8,128)(2,1)S(1)}, bf16[2,20,8,768]{3,2,1,0:T(8,128)(2,1)S(1)}, u32[]{:S(2)}, u32[]{:S(2)}) collective-permute-start(bf16[2,20,8,768]{3,2,1,0:T(8,128)(2,1)S(1)} %slice.1008), channel_id=1, source_target_pairs={{0,4},{4,0},{1,5},{5,1},{2,6},{6,2},{3,7},{7,3},{8,12},{12,8},{9,1... | collective-permute-start | bytes 1474568 | tf_op jit(solution)/shard_map/ppermute | solution.py:36
  77.3 13.4 %collective-permute-start.12 = (bf16[2,20,8,768]{3,2,1,0:T(8,128)(2,1)S(1)}, bf16[2,20,8,768]{3,2,1,0:T(8,128)(2,1)S(1)}, u32[]{:S(2)}, u32[]{:S(2)}) collective-permute-start(bf16[2,20,8,768]{3,2,1,0:T(8,128)(2,1)S(1)} %slice.1009), channel_id=1, source_target_pairs={{0,1},{1,0},{2,3},{3,2},{4,5},{5,4},{6,7},{7,6},{8,9},{9,8},{10,11... | collective-permute-start | bytes 1474568 | tf_op jit(solution)/shard_map/ppermute | solution.py:33
  90.7 17.4 %collective-permute-start.25 = (bf16[2,12,8,1024]{3,2,1,0:T(8,128)(2,1)S(1)}, bf16[2,12,8,1024]{3,2,1,0:T(8,128)(2,1)S(1)}, u32[]{:S(2)}, u32[]{:S(2)}) collective-permute-start(bf16[2,12,8,1024]{3,2,1,0:T(8,128)(2,1)S(1)} %pad_maximum_fusion.18), channel_id=1, source_target_pairs={{0,1},{1,0},{2,3},{3,2},{4,5},{5,4},{6,7},{7,6},{8,9},{9,8},{10,11... | collective-permute-start | bytes 1179656 | tf_op jit(solution)/shard_map/ppermute | solution.py:33
  92.1 16.0 %collective-permute-start.27 = (bf16[2,12,8,1024]{3,2,1,0:T(8,128)(2,1)S(1)}, bf16[2,12,8,1024]{3,2,1,0:T(8,128)(2,1)S(1)}, u32[]{:S(2)}, u32[]{:S(2)}) collective-permute-start(bf16[2,12,8,1024]{3,2,1,0:T(8,128)(2,1)S(1)} %pad_maximum_fusion.18), channel_id=1, source_target_pairs={{0,4},{4,0},{1,5},{5,1},{2,6},{6,2},{3,7},{7,3},{8,12},{12,8},{9,1... | collective-permute-start | bytes 1179656 | tf_op jit(solution)/shard_map/ppermute | solution.py:36
  93.6 14.3 %collective-permute-start.26 = (bf16[24,8,768]{2,1,0:T(8,128)(2,1)S(1)}, bf16[24,8,768]{2,1,0:T(8,128)(2,1)S(1)}, u32[]{:S(2)}, u32[]{:S(2)}) collective-permute-start(bf16[24,8,768]{2,1,0:T(8,128)(2,1)S(1)} %pad_maximum_fusion.25), channel_id=1, source_target_pairs={{0,16},{16,0},{1,17},{17,1},{2,18},{18,2},{3,19},{19,3},{4,20},{20... | collective-permute-start | bytes 884744 | tf_op jit(solution)/shard_map/ppermute | solution.py:43
  103.4 22.8 %collective-permute-start.15 = (bf16[384,1024]{1,0:T(8,128)(2,1)S(1)}, bf16[384,1024]{1,0:T(8,128)(2,1)S(1)}, u32[]{:S(2)}, u32[]{:S(2)}) collective-permute-start(bf16[384,1024]{1,0:T(8,128)(2,1)S(1)} %get-tuple-element.256), channel_id=1, source_target_pairs={{0,2},{2,0},{1,3},{3,1},{4,6},{6,4},{5,7},{7,5},{8,10},{10,8},{9,1... | collective-permute-start | bytes 2359304 | tf_op jit(solution)/shard_map/ppermute | solution.py:30
  108.1 24.3 %collective-permute-start.29 = (bf16[2,24,8,768]{3,2,1,0:T(8,128)(2,1)S(1)}, bf16[2,24,8,768]{3,2,1,0:T(8,128)(2,1)S(1)}, u32[]{:S(2)}, u32[]{:S(2)}) collective-permute-start(bf16[2,24,8,768]{3,2,1,0:T(8,128)(2,1)S(1)} %pad_maximum_fusion.6), channel_id=1, source_target_pairs={{0,4},{4,0},{1,5},{5,1},{2,6},{6,2},{3,7},{7,3},{8,12},{12,8},{9,1... | collective-permute-start | bytes 1769480 | tf_op jit(solution)/shard_map/ppermute | solution.py:36
  108.7 23.7 %collective-permute-start.28 = (bf16[2,24,8,768]{3,2,1,0:T(8,128)(2,1)S(1)}, bf16[2,24,8,768]{3,2,1,0:T(8,128)(2,1)S(1)}, u32[]{:S(2)}, u32[]{:S(2)}) collective-permute-start(bf16[2,24,8,768]{3,2,1,0:T(8,128)(2,1)S(1)} %pad_maximum_fusion.6), channel_id=1, source_target_pairs={{0,1},{1,0},{2,3},{3,2},{4,5},{5,4},{6,7},{7,6},{8,9},{9,8},{10,11... | collective-permute-start | bytes 1769480 | tf_op jit(solution)/shard_map/ppermute | solution.py:33
  109.4 16.6 %collective-permute-start.30 = (bf16[31,8,768]{2,1,0:T(8,128)(2,1)S(1)}, bf16[31,8,768]{2,1,0:T(8,128)(2,1)S(1)}, u32[]{:S(2)}, u32[]{:S(2)}) collective-permute-start(bf16[31,8,768]{2,1,0:T(8,128)(2,1)S(1)} %pad_maximum_fusion.23), channel_id=1, source_target_pairs={{0,16},{16,0},{1,17},{17,1},{2,18},{18,2},{3,19},{19,3},{4,20},{20... | collective-permute-start | bytes 1142792 | tf_op jit(solution)/shard_map/ppermute | solution.py:43
  109.5 22.4 %collective-permute-start.31 = (bf16[2,12,8,1024]{3,2,1,0:T(8,128)(2,1)S(1)}, bf16[2,12,8,1024]{3,2,1,0:T(8,128)(2,1)S(1)}, u32[]{:S(2)}, u32[]{:S(2)}) collective-permute-start(bf16[2,12,8,1024]{3,2,1,0:T(8,128)(2,1)S(1)} %collective-permute-done.25), channel_id=1, source_target_pairs={{0,4},{4,0},{1,5},{5,1},{2,6},{6,2},{3,7},{7,3},{8,12},{12,8},{9,1... | collective-permute-start | bytes 1179656 | tf_op jit(solution)/shard_map/ppermute | solution.py:36
  126.3 22.3 %collective-permute-start.16 = (bf16[384,1024]{1,0:T(8,128)(2,1)S(1)}, bf16[384,1024]{1,0:T(8,128)(2,1)S(1)}, u32[]{:S(2)}, u32[]{:S(2)}) collective-permute-start(bf16[384,1024]{1,0:T(8,128)(2,1)S(1)} %shard_map.357), channel_id=1, source_target_pairs={{0,8},{8,0},{1,9},{9,1},{2,10},{10,2},{3,11},{11,3},{4,12},{12,4},... | collective-permute-start | bytes 2359304 | tf_op jit(solution)/shard_map/ppermute | solution.py:39
  132.5 25.1 %collective-permute-start.37 = (bf16[2,31,8,768]{3,2,1,0:T(8,128)(2,1)S(1)}, bf16[2,31,8,768]{3,2,1,0:T(8,128)(2,1)S(1)}, u32[]{:S(2)}, u32[]{:S(2)}) collective-permute-start(bf16[2,31,8,768]{3,2,1,0:T(8,128)(2,1)S(1)} %pad_maximum_fusion.3), channel_id=1, source_target_pairs={{0,1},{1,0},{2,3},{3,2},{4,5},{5,4},{6,7},{7,6},{8,9},{9,8},{10,11... | collective-permute-start | bytes 2285576 | tf_op jit(solution)/shard_map/ppermute | solution.py:33
  133.0 24.6 %collective-permute-start.38 = (bf16[2,31,8,768]{3,2,1,0:T(8,128)(2,1)S(1)}, bf16[2,31,8,768]{3,2,1,0:T(8,128)(2,1)S(1)}, u32[]{:S(2)}, u32[]{:S(2)}) collective-permute-start(bf16[2,31,8,768]{3,2,1,0:T(8,128)(2,1)S(1)} %pad_maximum_fusion.3), channel_id=1, source_target_pairs={{0,4},{4,0},{1,5},{5,1},{2,6},{6,2},{3,7},{7,3},{8,12},{12,8},{9,1... | collective-permute-start | bytes 2285576 | tf_op jit(solution)/shard_map/ppermute | solution.py:36
  133.9 23.2 %collective-permute-start.32 = (bf16[2,12,8,768]{3,2,1,0:T(8,128)(2,1)S(1)}, bf16[2,12,8,768]{3,2,1,0:T(8,128)(2,1)S(1)}, u32[]{:S(2)}, u32[]{:S(2)}) collective-permute-start(bf16[2,12,8,768]{3,2,1,0:T(8,128)(2,1)S(1)} %get-tuple-element.270), channel_id=1, source_target_pairs={{0,4},{4,0},{1,5},{5,1},{2,6},{6,2},{3,7},{7,3},{8,12},{12,8},{9,1... | collective-permute-start | bytes 884744 | tf_op jit(solution)/shard_map/ppermute | solution.py:36
  161.7 18.7 %collective-permute-start.40 = (bf16[2,31,8,768]{3,2,1,0:T(8,128)(2,1)S(1)}, bf16[2,31,8,768]{3,2,1,0:T(8,128)(2,1)S(1)}, u32[]{:S(2)}, u32[]{:S(2)}) collective-permute-start(bf16[2,31,8,768]{3,2,1,0:T(8,128)(2,1)S(1)} %collective-permute-done.37), channel_id=1, source_target_pairs={{0,4},{4,0},{1,5},{5,1},{2,6},{6,2},{3,7},{7,3},{8,12},{12,8},{9,1... | collective-permute-start | bytes 2285576 | tf_op jit(solution)/shard_map/ppermute | solution.py:36
  168.7 19.7 %collective-permute-start.35 = (bf16[384,1024]{1,0:T(8,128)(2,1)S(1)}, bf16[384,1024]{1,0:T(8,128)(2,1)S(1)}, u32[]{:S(2)}, u32[]{:S(2)}) collective-permute-start(bf16[384,1024]{1,0:T(8,128)(2,1)S(1)} %shard_map.360), channel_id=1, source_target_pairs={{0,8},{8,0},{1,9},{9,1},{2,10},{10,2},{3,11},{11,3},{4,12},{12,4},... | collective-permute-start | bytes 2359304 | tf_op jit(solution)/shard_map/ppermute | solution.py:39
  180.4 17.3 %collective-permute-start.47 = (bf16[2,24,8,768]{3,2,1,0:T(8,128)(2,1)S(1)}, bf16[2,24,8,768]{3,2,1,0:T(8,128)(2,1)S(1)}, u32[]{:S(2)}, u32[]{:S(2)}) collective-permute-start(bf16[2,24,8,768]{3,2,1,0:T(8,128)(2,1)S(1)} %pad_maximum_fusion.7), channel_id=1, source_target_pairs={{0,1},{1,0},{2,3},{3,2},{4,5},{5,4},{6,7},{7,6},{8,9},{9,8},{10,11... | collective-permute-start | bytes 1769480 | tf_op jit(solution)/shard_map/ppermute | solution.py:33
  182.0 15.7 %collective-permute-start.48 = (bf16[2,24,8,768]{3,2,1,0:T(8,128)(2,1)S(1)}, bf16[2,24,8,768]{3,2,1,0:T(8,128)(2,1)S(1)}, u32[]{:S(2)}, u32[]{:S(2)}) collective-permute-start(bf16[2,24,8,768]{3,2,1,0:T(8,128)(2,1)S(1)} %pad_maximum_fusion.7), channel_id=1, source_target_pairs={{0,4},{4,0},{1,5},{5,1},{2,6},{6,2},{3,7},{7,3},{8,12},{12,8},{9,1... | collective-permute-start | bytes 1769480 | tf_op jit(solution)/shard_map/ppermute | solution.py:36
  204.8 14.9 %collective-permute-start.50 = (bf16[2,24,8,768]{3,2,1,0:T(8,128)(2,1)S(1)}, bf16[2,24,8,768]{3,2,1,0:T(8,128)(2,1)S(1)}, u32[]{:S(2)}, u32[]{:S(2)}) collective-permute-start(bf16[2,24,8,768]{3,2,1,0:T(8,128)(2,1)S(1)} %collective-permute-done.48), channel_id=1, source_target_pairs={{0,1},{1,0},{2,3},{3,2},{4,5},{5,4},{6,7},{7,6},{8,9},{9,8},{10,11... | collective-permute-start | bytes 1769480 | tf_op jit(solution)/shard_map/ppermute | solution.py:33
  206.5 18.9 %collective-permute-start.42 = (bf16[384,1024]{1,0:T(8,128)(2,1)S(1)}, bf16[384,1024]{1,0:T(8,128)(2,1)S(1)}, u32[]{:S(2)}, u32[]{:S(2)}) collective-permute-start(bf16[384,1024]{1,0:T(8,128)(2,1)S(1)} %shard_map.363), channel_id=1, source_target_pairs={{0,8},{8,0},{1,9},{9,1},{2,10},{10,2},{3,11},{11,3},{4,12},{12,4},... | collective-permute-start | bytes 2359304 | tf_op jit(solution)/shard_map/ppermute | solution.py:39
  234.6 28.2 %collective-permute-start.52 = (bf16[384,1024]{1,0:T(8,128)(2,1)S(1)}, bf16[384,1024]{1,0:T(8,128)(2,1)S(1)}, u32[]{:S(2)}, u32[]{:S(2)}) collective-permute-start(bf16[384,1024]{1,0:T(8,128)(2,1)S(1)} %shard_map.366), channel_id=1, source_target_pairs={{0,8},{8,0},{1,9},{9,1},{2,10},{10,2},{3,11},{11,3},{4,12},{12,4},... | collective-permute-start | bytes 2359304 | tf_op jit(solution)/shard_map/ppermute | solution.py:39
  235.4 27.2 %collective-permute-start.53 = (bf16[192,1024]{1,0:T(8,128)(2,1)S(1)}, bf16[192,1024]{1,0:T(8,128)(2,1)S(1)}, u32[]{:S(2)}, u32[]{:S(2)}) collective-permute-start(bf16[192,1024]{1,0:T(8,128)(2,1)S(1)} %maximum_maximum_fusion.1), channel_id=1, source_target_pairs={{0,8},{8,0},{1,9},{9,1},{2,10},{10,2},{3,11},{11,3},{4,12},{12,4},... | collective-permute-start | bytes 1179656 | tf_op jit(solution)/shard_map/ppermute | solution.py:39
  279.3 19.6 %collective-permute-start.56 = (bf16[384,1024]{1,0:T(8,128)(2,1)S(1)}, bf16[384,1024]{1,0:T(8,128)(2,1)S(1)}, u32[]{:S(2)}, u32[]{:S(2)}) collective-permute-start(bf16[384,1024]{1,0:T(8,128)(2,1)S(1)} %shard_map.370), channel_id=1, source_target_pairs={{0,8},{8,0},{1,9},{9,1},{2,10},{10,2},{3,11},{11,3},{4,12},{12,4},... | collective-permute-start | bytes 2359304 | tf_op jit(solution)/shard_map/ppermute | solution.py:39
  287.3 15.4 %collective-permute-start.57 = (bf16[2,24,8,768]{3,2,1,0:T(8,128)(2,1)S(1)}, bf16[2,24,8,768]{3,2,1,0:T(8,128)(2,1)S(1)}, u32[]{:S(2)}, u32[]{:S(2)}) collective-permute-start(bf16[2,24,8,768]{3,2,1,0:T(8,128)(2,1)S(1)} %pad_maximum_fusion.8), channel_id=1, source_target_pairs={{0,4},{4,0},{1,5},{5,1},{2,6},{6,2},{3,7},{7,3},{8,12},{12,8},{9,1... | collective-permute-start | bytes 1769480 | tf_op jit(solution)/shard_map/ppermute | solution.py:36
  314.1 24.6 %collective-permute-start.62 = (bf16[2,24,8,768]{3,2,1,0:T(8,128)(2,1)}, bf16[2,24,8,768]{3,2,1,0:T(8,128)(2,1)}, u32[]{:S(2)}, u32[]{:S(2)}) collective-permute-start(bf16[2,24,8,768]{3,2,1,0:T(8,128)(2,1)} %pad_maximum_fusion.9), channel_id=1, source_target_pairs={{0,4},{4,0},{1,5},{5,1},{2,6},{6,2},{3,7},{7,3},{8,12},{12,8},{9,1... | collective-permute-start | bytes 1769480 | tf_op jit(solution)/shard_map/ppermute | solution.py:36
  316.4 20.1 %collective-permute-start.60 = (bf16[384,1024]{1,0:T(8,128)(2,1)}, bf16[384,1024]{1,0:T(8,128)(2,1)}, u32[]{:S(2)}, u32[]{:S(2)}) collective-permute-start(bf16[384,1024]{1,0:T(8,128)(2,1)} %shard_map.374), channel_id=1, source_target_pairs={{0,8},{8,0},{1,9},{9,1},{2,10},{10,2},{3,11},{11,3},{4,12},{12,4},... | collective-permute-start | bytes 2359304 | tf_op jit(solution)/shard_map/ppermute | solution.py:39
  318.6 20.2 %collective-permute-start.61 = (bf16[2,24,8,768]{3,2,1,0:T(8,128)(2,1)}, bf16[2,24,8,768]{3,2,1,0:T(8,128)(2,1)}, u32[]{:S(2)}, u32[]{:S(2)}) collective-permute-start(bf16[2,24,8,768]{3,2,1,0:T(8,128)(2,1)} %add_convert_fusion.6), channel_id=1, source_target_pairs={{0,1},{1,0},{2,3},{3,2},{4,5},{5,4},{6,7},{7,6},{8,9},{9,8},{10,11... | collective-permute-start | bytes 1769480 | tf_op jit(solution)/shard_map/ppermute | solution.py:33
  339.4 35.6 %collective-permute-start.67 = (bf16[2,31,8,768]{3,2,1,0:T(8,128)(2,1)S(1)}, bf16[2,31,8,768]{3,2,1,0:T(8,128)(2,1)S(1)}, u32[]{:S(2)}, u32[]{:S(2)}) collective-permute-start(bf16[2,31,8,768]{3,2,1,0:T(8,128)(2,1)S(1)} %pad_maximum_fusion.4), channel_id=1, source_target_pairs={{0,1},{1,0},{2,3},{3,2},{4,5},{5,4},{6,7},{7,6},{8,9},{9,8},{10,11... | collective-permute-start | bytes 2285576 | tf_op jit(solution)/shard_map/ppermute | solution.py:33
  343.8 31.2 %collective-permute-start.68 = (bf16[2,12,8,1024]{3,2,1,0:T(8,128)(2,1)S(1)}, bf16[2,12,8,1024]{3,2,1,0:T(8,128)(2,1)S(1)}, u32[]{:S(2)}, u32[]{:S(2)}) collective-permute-start(bf16[2,12,8,1024]{3,2,1,0:T(8,128)(2,1)S(1)} %pad_maximum_fusion.19), channel_id=1, source_target_pairs={{0,4},{4,0},{1,5},{5,1},{2,6},{6,2},{3,7},{7,3},{8,12},{12,8},{9,1... | collective-permute-start | bytes 1179656 | tf_op jit(solution)/shard_map/ppermute | solution.py:36
  347.0 25.8 %collective-permute-start.65 = (bf16[384,1024]{1,0:T(8,128)(2,1)S(1)}, bf16[384,1024]{1,0:T(8,128)(2,1)S(1)}, u32[]{:S(2)}, u32[]{:S(2)}) collective-permute-start(bf16[384,1024]{1,0:T(8,128)(2,1)S(1)} %shard_map.378), channel_id=1, source_target_pairs={{0,8},{8,0},{1,9},{9,1},{2,10},{10,2},{3,11},{11,3},{4,12},{12,4},... | collective-permute-start | bytes 2359304 | tf_op jit(solution)/shard_map/ppermute | solution.py:39
  350.3 24.7 %collective-permute-start.69 = (bf16[2,24,8,768]{3,2,1,0:T(8,128)(2,1)S(1)}, bf16[2,24,8,768]{3,2,1,0:T(8,128)(2,1)S(1)}, u32[]{:S(2)}, u32[]{:S(2)}) collective-permute-start(bf16[2,24,8,768]{3,2,1,0:T(8,128)(2,1)S(1)} %pad_maximum_fusion.10), channel_id=1, source_target_pairs={{0,4},{4,0},{1,5},{5,1},{2,6},{6,2},{3,7},{7,3},{8,12},{12,8},{9,1... | collective-permute-start | bytes 1769480 | tf_op jit(solution)/shard_map/ppermute | solution.py:36
  351.1 23.8 %collective-permute-start.66 = (bf16[24,8,768]{2,1,0:T(8,128)(2,1)S(1)}, bf16[24,8,768]{2,1,0:T(8,128)(2,1)S(1)}, u32[]{:S(2)}, u32[]{:S(2)}) collective-permute-start(bf16[24,8,768]{2,1,0:T(8,128)(2,1)S(1)} %dynamic-slice_bitcast_fusion.39), channel_id=1, source_target_pairs={{0,16},{16,0},{1,17},{17,1},{2,18},{18,2},{3,19},{19,3},{4,20},{20... | collective-permute-start | bytes 884744 | tf_op jit(solution)/shard_map/ppermute | solution.py:43
  372.8 23.3 %collective-permute-start.73 = (bf16[2,31,8,768]{3,2,1,0:T(8,128)(2,1)S(1)}, bf16[2,31,8,768]{3,2,1,0:T(8,128)(2,1)S(1)}, u32[]{:S(2)}, u32[]{:S(2)}) collective-permute-start(bf16[2,31,8,768]{3,2,1,0:T(8,128)(2,1)S(1)} %pad_maximum_fusion.5), channel_id=1, source_target_pairs={{0,1},{1,0},{2,3},{3,2},{4,5},{5,4},{6,7},{7,6},{8,9},{9,8},{10,11... | collective-permute-start | bytes 2285576 | tf_op jit(solution)/shard_map/ppermute | solution.py:33
  375.1 21.0 %collective-permute-start.76 = (bf16[2,12,8,1024]{3,2,1,0:T(8,128)(2,1)S(1)}, bf16[2,12,8,1024]{3,2,1,0:T(8,128)(2,1)S(1)}, u32[]{:S(2)}, u32[]{:S(2)}) collective-permute-start(bf16[2,12,8,1024]{3,2,1,0:T(8,128)(2,1)S(1)} %pad_maximum_fusion.20), channel_id=1, source_target_pairs={{0,4},{4,0},{1,5},{5,1},{2,6},{6,2},{3,7},{7,3},{8,12},{12,8},{9,1... | collective-permute-start | bytes 1179656 | tf_op jit(solution)/shard_map/ppermute | solution.py:36
  388.0 19.9 %collective-permute-start.74 = (bf16[2,31,8,768]{3,2,1,0:T(8,128)(2,1)S(1)}, bf16[2,31,8,768]{3,2,1,0:T(8,128)(2,1)S(1)}, u32[]{:S(2)}, u32[]{:S(2)}) collective-permute-start(bf16[2,31,8,768]{3,2,1,0:T(8,128)(2,1)S(1)} %add_convert_fusion.2), channel_id=1, source_target_pairs={{0,4},{4,0},{1,5},{5,1},{2,6},{6,2},{3,7},{7,3},{8,12},{12,8},{9,1... | collective-permute-start | bytes 2285576 | tf_op jit(solution)/shard_map/ppermute | solution.py:36
  391.6 28.9 %collective-permute-start.81 = (bf16[2,24,8,768]{3,2,1,0:T(8,128)(2,1)S(1)}, bf16[2,24,8,768]{3,2,1,0:T(8,128)(2,1)S(1)}, u32[]{:S(2)}, u32[]{:S(2)}) collective-permute-start(bf16[2,24,8,768]{3,2,1,0:T(8,128)(2,1)S(1)} %pad_maximum_fusion.11), channel_id=1, source_target_pairs={{0,4},{4,0},{1,5},{5,1},{2,6},{6,2},{3,7},{7,3},{8,12},{12,8},{9,1... | collective-permute-start | bytes 1769480 | tf_op jit(solution)/shard_map/ppermute | solution.py:36
  408.1 31.0 %collective-permute-start.80 = (bf16[2,24,8,768]{3,2,1,0:T(8,128)(2,1)S(1)}, bf16[2,24,8,768]{3,2,1,0:T(8,128)(2,1)S(1)}, u32[]{:S(2)}, u32[]{:S(2)}) collective-permute-start(bf16[2,24,8,768]{3,2,1,0:T(8,128)(2,1)S(1)} %add_convert_fusion.4), channel_id=1, source_target_pairs={{0,1},{1,0},{2,3},{3,2},{4,5},{5,4},{6,7},{7,6},{8,9},{9,8},{10,11... | collective-permute-start | bytes 1769480 | tf_op jit(solution)/shard_map/ppermute | solution.py:33
  409.6 17.5 %collective-permute-start.79 = (bf16[31,8,768]{2,1,0:T(8,128)(2,1)S(1)}, bf16[31,8,768]{2,1,0:T(8,128)(2,1)S(1)}, u32[]{:S(2)}, u32[]{:S(2)}) collective-permute-start(bf16[31,8,768]{2,1,0:T(8,128)(2,1)S(1)} %dynamic-slice_bitcast_fusion.13), channel_id=1, source_target_pairs={{0,16},{16,0},{1,17},{17,1},{2,18},{18,2},{3,19},{19,3},{4,20},{20... | collective-permute-start | bytes 1142792 | tf_op jit(solution)/shard_map/ppermute | solution.py:43
  410.1 18.2 %collective-permute-start.77 = (bf16[2,16,8,768]{3,2,1,0:T(8,128)(2,1)S(1)}, bf16[2,16,8,768]{3,2,1,0:T(8,128)(2,1)S(1)}, u32[]{:S(2)}, u32[]{:S(2)}) collective-permute-start(bf16[2,16,8,768]{3,2,1,0:T(8,128)(2,1)S(1)} %get-tuple-element.583), channel_id=1, source_target_pairs={{0,4},{4,0},{1,5},{5,1},{2,6},{6,2},{3,7},{7,3},{8,12},{12,8},{9,1... | collective-permute-start | bytes 1179656 | tf_op jit(solution)/shard_map/ppermute | solution.py:36
  411.2 27.8 %collective-permute-start.72 = (bf16[384,1024]{1,0:T(8,128)(2,1)S(1)}, bf16[384,1024]{1,0:T(8,128)(2,1)S(1)}, u32[]{:S(2)}, u32[]{:S(2)}) collective-permute-start(bf16[384,1024]{1,0:T(8,128)(2,1)S(1)} %shard_map.382), channel_id=1, source_target_pairs={{0,8},{8,0},{1,9},{9,1},{2,10},{10,2},{3,11},{11,3},{4,12},{12,4},... | collective-permute-start | bytes 2359304 | tf_op jit(solution)/shard_map/ppermute | solution.py:39
  428.3 14.8 %collective-permute-start.98 = (f32[16,1024]{1,0:T(8,128)S(1)}, f32[16,1024]{1,0:T(8,128)S(1)}, u32[]{:S(2)}, u32[]{:S(2)}) collective-permute-start(f32[16,1024]{1,0:T(8,128)S(1)} %fusion.37), channel_id=1, source_target_pairs={{0,1},{1,0},{2,3},{3,2},{4,5},{5,4},{6,7},{7,6},{8,9},{9,8},{10,11... | collective-permute-start | bytes 196616 | tf_op jit(solution)/shard_map/ppermute | solution.py:33
  430.5 16.9 %collective-permute-start.86 = (bf16[2,12,8,1024]{3,2,1,0:T(8,128)(2,1)S(1)}, bf16[2,12,8,1024]{3,2,1,0:T(8,128)(2,1)S(1)}, u32[]{:S(2)}, u32[]{:S(2)}) collective-permute-start(bf16[2,12,8,1024]{3,2,1,0:T(8,128)(2,1)S(1)} %pad_maximum_fusion.22), channel_id=1, source_target_pairs={{0,4},{4,0},{1,5},{5,1},{2,6},{6,2},{3,7},{7,3},{8,12},{12,8},{9,1... | collective-permute-start | bytes 1179656 | tf_op jit(solution)/shard_map/ppermute | solution.py:36
  439.2 26.9 %collective-permute-start.84 = (bf16[2,32,8,768]{3,2,1,0:T(8,128)(2,1)S(1)}, bf16[2,32,8,768]{3,2,1,0:T(8,128)(2,1)S(1)}, u32[]{:S(2)}, u32[]{:S(2)}) collective-permute-start(bf16[2,32,8,768]{3,2,1,0:T(8,128)(2,1)S(1)} %fusion.5), channel_id=1, source_target_pairs={{0,4},{4,0},{1,5},{5,1},{2,6},{6,2},{3,7},{7,3},{8,12},{12,8},{9,1... | collective-permute-start | bytes 2359304 | tf_op jit(solution)/shard_map/ppermute | solution.py:36
  440.4 25.8 %collective-permute-start.83 = (bf16[2,32,8,768]{3,2,1,0:T(8,128)(2,1)S(1)}, bf16[2,32,8,768]{3,2,1,0:T(8,128)(2,1)S(1)}, u32[]{:S(2)}, u32[]{:S(2)}) collective-permute-start(bf16[2,32,8,768]{3,2,1,0:T(8,128)(2,1)S(1)} %fusion.7), channel_id=1, source_target_pairs={{0,1},{1,0},{2,3},{3,2},{4,5},{5,4},{6,7},{7,6},{8,9},{9,8},{10,11... | collective-permute-start | bytes 2359304 | tf_op jit(solution)/shard_map/ppermute | solution.py:33
  442.1 24.1 %collective-permute-start.85 = (bf16[2,12,8,1024]{3,2,1,0:T(8,128)(2,1)S(1)}, bf16[2,12,8,1024]{3,2,1,0:T(8,128)(2,1)S(1)}, u32[]{:S(2)}, u32[]{:S(2)}) collective-permute-start(bf16[2,12,8,1024]{3,2,1,0:T(8,128)(2,1)S(1)} %add_convert_fusion.9), channel_id=1, source_target_pairs={{0,1},{1,0},{2,3},{3,2},{4,5},{5,4},{6,7},{7,6},{8,9},{9,8},{10,11... | collective-permute-start | bytes 1179656 | tf_op jit(solution)/shard_map/ppermute | solution.py:33
  443.1 21.5 %collective-permute-start.88 = (bf16[24,8,768]{2,1,0:T(8,128)(2,1)S(1)}, bf16[24,8,768]{2,1,0:T(8,128)(2,1)S(1)}, u32[]{:S(2)}, u32[]{:S(2)}) collective-permute-start(bf16[24,8,768]{2,1,0:T(8,128)(2,1)S(1)} %dynamic-slice_bitcast_fusion.22), channel_id=1, source_target_pairs={{0,16},{16,0},{1,17},{17,1},{2,18},{18,2},{3,19},{19,3},{4,20},{20... | collective-permute-start | bytes 884744 | tf_op jit(solution)/shard_map/ppermute | solution.py:43
  447.5 17.1 %collective-permute-start.87 = (bf16[12,8,1024]{2,1,0:T(8,128)(2,1)S(1)}, bf16[12,8,1024]{2,1,0:T(8,128)(2,1)S(1)}, u32[]{:S(2)}, u32[]{:S(2)}) collective-permute-start(bf16[12,8,1024]{2,1,0:T(8,128)(2,1)S(1)} %dynamic-slice_bitcast_fusion.49), channel_id=1, source_target_pairs={{0,16},{16,0},{1,17},{17,1},{2,18},{18,2},{3,19},{19,3},{4,20},{20... | collective-permute-start | bytes 589832 | tf_op jit(solution)/shard_map/ppermute | solution.py:43
  466.1 31.5 %collective-permute-start.99 = (f32[16,1024]{1,0:T(8,128)S(1)}, f32[16,1024]{1,0:T(8,128)S(1)}, u32[]{:S(2)}, u32[]{:S(2)}) collective-permute-start(f32[16,1024]{1,0:T(8,128)S(1)} %add.936), channel_id=1, source_target_pairs={{0,4},{4,0},{1,5},{5,1},{2,6},{6,2},{3,7},{7,3},{8,12},{12,8},{9,1... | collective-permute-start | bytes 196616 | tf_op jit(solution)/shard_map/ppermute | solution.py:36
  467.6 29.9 %collective-permute-start.89 = (bf16[32,8,768]{2,1,0:T(8,128)(2,1)S(1)}, bf16[32,8,768]{2,1,0:T(8,128)(2,1)S(1)}, u32[]{:S(2)}, u32[]{:S(2)}) collective-permute-start(bf16[32,8,768]{2,1,0:T(8,128)(2,1)S(1)} %dynamic-slice_bitcast_fusion.4), channel_id=1, source_target_pairs={{0,16},{16,0},{1,17},{17,1},{2,18},{18,2},{3,19},{19,3},{4,20},{20... | collective-permute-start | bytes 1179656 | tf_op jit(solution)/shard_map/ppermute | solution.py:43
  467.9 29.6 %collective-permute-start.90 = (bf16[12,8,1024]{2,1,0:T(8,128)(2,1)S(1)}, bf16[12,8,1024]{2,1,0:T(8,128)(2,1)S(1)}, u32[]{:S(2)}, u32[]{:S(2)}) collective-permute-start(bf16[12,8,1024]{2,1,0:T(8,128)(2,1)S(1)} %dynamic-slice_bitcast_fusion.48), channel_id=1, source_target_pairs={{0,16},{16,0},{1,17},{17,1},{2,18},{18,2},{3,19},{19,3},{4,20},{20... | collective-permute-start | bytes 589832 | tf_op jit(solution)/shard_map/ppermute | solution.py:43
  471.4 28.9 %collective-permute-start.94 = (bf16[2,112,768]{2,1,0:T(8,128)(2,1)S(1)}, bf16[2,112,768]{2,1,0:T(8,128)(2,1)S(1)}, u32[]{:S(2)}, u32[]{:S(2)}) collective-permute-start(bf16[2,112,768]{2,1,0:T(8,128)(2,1)S(1)} %get-tuple-element.525), channel_id=1, source_target_pairs={{0,8},{8,0},{1,9},{9,1},{2,10},{10,2},{3,11},{11,3},{4,12},{12,4},... | collective-permute-start | bytes 1032200 | tf_op jit(solution)/shard_map/ppermute | solution.py:39
  471.5 47.6 %collective-permute-start.96 = (bf16[184,1024]{1,0:T(8,128)(2,1)S(1)}, bf16[184,1024]{1,0:T(8,128)(2,1)S(1)}, u32[]{:S(2)}, u32[]{:S(2)}) collective-permute-start(bf16[184,1024]{1,0:T(8,128)(2,1)S(1)} %fusion.27), channel_id=1, source_target_pairs={{0,0},{2,16},{16,2},{18,18},{1,1},{3,17},{17,3},{19,19},{4,4},{6,2... | collective-permute-start | bytes 1130504 | tf_op jit(solution)/shard_map/ppermute | solution.py:46
  497.7 17.2 %collective-permute-start.100 = (f32[16,1024]{1,0:T(8,128)S(1)}, f32[16,1024]{1,0:T(8,128)S(1)}, u32[]{:S(2)}, u32[]{:S(2)}) collective-permute-start(f32[16,1024]{1,0:T(8,128)S(1)} %add.937), channel_id=1, source_target_pairs={{0,8},{8,0},{1,9},{9,1},{2,10},{10,2},{3,11},{11,3},{4,12},{12,4},... | collective-permute-start | bytes 196616 | tf_op jit(solution)/shard_map/ppermute | solution.py:39
  498.1 16.4 %collective-permute-start.91 = (bf16[2,112,768]{2,1,0:T(8,128)(2,1)S(1)}, bf16[2,112,768]{2,1,0:T(8,128)(2,1)S(1)}, u32[]{:S(2)}, u32[]{:S(2)}) collective-permute-start(bf16[2,112,768]{2,1,0:T(8,128)(2,1)S(1)} %get-tuple-element.529), channel_id=1, source_target_pairs={{0,8},{8,0},{1,9},{9,1},{2,10},{10,2},{3,11},{11,3},{4,12},{12,4},... | collective-permute-start | bytes 1032200 | tf_op jit(solution)/shard_map/ppermute | solution.py:39
  500.3 17.5 %collective-permute-start.93 = (bf16[192,1024]{1,0:T(8,128)(2,1)S(1)}, bf16[192,1024]{1,0:T(8,128)(2,1)S(1)}, u32[]{:S(2)}, u32[]{:S(2)}) collective-permute-start(bf16[192,1024]{1,0:T(8,128)(2,1)S(1)} %fusion.22), channel_id=1, source_target_pairs={{0,0},{2,16},{16,2},{18,18},{1,1},{3,17},{17,3},{19,19},{4,4},{6,2... | collective-permute-start | bytes 1179656 | tf_op jit(solution)/shard_map/ppermute | solution.py:46
  (188 other events, 1000.3 us)
